TPU v7x, 32 devices: a whole 2x2x4 slice. The times are simulated.
32 devices in a mesh: groups: 2 (over x), batch: 16 (over z, y, core), feat: 1.
Axes of the slice: x: 2, y: 2, z: 4, core: 2. Of those that a mesh axis runs over, the one named last changes fastest.
Arguments:
- view_one: bfloat16 [6144, 4096], P(('groups', 'batch'), 'feat'), parts along dimension 0, may hold values from -1000 to 1000, as said below
- view_two: bfloat16 [6144, 4096], P(('groups', 'batch'), 'feat'), parts along dimension 0, may hold values from -1000 to 1000
Outputs:
- grad_one: bfloat16 [6144, 4096], P(('groups', 'batch'), 'feat'), parts along dimension 0
- grad_two: bfloat16 [6144, 4096], P(('groups', 'batch'), 'feat'), parts along dimension 0
- loss_value: float32 [2], P('groups'), parts along dimension 0
There are 2 independent parts, one for each index of `groups`. A program takes and returns all parts, laid end to end along the dimension named above; each array names one. Nothing has to cross between parts.
Inputs may be any that keep to these rules, and one draw needn't show every extreme that they name: `view_one`: the two views are projector outputs of the same samples.
All inputs are finite; a program needn't handle non-finite values.
Results may differ from a plain program's by a relative error of at most 0.013.
Values may be sent and summed in bfloat16 or wider, within the bound.
No kernel may reach another device: no remote copies, remote signals or barrier semaphores. Data moves between devices by JAX's collectives and lax.ppermute only.
A program may use at most 128 MiB of HBM per device.

v0:
```python
import jax
import jax.numpy as jnp
from jax import lax
from jax.sharding import PartitionSpec as P

off_weight = 0.0051


def local_term(columns, full_two):
    return lax.dot_general(
        columns, full_two, (((0,), (0,)), ((), ())), preferred_element_type=jnp.float32
    )


def tile_grad(summed, row_base, samples):
    corr = summed / samples
    row_ids = row_base + lax.broadcasted_iota(jnp.int32, corr.shape, 0)
    col_ids = lax.broadcasted_iota(jnp.int32, corr.shape, 1)
    diag = row_ids == col_ids
    grad = jnp.where(diag, -2.0 * (1.0 - corr), 2.0 * off_weight * corr).astype(jnp.bfloat16)
    part_loss = jnp.sum(jnp.where(diag, (1.0 - corr) ** 2, off_weight * corr * corr))
    return (grad, part_loss)


def fold_step(columns, full_two, piece):
    contrib = lax.dot_general(
        full_two, piece, (((1,), (1,)), ((), ())), preferred_element_type=jnp.float32
    )
    back_mix = jnp.dot(columns, piece, preferred_element_type=jnp.float32)
    return (contrib, back_mix)


def finish(back, normed, inv, sum_back, sum_prod, samples):
    normal_f = normed.astype(jnp.float32)
    return (inv * (back - sum_back / samples - normal_f * sum_prod / samples)).astype(jnp.bfloat16)


def shards(view_one, view_two):
    rows, half_feat = view_one.shape
    batches = lax.axis_size("batch")
    samples = rows * batches
    values_one = view_one.astype(jnp.float32)
    values_two = view_two.astype(jnp.float32)
    sums = lax.psum(
        (
            jnp.sum(values_one, axis=0),
            jnp.sum(values_one * values_one, axis=0),
            jnp.sum(values_two, axis=0),
            jnp.sum(values_two * values_two, axis=0),
        ),
        "batch",
    )
    mean_one = sums[0] / samples
    mean_two = sums[2] / samples
    inv_one = 1.0 / jnp.sqrt(sums[1] / samples - mean_one * mean_one + 1e-05)
    inv_two = 1.0 / jnp.sqrt(sums[3] / samples - mean_two * mean_two + 1e-05)
    norm_one = ((values_one - mean_one) * inv_one).astype(jnp.bfloat16)
    norm_two = ((values_two - mean_two) * inv_two).astype(jnp.bfloat16)
    full_two = lax.all_gather(norm_two, "feat", axis=1, tiled=True)
    width = full_two.shape[1]
    tile = half_feat // batches
    row_base = lax.axis_index("feat") * half_feat + lax.axis_index("batch") * tile
    summed = lax.psum_scatter(
        local_term(norm_one, full_two), "batch", scatter_dimension=0, tiled=True
    )
    grad, part_loss = tile_grad(summed, row_base, samples)
    back_one, back_mix = fold_step(
        norm_one, full_two, lax.all_gather(grad, "batch", axis=0, tiled=True)
    )
    back_two = lax.psum_scatter(back_mix, "feat", scatter_dimension=1, tiled=True)
    loss = lax.psum(part_loss, ("batch", "feat")) / width
    norm_one_f = norm_one.astype(jnp.float32)
    norm_two_f = norm_two.astype(jnp.float32)
    stats = (
        lax.psum(jnp.sum(back_one, axis=0).astype(jnp.bfloat16), "batch").astype(jnp.float32),
        lax.psum(jnp.sum(back_one * norm_one_f, axis=0).astype(jnp.bfloat16), "batch").astype(
            jnp.float32
        ),
        lax.psum(jnp.sum(back_two, axis=0).astype(jnp.bfloat16), "batch").astype(jnp.float32),
        lax.psum(jnp.sum(back_two * norm_two_f, axis=0).astype(jnp.bfloat16), "batch").astype(
            jnp.float32
        ),
    )
    grad_one = finish(back_one, norm_one, inv_one, stats[0], stats[1], samples)
    grad_two = finish(back_two, norm_two, inv_two, stats[2], stats[3], samples)
    return (grad_one, grad_two, jnp.reshape(loss, (1,)))


def solution(mesh):
    placed = (P(("groups", "batch"), "feat"), P(("groups", "batch"), "feat"))
    return jax.shard_map(
        shards,
        mesh=mesh,
        in_specs=placed,
        out_specs=(P(("groups", "batch"), "feat"), P(("groups", "batch"), "feat"), P("groups")),
        check_vma=False,
    )
```

profile of v0, /device:TPU:1, one launch (start us, length us, event | category | flops | bytes accessed | tf_op | source)
XLA Modules:
  0.0 1039.5 jit_solution(18412247010652149829)
XLA Ops:
  7.2 0.0 copy-start
  7.2 0.0 all-reduce.4.cloned.1.call-start
  7.2 2.6 convert_reduce_fusion
  9.9 2.5 fusion.10
  12.3 0.0 all-reduce.4.cloned.1.call-update
  12.4 0.0 reduce-scatter.2.cloned.1.call-start
  12.4 87.6 %all-reduce.4.cloned.1.call-done = (f32[4096]{0:T(1024)}, f32[4096]{0:T(1024)}, f32[4096]{0:T(1024)}, f32[4096]{0:T(1024)}) async-done(((f32[4096]{0:T(1024)}, f32[4096]{0:T(1024)}, f32[4096]{0:T(1024)}, f32[4096]{0:T(1024)}), (f32[4096]{0:T(1024)}, f32[4096]{0:T(1024)}, f32[4096]{0:T(1024)}, f32[4096]{0:T(1024)})) %all-reduce.4.cloned.1.call-update) | async-done | bytes 65552 | tf_op jit(solution)/shard_map/psum | solution.py:44
  100.0 0.8 add_rsqrt_fusion.1
  100.8 0.0 copy-done.1
  100.8 0.0 copy-done
  100.8 23.2 %fusion.18 = f32[4096,4096]{1,0:T(8,128)} fusion(bf16[192,4096]{1,0:T(8,128)(2,1)S(1)} %copy-done.1, f32[4096]{0:T(1024)S(1)} %get-tuple-element.27, f32[4096]{0:T(1024)S(1)} %get-tuple-element.28, bf16[192,4096]{1,0:T(8,128)(2,1)S(1)} %copy-done, f32[4096]{0:T(1024)S(1)} %get-tuple-element.22, f32[4096]{0:T(1024)S(1)} %get-tuple-element.21), kind=kOutput, calls=%fused_computation.30 | convolution fusion | flops 6448742400 | bytes 70320128 | tf_op jit(solution)/shard_map/dot_general | solution.py:10
  124.0 0.0 reduce-scatter.2.cloned.1.call-update
  124.1 0.0 all-gather.2.cloned.1.call-start
  124.1 638.6 %reduce-scatter.2.cloned.1.call-done = f32[256,4096]{1,0:T(8,128)} async-done(((f32[4096,4096]{1,0:T(8,128)}), f32[256,4096]{1,0:T(8,128)}) %reduce-scatter.2.cloned.1.call-update) | async-done | bytes 4194320 | tf_op jit(solution)/shard_map/reduce_scatter | solution.py:63
  762.7 5.0 select_reduce_fusion
  767.7 0.0 all-gather.2.cloned.1.call-update
  767.7 30.7 %psum.71 = f32[]{:T(128)} all-reduce(f32[]{:T(128)} %get-tuple-element.19), channel_id=1, replica_groups=mesh['groups'=2,'batch'=16,'feat'=1] {'batch','feat'}, use_global_device_ids=true, to_apply=%region_18.19 | all-reduce | flops 1 | bytes 8 | tf_op jit(solution)/shard_map/psum | solution.py:71
  799.1 136.4 %all-gather.2.cloned.1.call-done = bf16[4096,4096]{1,0:T(8,128)(2,1)} async-done(((bf16[256,4096]{1,0:T(8,128)(2,1)}), bf16[4096,4096]{1,0:T(8,128)(2,1)}) %all-gather.2.cloned.1.call-update) | async-done | bytes 33554448 | tf_op jit(solution)/shard_map/all_gather | solution.py:68
  935.5 15.7 %fusion.23 = (bf16[4096]{0:T(1024)(128)(2,1)S(1)}, bf16[4096]{0:T(1024)(128)(2,1)S(1)}, f32[192,4096]{1,0:T(8,128)}) fusion(f32[4096]{0:T(1024)S(1)} %get-tuple-element.27, f32[4096]{0:T(1024)S(1)} %get-tuple-element.28, bf16[192,4096]{1,0:T(8,128)(2,1)S(1)} %copy-done.1, bf16[4096,4096]{1,0:T(8,128)(2,1)} %all-gather.2.cloned.1.call-done, ...), kind=kOutput, calls=%fused_computation.39 | convolution fusion | flops 6451879936 | bytes 39927808 | tf_op jit(solution)/shard_map/dot_general | solution.py:29
  951.2 18.5 %fusion.24 = (bf16[4096]{0:T(1024)(128)(2,1)S(1)}, bf16[4096]{0:T(1024)(128)(2,1)S(1)}, f32[192,4096]{1,0:T(8,128)}) fusion(f32[4096]{0:T(1024)S(1)} %get-tuple-element.21, f32[4096]{0:T(1024)S(1)} %get-tuple-element.22, bf16[192,4096]{1,0:T(8,128)(2,1)S(1)} %copy-done, bf16[4096,4096]{1,0:T(8,128)(2,1)} %all-gather.2.cloned.1.call-done, ...), kind=kOutput, calls=%fused_computation.40 | convolution fusion | flops 6451879936 | bytes 39927808 | tf_op jit(solution)/shard_map/dot_general | solution.py:26
  969.7 56.0 %all-reduce.1 = (bf16[4096]{0:T(1024)(128)(2,1)S(1)}, bf16[4096]{0:T(1024)(128)(2,1)S(1)}, bf16[4096]{0:T(1024)(128)(2,1)S(1)}, bf16[4096]{0:T(1024)(128)(2,1)S(1)}) all-reduce(bf16[4096]{0:T(1024)(128)(2,1)S(1)} %get-tuple-element.6, ...), channel_id=1, replica_groups=mesh['groups'=2,'batch'=16,'feat'=1] {'batch'}, use_global_device_ids=true, to_apply=%region_12.13 | all-reduce | flops 16384 | bytes 65536 | tf_op jit(solution)/shard_map/psum | solution.py:76
  1025.7 0.0 copy-start.2
  1025.7 4.1 fusion.9
  1029.8 2.0 fusion.4
  (7 shorter events, 0.0 us)
Async XLA Ops:
  7.2 93.7 %copy-start.1 = (bf16[192,4096]{1,0:T(8,128)(2,1)S(1)}, bf16[192,4096]{1,0:T(8,128)(2,1)}, u32[]{:S(2)}) copy-start(bf16[192,4096]{1,0:T(8,128)(2,1)} %param.3) | copy-start | bytes 4718596
  7.2 93.7 %copy-start = (bf16[192,4096]{1,0:T(8,128)(2,1)S(1)}, bf16[192,4096]{1,0:T(8,128)(2,1)}, u32[]{:S(2)}) copy-start(bf16[192,4096]{1,0:T(8,128)(2,1)} %param.2) | copy-start | bytes 4718596
  7.2 92.8 %all-reduce.4.cloned.1.call-start = ((), (), s32[]{:S(2)}) async-start(), calls=%async_computation.3 | async-start | bytes 131072 | tf_op jit(solution)/shard_map/psum | solution.py:44
  12.4 750.3 %reduce-scatter.2.cloned.1.call-start = ((), (), s32[]{:S(2)}) async-start(), calls=%async_computation.1 | async-start | bytes 71303168 | tf_op jit(solution)/shard_map/reduce_scatter | solution.py:63
  124.1 811.4 %all-gather.2.cloned.1.call-start = ((), (), s32[]{:S(2)}) async-start(), calls=%async_computation.2 | async-start | bytes 35651584 | tf_op jit(solution)/shard_map/all_gather | solution.py:68
  1025.7 4.1 copy-start.2
Sparse Core Ops, SparseCore 0:
  12.5 87.5 all-reduce.3
  124.2 638.4 reduce-scatter.1
  767.8 167.6 all-gather.1
where the time goes:
time: 1040 us
  waiting for transfers between devices  863 us (83%)
  blocking collectives  86.7 us (8%)
  matrix products  57.4 us (6%)
  other arithmetic  16.9 us (2%)
  between operations  15.6 us (2%)
    reduce_scatter x1, waiting for transfers between devices, shards(): lax.psum_scatter(local_term(norm_one, full_two), 'batch', scatter_dimensi...  639 us
    all_gather x1, waiting for transfers between devices, shards(): lax.all_gather(grad, 'batch', axis=0, tiled=True)  136 us
    psum x1, waiting for transfers between devices, shards(): lax.psum((jnp.sum(values_one, axis=0), jnp.sum(values_one * values_one, a...  87.6 us
    psum x1, blocking collectives, shards(): lax.psum(jnp.sum(back_one * norm_one_f, axis=0).astype(jnp.bfloat16), 'ba...  56 us
    psum x1, blocking collectives, shards(): loss = lax.psum(part_loss, ('batch', 'feat')) / width  30.7 us
    dot_general x1, matrix products, local_term(): lax.dot_general(columns, full_two, (((0,), (0,)), ((), ())), preferred_el...  23.2 us
  transfers between devices with their start and end apart: 3, of which 3 were waited for; matrix products, arithmetic and copies ran while one was open for 0% of the time, Pallas kernels for 0%

commit v1 on v0

--- a/solution.py
+++ b/solution.py
@@ -4,6 +4,7 @@
 from jax.sharding import PartitionSpec as P
 
 off_weight = 0.0051
+chunks = 8
 
 
 def local_term(columns, full_two):
@@ -86,10 +87,102 @@
     return (grad_one, grad_two, jnp.reshape(loss, (1,)))
 
 
+def normalize(raw, samples):
+    values = raw.astype(jnp.float32)
+    mean = jnp.sum(values, axis=0) / samples
+    var = jnp.sum(values * values, axis=0) / samples - mean * mean
+    inv = 1.0 / jnp.sqrt(var + 1e-05)
+    return (((values - mean) * inv).astype(jnp.bfloat16), inv)
+
+
+def corr_chunk(normed_one, normed_two, row_base, col_base, samples):
+    summed = local_term(normed_one, normed_two)
+    corr = summed / samples
+    row_ids = row_base + lax.broadcasted_iota(jnp.int32, corr.shape, 0)
+    col_ids = col_base + lax.broadcasted_iota(jnp.int32, corr.shape, 1)
+    diag = row_ids == col_ids
+    grad = jnp.where(diag, -2.0 * (1.0 - corr), 2.0 * off_weight * corr).astype(jnp.bfloat16)
+    loss = jnp.sum(jnp.where(diag, (1.0 - corr) ** 2, off_weight * corr * corr))
+    grad_f = grad.astype(jnp.float32)
+    total_one = jnp.sum(normed_one.astype(jnp.float32), axis=0)
+    total_two = jnp.sum(normed_two.astype(jnp.float32), axis=0)
+    prod = grad_f * summed
+    return (
+        grad,
+        loss,
+        jnp.sum(grad_f * total_two[None, :], axis=1),
+        jnp.sum(prod, axis=1),
+        jnp.sum(grad_f * total_one[:, None], axis=0),
+        jnp.sum(prod, axis=0),
+    )
+
+
+def pair_shards(view_one, view_two):
+    rows, width = view_one.shape
+    batches = lax.axis_size("batch")
+    samples = rows * batches
+    half = width // 2
+    place = lax.axis_index("batch")
+    side = place % 2
+    first_row = (place // 2) * 2 * rows
+    swap = [(i, i ^ 1) for i in range(batches)]
+
+    def mine(both):
+        return lax.dynamic_slice_in_dim(both, side * rows, rows, axis=0)
+
+    def theirs(both):
+        return lax.dynamic_slice_in_dim(both, (1 - side) * rows, rows, axis=0)
+
+    def pair_rows(full):
+        return lax.dynamic_slice_in_dim(full, first_row, 2 * rows, axis=0)
+
+    gathered_one = lax.all_gather(view_one, "batch", axis=0, tiled=True)
+    raw_one = lax.dynamic_slice_in_dim(gathered_one, side * half, half, axis=1)
+    norm_one, inv_one = normalize(raw_one, samples)
+    pair_one = pair_rows(norm_one)
+    step = width // chunks
+    back_one = jnp.zeros((2 * rows, half), jnp.float32)
+    sum_back = jnp.zeros((half,), jnp.float32)
+    sum_prod = jnp.zeros((half,), jnp.float32)
+    loss = jnp.zeros((), jnp.float32)
+    grad_two = []
+    for index in range(chunks):
+        base = index * step
+        raw_two = lax.all_gather(view_two[:, base : base + step], "batch", axis=0, tiled=True)
+        norm_two, inv_two = normalize(raw_two, samples)
+        pair_two = pair_rows(norm_two)
+        grad, part_loss, back_row, prod_row, back_col, prod_col = corr_chunk(
+            norm_one, norm_two, side * half, base, samples
+        )
+        loss = loss + part_loss
+        sum_back = sum_back + back_row
+        sum_prod = sum_prod + prod_row
+        back_one = back_one + lax.dot_general(
+            pair_two, grad, (((1,), (1,)), ((), ())), preferred_element_type=jnp.float32
+        )
+        back_two = jnp.dot(pair_one, grad, preferred_element_type=jnp.float32)
+        done_two = inv_two * (
+            back_two - back_col / samples - pair_two.astype(jnp.float32) * prod_col / samples
+        )
+        other = lax.ppermute(theirs(done_two), "batch", swap)
+        grad_two.append((mine(done_two) + other).astype(jnp.bfloat16))
+    done_one = finish(back_one, pair_one, inv_one, sum_back, sum_prod, samples)
+    own = mine(done_one)
+    other = lax.ppermute(theirs(done_one), "batch", swap)
+    grad_one = jnp.where(
+        side == 0,
+        jnp.concatenate([own, other], axis=1),
+        jnp.concatenate([other, own], axis=1),
+    )
+    loss = (loss + lax.ppermute(loss, "batch", swap)) / width
+    return (grad_one, jnp.concatenate(grad_two, axis=1), jnp.reshape(loss, (1,)))
+
+
 def solution(mesh):
     placed = (P(("groups", "batch"), "feat"), P(("groups", "batch"), "feat"))
+    paired = mesh.shape["feat"] == 1 and mesh.shape["batch"] % 2 == 0
     return jax.shard_map(
-        shards,
+        pair_shards if paired else shards,
         mesh=mesh,
         in_specs=placed,
         out_specs=(P(("groups", "batch"), "feat"), P(("groups", "batch"), "feat"), P("groups")),

time: 1040 us -> 711 us (0.68)
  waiting for transfers between devices: 863 us -> 452 us
  blocking collectives: 86.7 us -> 0 us
  matrix products: 57.4 us -> 135 us
  other arithmetic: 16.9 us -> 74.9 us
  local copies, waits for them, and re-layouts: 0.01 us -> 12.7 us
    reduce_scatter x1 -> x0, waiting for transfers between devices: 639 us -> none  [shards(): lax.psum_scatter(local_term(norm_one, full_two), 'batch', scatter_dimensi...]
    all_gather x1 -> x9, waiting for transfers between devices: 136 us -> 447 us  [the longest x8 345 us: pair_shards(): lax.all_gather(view_two[:, base:base + step], 'batch', axis=0, tiled=True)]
    psum x1 -> x0, waiting for transfers between devices: 87.6 us -> none  [shards(): lax.psum((jnp.sum(values_one, axis=0), jnp.sum(values_one * values_one, a...]
    psum x2 -> x0, blocking collectives: 86.7 us -> none  [the longest x1 56 us: shards(): lax.psum(jnp.sum(back_one * norm_one_f, axis=0).astype(jnp.bfloat16), 'ba...]
    dot_general x1 -> x8, matrix products: 23.2 us -> 92.1 us  [local_term(): lax.dot_general(columns, full_two, (((0,), (0,)), ((), ())), preferred_el...]
    reduce_sum x3 -> x18, other arithmetic: 10.1 us -> 62.5 us  [the longest x9 30.2 us: normalize(): mean = jnp.sum(values, axis=0) / samples]
    dot_general x2 -> x16, matrix products: 34.2 us -> 43 us  [the longest x8 24.3 us: pair_shards(): lax.dot_general(pair_two, grad, (((1,), (1,)), ((), ())), preferred_eleme...]
  transfers between devices with their start and end apart: 3 -> 19, of which waited for: 3 -> 9; matrix products, arithmetic and copies ran while one was open for 0% -> 21% of each run, Pallas kernels for 0% -> 0%
where the time goes in v1:
time: 711 us; the launch traced here: 701 us
  waiting for transfers between devices  452 us (64%)
  matrix products  135 us (19%)
  other arithmetic  74.9 us (11%)
  between operations  22.3 us (3%)
  local copies, waits for them, and re-layouts  12.7 us (2%)
    all_gather x8, waiting for transfers between devices, pair_shards(): lax.all_gather(view_two[:, base:base + step], 'batch', axis=0, tiled=True)  345 us
    all_gather x1, waiting for transfers between devices, pair_shards(): gathered_one = lax.all_gather(view_one, 'batch', axis=0, tiled=True)  102 us
    dot_general x8, matrix products, local_term(): lax.dot_general(columns, full_two, (((0,), (0,)), ((), ())), preferred_el...  92.1 us
    reduce_sum x9, other arithmetic, normalize(): mean = jnp.sum(values, axis=0) / samples  30.2 us
    dot_general x8, matrix products, pair_shards(): lax.dot_general(pair_two, grad, (((1,), (1,)), ((), ())), preferred_eleme...  24.3 us
    reduce_sum x8, other arithmetic, corr_chunk(): total_two = jnp.sum(normed_two.astype(jnp.float32), axis=0)  23.6 us
    dot_general x8, matrix products, pair_shards(): back_two = jnp.dot(pair_one, grad, preferred_element_type=jnp.float32)  18.7 us
  transfers between devices with their start and end apart: 19, of which 9 were waited for; matrix products, arithmetic and copies ran while one was open for 21% of the time, Pallas kernels for 0%

profile of v1, /device:TPU:1, one launch (start us, length us, event | category | flops | bytes accessed | tf_op | source)
XLA Modules:
  0.0 700.9 jit_solution(6756687308626978707)
XLA Ops:
  18.3 39.7 %all-gather.24.cloned.1.call-done = bf16[3072,512]{1,0:T(8,128)(2,1)} async-done(((bf16[192,512]{1,0:T(8,128)(2,1)}), bf16[3072,512]{1,0:T(8,128)(2,1)}) %all-gather.24.cloned.1.call-update) | async-done | bytes 3145744 | tf_op jit(solution)/shard_map/all_gather | solution.py:151
  60.8 43.5 %all-gather.12.cloned.1.call-done = bf16[3072,512]{1,0:T(8,128)(2,1)} async-done(((bf16[192,512]{1,0:T(8,128)(2,1)}), bf16[3072,512]{1,0:T(8,128)(2,1)}) %all-gather.12.cloned.1.call-update) | async-done | bytes 3145744 | tf_op jit(solution)/shard_map/all_gather | solution.py:151
  107.1 43.5 %all-gather.14.cloned.1.call-done = bf16[3072,512]{1,0:T(8,128)(2,1)} async-done(((bf16[192,512]{1,0:T(8,128)(2,1)}), bf16[3072,512]{1,0:T(8,128)(2,1)}) %all-gather.14.cloned.1.call-update) | async-done | bytes 3145744 | tf_op jit(solution)/shard_map/all_gather | solution.py:151
  153.4 43.4 %all-gather.16.cloned.1.call-done = bf16[3072,512]{1,0:T(8,128)(2,1)} async-done(((bf16[192,512]{1,0:T(8,128)(2,1)}), bf16[3072,512]{1,0:T(8,128)(2,1)}) %all-gather.16.cloned.1.call-update) | async-done | bytes 3145744 | tf_op jit(solution)/shard_map/all_gather | solution.py:151
  199.6 43.4 %all-gather.18.cloned.1.call-done = bf16[3072,512]{1,0:T(8,128)(2,1)} async-done(((bf16[192,512]{1,0:T(8,128)(2,1)}), bf16[3072,512]{1,0:T(8,128)(2,1)}) %all-gather.18.cloned.1.call-update) | async-done | bytes 3145744 | tf_op jit(solution)/shard_map/all_gather | solution.py:151
  245.8 43.4 %all-gather.20.cloned.1.call-done = bf16[3072,512]{1,0:T(8,128)(2,1)} async-done(((bf16[192,512]{1,0:T(8,128)(2,1)}), bf16[3072,512]{1,0:T(8,128)(2,1)}) %all-gather.20.cloned.1.call-update) | async-done | bytes 3145744 | tf_op jit(solution)/shard_map/all_gather | solution.py:151
  291.9 44.1 %all-gather.22.cloned.1.call-done = bf16[3072,512]{1,0:T(8,128)(2,1)} async-done(((bf16[192,512]{1,0:T(8,128)(2,1)}), bf16[3072,512]{1,0:T(8,128)(2,1)}) %all-gather.22.cloned.1.call-update) | async-done | bytes 3145744 | tf_op jit(solution)/shard_map/all_gather | solution.py:151
  338.8 44.1 %all-gather.26.cloned.1.call-done = bf16[3072,512]{1,0:T(8,128)(2,1)} async-done(((bf16[192,512]{1,0:T(8,128)(2,1)}), bf16[3072,512]{1,0:T(8,128)(2,1)}) %all-gather.26.cloned.1.call-update) | async-done | bytes 3145744 | tf_op jit(solution)/shard_map/all_gather | solution.py:151
  388.6 3.4 convert_reduce_fusion.17
  397.9 3.3 convert_reduce_fusion.14
  403.1 3.3 convert_reduce_fusion.12
  410.5 101.5 %all-gather.10.cloned.1.call-done = bf16[3072,4096]{1,0:T(8,128)(2,1)} async-done(((bf16[192,4096]{1,0:T(8,128)(2,1)}), bf16[3072,4096]{1,0:T(8,128)(2,1)}) %all-gather.10.cloned.1.call-update) | async-done | bytes 25165840 | tf_op jit(solution)/shard_map/all_gather | solution.py:139
  512.0 7.9 %convert_reduce_fusion = (f32[2048]{0:T(1024)S(1)}, f32[2048]{0:T(1024)S(1)}) fusion(bf16[3072,4096]{1,0:T(8,128)(2,1)} %all-gather.10.cloned.1.call-done, s32[]{:T(128)S(6)} %select_n.106), kind=kLoop, calls=%fused_computation.1 | loop fusion | flops 25161728 | bytes 12599300 | tf_op jit(solution)/shard_map/reduce_sum | solution.py:92
  519.9 8.7 %convert_reduce_fusion.1 = (f32[2048]{0:T(1024)S(1)}, bf16[3072,2048]{1,0:T(8,128)(2,1)S(1)}) fusion(f32[2048]{0:T(1024)S(1)} %get-tuple-element.134, f32[2048]{0:T(1024)S(1)} %get-tuple-element.133, bf16[3072,4096]{1,0:T(8,128)(2,1)} %all-gather.10.cloned.1.call-done, s32[]{:T(128)S(6)} %select_n.106), kind=kLoop, calls=%fused_computation.6 | loop fusion | flops 37746688 | bytes 25190404 | tf_op jit(solution)/shard_map/reduce_sum | solution.py:107
  528.6 8.2 %fusion.157 = f32[2048,512]{1,0:T(8,128)} fusion(bf16[3072,2048]{1,0:T(8,128)(2,1)S(1)} %get-tuple-element.86, bf16[3072,512]{1,0:T(8,128)(2,1)S(1)} %copy-done.14), kind=kOutput, calls=%fused_computation.282 | convolution fusion | flops 6442450944 | bytes 19922944 | tf_op jit(solution)/shard_map/dot_general | solution.py:11
  536.9 8.2 %fusion.156 = f32[2048,512]{1,0:T(8,128)} fusion(bf16[3072,2048]{1,0:T(8,128)(2,1)S(1)} %get-tuple-element.86, bf16[3072,512]{1,0:T(8,128)(2,1)S(1)} %get-tuple-element.75), kind=kOutput, calls=%fused_computation.281 | convolution fusion | flops 6442450944 | bytes 19922944 | tf_op jit(solution)/shard_map/dot_general | solution.py:11
  545.1 8.2 %fusion.155 = f32[2048,512]{1,0:T(8,128)} fusion(bf16[3072,2048]{1,0:T(8,128)(2,1)S(1)} %get-tuple-element.86, bf16[3072,512]{1,0:T(8,128)(2,1)S(1)} %copy-done.16), kind=kOutput, calls=%fused_computation.280 | convolution fusion | flops 6442450944 | bytes 19922944 | tf_op jit(solution)/shard_map/dot_general | solution.py:11
  553.4 8.2 %fusion.154 = f32[2048,512]{1,0:T(8,128)} fusion(bf16[3072,2048]{1,0:T(8,128)(2,1)S(1)} %get-tuple-element.86, bf16[3072,512]{1,0:T(8,128)(2,1)S(1)} %copy-done.18), kind=kOutput, calls=%fused_computation.279 | convolution fusion | flops 6442450944 | bytes 19922944 | tf_op jit(solution)/shard_map/dot_general | solution.py:11
  561.6 14.8 %fusion.59 = (f32[512]{0:T(512)S(1)}, f32[2048]{0:T(1024)S(1)}, f32[]{:T(128)}, f32[512]{0:T(512)S(1)}, f32[2048]{0:T(1024)}, /*index=5*/bf16[2048,512]{1,0:T(8,...) fusion(s32[512]{0:T(512)S(1)} %iota_add_fusion.7, ...), kind=kOutput, calls=%fused_computation.137 | convolution fusion | flops 6484383744 | bytes 24182792 | tf_op jit(solution)/shard_map/dot_general | solution.py:11
  586.1 8.2 %fusion.153 = f32[2048,512]{1,0:T(8,128)} fusion(bf16[3072,2048]{1,0:T(8,128)(2,1)S(1)} %get-tuple-element.86, bf16[3072,512]{1,0:T(8,128)(2,1)S(1)} %copy-done.15), kind=kOutput, calls=%fused_computation.278 | convolution fusion | flops 6442450944 | bytes 19922944 | tf_op jit(solution)/shard_map/dot_general | solution.py:11
  594.5 8.2 %fusion.158 = f32[2048,512]{1,0:T(8,128)} fusion(bf16[3072,2048]{1,0:T(8,128)(2,1)S(1)} %get-tuple-element.86, bf16[3072,512]{1,0:T(8,128)(2,1)S(1)} %copy-done.11), kind=kOutput, calls=%fused_computation.283 | convolution fusion | flops 6442450944 | bytes 19922944 | tf_op jit(solution)/shard_map/dot_general | solution.py:11
  602.8 27.9 %fusion.71 = (f32[512]{0:T(512)}, f32[2048]{0:T(1024)}, f32[]{:T(128)}, f32[512]{0:T(512)S(1)}, f32[2048]{0:T(1024)}, /*index=5*/bf16[2048,512]{1,0:T(8,128)(2,1...) fusion(s32[512]{0:T(512)S(1)} %copy-done.80, ...), kind=kOutput, calls=%fused_computation.149 | convolution fusion | flops 6568249344 | bytes 49444888 | tf_op jit(solution)/shard_map/dot_general | solution.py:11
  656.9 3.7 fusion.90
  672.9 5.4 multiply_convert_fusion
  (294 shorter events, 104.1 us)
Async XLA Ops:
  7.2 50.8 %all-gather.24.cloned.1.call-start = ((), (), s32[]{:S(2)}) async-start(), calls=%async_computation.7 | async-start | bytes 3342336 | tf_op jit(solution)/shard_map/all_gather | solution.py:151
  9.8 94.5 %all-gather.12.cloned.1.call-start = ((), (), s32[]{:S(2)}) async-start(), calls=%async_computation.1 | async-start | bytes 3342336 | tf_op jit(solution)/shard_map/all_gather | solution.py:151
  10.6 140.1 %all-gather.14.cloned.1.call-start = ((), (), s32[]{:S(2)}) async-start(), calls=%async_computation.2 | async-start | bytes 3342336 | tf_op jit(solution)/shard_map/all_gather | solution.py:151
  11.3 185.5 %all-gather.16.cloned.1.call-start = ((), (), s32[]{:S(2)}) async-start(), calls=%async_computation.3 | async-start | bytes 3342336 | tf_op jit(solution)/shard_map/all_gather | solution.py:151
  11.9 231.1 %all-gather.18.cloned.1.call-start = ((), (), s32[]{:S(2)}) async-start(), calls=%async_computation.4 | async-start | bytes 3342336 | tf_op jit(solution)/shard_map/all_gather | solution.py:151
  12.5 276.7 %all-gather.20.cloned.1.call-start = ((), (), s32[]{:S(2)}) async-start(), calls=%async_computation.5 | async-start | bytes 3342336 | tf_op jit(solution)/shard_map/all_gather | solution.py:151
  13.1 323.0 %all-gather.22.cloned.1.call-start = ((), (), s32[]{:S(2)}) async-start(), calls=%async_computation.6 | async-start | bytes 3342336 | tf_op jit(solution)/shard_map/all_gather | solution.py:151
  13.8 369.1 %all-gather.26.cloned.1.call-start = ((), (), s32[]{:S(2)}) async-start(), calls=%async_computation.8 | async-start | bytes 3342336 | tf_op jit(solution)/shard_map/all_gather | solution.py:151
  14.6 497.4 %all-gather.10.cloned.1.call-start = ((), (), s32[]{:S(2)}) async-start(), calls=%async_computation | async-start | bytes 26738688 | tf_op jit(solution)/shard_map/all_gather | solution.py:139
  18.3 543.3 %copy-start.69 = (s32[2048]{0:T(1024)}, s32[2048]{0:T(1024)S(1)}, u32[]{:S(2)}) copy-start(s32[2048]{0:T(1024)S(1)} %iota_add_fusion) | copy-start | bytes 24580
  60.8 325.1 %copy-start.42 = (f32[512]{0:T(512)}, f32[512]{0:T(512)S(1)}, u32[]{:S(2)}) copy-start(f32[512]{0:T(512)S(1)} %get-tuple-element.150) | copy-start | bytes 6148
  107.1 281.5 %copy-start.44 = (f32[512]{0:T(512)}, f32[512]{0:T(512)S(1)}, u32[]{:S(2)}) copy-start(f32[512]{0:T(512)S(1)} %get-tuple-element.140) | copy-start | bytes 6148
  245.8 152.1 %copy-start.48 = (f32[512]{0:T(512)}, f32[512]{0:T(512)S(1)}, u32[]{:S(2)}) copy-start(f32[512]{0:T(512)S(1)} %get-tuple-element.144) | copy-start | bytes 6148
  245.8 140.1 %copy-start.3 = (bf16[3072,512]{1,0:T(8,128)(2,1)S(1)}, bf16[3072,512]{1,0:T(8,128)(2,1)}, u32[]{:S(2)}) copy-start(bf16[3072,512]{1,0:T(8,128)(2,1)} %all-gather.24.cloned.1.call-done) | copy-start | bytes 9437188
  581.1 106.8 %collective-permute-start.3 = (f32[192,512]{1,0:T(8,128)}, f32[192,512]{1,0:T(8,128)S(1)}, u32[]{:S(2)}, u32[]{:S(2)}) collective-permute-start(f32[192,512]{1,0:T(8,128)} %constant_dynamic-slice_fusion.5), channel_id=1, source_target_pairs={{0,1},{1,0},{2,3},{3,2},{4,5},{5,4},{6,7},{7,6},{8,9},{9,8},{10,11... | collective-permute-start | bytes 1179656 | tf_op jit(solution)/shard_map/ppermute | solution.py:167
  585.9 100.6 %collective-permute-start.2 = (f32[192,512]{1,0:T(8,128)}, f32[192,512]{1,0:T(8,128)}, u32[]{:S(2)}, u32[]{:S(2)}) collective-permute-start(f32[192,512]{1,0:T(8,128)} %constant_dynamic-slice_fusion.6), channel_id=1, source_target_pairs={{0,1},{1,0},{2,3},{3,2},{4,5},{5,4},{6,7},{7,6},{8,9},{9,8},{10,11... | collective-permute-start | bytes 1179656 | tf_op jit(solution)/shard_map/ppermute | solution.py:167
  638.7 45.2 %collective-permute-start.9 = (f32[]{:T(128)}, f32[]{:T(128)}, u32[]{:S(2)}, u32[]{:S(2)}) collective-permute-start(f32[]{:T(128)} %add.410), channel_id=1, source_target_pairs={{0,1},{1,0},{2,3},{3,2},{4,5},{5,4},{6,7},{7,6},{8,9},{9,8},{10,11... | collective-permute-start | bytes 20 | tf_op jit(solution)/shard_map/ppermute | solution.py:177
  646.3 38.5 %collective-permute-start.1 = (f32[192,512]{1,0:T(8,128)}, f32[192,512]{1,0:T(8,128)}, u32[]{:S(2)}, u32[]{:S(2)}) collective-permute-start(f32[192,512]{1,0:T(8,128)} %constant_dynamic-slice_fusion.7), channel_id=1, source_target_pairs={{0,1},{1,0},{2,3},{3,2},{4,5},{5,4},{6,7},{7,6},{8,9},{9,8},{10,11... | collective-permute-start | bytes 1179656 | tf_op jit(solution)/shard_map/ppermute | solution.py:167
  652.4 35.9 %collective-permute-start.4 = (f32[192,512]{1,0:T(8,128)}, f32[192,512]{1,0:T(8,128)}, u32[]{:S(2)}, u32[]{:S(2)}) collective-permute-start(f32[192,512]{1,0:T(8,128)} %constant_dynamic-slice_fusion.4), channel_id=1, source_target_pairs={{0,1},{1,0},{2,3},{3,2},{4,5},{5,4},{6,7},{7,6},{8,9},{9,8},{10,11... | collective-permute-start | bytes 1179656 | tf_op jit(solution)/shard_map/ppermute | solution.py:167
  683.9 5.9 collective-permute-start.5
  684.8 6.0 collective-permute-start.6
  686.5 4.5 collective-permute-start.7
  687.9 3.1 collective-permute-start.8
  688.3 2.9 collective-permute-start
  (87 other events, 801.2 us)
Sparse Core Ops, SparseCore 0:
  10.3 47.6 all-gather.23
  60.3 43.9 all-gather.11
  106.6 43.9 all-gather.13
  152.8 43.9 all-gather.15
  199.0 43.9 all-gather.17
  245.1 43.9 all-gather.19
  292.0 43.9 all-gather.21
  338.9 43.9 all-gather.25
  384.5 127.3 all-gather.9

commit v2 on v0

--- a/solution.py
+++ b/solution.py
@@ -4,6 +4,7 @@
 from jax.sharding import PartitionSpec as P
 
 off_weight = 0.0051
+chunks = 4
 
 
 def local_term(columns, full_two):
@@ -86,10 +87,148 @@
     return (grad_one, grad_two, jnp.reshape(loss, (1,)))
 
 
+def normalize(raw, samples):
+    values = raw.astype(jnp.float32)
+    mean = jnp.sum(values, axis=0) / samples
+    var = jnp.sum(values * values, axis=0) / samples - mean * mean
+    inv = 1.0 / jnp.sqrt(var + 1e-05)
+    return (((values - mean) * inv).astype(jnp.bfloat16), inv)
+
+
+def corr_chunk(normed_one, normed_two, row_base, col_base, samples):
+    summed = local_term(normed_one, normed_two)
+    corr = summed / samples
+    row_ids = row_base + lax.broadcasted_iota(jnp.int32, corr.shape, 0)
+    col_ids = col_base + lax.broadcasted_iota(jnp.int32, corr.shape, 1)
+    diag = row_ids == col_ids
+    grad = jnp.where(diag, -2.0 * (1.0 - corr), 2.0 * off_weight * corr).astype(jnp.bfloat16)
+    loss = jnp.sum(jnp.where(diag, (1.0 - corr) ** 2, off_weight * corr * corr))
+    grad_f = grad.astype(jnp.float32)
+    total_one = jnp.sum(normed_one.astype(jnp.float32), axis=0)
+    total_two = jnp.sum(normed_two.astype(jnp.float32), axis=0)
+    prod = grad_f * summed
+    return (
+        grad,
+        loss,
+        jnp.sum(grad_f * total_two[None, :], axis=1),
+        jnp.sum(prod, axis=1),
+        jnp.sum(grad_f * total_one[:, None], axis=0),
+        jnp.sum(prod, axis=0),
+    )
+
+
+def pair_shards(view_one, view_two):
+    rows, width = view_one.shape
+    batches = lax.axis_size("batch")
+    samples = rows * batches
+    half = width // 2
+    step = half // chunks
+    chips = batches // 2
+    side = lax.axis_index("batch") % 2
+    swap = [(i, i ^ 1) for i in range(batches)]
+    line = chips // 2
+    order = [2 * r for r in range(line)] + [2 * r + 1 for r in reversed(range(line))]
+    ahead = [
+        (2 * order[r] + c, 2 * order[(r + 1) % chips] + c) for r in range(chips) for c in range(2)
+    ]
+    behind = [(there, here) for here, there in ahead]
+
+    def mine(both, axis=0):
+        size = both.shape[axis] // 2
+        return lax.dynamic_slice_in_dim(both, side * size, size, axis=axis)
+
+    def theirs(both, axis=0):
+        size = both.shape[axis] // 2
+        return lax.dynamic_slice_in_dim(both, (1 - side) * size, size, axis=axis)
+
+    def in_order(own, other, axis):
+        return jnp.where(
+            side == 0,
+            jnp.concatenate([own, other], axis=axis),
+            jnp.concatenate([other, own], axis=axis),
+        )
+
+    def chip_rows(view):
+        other = lax.ppermute(theirs(view, 1), "batch", swap)
+        return in_order(mine(view, 1), other, 0)
+
+    def ring(block, after):
+        if after is not None:
+            block, _ = lax.optimization_barrier((block, after))
+        up = down = block
+        parts = [block]
+        for hop in range(1, chips // 2):
+            up = lax.ppermute(up, "batch", ahead)
+            down = lax.ppermute(down, "batch", behind)
+            parts += [up, down]
+        parts.append(lax.ppermute(up[:rows], "batch", ahead))
+        parts.append(lax.ppermute(down[rows:], "batch", behind))
+        return (parts, (parts[3], parts[4]))
+
+    block_one = chip_rows(view_one)
+    block_two = chip_rows(view_two)
+    after = None
+    norms, invs = [], []
+    for index in range(chunks):
+        piece = block_one[:, index * step : (index + 1) * step]
+        parts, after = ring(piece, after)
+        norm, inv = normalize(jnp.concatenate(parts, axis=0), samples)
+        norms.append(norm)
+        invs.append(inv)
+    norm_one = jnp.concatenate(norms, axis=1)
+    inv_one = jnp.concatenate(invs)
+    pair_one = norm_one[: 2 * rows]
+    back_one = jnp.zeros((2 * rows, half), jnp.float32)
+    sum_back = jnp.zeros((half,), jnp.float32)
+    sum_prod = jnp.zeros((half,), jnp.float32)
+    loss = jnp.zeros((), jnp.float32)
+    grad_own, grad_far = [], []
+    for index in range(chunks):
+        piece = block_two[:, index * step : (index + 1) * step]
+        parts, after = ring(piece, after)
+        own_norm, own_inv = normalize(jnp.concatenate(parts, axis=0), samples)
+        far_norm = lax.ppermute(own_norm, "batch", swap)
+        far_inv = lax.ppermute(own_inv, "batch", swap)
+        for norm_two, inv_two, column_half, grads in (
+            (own_norm, own_inv, side, grad_own),
+            (far_norm, far_inv, 1 - side, grad_far),
+        ):
+            base = column_half * half + index * step
+            pair_two = norm_two[: 2 * rows]
+            grad, part_loss, back_row, prod_row, back_col, prod_col = corr_chunk(
+                norm_one, norm_two, side * half, base, samples
+            )
+            loss = loss + part_loss
+            sum_back = sum_back + back_row
+            sum_prod = sum_prod + prod_row
+            back_one = back_one + lax.dot_general(
+                pair_two, grad, (((1,), (1,)), ((), ())), preferred_element_type=jnp.float32
+            )
+            back_two = jnp.dot(pair_one, grad, preferred_element_type=jnp.float32)
+            grads.append(
+                inv_two
+                * (back_two - back_col / samples - pair_two.astype(jnp.float32) * prod_col / samples)
+            )
+    done_one = finish(back_one, pair_one, inv_one, sum_back, sum_prod, samples)
+    grad_one = in_order(mine(done_one), lax.ppermute(theirs(done_one), "batch", swap), 1)
+    columns_own, columns_far = [], []
+    for index in range(chunks):
+        sent_far = lax.ppermute(theirs(grad_far[index]), "batch", swap)
+        sent_own = lax.ppermute(theirs(grad_own[index]), "batch", swap)
+        columns_own.append((mine(grad_own[index]) + sent_far).astype(jnp.bfloat16))
+        columns_far.append((mine(grad_far[index]) + sent_own).astype(jnp.bfloat16))
+    grad_two = in_order(
+        jnp.concatenate(columns_own, axis=1), jnp.concatenate(columns_far, axis=1), 1
+    )
+    loss = (loss + lax.ppermute(loss, "batch", swap)) / width
+    return (grad_one, grad_two, jnp.reshape(loss, (1,)))
+
+
 def solution(mesh):
     placed = (P(("groups", "batch"), "feat"), P(("groups", "batch"), "feat"))
+    paired = mesh.shape["feat"] == 1 and mesh.shape["batch"] % 4 == 0
     return jax.shard_map(
-        shards,
+        pair_shards if paired else shards,
         mesh=mesh,
         in_specs=placed,
         out_specs=(P(("groups", "batch"), "feat"), P(("groups", "batch"), "feat"), P("groups")),

time: 1040 us -> 470 us (0.45)
  waiting for transfers between devices: 863 us -> 144 us
  matrix products: 57.4 us -> 151 us
  starting transfers between devices: 0.12 us -> 89.9 us
  blocking collectives: 86.7 us -> 0 us
  other arithmetic: 16.9 us -> 52.1 us
  local copies, waits for them, and re-layouts: 0.01 us -> 15.1 us
    reduce_scatter x1 -> x0, waiting for transfers between devices: 639 us -> none  [shards(): lax.psum_scatter(local_term(norm_one, full_two), 'batch', scatter_dimensi...]
    ppermute x0 -> x84, waiting for transfers between devices: none -> 144 us  [the longest x24 99.9 us: ring(): down = lax.ppermute(down, 'batch', behind)]
    all_gather x1 -> x0, waiting for transfers between devices: 136 us -> none  [shards(): lax.all_gather(grad, 'batch', axis=0, tiled=True)]
    ppermute x0 -> x84, starting transfers between devices: none -> 89.9 us  [the longest x24 23.1 us: ring(): down = lax.ppermute(down, 'batch', behind)]
    psum x1 -> x0, waiting for transfers between devices: 87.6 us -> none  [shards(): lax.psum((jnp.sum(values_one, axis=0), jnp.sum(values_one * values_one, a...]
    psum x2 -> x0, blocking collectives: 86.7 us -> none  [the longest x1 56 us: shards(): lax.psum(jnp.sum(back_one * norm_one_f, axis=0).astype(jnp.bfloat16), 'ba...]
    dot_general x1 -> x8, matrix products: 23.2 us -> 103 us  [local_term(): lax.dot_general(columns, full_two, (((0,), (0,)), ((), ())), preferred_el...]
    reduce_sum x3 -> x17, other arithmetic: 10.1 us -> 25.5 us  [the longest x8 15.5 us: corr_chunk(): total_two = jnp.sum(normed_two.astype(jnp.float32), axis=0)]
  transfers between devices with their start and end apart: 3 -> 84, of which waited for: 3 -> 31; matrix products, arithmetic and copies ran while one was open for 0% -> 45% of each run, Pallas kernels for 0% -> 0%
where the time goes in v2:
time: 470 us; the launch traced here: 461 us
  matrix products  151 us (32%)
  waiting for transfers between devices  144 us (31%)
  starting transfers between devices  89.9 us (19%)
  other arithmetic  52.1 us (11%)
  local copies, waits for them, and re-layouts  15.1 us (3%)
  between operations  9.23 us (2%)
    dot_general x8, matrix products, local_term(): lax.dot_general(columns, full_two, (((0,), (0,)), ((), ())), preferred_el...  103 us
    ppermute x24, waiting for transfers between devices, ring(): down = lax.ppermute(down, 'batch', behind)  99.9 us
    ppermute x8, waiting for transfers between devices, ring(): parts.append(lax.ppermute(up[:rows], 'batch', ahead))  34.1 us
    dot_general x8, matrix products, pair_shards(): lax.dot_general(pair_two, grad, (((1,), (1,)), ((), ())), preferred_eleme...  31.4 us
    ppermute x24, starting transfers between devices, ring(): down = lax.ppermute(down, 'batch', behind)  23.1 us
    ppermute x4, starting transfers between devices, pair_shards(): far_norm = lax.ppermute(own_norm, 'batch', swap)  17.6 us
    ppermute x4, starting transfers between devices, pair_shards(): far_inv = lax.ppermute(own_inv, 'batch', swap)  17.4 us
    dot_general x8, matrix products, pair_shards(): back_two = jnp.dot(pair_one, grad, preferred_element_type=jnp.float32)  16.9 us
  transfers between devices with their start and end apart: 84, of which 31 were waited for; matrix products, arithmetic and copies ran while one was open for 45% of the time, Pallas kernels for 0%

profile of v2, /device:TPU:1, one launch (start us, length us, event | category | flops | bytes accessed | tf_op | source)
XLA Modules:
  0.0 460.9 jit_solution(18315897216809846899)
XLA Ops:
  14.3 7.6 %collective-permute-done.2 = bf16[384,512]{1,0:T(8,128)(2,1)S(1)} collective-permute-done((bf16[384,512]{1,0:T(8,128)(2,1)S(1)}, bf16[384,512]{1,0:T(8,128)(2,1)S(1)}, u32[]{:S(2)}, u32[]{:S(2)}) %collective-permute-start.2) | collective-permute-done | bytes 393248 | tf_op jit(solution)/shard_map/ppermute | solution.py:162
  23.5 8.3 %collective-permute-done.4 = bf16[384,512]{1,0:T(8,128)(2,1)S(1)} collective-permute-done((bf16[384,512]{1,0:T(8,128)(2,1)S(1)}, bf16[384,512]{1,0:T(8,128)(2,1)S(1)}, u32[]{:S(2)}, u32[]{:S(2)}) %collective-permute-start.4) | collective-permute-done | bytes 393248 | tf_op jit(solution)/shard_map/ppermute | solution.py:162
  35.5 13.8 %collective-permute-done.6 = bf16[384,512]{1,0:T(8,128)(2,1)S(1)} collective-permute-done((bf16[384,512]{1,0:T(8,128)(2,1)S(1)}, bf16[384,512]{1,0:T(8,128)(2,1)S(1)}, u32[]{:S(2)}, u32[]{:S(2)}) %collective-permute-start.6) | collective-permute-done | bytes 393248 | tf_op jit(solution)/shard_map/ppermute | solution.py:162
  56.2 4.9 %collective-permute-done.12 = bf16[384,512]{1,0:T(8,128)(2,1)S(1)} collective-permute-done((bf16[384,512]{1,0:T(8,128)(2,1)S(1)}, bf16[384,512]{1,0:T(8,128)(2,1)S(1)}, u32[]{:S(2)}, u32[]{:S(2)}) %collective-permute-start.12) | collective-permute-done | bytes 393248 | tf_op jit(solution)/shard_map/ppermute | solution.py:162
  66.0 10.9 %collective-permute-done.14 = bf16[384,512]{1,0:T(8,128)(2,1)S(1)} collective-permute-done((bf16[384,512]{1,0:T(8,128)(2,1)S(1)}, bf16[384,512]{1,0:T(8,128)(2,1)S(1)}, u32[]{:S(2)}, u32[]{:S(2)}) %collective-permute-start.14) | collective-permute-done | bytes 393248 | tf_op jit(solution)/shard_map/ppermute | solution.py:162
  93.2 10.9 %collective-permute-done.22 = bf16[384,512]{1,0:T(8,128)(2,1)S(1)} collective-permute-done((bf16[384,512]{1,0:T(8,128)(2,1)S(1)}, bf16[384,512]{1,0:T(8,128)(2,1)S(1)}, u32[]{:S(2)}, u32[]{:S(2)}) %collective-permute-start.22) | collective-permute-done | bytes 393248 | tf_op jit(solution)/shard_map/ppermute | solution.py:162
  122.5 11.1 %collective-permute-done.30 = bf16[384,512]{1,0:T(8,128)(2,1)S(1)} collective-permute-done((bf16[384,512]{1,0:T(8,128)(2,1)S(1)}, bf16[384,512]{1,0:T(8,128)(2,1)S(1)}, u32[]{:S(2)}, u32[]{:S(2)}) %collective-permute-start.30) | collective-permute-done | bytes 393248 | tf_op jit(solution)/shard_map/ppermute | solution.py:162
  137.8 5.0 %collective-permute-done.31 = bf16[192,512]{1,0:T(8,128)(2,1)S(1)} collective-permute-done((bf16[192,512]{1,0:T(8,128)(2,1)S(1)}, bf16[192,512]{1,0:T(8,128)(2,1)S(1)}, u32[]{:S(2)}, u32[]{:S(2)}) %collective-permute-start.31) | collective-permute-done | bytes 196640 | tf_op jit(solution)/shard_map/ppermute | solution.py:164
  154.9 13.8 %collective-permute-done.39 = bf16[384,512]{1,0:T(8,128)(2,1)S(1)} collective-permute-done((bf16[384,512]{1,0:T(8,128)(2,1)S(1)}, bf16[384,512]{1,0:T(8,128)(2,1)S(1)}, u32[]{:S(2)}, u32[]{:S(2)}) %collective-permute-start.39) | collective-permute-done | bytes 393248 | tf_op jit(solution)/shard_map/ppermute | solution.py:162
  177.2 17.2 %collective-permute-start.71 = (f32[512]{0:T(512)S(1)}, f32[512]{0:T(512)}, u32[]{:S(2)}, u32[]{:S(2)}) collective-permute-start(f32[512]{0:T(512)S(1)} %get-tuple-element.159), channel_id=1, source_target_pairs={{0,1},{1,0},{2,3},{3,2},{4,5},{5,4},{6,7},{7,6},{8,9},{9,8},{10,11... | collective-permute-start | bytes 6152 | tf_op jit(solution)/shard_map/ppermute | solution.py:191
  198.6 8.2 %fusion.123 = f32[2048,512]{1,0:T(8,128)} fusion(bf16[3072,2048]{1,0:T(8,128)(2,1)S(1)} %get-tuple-element.106, bf16[3072,512]{1,0:T(8,128)(2,1)S(1)} %get-tuple-element.92), kind=kOutput, calls=%fused_computation.346 | convolution fusion | flops 6442450944 | bytes 19922944 | tf_op jit(solution)/shard_map/dot_general | solution.py:11
  206.9 5.8 %collective-permute-done.48 = bf16[384,512]{1,0:T(8,128)(2,1)S(1)} collective-permute-done((bf16[384,512]{1,0:T(8,128)(2,1)S(1)}, bf16[384,512]{1,0:T(8,128)(2,1)S(1)}, u32[]{:S(2)}, u32[]{:S(2)}) %collective-permute-start.48) | collective-permute-done | bytes 393248 | tf_op jit(solution)/shard_map/ppermute | solution.py:162
  226.5 10.6 %fusion.124 = f32[2048,512]{1,0:T(8,128)} fusion(bf16[3072,2048]{1,0:T(8,128)(2,1)S(1)} %get-tuple-element.106, bf16[3072,512]{1,0:T(8,128)(2,1)} %get-tuple-element.95), kind=kOutput, calls=%fused_computation.347 | convolution fusion | flops 6442450944 | bytes 19922944 | tf_op jit(solution)/shard_map/dot_general | solution.py:11
  238.7 5.7 %collective-permute-start.42 = (bf16[3072,512]{1,0:T(8,128)(2,1)S(1)}, bf16[3072,512]{1,0:T(8,128)(2,1)S(1)}, u32[]{:S(2)}, u32[]{:S(2)}) collective-permute-start(bf16[3072,512]{1,0:T(8,128)(2,1)S(1)} %get-tuple-element.92), channel_id=1, source_target_pairs={{0,1},{1,0},{2,3},{3,2},{4,5},{5,4},{6,7},{7,6},{8,9},{9,8},{10,11... | collective-permute-start | bytes 9437192 | tf_op jit(solution)/shard_map/ppermute | solution.py:190
  246.3 5.4 %collective-permute-done.58 = bf16[192,512]{1,0:T(8,128)(2,1)S(1)} collective-permute-done((bf16[192,512]{1,0:T(8,128)(2,1)S(1)}, bf16[192,512]{1,0:T(8,128)(2,1)S(1)}, u32[]{:S(2)}, u32[]{:S(2)}) %collective-permute-start.58) | collective-permute-done | bytes 196640 | tf_op jit(solution)/shard_map/ppermute | solution.py:164
  261.9 10.7 %fusion.126 = f32[2048,512]{1,0:T(8,128)} fusion(bf16[3072,2048]{1,0:T(8,128)(2,1)S(1)} %get-tuple-element.106, bf16[3072,512]{1,0:T(8,128)(2,1)} %get-tuple-element.99), kind=kOutput, calls=%fused_computation.349 | convolution fusion | flops 6442450944 | bytes 19922944 | tf_op jit(solution)/shard_map/dot_general | solution.py:11
  274.5 5.5 %collective-permute-done.67 = bf16[192,512]{1,0:T(8,128)(2,1)S(1)} collective-permute-done((bf16[192,512]{1,0:T(8,128)(2,1)S(1)}, bf16[192,512]{1,0:T(8,128)(2,1)S(1)}, u32[]{:S(2)}, u32[]{:S(2)}) %collective-permute-start.67) | collective-permute-done | bytes 196640 | tf_op jit(solution)/shard_map/ppermute | solution.py:164
  280.1 10.9 %collective-permute-start.51 = (bf16[3072,512]{1,0:T(8,128)(2,1)}, bf16[3072,512]{1,0:T(8,128)(2,1)}, u32[]{:S(2)}, u32[]{:S(2)}) collective-permute-start(bf16[3072,512]{1,0:T(8,128)(2,1)} %get-tuple-element.95), channel_id=1, source_target_pairs={{0,1},{1,0},{2,3},{3,2},{4,5},{5,4},{6,7},{7,6},{8,9},{9,8},{10,11... | collective-permute-start | bytes 9437192 | tf_op jit(solution)/shard_map/ppermute | solution.py:190
  293.8 8.2 %fusion.128 = f32[2048,512]{1,0:T(8,128)} fusion(bf16[3072,2048]{1,0:T(8,128)(2,1)S(1)} %get-tuple-element.106, bf16[3072,512]{1,0:T(8,128)(2,1)S(1)} %get-tuple-element.103), kind=kOutput, calls=%fused_computation.351 | convolution fusion | flops 6442450944 | bytes 19922944 | tf_op jit(solution)/shard_map/dot_general | solution.py:11
  303.0 17.5 %fusion.58 = (f32[512]{0:T(512)S(1)}, f32[2048]{0:T(1024)}, f32[]{:T(128)}, f32[512]{0:T(512)S(1)}, f32[2048]{0:T(1024)}, /*index=5*/bf16[2048,512]{1,0:T(8,128)...) fusion(s32[512]{0:T(512)S(1)} %iota_add_fusion.7, ...), kind=kOutput, calls=%fused_computation.133 | convolution fusion | flops 6505350144 | bytes 30498828 | tf_op jit(solution)/shard_map/dot_general | solution.py:11
  343.5 12.3 %fusion.125 = f32[2048,512]{1,0:T(8,128)} fusion(bf16[3072,2048]{1,0:T(8,128)(2,1)} %copy-done, bf16[3072,512]{1,0:T(8,128)(2,1)} %collective-permute-done.51), kind=kOutput, calls=%fused_computation.348 | convolution fusion | flops 6442450944 | bytes 19922944 | tf_op jit(solution)/shard_map/dot_general | solution.py:11
  358.3 10.7 %fusion.127 = f32[2048,512]{1,0:T(8,128)} fusion(bf16[3072,2048]{1,0:T(8,128)(2,1)S(1)} %bitcast.34, bf16[3072,512]{1,0:T(8,128)(2,1)} %collective-permute-done.60), kind=kOutput, calls=%fused_computation.350 | convolution fusion | flops 6442450944 | bytes 19922944 | tf_op jit(solution)/shard_map/dot_general | solution.py:11
  370.1 24.4 %fusion.70 = (f32[512]{0:T(512)}, f32[2048]{0:T(1024)S(1)}, f32[]{:T(128)}, f32[512]{0:T(512)S(1)}, f32[2048]{0:T(1024)S(1)}, /*index=5*/bf16[2048,512]{1,0:T(8,...) fusion(s32[512]{0:T(512)S(1)} %copy-done.44, ...), kind=kOutput, calls=%fused_computation.145 | convolution fusion | flops 6547282944 | bytes 43130900 | tf_op jit(solution)/shard_map/dot_general | solution.py:11
  413.1 8.3 %multiply_convert_fusion = bf16[384,2048]{1,0:T(8,128)(2,1)S(1)} fusion(f32[384,2048]{1,0:T(8,128)} %fusion.88, f32[384,2048]{1,0:T(8,128)} %fusion.90, f32[384,2048]{1,0:T(8,128)} %fusion.92, f32[384,2048]{1,0:T(8,128)} %fusion.94, f32[384,2048]{1,0:T(8,128)S(1)} %copy-done.1, f32[384,2048]{1,0:T(8,128)S(1)} %fusion.100, f32[384,2048]{1,0:T(8,128)} %fusion.98, ...), kind=kOutput, calls=%fused_computation.130 | convolution fusion | flops 816316416 | bytes 27680768 | tf_op jit(solution)/shard_map/dot_general | solution.py:204
  (437 shorter events, 203.9 us)
Async XLA Ops:
  32.4 18.5 %collective-permute-start.10 = (bf16[384,512]{1,0:T(8,128)(2,1)S(1)}, bf16[384,512]{1,0:T(8,128)(2,1)S(1)}, u32[]{:S(2)}, u32[]{:S(2)}) collective-permute-start(bf16[384,512]{1,0:T(8,128)(2,1)S(1)} %get-tuple-element.10), channel_id=1, source_target_pairs={{4,0},{5,1},{8,4},{9,5},{12,8},{13,9},{14,12},{15,13},{10,14},{11,... | collective-permute-start | bytes 1179656 | tf_op jit(solution)/shard_map/ppermute | solution.py:162
  33.7 18.5 %collective-permute-start.9 = (bf16[384,512]{1,0:T(8,128)(2,1)S(1)}, bf16[384,512]{1,0:T(8,128)(2,1)S(1)}, u32[]{:S(2)}, u32[]{:S(2)}) collective-permute-start(bf16[384,512]{1,0:T(8,128)(2,1)S(1)} %get-tuple-element.10), channel_id=1, source_target_pairs={{0,4},{1,5},{4,8},{5,9},{8,12},{9,13},{12,14},{13,15},{14,10},{15,... | collective-permute-start | bytes 1179656 | tf_op jit(solution)/shard_map/ppermute | solution.py:161
  89.4 16.4 %collective-permute-start.26 = (bf16[384,512]{1,0:T(8,128)(2,1)S(1)}, bf16[384,512]{1,0:T(8,128)(2,1)S(1)}, u32[]{:S(2)}, u32[]{:S(2)}) collective-permute-start(bf16[384,512]{1,0:T(8,128)(2,1)S(1)} %get-tuple-element.12), channel_id=1, source_target_pairs={{4,0},{5,1},{8,4},{9,5},{12,8},{13,9},{14,12},{15,13},{10,14},{11,... | collective-permute-start | bytes 1179656 | tf_op jit(solution)/shard_map/ppermute | solution.py:162
  118.5 17.4 %collective-permute-start.35 = (bf16[384,512]{1,0:T(8,128)(2,1)S(1)}, bf16[384,512]{1,0:T(8,128)(2,1)S(1)}, u32[]{:S(2)}, u32[]{:S(2)}) collective-permute-start(bf16[384,512]{1,0:T(8,128)(2,1)S(1)} %get-tuple-element.13), channel_id=1, source_target_pairs={{4,0},{5,1},{8,4},{9,5},{12,8},{13,9},{14,12},{15,13},{10,14},{11,... | collective-permute-start | bytes 1179656 | tf_op jit(solution)/shard_map/ppermute | solution.py:162
  120.2 17.3 %collective-permute-start.34 = (bf16[384,512]{1,0:T(8,128)(2,1)S(1)}, bf16[384,512]{1,0:T(8,128)(2,1)S(1)}, u32[]{:S(2)}, u32[]{:S(2)}) collective-permute-start(bf16[384,512]{1,0:T(8,128)(2,1)S(1)} %get-tuple-element.13), channel_id=1, source_target_pairs={{0,4},{1,5},{4,8},{5,9},{8,12},{9,13},{12,14},{13,15},{14,10},{15,... | collective-permute-start | bytes 1179656 | tf_op jit(solution)/shard_map/ppermute | solution.py:161
  151.3 19.0 %collective-permute-start.44 = (bf16[384,512]{1,0:T(8,128)(2,1)S(1)}, bf16[384,512]{1,0:T(8,128)(2,1)S(1)}, u32[]{:S(2)}, u32[]{:S(2)}) collective-permute-start(bf16[384,512]{1,0:T(8,128)(2,1)S(1)} %get-tuple-element.14), channel_id=1, source_target_pairs={{4,0},{5,1},{8,4},{9,5},{12,8},{13,9},{14,12},{15,13},{10,14},{11,... | collective-permute-start | bytes 1179656 | tf_op jit(solution)/shard_map/ppermute | solution.py:162
  152.2 18.8 %collective-permute-start.43 = (bf16[384,512]{1,0:T(8,128)(2,1)S(1)}, bf16[384,512]{1,0:T(8,128)(2,1)S(1)}, u32[]{:S(2)}, u32[]{:S(2)}) collective-permute-start(bf16[384,512]{1,0:T(8,128)(2,1)S(1)} %get-tuple-element.14), channel_id=1, source_target_pairs={{0,4},{1,5},{4,8},{5,9},{8,12},{9,13},{12,14},{13,15},{14,10},{15,... | collective-permute-start | bytes 1179656 | tf_op jit(solution)/shard_map/ppermute | solution.py:161
  170.3 25.2 %collective-permute-start.46 = (bf16[384,512]{1,0:T(8,128)(2,1)S(1)}, bf16[384,512]{1,0:T(8,128)(2,1)S(1)}, u32[]{:S(2)}, u32[]{:S(2)}) collective-permute-start(bf16[384,512]{1,0:T(8,128)(2,1)S(1)} %collective-permute-done.44), channel_id=1, source_target_pairs={{4,0},{5,1},{8,4},{9,5},{12,8},{13,9},{14,12},{15,13},{10,14},{11,... | collective-permute-start | bytes 1179656 | tf_op jit(solution)/shard_map/ppermute | solution.py:162
  171.0 24.6 %collective-permute-start.45 = (bf16[384,512]{1,0:T(8,128)(2,1)S(1)}, bf16[384,512]{1,0:T(8,128)(2,1)S(1)}, u32[]{:S(2)}, u32[]{:S(2)}) collective-permute-start(bf16[384,512]{1,0:T(8,128)(2,1)S(1)} %collective-permute-done.43), channel_id=1, source_target_pairs={{0,4},{1,5},{4,8},{5,9},{8,12},{9,13},{12,14},{13,15},{14,10},{15,... | collective-permute-start | bytes 1179656 | tf_op jit(solution)/shard_map/ppermute | solution.py:161
  177.2 152.0 %collective-permute-start.71 = (f32[512]{0:T(512)S(1)}, f32[512]{0:T(512)}, u32[]{:S(2)}, u32[]{:S(2)}) collective-permute-start(f32[512]{0:T(512)S(1)} %get-tuple-element.159), channel_id=1, source_target_pairs={{0,1},{1,0},{2,3},{3,2},{4,5},{5,4},{6,7},{7,6},{8,9},{9,8},{10,11... | collective-permute-start | bytes 6152 | tf_op jit(solution)/shard_map/ppermute | solution.py:191
  195.6 18.7 %collective-permute-start.53 = (bf16[384,512]{1,0:T(8,128)(2,1)S(1)}, bf16[384,512]{1,0:T(8,128)(2,1)S(1)}, u32[]{:S(2)}, u32[]{:S(2)}) collective-permute-start(bf16[384,512]{1,0:T(8,128)(2,1)S(1)} %get-tuple-element.15), channel_id=1, source_target_pairs={{4,0},{5,1},{8,4},{9,5},{12,8},{13,9},{14,12},{15,13},{10,14},{11,... | collective-permute-start | bytes 1179656 | tf_op jit(solution)/shard_map/ppermute | solution.py:162
  195.7 18.7 %collective-permute-start.52 = (bf16[384,512]{1,0:T(8,128)(2,1)S(1)}, bf16[384,512]{1,0:T(8,128)(2,1)S(1)}, u32[]{:S(2)}, u32[]{:S(2)}) collective-permute-start(bf16[384,512]{1,0:T(8,128)(2,1)S(1)} %get-tuple-element.15), channel_id=1, source_target_pairs={{0,4},{1,5},{4,8},{5,9},{8,12},{9,13},{12,14},{13,15},{14,10},{15,... | collective-permute-start | bytes 1179656 | tf_op jit(solution)/shard_map/ppermute | solution.py:161
  224.8 19.6 %collective-permute-start.56 = (bf16[384,512]{1,0:T(8,128)(2,1)S(1)}, bf16[384,512]{1,0:T(8,128)(2,1)S(1)}, u32[]{:S(2)}, u32[]{:S(2)}) collective-permute-start(bf16[384,512]{1,0:T(8,128)(2,1)S(1)} %collective-permute-done.54), channel_id=1, source_target_pairs={{0,4},{1,5},{4,8},{5,9},{8,12},{9,13},{12,14},{13,15},{14,10},{15,... | collective-permute-start | bytes 1179656 | tf_op jit(solution)/shard_map/ppermute | solution.py:161
  238.7 63.2 %collective-permute-start.42 = (bf16[3072,512]{1,0:T(8,128)(2,1)S(1)}, bf16[3072,512]{1,0:T(8,128)(2,1)S(1)}, u32[]{:S(2)}, u32[]{:S(2)}) collective-permute-start(bf16[3072,512]{1,0:T(8,128)(2,1)S(1)} %get-tuple-element.92), channel_id=1, source_target_pairs={{0,1},{1,0},{2,3},{3,2},{4,5},{5,4},{6,7},{7,6},{8,9},{9,8},{10,11... | collective-permute-start | bytes 9437192 | tf_op jit(solution)/shard_map/ppermute | solution.py:190
  244.4 150.1 %collective-permute-start.73 = (f32[512]{0:T(512)S(1)}, f32[512]{0:T(512)}, u32[]{:S(2)}, u32[]{:S(2)}) collective-permute-start(f32[512]{0:T(512)S(1)} %get-tuple-element.161), channel_id=1, source_target_pairs={{0,1},{1,0},{2,3},{3,2},{4,5},{5,4},{6,7},{7,6},{8,9},{9,8},{10,11... | collective-permute-start | bytes 6152 | tf_op jit(solution)/shard_map/ppermute | solution.py:191
  272.7 18.3 %collective-permute-start.68 = (bf16[192,512]{1,0:T(8,128)(2,1)S(1)}, bf16[192,512]{1,0:T(8,128)(2,1)S(1)}, u32[]{:S(2)}, u32[]{:S(2)}) collective-permute-start(bf16[192,512]{1,0:T(8,128)(2,1)S(1)} %slice.161), channel_id=1, source_target_pairs={{4,0},{5,1},{8,4},{9,5},{12,8},{13,9},{14,12},{15,13},{10,14},{11,... | collective-permute-start | bytes 589832 | tf_op jit(solution)/shard_map/ppermute | solution.py:165
  280.1 60.5 %collective-permute-start.51 = (bf16[3072,512]{1,0:T(8,128)(2,1)}, bf16[3072,512]{1,0:T(8,128)(2,1)}, u32[]{:S(2)}, u32[]{:S(2)}) collective-permute-start(bf16[3072,512]{1,0:T(8,128)(2,1)} %get-tuple-element.95), channel_id=1, source_target_pairs={{0,1},{1,0},{2,3},{3,2},{4,5},{5,4},{6,7},{7,6},{8,9},{9,8},{10,11... | collective-permute-start | bytes 9437192 | tf_op jit(solution)/shard_map/ppermute | solution.py:190
  291.0 140.5 %collective-permute-start.75 = (f32[512]{0:T(512)}, f32[512]{0:T(512)}, u32[]{:S(2)}, u32[]{:S(2)}) collective-permute-start(f32[512]{0:T(512)} %get-tuple-element.163), channel_id=1, source_target_pairs={{0,1},{1,0},{2,3},{3,2},{4,5},{5,4},{6,7},{7,6},{8,9},{9,8},{10,11... | collective-permute-start | bytes 6152 | tf_op jit(solution)/shard_map/ppermute | solution.py:191
  301.9 53.9 %collective-permute-start.60 = (bf16[3072,512]{1,0:T(8,128)(2,1)}, bf16[3072,512]{1,0:T(8,128)(2,1)}, u32[]{:S(2)}, u32[]{:S(2)}) collective-permute-start(bf16[3072,512]{1,0:T(8,128)(2,1)} %get-tuple-element.99), channel_id=1, source_target_pairs={{0,1},{1,0},{2,3},{3,2},{4,5},{5,4},{6,7},{7,6},{8,9},{9,8},{10,11... | collective-permute-start | bytes 9437192 | tf_op jit(solution)/shard_map/ppermute | solution.py:190
  338.7 99.3 %collective-permute-start.77 = (f32[512]{0:T(512)S(1)}, f32[512]{0:T(512)}, u32[]{:S(2)}, u32[]{:S(2)}) collective-permute-start(f32[512]{0:T(512)S(1)} %get-tuple-element.165), channel_id=1, source_target_pairs={{0,1},{1,0},{2,3},{3,2},{4,5},{5,4},{6,7},{7,6},{8,9},{9,8},{10,11... | collective-permute-start | bytes 6152 | tf_op jit(solution)/shard_map/ppermute | solution.py:191
  340.5 28.5 %collective-permute-start.69 = (bf16[3072,512]{1,0:T(8,128)(2,1)S(1)}, bf16[3072,512]{1,0:T(8,128)(2,1)S(1)}, u32[]{:S(2)}, u32[]{:S(2)}) collective-permute-start(bf16[3072,512]{1,0:T(8,128)(2,1)S(1)} %copy-done.3), channel_id=1, source_target_pairs={{0,1},{1,0},{2,3},{3,2},{4,5},{5,4},{6,7},{7,6},{8,9},{9,8},{10,11... | collective-permute-start | bytes 9437192 | tf_op jit(solution)/shard_map/ppermute | solution.py:190
  355.8 72.8 %collective-permute-start.80 = (f32[192,512]{1,0:T(8,128)}, f32[192,512]{1,0:T(8,128)}, u32[]{:S(2)}, u32[]{:S(2)}) collective-permute-start(f32[192,512]{1,0:T(8,128)} %constant_dynamic-slice_fusion.2), channel_id=1, source_target_pairs={{0,1},{1,0},{2,3},{3,2},{4,5},{5,4},{6,7},{7,6},{8,9},{9,8},{10,11... | collective-permute-start | bytes 1179656 | tf_op jit(solution)/shard_map/ppermute | solution.py:217
  369.0 79.6 %collective-permute-start.72 = (f32[192,512]{1,0:T(8,128)}, f32[192,512]{1,0:T(8,128)}, u32[]{:S(2)}, u32[]{:S(2)}) collective-permute-start(f32[192,512]{1,0:T(8,128)} %constant_dynamic-slice_fusion.7), channel_id=1, source_target_pairs={{0,1},{1,0},{2,3},{3,2},{4,5},{5,4},{6,7},{7,6},{8,9},{9,8},{10,11... | collective-permute-start | bytes 1179656 | tf_op jit(solution)/shard_map/ppermute | solution.py:216
  398.7 51.7 %collective-permute-start.74 = (f32[192,512]{1,0:T(8,128)}, f32[192,512]{1,0:T(8,128)}, u32[]{:S(2)}, u32[]{:S(2)}) collective-permute-start(f32[192,512]{1,0:T(8,128)} %constant_dynamic-slice_fusion.6), channel_id=1, source_target_pairs={{0,1},{1,0},{2,3},{3,2},{4,5},{5,4},{6,7},{7,6},{8,9},{9,8},{10,11... | collective-permute-start | bytes 1179656 | tf_op jit(solution)/shard_map/ppermute | solution.py:216
  (111 other events, 1371.9 us)

commit v3 on v0

--- a/solution.py
+++ b/solution.py
@@ -1,9 +1,18 @@
+import functools
+
 import jax
 import jax.numpy as jnp
 from jax import lax
+from jax.experimental import pallas as pl
+from jax.experimental.pallas import tpu as pltpu
 from jax.sharding import PartitionSpec as P
 
 off_weight = 0.0051
+chunks = 4
+lanes = 256
+tile_rows = 512
+spare = 16
+vmem = 44 * 1024 * 1024
 
 
 def local_term(columns, full_two):
@@ -86,10 +95,347 @@
     return (grad_one, grad_two, jnp.reshape(loss, (1,)))
 
 
+def norm_kernel(samples, turned, count, *refs):
+    parts = refs[:count]
+    if turned:
+        norm_ref, pair_ref, stat_ref = refs[-3:]
+    else:
+        norm_ref, stat_ref = refs[-2:]
+    total = jnp.zeros((1, lanes), jnp.float32)
+    square = jnp.zeros((1, lanes), jnp.float32)
+    for part in parts:
+        values = part[...].astype(jnp.float32)
+        total += jnp.sum(values, axis=0, keepdims=True)
+        square += jnp.sum(values * values, axis=0, keepdims=True)
+    mean = total / samples
+    inv = 1.0 / jnp.sqrt(square / samples - mean * mean + 1e-05)
+    norm_total = jnp.zeros((1, lanes), jnp.float32)
+    start = 0
+    late = []
+    for place, part in enumerate(parts):
+        norm = ((part[...].astype(jnp.float32) - mean) * inv).astype(jnp.bfloat16)
+        norm_total += jnp.sum(norm.astype(jnp.float32), axis=0, keepdims=True)
+        if not turned:
+            norm_ref[start : start + part.shape[0], :] = norm
+            start += part.shape[0]
+            continue
+        if place == 0:
+            pair_ref[: part.shape[0], :] = norm
+        if place >= count - 2:
+            late.append(norm)
+            if place < count - 1:
+                continue
+            norm = jnp.concatenate(late, axis=0)
+        norm_ref[:, start : start + norm.shape[0]] = norm.T
+        start += norm.shape[0]
+    row = lax.broadcasted_iota(jnp.int32, (8, lanes), 0)
+    stat_ref[...] = jnp.where(row == 0, inv, jnp.where(row == 1, norm_total, 0.0))
+    if turned:
+        pair_ref[parts[0].shape[0] :, :] = total_rows(norm_total)
+
+
+def total_rows(total):
+    high = total.astype(jnp.bfloat16).astype(jnp.float32)
+    row = lax.broadcasted_iota(jnp.int32, (spare, total.shape[1]), 0)
+    both = jnp.where(row == 0, high, jnp.where(row == 1, total - high, 0.0))
+    return both.astype(jnp.bfloat16)
+
+
+def norm_one_chunk(parts, held, index, half, samples):
+    step = parts[0].shape[1]
+    rows = parts[0].shape[0]
+    tiles = step // lanes
+    place = lambda tile: (0, index * tiles + tile)
+    any_spec = pl.BlockSpec(memory_space=pl.ANY)
+    count = len(parts)
+    return pl.pallas_call(
+        functools.partial(norm_kernel, samples, True, count),
+        grid=(tiles,),
+        in_specs=[pl.BlockSpec((part.shape[0], lanes), lambda tile: (0, tile)) for part in parts]
+        + [any_spec] * len(held),
+        out_specs=[
+            pl.BlockSpec((lanes, samples), lambda tile: (index * tiles + tile, 0)),
+            pl.BlockSpec((rows + spare, lanes), place),
+            pl.BlockSpec((8, lanes), place),
+        ],
+        out_shape=[
+            jax.ShapeDtypeStruct((half, samples), jnp.bfloat16),
+            jax.ShapeDtypeStruct((rows + spare, half), jnp.bfloat16),
+            jax.ShapeDtypeStruct((8, half), jnp.float32),
+        ],
+        input_output_aliases={count + k: k for k in range(len(held))},
+        compiler_params=pltpu.CompilerParams(vmem_limit_bytes=vmem),
+        cost_estimate=pl.CostEstimate(
+            flops=10 * samples * step, bytes_accessed=4 * samples * step, transcendentals=0
+        ),
+        name="norm_one_chunk",
+    )(*parts, *held)
+
+
+def norm_two_chunk(parts, samples):
+    step = parts[0].shape[1]
+    return pl.pallas_call(
+        functools.partial(norm_kernel, samples, False, len(parts)),
+        grid=(step // lanes,),
+        in_specs=[pl.BlockSpec((part.shape[0], lanes), lambda tile: (0, tile)) for part in parts],
+        out_specs=[
+            pl.BlockSpec((samples, lanes), lambda tile: (0, tile)),
+            pl.BlockSpec((8, lanes), lambda tile: (0, tile)),
+        ],
+        out_shape=[
+            jax.ShapeDtypeStruct((samples, step), jnp.bfloat16),
+            jax.ShapeDtypeStruct((8, step), jnp.float32),
+        ],
+        compiler_params=pltpu.CompilerParams(vmem_limit_bytes=vmem),
+        cost_estimate=pl.CostEstimate(
+            flops=10 * samples * step, bytes_accessed=4 * samples * step, transcendentals=0
+        ),
+        name="norm_two_chunk",
+    )(*parts)
+
+
+def corr_kernel(samples, diag_at, begins, fresh, opens, closes, *refs):
+    one_ref, pair_ref, two_ref, stat_ref = refs[:4]
+    rest = list(refs[4:])
+    acc_in = None if begins else rest.pop(0)
+    loss_in = None if begins else rest.pop(0)
+    back_in = None if opens else rest.pop(0)
+    acc_out, loss_out, back_out, ext_ref, back_ref = rest
+    rows = pair_ref.shape[0] - spare
+    tile = pl.program_id(0)
+
+    @pl.when(tile == 0)
+    def _():
+        ext_ref[:rows, :] = two_ref[:rows, :]
+        ext_ref[rows:, :] = total_rows(stat_ref[1:2, :])
+        back_ref[...] = jnp.zeros_like(back_ref) if opens else back_in[...]
+        loss_out[...] = jnp.zeros_like(loss_out) if begins else loss_in[...]
+
+    summed = jnp.dot(one_ref[...], two_ref[...], preferred_element_type=jnp.float32)
+    corr = summed * (1.0 / samples)
+    grad = (2.0 * off_weight) * corr
+    loss = off_weight * corr * corr
+    if diag_at is not None:
+        ahead = lax.broadcasted_iota(jnp.int32, corr.shape, 1) - lax.broadcasted_iota(
+            jnp.int32, corr.shape, 0
+        )
+        diag = ahead == tile * corr.shape[0] - diag_at
+        grad = jnp.where(diag, 2.0 * corr - 2.0, grad)
+        loss = jnp.where(diag, (1.0 - corr) ** 2, loss)
+    grad = grad.astype(jnp.bfloat16)
+    prod = grad.astype(jnp.float32) * summed
+    height, width = summed.shape
+    loss_out[...] += jnp.sum(loss.reshape(height // 8, 8, width), axis=0)
+    folded = prod[:, :128]
+    for start in range(128, width, 128):
+        folded += prod[:, start : start + 128]
+    prod_row = jnp.sum(folded.T, axis=0, keepdims=True)
+    back = lax.dot_general(
+        ext_ref[...], grad, (((1,), (1,)), ((), ())), preferred_element_type=jnp.float32
+    )
+    acc_out[...] = back if fresh else acc_in[...] + back
+    row = lax.broadcasted_iota(jnp.int32, (8, height), 0)
+    acc_out[rows + 8 :, :] += jnp.where(row == 0, prod_row, 0.0)
+    back_ref[...] += jnp.dot(pair_ref[...], grad, preferred_element_type=jnp.float32)
+    back_ref[rows + 8 :, :] += jnp.sum(prod.reshape(height // 8, 8, width), axis=0)
+
+    @pl.when(tile == pl.num_programs(0) - 1)
+    def _():
+        if not closes:
+            back_out[...] = back_ref[...]
+        else:
+            sum_back = (back_ref[rows : rows + 1, :] + back_ref[rows + 1 : rows + 2, :]) / samples
+            sum_prod = jnp.sum(back_ref[rows + 8 :, :], axis=0, keepdims=True) / samples
+            normal = two_ref[:rows, :].astype(jnp.float32)
+            back_out[...] = stat_ref[0:1, :] * (back_ref[:rows, :] - sum_back - normal * sum_prod)
+
+
+def corr_piece(norm_one, pair_one, norm_two, stat_two, acc, back, fresh, piece, pieces, diag_at):
+    half, samples = norm_one.shape
+    width = norm_two.shape[1]
+    ext = pair_one.shape[0]
+    rows = ext - spare
+    tiles = half // pieces // tile_rows
+    first = piece * tiles
+    opens, closes = piece == 0, piece == pieces - 1
+    whole = lambda shape: pl.BlockSpec(shape, lambda tile: (0, 0))
+    acc_spec = pl.BlockSpec((ext, tile_rows), lambda tile: (0, first + tile))
+    operands = [norm_one, pair_one, norm_two, stat_two]
+    in_specs = [
+        pl.BlockSpec((tile_rows, samples), lambda tile: (first + tile, 0)),
+        acc_spec,
+        whole((samples, width)),
+        whole((8, width)),
+    ]
+    aliases = {}
+    if acc is not None:
+        aliases = {4: 0, 5: 1}
+        operands += list(acc)
+        in_specs += [acc_spec, whole((8, width))]
+    if not opens:
+        operands.append(back)
+        in_specs.append(whole((ext, width)))
+    back_shape = (rows if closes else ext, width)
+    if diag_at is not None:
+        diag_at = diag_at - piece * tiles * tile_rows
+    return pl.pallas_call(
+        functools.partial(corr_kernel, samples, diag_at, acc is None, fresh, opens, closes),
+        grid=(tiles,),
+        in_specs=in_specs,
+        out_specs=[acc_spec, whole((8, width)), whole(back_shape)],
+        out_shape=[
+            jax.ShapeDtypeStruct((ext, half), jnp.float32),
+            jax.ShapeDtypeStruct((8, width), jnp.float32),
+            jax.ShapeDtypeStruct(back_shape, jnp.float32),
+        ],
+        scratch_shapes=[
+            pltpu.VMEM((ext, width), jnp.bfloat16),
+            pltpu.VMEM((ext, width), jnp.float32),
+        ],
+        input_output_aliases=aliases,
+        compiler_params=pltpu.CompilerParams(vmem_limit_bytes=vmem),
+        cost_estimate=pl.CostEstimate(
+            flops=2 * tiles * tile_rows * width * (samples + 2 * ext),
+            bytes_accessed=2 * samples * (tiles * tile_rows + width),
+            transcendentals=0,
+        ),
+        name="corr_piece",
+    )(*operands)
+
+
+def pair_shards(view_one, view_two):
+    rows, width = view_one.shape
+    batches = lax.axis_size("batch")
+    samples = rows * batches
+    half = width // 2
+    step = half // chunks
+    chips = batches // 2
+    side = lax.axis_index("batch") % 2
+    swap = [(i, i ^ 1) for i in range(batches)]
+    line = chips // 2
+    order = [2 * r for r in range(line)] + [2 * r + 1 for r in reversed(range(line))]
+    ahead = [
+        (2 * order[r] + c, 2 * order[(r + 1) % chips] + c) for r in range(chips) for c in range(2)
+    ]
+    behind = [(there, here) for here, there in ahead]
+
+    def mine(both, axis=0):
+        size = both.shape[axis] // 2
+        return lax.dynamic_slice_in_dim(both, side * size, size, axis=axis)
+
+    def theirs(both, axis=0):
+        size = both.shape[axis] // 2
+        return lax.dynamic_slice_in_dim(both, (1 - side) * size, size, axis=axis)
+
+    def swapped(value):
+        return lax.ppermute(value, "batch", swap)
+
+    def in_order(own, other, axis):
+        return jnp.where(
+            side == 0,
+            jnp.concatenate([own, other], axis=axis),
+            jnp.concatenate([other, own], axis=axis),
+        )
+
+    def chip_rows(view):
+        return in_order(mine(view, 1), swapped(theirs(view, 1)), 0)
+
+    blocks = (chip_rows(view_one), chip_rows(view_two))
+    hops = chips // 2
+    flows = [(view, index) for view in range(2) for index in range(chunks)]
+    slots = {}
+    for flow in range(len(flows)):
+        for hop in range(hops):
+            slots[hops * flow + flow % 2 + 2 * hop] = (flow, hop)
+    last_hop = {hops * flow + flow % 2 + 2 * (hops - 1): flow for flow in range(len(flows))}
+    ends = {}
+    arrived = {}
+    held = []
+    state = {"acc": None, "back": None, "token": None}
+    grad_own, grad_far = [], []
+    work = []
+    pieces = 2
+
+    def run_piece(norm, stat, piece, diag_at, grads):
+        acc, loss, back = corr_piece(
+            held[0],
+            held[1],
+            norm,
+            stat,
+            state["acc"],
+            state["back"],
+            not grads and diag_at == 0,
+            piece,
+            pieces,
+            diag_at,
+        )
+        state["acc"], state["back"], state["token"] = (acc, loss), back, loss
+        if piece == pieces - 1:
+            grads.append(back)
+
+    def take(flow):
+        view, index = flows[flow]
+        if view == 0:
+            held[:] = norm_one_chunk(arrived[flow], held, index, half, samples)
+            state["token"] = held[2]
+            return
+        norm, stat = norm_two_chunk(arrived[flow], samples)
+        state["token"] = stat
+        far_norm, far_stat = swapped(norm), swapped(stat)
+        for piece in range(pieces):
+            work.append(functools.partial(run_piece, norm, stat, piece, index * step, grad_own))
+        for piece in range(pieces):
+            work.append(functools.partial(run_piece, far_norm, far_stat, piece, None, grad_far))
+
+    for slot in range(max(slots) + 2):
+        if slot in slots:
+            flow, hop = slots[slot]
+            view, index = flows[flow]
+            if hop == 0:
+                block = blocks[view][:, index * step : (index + 1) * step]
+                ends[flow] = (block, block)
+                arrived[flow] = [block]
+            up, down = ends[flow]
+            if hop == hops - 1:
+                up, down = up[:rows], down[rows:]
+            if state["token"] is not None:
+                up, down, _ = lax.optimization_barrier((up, down, state["token"]))
+            up = lax.ppermute(up, "batch", ahead)
+            down = lax.ppermute(down, "batch", behind)
+            ends[flow] = (up, down)
+            arrived[flow] += [up, down]
+        if slot - 1 in last_hop:
+            take(last_hop[slot - 1])
+        if work:
+            work.pop(0)()
+    while work:
+        work.pop(0)()
+
+    acc, loss = state["acc"]
+    pair_f = held[1][: 2 * rows].astype(jnp.float32)
+    sum_back = acc[2 * rows] + acc[2 * rows + 1]
+    sum_prod = acc[2 * rows + 8]
+    done_one = (
+        held[2][0] * (acc[: 2 * rows] - sum_back / samples - pair_f * sum_prod / samples)
+    ).astype(jnp.bfloat16)
+    grad_one = in_order(mine(done_one), swapped(theirs(done_one)), 1)
+    columns_own, columns_far = [], []
+    for own, far in zip(grad_own, grad_far):
+        columns_own.append((mine(own) + swapped(theirs(far))).astype(jnp.bfloat16))
+        columns_far.append((mine(far) + swapped(theirs(own))).astype(jnp.bfloat16))
+    grad_two = in_order(
+        jnp.concatenate(columns_own, axis=1), jnp.concatenate(columns_far, axis=1), 1
+    )
+    loss = jnp.sum(loss)
+    loss = (loss + swapped(loss)) / width
+    return (grad_one, grad_two, jnp.reshape(loss, (1,)))
+
+
 def solution(mesh):
     placed = (P(("groups", "batch"), "feat"), P(("groups", "batch"), "feat"))
+    paired = mesh.shape["feat"] == 1 and mesh.shape["batch"] % 4 == 0
     return jax.shard_map(
-        shards,
+        pair_shards if paired else shards,
         mesh=mesh,
         in_specs=placed,
         out_specs=(P(("groups", "batch"), "feat"), P(("groups", "batch"), "feat"), P("groups")),

time: 1040 us -> 454 us (0.44)
  waiting for transfers between devices: 863 us -> 163 us
  Pallas kernels: 0 us -> 158 us
  blocking collectives: 86.7 us -> 0 us
  starting transfers between devices: 0.12 us -> 76.9 us
  matrix products: 57.4 us -> 0 us
  local copies, waits for them, and re-layouts: 0.01 us -> 21.2 us
  between operations: 15.6 us -> 4.31 us
    reduce_scatter x1 -> x0, waiting for transfers between devices: 639 us -> none  [shards(): lax.psum_scatter(local_term(norm_one, full_two), 'batch', scatter_dimensi...]
    ppermute x0 -> x84, waiting for transfers between devices: none -> 163 us  [the longest x32 138 us: pair_shards(): up = lax.ppermute(up, 'batch', ahead)]
    pallas_call x0 -> x24, Pallas kernels: none -> 158 us  [the longest x16 129 us: corr_piece(): pl.pallas_call(functools.partial(corr_kernel, samples, diag_at, acc is No...]
    all_gather x1 -> x0, waiting for transfers between devices: 136 us -> none  [shards(): lax.all_gather(grad, 'batch', axis=0, tiled=True)]
    psum x1 -> x0, waiting for transfers between devices: 87.6 us -> none  [shards(): lax.psum((jnp.sum(values_one, axis=0), jnp.sum(values_one * values_one, a...]
    psum x2 -> x0, blocking collectives: 86.7 us -> none  [the longest x1 56 us: shards(): lax.psum(jnp.sum(back_one * norm_one_f, axis=0).astype(jnp.bfloat16), 'ba...]
    ppermute x0 -> x84, starting transfers between devices: none -> 76.9 us  [the longest x32 30.9 us: pair_shards(): up = lax.ppermute(up, 'batch', ahead)]
    dot_general x3 -> x0, matrix products: 57.4 us -> none  [the longest x1 23.2 us: local_term(): lax.dot_general(columns, full_two, (((0,), (0,)), ((), ())), preferred_el...]
  transfers between devices with their start and end apart: 3 -> 84, of which waited for: 3 -> 46; matrix products, arithmetic and copies ran while one was open for 0% -> 7% of each run, Pallas kernels for 0% -> 29%
where the time goes in v3:
time: 454 us; the launch traced here: 445 us
  waiting for transfers between devices  163 us (36%)
  Pallas kernels  158 us (35%)
  starting transfers between devices  76.9 us (17%)
  other arithmetic  22 us (5%)
  local copies, waits for them, and re-layouts  21.2 us (5%)
    ppermute x32, waiting for transfers between devices, pair_shards(): up = lax.ppermute(up, 'batch', ahead)  138 us
    pallas_call x16, Pallas kernels, corr_piece(): pl.pallas_call(functools.partial(corr_kernel, samples, diag_at, acc is No...  129 us
    ppermute x32, starting transfers between devices, pair_shards(): up = lax.ppermute(up, 'batch', ahead)  30.9 us
    ppermute x20, starting transfers between devices, swapped(): return lax.ppermute(value, 'batch', swap)  27.4 us
    ppermute x32, starting transfers between devices, pair_shards(): down = lax.ppermute(down, 'batch', behind)  18.6 us
    ppermute x32, waiting for transfers between devices, pair_shards(): down = lax.ppermute(down, 'batch', behind)  17.4 us
    pallas_call x4, Pallas kernels, norm_one_chunk(): pl.pallas_call(functools.partial(norm_kernel, samples, True, count), grid...  14.8 us
    pallas_call x4, Pallas kernels, norm_two_chunk(): pl.pallas_call(functools.partial(norm_kernel, samples, False, len(parts))...  13.6 us
  transfers between devices with their start and end apart: 84, of which 46 were waited for; matrix products, arithmetic and copies ran while one was open for 7% of the time, Pallas kernels for 29%

profile of v3, /device:TPU:1, one launch (start us, length us, event | category | flops | bytes accessed | tf_op | source)
XLA Modules:
  0.0 444.9 jit_solution(13051955234423045249)
XLA Ops:
  11.3 9.3 %collective-permute-done.5.refs_1_ = bf16[384,512]{1,0:T(8,128)(2,1)S(1)} collective-permute-done((bf16[384,512]{1,0:T(8,128)(2,1)S(1)}, bf16[384,512]{1,0:T(8,128)(2,1)S(1)}, u32[]{:S(2)}, u32[]{:S(2)}) %collective-permute-start.5) | collective-permute-done | bytes 393248 | tf_op jit(solution)/shard_map/ppermute | solution.py:403
  22.1 8.5 %collective-permute-done.7.refs_3_ = bf16[384,512]{1,0:T(8,128)(2,1)S(1)} collective-permute-done((bf16[384,512]{1,0:T(8,128)(2,1)S(1)}, bf16[384,512]{1,0:T(8,128)(2,1)S(1)}, u32[]{:S(2)}, u32[]{:S(2)}) %collective-permute-start.7) | collective-permute-done | bytes 393248 | tf_op jit(solution)/shard_map/ppermute | solution.py:403
  41.1 11.0 %collective-permute-done.11.refs_7_ = bf16[192,512]{1,0:T(8,128)(2,1)S(1)} collective-permute-done((bf16[192,512]{1,0:T(8,128)(2,1)S(1)}, bf16[192,512]{1,0:T(8,128)(2,1)S(1)}, u32[]{:S(2)}, u32[]{:S(2)}) %collective-permute-start.11) | collective-permute-done | bytes 196640 | tf_op jit(solution)/shard_map/ppermute | solution.py:403
  91.7 10.1 %collective-permute-done.15.refs_7_ = bf16[192,512]{1,0:T(8,128)(2,1)S(1)} collective-permute-done((bf16[192,512]{1,0:T(8,128)(2,1)S(1)}, bf16[192,512]{1,0:T(8,128)(2,1)S(1)}, u32[]{:S(2)}, u32[]{:S(2)}) %collective-permute-start.15) | collective-permute-done | bytes 196640 | tf_op jit(solution)/shard_map/ppermute | solution.py:403
  154.8 10.1 %collective-permute-done.31.refs_7_ = bf16[192,512]{1,0:T(8,128)(2,1)S(1)} collective-permute-done((bf16[192,512]{1,0:T(8,128)(2,1)S(1)}, bf16[192,512]{1,0:T(8,128)(2,1)S(1)}, u32[]{:S(2)}, u32[]{:S(2)}) %collective-permute-start.31) | collective-permute-done | bytes 196640 | tf_op jit(solution)/shard_map/ppermute | solution.py:403
  177.9 8.1 %collective-permute-start.48 = (bf16[3072,512]{1,0:T(8,128)(2,1)S(1)}, bf16[3072,512]{1,0:T(8,128)(2,1)S(1)}, u32[]{:S(2)}, u32[]{:S(2)}) collective-permute-start(bf16[3072,512]{1,0:T(8,128)(2,1)S(1)} %get-tuple-element.167.refs_2_), channel_id=1, source_target_pairs={{0,1},{1,0},{2,3},{3,2},{4,5},{5,4},{6,7},{7,6},{8,9},{9,8},{10,11... | collective-permute-start | bytes 9437192 | tf_op jit(solution)/shard_map/ppermute | solution.py:331
  187.4 9.2 %collective-permute-done.34.refs_1_ = bf16[384,512]{1,0:T(8,128)(2,1)S(1)} collective-permute-done((bf16[384,512]{1,0:T(8,128)(2,1)S(1)}, bf16[384,512]{1,0:T(8,128)(2,1)S(1)}, u32[]{:S(2)}, u32[]{:S(2)}) %collective-permute-start.34) | collective-permute-done | bytes 393248 | tf_op jit(solution)/shard_map/ppermute | solution.py:403
  198.2 7.9 %corr_piece.16 = (f32[400,2048]{1,0:T(8,128)S(1)}, f32[8,512]{1,0:T(8,128)S(1)}, f32[400,512]{1,0:T(8,128)S(1)}) custom-call(bf16[2048,3072]{1,0:T(8,128)(2,1)} %get-tuple-element.153.refs_0_, bf16[400,2048]{1,0:T(8,128)(2,1)S(1)} %get-tuple-element.154.refs_1_, bf16[3072,512]{1,0:T(8,128)(2,1)S(1)} %get-tuple-element.167.refs_2_, ...), custom_call_target="tpu_custom_call" | custom-call | flops 4060086272 | bytes 9437184 | tf_op jit(solution)/shard_map/corr_piece/pallas_call | solution.py:281
  206.1 8.0 %corr_piece.17 = (f32[400,2048]{1,0:T(8,128)S(1)}, f32[8,512]{1,0:T(8,128)S(1)}, f32[384,512]{1,0:T(8,128)S(1)}) custom-call(bf16[2048,3072]{1,0:T(8,128)(2,1)} %get-tuple-element.153.refs_0_, bf16[400,2048]{1,0:T(8,128)(2,1)S(1)} %get-tuple-element.154.refs_1_, ...), custom_call_target="tpu_custom_call", output_to_operand_aliasing={{0}: (4, {}), {1}: (5, {})} | custom-call | flops 4060086272 | bytes 9437184 | tf_op jit(solution)/shard_map/corr_piece/pallas_call | solution.py:281
  224.2 7.2 %corr_piece.18 = (f32[400,2048]{1,0:T(8,128)S(1)}, f32[8,512]{1,0:T(8,128)S(1)}, f32[400,512]{1,0:T(8,128)S(1)}) custom-call(bf16[2048,3072]{1,0:T(8,128)(2,1)} %get-tuple-element.153.refs_0_, bf16[400,2048]{1,0:T(8,128)(2,1)S(1)} %get-tuple-element.154.refs_1_, ...), custom_call_target="tpu_custom_call", output_to_operand_aliasing={{0}: (4, {}), {1}: (5, {})} | custom-call | flops 4060086272 | bytes 9437184 | tf_op jit(solution)/shard_map/corr_piece/pallas_call | solution.py:281
  231.5 7.3 %corr_piece.19 = (f32[400,2048]{1,0:T(8,128)S(1)}, f32[8,512]{1,0:T(8,128)S(1)}, f32[384,512]{1,0:T(8,128)S(1)}) custom-call(bf16[2048,3072]{1,0:T(8,128)(2,1)} %get-tuple-element.153.refs_0_, bf16[400,2048]{1,0:T(8,128)(2,1)S(1)} %get-tuple-element.154.refs_1_, ...), custom_call_target="tpu_custom_call", output_to_operand_aliasing={{0}: (4, {}), {1}: (5, {})} | custom-call | flops 4060086272 | bytes 9437184 | tf_op jit(solution)/shard_map/corr_piece/pallas_call | solution.py:281
  256.9 9.3 %collective-permute-done.60.refs_3_ = bf16[384,512]{1,0:T(8,128)(2,1)S(1)} collective-permute-done((bf16[384,512]{1,0:T(8,128)(2,1)S(1)}, bf16[384,512]{1,0:T(8,128)(2,1)S(1)}, u32[]{:S(2)}, u32[]{:S(2)}) %collective-permute-start.60) | collective-permute-done | bytes 393248 | tf_op jit(solution)/shard_map/ppermute | solution.py:403
  267.7 8.9 %corr_piece.20 = (f32[400,2048]{1,0:T(8,128)S(1)}, f32[8,512]{1,0:T(8,128)S(1)}, f32[400,512]{1,0:T(8,128)S(1)}) custom-call(bf16[2048,3072]{1,0:T(8,128)(2,1)} %get-tuple-element.153.refs_0_, bf16[400,2048]{1,0:T(8,128)(2,1)S(1)} %get-tuple-element.154.refs_1_, ...), custom_call_target="tpu_custom_call", output_to_operand_aliasing={{0}: (4, {}), {1}: (5, {})} | custom-call | flops 4060086272 | bytes 9437184 | tf_op jit(solution)/shard_map/corr_piece/pallas_call | solution.py:281
  276.6 9.0 %corr_piece.21 = (f32[400,2048]{1,0:T(8,128)S(1)}, f32[8,512]{1,0:T(8,128)S(1)}, f32[384,512]{1,0:T(8,128)S(1)}) custom-call(bf16[2048,3072]{1,0:T(8,128)(2,1)} %get-tuple-element.153.refs_0_, bf16[400,2048]{1,0:T(8,128)(2,1)S(1)} %get-tuple-element.154.refs_1_, ...), custom_call_target="tpu_custom_call", output_to_operand_aliasing={{0}: (4, {}), {1}: (5, {})} | custom-call | flops 4060086272 | bytes 9437184 | tf_op jit(solution)/shard_map/corr_piece/pallas_call | solution.py:281
  302.2 7.2 %corr_piece.22 = (f32[400,2048]{1,0:T(8,128)S(1)}, f32[8,512]{1,0:T(8,128)S(1)}, f32[400,512]{1,0:T(8,128)S(1)}) custom-call(bf16[2048,3072]{1,0:T(8,128)(2,1)} %get-tuple-element.153.refs_0_, bf16[400,2048]{1,0:T(8,128)(2,1)S(1)} %get-tuple-element.154.refs_1_, ...), custom_call_target="tpu_custom_call", output_to_operand_aliasing={{0}: (4, {}), {1}: (5, {})} | custom-call | flops 4060086272 | bytes 9437184 | tf_op jit(solution)/shard_map/corr_piece/pallas_call | solution.py:281
  311.1 7.3 %corr_piece.23 = (f32[400,2048]{1,0:T(8,128)S(1)}, f32[8,512]{1,0:T(8,128)S(1)}, f32[384,512]{1,0:T(8,128)S(1)}) custom-call(bf16[2048,3072]{1,0:T(8,128)(2,1)} %get-tuple-element.153.refs_0_, bf16[400,2048]{1,0:T(8,128)(2,1)S(1)} %get-tuple-element.154.refs_1_, ...), custom_call_target="tpu_custom_call", output_to_operand_aliasing={{0}: (4, {}), {1}: (5, {})} | custom-call | flops 4060086272 | bytes 9437184 | tf_op jit(solution)/shard_map/corr_piece/pallas_call | solution.py:281
  318.5 8.2 %corr_piece.24 = (f32[400,2048]{1,0:T(8,128)S(1)}, f32[8,512]{1,0:T(8,128)S(1)}, f32[400,512]{1,0:T(8,128)S(1)}) custom-call(bf16[2048,3072]{1,0:T(8,128)(2,1)} %get-tuple-element.153.refs_0_, bf16[400,2048]{1,0:T(8,128)(2,1)S(1)} %get-tuple-element.154.refs_1_, ...), custom_call_target="tpu_custom_call", output_to_operand_aliasing={{0}: (4, {}), {1}: (5, {})} | custom-call | flops 4060086272 | bytes 9437184 | tf_op jit(solution)/shard_map/corr_piece/pallas_call | solution.py:281
  329.7 8.0 %corr_piece.25 = (f32[400,2048]{1,0:T(8,128)S(1)}, f32[8,512]{1,0:T(8,128)S(1)}, f32[384,512]{1,0:T(8,128)S(1)}) custom-call(bf16[2048,3072]{1,0:T(8,128)(2,1)} %get-tuple-element.153.refs_0_, bf16[400,2048]{1,0:T(8,128)(2,1)S(1)} %get-tuple-element.154.refs_1_, ...), custom_call_target="tpu_custom_call", output_to_operand_aliasing={{0}: (4, {}), {1}: (5, {})} | custom-call | flops 4060086272 | bytes 9437184 | tf_op jit(solution)/shard_map/corr_piece/pallas_call | solution.py:281
  338.7 7.7 %corr_piece.26 = (f32[400,2048]{1,0:T(8,128)S(1)}, f32[8,512]{1,0:T(8,128)S(1)}, f32[400,512]{1,0:T(8,128)S(1)}) custom-call(bf16[2048,3072]{1,0:T(8,128)(2,1)} %get-tuple-element.153.refs_0_, bf16[400,2048]{1,0:T(8,128)(2,1)S(1)} %get-tuple-element.154.refs_1_, ...), custom_call_target="tpu_custom_call", output_to_operand_aliasing={{0}: (4, {}), {1}: (5, {})} | custom-call | flops 4060086272 | bytes 9437184 | tf_op jit(solution)/shard_map/corr_piece/pallas_call | solution.py:281
  375.1 7.3 %corr_piece.27 = (f32[400,2048]{1,0:T(8,128)S(1)}, f32[8,512]{1,0:T(8,128)S(1)}, f32[384,512]{1,0:T(8,128)S(1)}) custom-call(bf16[2048,3072]{1,0:T(8,128)(2,1)} %get-tuple-element.153.refs_0_, bf16[400,2048]{1,0:T(8,128)(2,1)S(1)} %copy-done.1, bf16[3072,512]{1,0:T(8,128)(2,1)S(1)} %copy-done.3, ...), custom_call_target="tpu_custom_call", output_to_operand_aliasing={{0}: (4, {}), {1}: (5, {})} | custom-call | flops 4060086272 | bytes 9437184 | tf_op jit(solution)/shard_map/corr_piece/pallas_call | solution.py:281
  384.5 9.3 %corr_piece.28 = (f32[400,2048]{1,0:T(8,128)S(1)}, f32[8,512]{1,0:T(8,128)S(1)}, f32[400,512]{1,0:T(8,128)S(1)}) custom-call(bf16[2048,3072]{1,0:T(8,128)(2,1)} %get-tuple-element.153.refs_0_, bf16[400,2048]{1,0:T(8,128)(2,1)S(1)} %copy-done.1, bf16[3072,512]{1,0:T(8,128)(2,1)} %get-tuple-element.219.refs_2_, ...), custom_call_target="tpu_custom_call", output_to_operand_aliasing={{0}: (4, {}), {1}: (5, {})} | custom-call | flops 4060086272 | bytes 9437184 | tf_op jit(solution)/shard_map/corr_piece/pallas_call | solution.py:281
  393.8 9.0 %corr_piece.29 = (f32[400,2048]{1,0:T(8,128)S(1)}, f32[8,512]{1,0:T(8,128)S(1)}, f32[384,512]{1,0:T(8,128)S(1)}) custom-call(bf16[2048,3072]{1,0:T(8,128)(2,1)} %get-tuple-element.153.refs_0_, bf16[400,2048]{1,0:T(8,128)(2,1)S(1)} %copy-done.1, bf16[3072,512]{1,0:T(8,128)(2,1)} %get-tuple-element.219.refs_2_, ...), custom_call_target="tpu_custom_call", output_to_operand_aliasing={{0}: (4, {}), {1}: (5, {})} | custom-call | flops 4060086272 | bytes 9437184 | tf_op jit(solution)/shard_map/corr_piece/pallas_call | solution.py:281
  403.8 8.2 %corr_piece.30 = (f32[400,2048]{1,0:T(8,128)S(1)}, f32[8,512]{1,0:T(8,128)S(1)}, f32[400,512]{1,0:T(8,128)S(1)}) custom-call(bf16[2048,3072]{1,0:T(8,128)(2,1)} %get-tuple-element.153.refs_0_, bf16[400,2048]{1,0:T(8,128)(2,1)S(1)} %copy-done.1, bf16[3072,512]{1,0:T(8,128)(2,1)} %collective-permute-done.72.refs_2_, ...), custom_call_target="tpu_custom_call", output_to_operand_aliasing={{0}: (4, {}), {1}: (5, {})} | custom-call | flops 4060086272 | bytes 9437184 | tf_op jit(solution)/shard_map/corr_piece/pallas_call | solution.py:281
  412.0 8.6 %corr_piece.31 = (f32[400,2048]{1,0:T(8,128)S(1)}, f32[8,512]{1,0:T(8,128)S(1)}, f32[384,512]{1,0:T(8,128)S(1)}) custom-call(bf16[2048,3072]{1,0:T(8,128)(2,1)} %get-tuple-element.153.refs_0_, bf16[400,2048]{1,0:T(8,128)(2,1)S(1)} %copy-done.1, bf16[3072,512]{1,0:T(8,128)(2,1)} %collective-permute-done.72.refs_2_, ...), custom_call_target="tpu_custom_call", output_to_operand_aliasing={{0}: (4, {}), {1}: (5, {})} | custom-call | flops 4060086272 | bytes 9437184 | tf_op jit(solution)/shard_map/corr_piece/pallas_call | solution.py:281
  (270 shorter events, 235.8 us)
Async XLA Ops:
  32.0 25.8 %collective-permute-start.1 = (bf16[384,512]{1,0:T(8,128)(2,1)S(1)}, bf16[384,512]{1,0:T(8,128)(2,1)S(1)}, u32[]{:S(2)}, u32[]{:S(2)}) collective-permute-start(bf16[384,512]{1,0:T(8,128)(2,1)S(1)} %get-tuple-element.271.refs_0_), channel_id=1, source_target_pairs={{0,4},{1,5},{4,8},{5,9},{8,12},{9,13},{12,14},{13,15},{14,10},{15,... | collective-permute-start | bytes 1179656 | tf_op jit(solution)/shard_map/ppermute | solution.py:403
  33.0 26.1 %collective-permute-start.2 = (bf16[384,512]{1,0:T(8,128)(2,1)S(1)}, bf16[384,512]{1,0:T(8,128)(2,1)S(1)}, u32[]{:S(2)}, u32[]{:S(2)}) collective-permute-start(bf16[384,512]{1,0:T(8,128)(2,1)S(1)} %get-tuple-element.271.refs_0_), channel_id=1, source_target_pairs={{4,0},{5,1},{8,4},{9,5},{12,8},{13,9},{14,12},{15,13},{10,14},{11,... | collective-permute-start | bytes 1179656 | tf_op jit(solution)/shard_map/ppermute | solution.py:404
  73.3 15.8 %collective-permute-start.13 = (bf16[384,512]{1,0:T(8,128)(2,1)S(1)}, bf16[384,512]{1,0:T(8,128)(2,1)S(1)}, u32[]{:S(2)}, u32[]{:S(2)}) collective-permute-start(bf16[384,512]{1,0:T(8,128)(2,1)S(1)} %collective-permute-done.3.refs_3_), channel_id=1, source_target_pairs={{0,4},{1,5},{4,8},{5,9},{8,12},{9,13},{12,14},{13,15},{14,10},{15,... | collective-permute-start | bytes 1179656 | tf_op jit(solution)/shard_map/ppermute | solution.py:403
  81.8 26.3 %collective-permute-start.25 = (bf16[384,512]{1,0:T(8,128)(2,1)S(1)}, bf16[384,512]{1,0:T(8,128)(2,1)S(1)}, u32[]{:S(2)}, u32[]{:S(2)}) collective-permute-start(bf16[384,512]{1,0:T(8,128)(2,1)S(1)} %collective-permute-done.23.refs_3_), channel_id=1, source_target_pairs={{0,4},{1,5},{4,8},{5,9},{8,12},{9,13},{12,14},{13,15},{14,10},{15,... | collective-permute-start | bytes 1179656 | tf_op jit(solution)/shard_map/ppermute | solution.py:403
  83.0 25.0 %collective-permute-start.26 = (bf16[384,512]{1,0:T(8,128)(2,1)S(1)}, bf16[384,512]{1,0:T(8,128)(2,1)S(1)}, u32[]{:S(2)}, u32[]{:S(2)}) collective-permute-start(bf16[384,512]{1,0:T(8,128)(2,1)S(1)} %collective-permute-done.24.refs_4_), channel_id=1, source_target_pairs={{4,0},{5,1},{8,4},{9,5},{12,8},{13,9},{14,12},{15,13},{10,14},{11,... | collective-permute-start | bytes 1179656 | tf_op jit(solution)/shard_map/ppermute | solution.py:404
  136.4 15.9 %collective-permute-start.29 = (bf16[384,512]{1,0:T(8,128)(2,1)S(1)}, bf16[384,512]{1,0:T(8,128)(2,1)S(1)}, u32[]{:S(2)}, u32[]{:S(2)}) collective-permute-start(bf16[384,512]{1,0:T(8,128)(2,1)S(1)} %collective-permute-done.19.refs_3_), channel_id=1, source_target_pairs={{0,4},{1,5},{4,8},{5,9},{8,12},{9,13},{12,14},{13,15},{14,10},{15,... | collective-permute-start | bytes 1179656 | tf_op jit(solution)/shard_map/ppermute | solution.py:403
  137.0 16.2 %collective-permute-start.30 = (bf16[384,512]{1,0:T(8,128)(2,1)S(1)}, bf16[384,512]{1,0:T(8,128)(2,1)S(1)}, u32[]{:S(2)}, u32[]{:S(2)}) collective-permute-start(bf16[384,512]{1,0:T(8,128)(2,1)S(1)} %collective-permute-done.20.refs_4_), channel_id=1, source_target_pairs={{4,0},{5,1},{8,4},{9,5},{12,8},{13,9},{14,12},{15,13},{10,14},{11,... | collective-permute-start | bytes 1179656 | tf_op jit(solution)/shard_map/ppermute | solution.py:404
  144.8 24.8 %collective-permute-start.42 = (bf16[384,512]{1,0:T(8,128)(2,1)S(1)}, bf16[384,512]{1,0:T(8,128)(2,1)S(1)}, u32[]{:S(2)}, u32[]{:S(2)}) collective-permute-start(bf16[384,512]{1,0:T(8,128)(2,1)S(1)} %collective-permute-done.40.refs_3_), channel_id=1, source_target_pairs={{0,4},{1,5},{4,8},{5,9},{8,12},{9,13},{12,14},{13,15},{14,10},{15,... | collective-permute-start | bytes 1179656 | tf_op jit(solution)/shard_map/ppermute | solution.py:403
  145.4 24.2 %collective-permute-start.43 = (bf16[384,512]{1,0:T(8,128)(2,1)S(1)}, bf16[384,512]{1,0:T(8,128)(2,1)S(1)}, u32[]{:S(2)}, u32[]{:S(2)}) collective-permute-start(bf16[384,512]{1,0:T(8,128)(2,1)S(1)} %collective-permute-done.41.refs_4_), channel_id=1, source_target_pairs={{4,0},{5,1},{8,4},{9,5},{12,8},{13,9},{14,12},{15,13},{10,14},{11,... | collective-permute-start | bytes 1179656 | tf_op jit(solution)/shard_map/ppermute | solution.py:404
  177.9 46.3 %collective-permute-start.48 = (bf16[3072,512]{1,0:T(8,128)(2,1)S(1)}, bf16[3072,512]{1,0:T(8,128)(2,1)S(1)}, u32[]{:S(2)}, u32[]{:S(2)}) collective-permute-start(bf16[3072,512]{1,0:T(8,128)(2,1)S(1)} %get-tuple-element.167.refs_2_), channel_id=1, source_target_pairs={{0,1},{1,0},{2,3},{3,2},{4,5},{5,4},{6,7},{7,6},{8,9},{9,8},{10,11... | collective-permute-start | bytes 9437192 | tf_op jit(solution)/shard_map/ppermute | solution.py:331
  196.7 17.4 %collective-permute-start.36 = (bf16[384,512]{1,0:T(8,128)(2,1)S(1)}, bf16[384,512]{1,0:T(8,128)(2,1)S(1)}, u32[]{:S(2)}, u32[]{:S(2)}) collective-permute-start(bf16[384,512]{1,0:T(8,128)(2,1)S(1)} %collective-permute-done.34.refs_1_), channel_id=1, source_target_pairs={{0,4},{1,5},{4,8},{5,9},{8,12},{9,13},{12,14},{13,15},{14,10},{15,... | collective-permute-start | bytes 1179656 | tf_op jit(solution)/shard_map/ppermute | solution.py:403
  197.0 17.1 %collective-permute-start.37 = (bf16[384,512]{1,0:T(8,128)(2,1)S(1)}, bf16[384,512]{1,0:T(8,128)(2,1)S(1)}, u32[]{:S(2)}, u32[]{:S(2)}) collective-permute-start(bf16[384,512]{1,0:T(8,128)(2,1)S(1)} %collective-permute-done.35.refs_2_), channel_id=1, source_target_pairs={{4,0},{5,1},{8,4},{9,5},{12,8},{13,9},{14,12},{15,13},{10,14},{11,... | collective-permute-start | bytes 1179656 | tf_op jit(solution)/shard_map/ppermute | solution.py:404
  248.8 53.4 %collective-permute-start.54 = (bf16[3072,512]{1,0:T(8,128)(2,1)}, bf16[3072,512]{1,0:T(8,128)(2,1)S(1)}, u32[]{:S(2)}, u32[]{:S(2)}) collective-permute-start(bf16[3072,512]{1,0:T(8,128)(2,1)} %get-tuple-element.182.refs_2_), channel_id=1, source_target_pairs={{0,1},{1,0},{2,3},{3,2},{4,5},{5,4},{6,7},{7,6},{8,9},{9,8},{10,11... | collective-permute-start | bytes 9437192 | tf_op jit(solution)/shard_map/ppermute | solution.py:331
  266.2 19.4 %collective-permute-start.62 = (bf16[384,512]{1,0:T(8,128)(2,1)S(1)}, bf16[384,512]{1,0:T(8,128)(2,1)S(1)}, u32[]{:S(2)}, u32[]{:S(2)}) collective-permute-start(bf16[384,512]{1,0:T(8,128)(2,1)S(1)} %collective-permute-done.60.refs_3_), channel_id=1, source_target_pairs={{0,4},{1,5},{4,8},{5,9},{8,12},{9,13},{12,14},{13,15},{14,10},{15,... | collective-permute-start | bytes 1179656 | tf_op jit(solution)/shard_map/ppermute | solution.py:403
  266.8 18.9 %collective-permute-start.63 = (bf16[384,512]{1,0:T(8,128)(2,1)S(1)}, bf16[384,512]{1,0:T(8,128)(2,1)S(1)}, u32[]{:S(2)}, u32[]{:S(2)}) collective-permute-start(bf16[384,512]{1,0:T(8,128)(2,1)S(1)} %collective-permute-done.61.refs_4_), channel_id=1, source_target_pairs={{4,0},{5,1},{8,4},{9,5},{12,8},{13,9},{14,12},{15,13},{10,14},{11,... | collective-permute-start | bytes 1179656 | tf_op jit(solution)/shard_map/ppermute | solution.py:404
  294.1 43.8 %collective-permute-start.68 = (bf16[3072,512]{1,0:T(8,128)(2,1)S(1)}, bf16[3072,512]{1,0:T(8,128)(2,1)S(1)}, u32[]{:S(2)}, u32[]{:S(2)}) collective-permute-start(bf16[3072,512]{1,0:T(8,128)(2,1)S(1)} %get-tuple-element.203.refs_2_), channel_id=1, source_target_pairs={{0,1},{1,0},{2,3},{3,2},{4,5},{5,4},{6,7},{7,6},{8,9},{9,8},{10,11... | collective-permute-start | bytes 9437192 | tf_op jit(solution)/shard_map/ppermute | solution.py:331
  309.5 17.2 %collective-permute-start.56 = (bf16[384,512]{1,0:T(8,128)(2,1)S(1)}, bf16[384,512]{1,0:T(8,128)(2,1)S(1)}, u32[]{:S(2)}, u32[]{:S(2)}) collective-permute-start(bf16[384,512]{1,0:T(8,128)(2,1)S(1)} %collective-permute-done.52.refs_1_), channel_id=1, source_target_pairs={{0,4},{1,5},{4,8},{5,9},{8,12},{9,13},{12,14},{13,15},{14,10},{15,... | collective-permute-start | bytes 1179656 | tf_op jit(solution)/shard_map/ppermute | solution.py:403
  310.7 16.0 %collective-permute-start.57 = (bf16[384,512]{1,0:T(8,128)(2,1)S(1)}, bf16[384,512]{1,0:T(8,128)(2,1)S(1)}, u32[]{:S(2)}, u32[]{:S(2)}) collective-permute-start(bf16[384,512]{1,0:T(8,128)(2,1)S(1)} %collective-permute-done.53.refs_2_), channel_id=1, source_target_pairs={{4,0},{5,1},{8,4},{9,5},{12,8},{13,9},{14,12},{15,13},{10,14},{11,... | collective-permute-start | bytes 1179656 | tf_op jit(solution)/shard_map/ppermute | solution.py:404
  357.3 46.5 %collective-permute-start.72 = (bf16[3072,512]{1,0:T(8,128)(2,1)}, bf16[3072,512]{1,0:T(8,128)(2,1)}, u32[]{:S(2)}, u32[]{:S(2)}) collective-permute-start(bf16[3072,512]{1,0:T(8,128)(2,1)} %get-tuple-element.219.refs_2_), channel_id=1, source_target_pairs={{0,1},{1,0},{2,3},{3,2},{4,5},{5,4},{6,7},{7,6},{8,9},{9,8},{10,11... | collective-permute-start | bytes 9437192 | tf_op jit(solution)/shard_map/ppermute | solution.py:331
  365.4 62.0 %collective-permute-start.75 = (f32[192,512]{1,0:T(8,128)}, f32[192,512]{1,0:T(8,128)}, u32[]{:S(2)}, u32[]{:S(2)}) collective-permute-start(f32[192,512]{1,0:T(8,128)} %constant_dynamic-slice_fusion.7), channel_id=1, source_target_pairs={{0,1},{1,0},{2,3},{3,2},{4,5},{5,4},{6,7},{7,6},{8,9},{9,8},{10,11... | collective-permute-start | bytes 1179656 | tf_op jit(solution)/shard_map/ppermute | solution.py:331
  370.6 60.0 %collective-permute-start.76 = (f32[192,512]{1,0:T(8,128)}, f32[192,512]{1,0:T(8,128)}, u32[]{:S(2)}, u32[]{:S(2)}) collective-permute-start(f32[192,512]{1,0:T(8,128)} %constant_dynamic-slice_fusion.6), channel_id=1, source_target_pairs={{0,1},{1,0},{2,3},{3,2},{4,5},{5,4},{6,7},{7,6},{8,9},{9,8},{10,11... | collective-permute-start | bytes 1179656 | tf_op jit(solution)/shard_map/ppermute | solution.py:331
  383.2 49.3 %collective-permute-start.77 = (f32[192,512]{1,0:T(8,128)}, f32[192,512]{1,0:T(8,128)}, u32[]{:S(2)}, u32[]{:S(2)}) collective-permute-start(f32[192,512]{1,0:T(8,128)} %constant_dynamic-slice_fusion.5), channel_id=1, source_target_pairs={{0,1},{1,0},{2,3},{3,2},{4,5},{5,4},{6,7},{7,6},{8,9},{9,8},{10,11... | collective-permute-start | bytes 1179656 | tf_op jit(solution)/shard_map/ppermute | solution.py:331
  384.3 19.4 %collective-permute-start.73 = (f32[8,512]{1,0:T(8,128)S(1)}, f32[8,512]{1,0:T(8,128)S(1)}, u32[]{:S(2)}, u32[]{:S(2)}) collective-permute-start(f32[8,512]{1,0:T(8,128)S(1)} %get-tuple-element.220.refs_3_), channel_id=1, source_target_pairs={{0,1},{1,0},{2,3},{3,2},{4,5},{5,4},{6,7},{7,6},{8,9},{9,8},{10,11... | collective-permute-start | bytes 49160 | tf_op jit(solution)/shard_map/ppermute | solution.py:331
  403.7 21.8 %collective-permute-start.82 = (f32[192,512]{1,0:T(8,128)}, f32[192,512]{1,0:T(8,128)}, u32[]{:S(2)}, u32[]{:S(2)}) collective-permute-start(f32[192,512]{1,0:T(8,128)} %constant_dynamic-slice_fusion), channel_id=1, source_target_pairs={{0,1},{1,0},{2,3},{3,2},{4,5},{5,4},{6,7},{7,6},{8,9},{9,8},{10,11... | collective-permute-start | bytes 1179656 | tf_op jit(solution)/shard_map/ppermute | solution.py:331
  (85 other events, 839.5 us)

commit v4 on v0

--- a/solution.py
+++ b/solution.py
@@ -1,9 +1,18 @@
+import functools
+
 import jax
 import jax.numpy as jnp
 from jax import lax
+from jax.experimental import pallas as pl
+from jax.experimental.pallas import tpu as pltpu
 from jax.sharding import PartitionSpec as P
 
 off_weight = 0.0051
+parts = (3, 3, 2)
+lanes = 256
+tile_rows = 512
+spare = 16
+vmem = 40 * 1024 * 1024
 
 
 def local_term(columns, full_two):
@@ -86,10 +95,355 @@
     return (grad_one, grad_two, jnp.reshape(loss, (1,)))
 
 
+def total_rows(total):
+    high = total.astype(jnp.bfloat16).astype(jnp.float32)
+    row = lax.broadcasted_iota(jnp.int32, (spare, total.shape[1]), 0)
+    both = jnp.where(row == 0, high, jnp.where(row == 1, total - high, 0.0))
+    return both.astype(jnp.bfloat16)
+
+
+def norm_kernel(rows, turned, place_ref, raw_ref, norm_ref, *rest):
+    samples = raw_ref.shape[0]
+    starts = range(0, samples, rows)
+    total = jnp.zeros((1, lanes), jnp.float32)
+    square = jnp.zeros((1, lanes), jnp.float32)
+    for start in starts:
+        values = raw_ref[start : start + rows, :].astype(jnp.float32)
+        total += jnp.sum(values, axis=0, keepdims=True)
+        square += jnp.sum(values * values, axis=0, keepdims=True)
+    mean = total / samples
+    inv = 1.0 / jnp.sqrt(square / samples - mean * mean + 1e-05)
+    norm_total = jnp.zeros((1, lanes), jnp.float32)
+
+    def normed(values):
+        return ((values.astype(jnp.float32) - mean) * inv).astype(jnp.bfloat16)
+
+    for start in starts:
+        norm = normed(raw_ref[start : start + rows, :])
+        norm_total += jnp.sum(norm.astype(jnp.float32), axis=0, keepdims=True)
+        if turned:
+            norm_ref[:, start : start + rows] = norm.T
+        else:
+            norm_ref[start : start + rows, :] = norm
+    stat_ref = rest[-1]
+    row = lax.broadcasted_iota(jnp.int32, (8, lanes), 0)
+    stat_ref[...] = jnp.where(row == 0, inv, jnp.where(row == 1, norm_total, 0.0))
+    if turned:
+        pair_ref = rest[0]
+        first = pl.multiple_of(place_ref[1] * rows, 16)
+        pair_ref[:rows, :] = normed(raw_ref[pl.ds(first, rows), :])
+        pair_ref[rows:, :] = total_rows(norm_total)
+
+
+def norm_half(place, raw, rows, turned):
+    samples, width = raw.shape
+    half = width // 2
+    tiles = half // lanes
+    column = lambda tile, place_ref: (0, tile)
+    if turned:
+        norm_spec = pl.BlockSpec((lanes, samples), lambda tile, place_ref: (tile, 0))
+        pair_specs = [pl.BlockSpec((rows + spare, lanes), column)]
+        norm_shape = (half, samples)
+        pair_shapes = [jax.ShapeDtypeStruct((rows + spare, half), jnp.bfloat16)]
+    else:
+        norm_spec = pl.BlockSpec((samples, lanes), column)
+        pair_specs, pair_shapes = [], []
+        norm_shape = (samples, half)
+    return pl.pallas_call(
+        functools.partial(norm_kernel, rows, turned),
+        grid_spec=pltpu.PrefetchScalarGridSpec(
+            num_scalar_prefetch=1,
+            grid=(tiles,),
+            in_specs=[
+                pl.BlockSpec(
+                    (samples, lanes), lambda tile, place_ref: (0, place_ref[0] * tiles + tile)
+                )
+            ],
+            out_specs=[norm_spec] + pair_specs + [pl.BlockSpec((8, lanes), column)],
+        ),
+        out_shape=[jax.ShapeDtypeStruct(norm_shape, jnp.bfloat16)]
+        + pair_shapes
+        + [jax.ShapeDtypeStruct((8, half), jnp.float32)],
+        compiler_params=pltpu.CompilerParams(vmem_limit_bytes=vmem),
+        cost_estimate=pl.CostEstimate(
+            flops=10 * samples * half, bytes_accessed=4 * samples * half, transcendentals=0
+        ),
+        name="norm_one" if turned else "norm_two",
+    )(place, raw)
+
+
+def corr_kernel(samples, diag_at, begins, *refs):
+    place_ref, one_ref, pair_ref, two_ref, stat_ref = refs[:5]
+    rest = list(refs[5:])
+    acc_in = None if begins else rest.pop(0)
+    loss_in = None if begins else rest.pop(0)
+    acc_out, loss_out, keep_out, send_out, ext_ref, grad_ref, prod_ref, back_ref = rest
+    ext = pair_ref.shape[0]
+    rows = ext - spare
+    tile = pl.program_id(0)
+    first = pl.multiple_of(place_ref[1] * rows, 16)
+
+    @pl.when(tile == 0)
+    def _():
+        ext_ref[:rows, :] = two_ref[pl.ds(first, rows), :]
+        ext_ref[rows:, :] = total_rows(stat_ref[1:2, :])
+        prod_ref[...] = jnp.zeros_like(prod_ref)
+        loss_out[...] = jnp.zeros_like(loss_out) if begins else loss_in[...]
+
+    summed = jnp.dot(one_ref[...], two_ref[...], preferred_element_type=jnp.float32)
+    height, width = summed.shape
+    grad = summed * (2.0 * off_weight / samples)
+    loss = summed * summed
+    if diag_at is not None:
+        ahead = lax.broadcasted_iota(jnp.int32, summed.shape, 1) - lax.broadcasted_iota(
+            jnp.int32, summed.shape, 0
+        )
+        diag = ahead == tile * height - diag_at
+        grad = jnp.where(diag, summed * (2.0 / samples) - 2.0, grad)
+        loss = jnp.where(diag, (samples - summed) ** 2 * (1.0 / off_weight), loss)
+    grad = grad.astype(jnp.bfloat16)
+    grad_ref[pl.ds(tile * height, height), :] = grad
+    prod = grad.astype(jnp.float32) * summed
+
+    def fold(value):
+        folded = value[:, :128]
+        for start in range(128, width, 128):
+            folded += value[:, start : start + 128]
+        return folded
+
+    loss_out[...] += fold(jnp.sum(loss.reshape(height // 8, 8, width), axis=0))
+    prod_ref[...] += jnp.sum(prod.reshape(height // 8, 8, width), axis=0)
+    prod_row = jnp.sum(fold(prod).T, axis=0, keepdims=True)
+    back = lax.dot_general(
+        ext_ref[...], grad, (((1,), (1,)), ((), ())), preferred_element_type=jnp.float32
+    )
+    acc_out[...] = back if begins else acc_in[...] + back
+    row = lax.broadcasted_iota(jnp.int32, (8, height), 0)
+    acc_out[rows + 8 :, :] += jnp.where(row == 0, prod_row, 0.0)
+
+    @pl.when(tile == pl.num_programs(0) - 1)
+    def _():
+        back_two = jnp.dot(pair_ref[...], grad_ref[...], preferred_element_type=jnp.float32)
+        sum_back = (back_two[rows : rows + 1, :] + back_two[rows + 1 : rows + 2, :]) / samples
+        sum_prod = jnp.sum(prod_ref[...], axis=0, keepdims=True) / samples
+        normal = ext_ref[:rows, :].astype(jnp.float32)
+        back_ref[...] = stat_ref[0:1, :] * (back_two[:rows, :] - sum_back - normal * sum_prod)
+        side = place_ref[0]
+        keep_out[...] = back_ref[pl.ds(pl.multiple_of(side * (rows // 2), 8), rows // 2), :]
+        send_out[...] = back_ref[pl.ds(pl.multiple_of((1 - side) * (rows // 2), 8), rows // 2), :]
+
+
+def corr_half(place, norm_one, pair_one, norm_two, stat_two, acc, diag_at):
+    half, samples = norm_one.shape
+    width = norm_two.shape[1]
+    ext = pair_one.shape[0]
+    rows = ext - spare
+    tiles = half // tile_rows
+
+    def whole(shape):
+        return pl.BlockSpec(shape, lambda tile: (0, 0), pipeline_mode=pl.Buffered(1))
+
+    def kept(shape):
+        return pl.BlockSpec(shape, lambda tile: (0, 0))
+
+    acc_spec = pl.BlockSpec((ext, tile_rows), lambda tile: (0, tile))
+    operands = [place, norm_one, pair_one, norm_two, stat_two]
+    in_specs = [
+        pl.BlockSpec(memory_space=pltpu.SMEM),
+        pl.BlockSpec((tile_rows, samples), lambda tile: (tile, 0)),
+        whole((ext, half)),
+        whole((samples, width)),
+        whole((8, width)),
+    ]
+    aliases = {}
+    if acc is not None:
+        aliases = {5: 0, 6: 1}
+        operands += list(acc)
+        in_specs += [acc_spec, kept((8, 128))]
+    return pl.pallas_call(
+        functools.partial(corr_kernel, samples, diag_at, acc is None),
+        grid=(tiles,),
+        in_specs=in_specs,
+        out_specs=[acc_spec, kept((8, 128)), kept((rows // 2, width)), kept((rows // 2, width))],
+        out_shape=[
+            jax.ShapeDtypeStruct((ext, half), jnp.float32),
+            jax.ShapeDtypeStruct((8, 128), jnp.float32),
+            jax.ShapeDtypeStruct((rows // 2, width), jnp.float32),
+            jax.ShapeDtypeStruct((rows // 2, width), jnp.float32),
+        ],
+        scratch_shapes=[
+            pltpu.VMEM((ext, width), jnp.bfloat16),
+            pltpu.VMEM((half, width), jnp.bfloat16),
+            pltpu.VMEM((8, width), jnp.float32),
+            pltpu.VMEM((rows, width), jnp.float32),
+        ],
+        input_output_aliases=aliases,
+        compiler_params=pltpu.CompilerParams(vmem_limit_bytes=vmem),
+        cost_estimate=pl.CostEstimate(
+            flops=2 * half * width * (samples + 2 * ext),
+            bytes_accessed=2 * samples * (half + width),
+            transcendentals=0,
+        ),
+        name="corr_half",
+    )(*operands)
+
+
+def place_kernel(side_ref, keep_ref, get_ref, *refs):
+    refs[-1][...] = (keep_ref[...] + get_ref[...]).astype(jnp.bfloat16)
+
+
+def place_two(side, keep, get, placed, far, first, width):
+    rows, step = keep.shape
+    half = width // 2
+
+    def column(tile, side_ref):
+        side = 1 - side_ref[0] if far else side_ref[0]
+        return (0, (side * half + first) // lanes + tile)
+
+    block = pl.BlockSpec((rows, lanes), lambda tile, side_ref: (0, tile))
+    held = [] if placed is None else [placed]
+    return pl.pallas_call(
+        place_kernel,
+        grid_spec=pltpu.PrefetchScalarGridSpec(
+            num_scalar_prefetch=1,
+            grid=(step // lanes,),
+            in_specs=[block, block] + [pl.BlockSpec(memory_space=pl.ANY)] * len(held),
+            out_specs=pl.BlockSpec((rows, lanes), column),
+        ),
+        out_shape=jax.ShapeDtypeStruct((rows, width), jnp.bfloat16),
+        input_output_aliases={3: 0} if held else {},
+        cost_estimate=pl.CostEstimate(
+            flops=rows * step, bytes_accessed=10 * rows * step, transcendentals=0
+        ),
+        name="place_two",
+    )(side, keep, get, *held)
+
+
+def finish_kernel(samples, side_ref, acc_ref, pair_ref, stat_ref, keep_out, send_out, done_ref):
+    rows = done_ref.shape[0]
+    sum_back = (acc_ref[rows : rows + 1, :] + acc_ref[rows + 1 : rows + 2, :]) / samples
+    sum_prod = acc_ref[rows + 8 : rows + 9, :] / samples
+    normal = pair_ref[:rows, :].astype(jnp.float32)
+    done_ref[...] = stat_ref[0:1, :] * (acc_ref[:rows, :] - sum_back - normal * sum_prod)
+    side = side_ref[0]
+    keep = done_ref[pl.ds(pl.multiple_of(side * (rows // 2), 8), rows // 2), :]
+    send = done_ref[pl.ds(pl.multiple_of((1 - side) * (rows // 2), 8), rows // 2), :]
+    keep_out[...] = keep.astype(jnp.bfloat16)
+    send_out[...] = send.astype(jnp.bfloat16)
+
+
+def finish_one(side, acc, pair, stat, samples):
+    ext, half = acc.shape
+    rows = ext - spare
+    block = lambda height: pl.BlockSpec((height, tile_rows), lambda tile: (0, tile))
+    return pl.pallas_call(
+        functools.partial(finish_kernel, samples),
+        grid=(half // tile_rows,),
+        in_specs=[pl.BlockSpec(memory_space=pltpu.SMEM), block(ext), block(ext), block(8)],
+        out_specs=[block(rows // 2), block(rows // 2)],
+        out_shape=[jax.ShapeDtypeStruct((rows // 2, half), jnp.bfloat16)] * 2,
+        scratch_shapes=[pltpu.VMEM((rows, tile_rows), jnp.float32)],
+        cost_estimate=pl.CostEstimate(
+            flops=5 * rows * half, bytes_accessed=8 * rows * half, transcendentals=0
+        ),
+        name="finish_one",
+    )(side, acc, pair, stat)
+
+
+def join_kernel(side_ref, keep_ref, get_ref, out_ref):
+    @pl.when(pl.program_id(0) == 0)
+    def _():
+        out_ref[...] = keep_ref[...]
+
+    @pl.when(pl.program_id(0) == 1)
+    def _():
+        out_ref[...] = get_ref[...]
+
+
+def join_one(side, keep, get):
+    rows, half = keep.shape
+    block = pl.BlockSpec((rows, half), lambda tile, side_ref: (0, 0))
+    column = lambda tile, side_ref: (0, side_ref[0] + tile - 2 * side_ref[0] * tile)
+    return pl.pallas_call(
+        join_kernel,
+        grid_spec=pltpu.PrefetchScalarGridSpec(
+            num_scalar_prefetch=1,
+            grid=(2,),
+            in_specs=[block, block],
+            out_specs=pl.BlockSpec((rows, half), column),
+        ),
+        out_shape=jax.ShapeDtypeStruct((rows, 2 * half), jnp.bfloat16),
+        cost_estimate=pl.CostEstimate(
+            flops=0, bytes_accessed=8 * rows * half, transcendentals=0
+        ),
+        name="join_one",
+    )(side, keep, get)
+
+
+def pair_shards(view_one, view_two):
+    rows, width = view_one.shape
+    batches = lax.axis_size("batch")
+    samples = rows * batches
+    half = width // 2
+    index = lax.axis_index("batch")
+    place = jnp.stack([index % 2, index // 2]).astype(jnp.int32)
+    swap = [(i, i ^ 1) for i in range(batches)]
+
+    def swapped(value):
+        return lax.ppermute(value, "batch", swap)
+
+    def gathered(block):
+        return lax.all_gather(block, "batch", axis=0, tiled=True)
+
+    steps = [half * part // sum(parts) for part in parts]
+    firsts = [sum(steps[:count]) for count in range(len(parts))]
+
+    def columns(count):
+        first, last = firsts[count], firsts[count] + steps[count]
+        return jnp.concatenate(
+            [view_two[:, side * half + first : side * half + last] for side in range(2)], axis=1
+        )
+
+    raw_one = gathered(view_one)
+    block, raw_one = lax.optimization_barrier((columns(0), raw_one))
+    raw_two = gathered(block)
+    one = norm_half(place, raw_one, 2 * rows, True)
+    acc = None
+    grad_two = None
+    for count, (step, first) in enumerate(zip(steps, firsts)):
+        if count + 1 < len(parts):
+            block = columns(count + 1)
+            if acc is None:
+                block, raw_two, *one = lax.optimization_barrier((block, raw_two, *one))
+            else:
+                block, raw_two, *acc = lax.optimization_barrier((block, raw_two, *acc))
+            raw_next = gathered(block)
+        else:
+            raw_two, grad_two, *acc = lax.optimization_barrier((raw_two, grad_two, *acc))
+        norm_one, pair_one, stat_one = one
+        norm, stat = norm_half(place, raw_two, 2 * rows, False)
+        far_norm, far_stat = swapped(norm), swapped(stat)
+        *acc, keep_own, send_own = corr_half(place, norm_one, pair_one, norm, stat, acc, first)
+        *acc, keep_far, send_far = corr_half(
+            place, norm_one, pair_one, far_norm, far_stat, acc, None
+        )
+        get_own, get_far = swapped(send_far), swapped(send_own)
+        grad_two = place_two(place, keep_own, get_own, grad_two, False, first, width)
+        grad_two = place_two(place, keep_far, get_far, grad_two, True, first, width)
+        raw_two = raw_next
+    acc, loss = acc
+    keep, send = finish_one(place, acc, pair_one, stat_one, samples)
+    grad_one = join_one(place, keep, swapped(send))
+    loss = jnp.sum(loss) * (off_weight / (samples * samples))
+    loss = (loss + swapped(loss)) / width
+    return (grad_one, grad_two, jnp.reshape(loss, (1,)))
+
+
 def solution(mesh):
     placed = (P(("groups", "batch"), "feat"), P(("groups", "batch"), "feat"))
+    paired = mesh.shape["feat"] == 1 and mesh.shape["batch"] % 4 == 0
     return jax.shard_map(
-        shards,
+        pair_shards if paired else shards,
         mesh=mesh,
         in_specs=placed,
         out_specs=(P(("groups", "batch"), "feat"), P(("groups", "batch"), "feat"), P("groups")),

time: 1040 us -> 442 us (0.42)
  waiting for transfers between devices: 863 us -> 225 us
  Pallas kernels: 0 us -> 161 us
  blocking collectives: 86.7 us -> 0 us
  matrix products: 57.4 us -> 0 us
  local copies, waits for them, and re-layouts: 0.01 us -> 30.7 us
  other arithmetic: 16.9 us -> 3.18 us
    reduce_scatter x1 -> x0, waiting for transfers between devices: 639 us -> none  [shards(): lax.psum_scatter(local_term(norm_one, full_two), 'batch', scatter_dimensi...]
    pallas_call x0 -> x18, Pallas kernels: none -> 161 us  [the longest x6 106 us: corr_half(): pl.pallas_call(functools.partial(corr_kernel, samples, diag_at, acc is No...]
    psum x1 -> x0, waiting for transfers between devices: 87.6 us -> none  [shards(): lax.psum((jnp.sum(values_one, axis=0), jnp.sum(values_one * values_one, a...]
    all_gather x1 -> x4, waiting for transfers between devices: 136 us -> 224 us  [gathered(): return lax.all_gather(block, 'batch', axis=0, tiled=True)]
    psum x2 -> x0, blocking collectives: 86.7 us -> none  [the longest x1 56 us: shards(): lax.psum(jnp.sum(back_one * norm_one_f, axis=0).astype(jnp.bfloat16), 'ba...]
    dot_general x3 -> x0, matrix products: 57.4 us -> none  [the longest x1 23.2 us: local_term(): lax.dot_general(columns, full_two, (((0,), (0,)), ((), ())), preferred_el...]
    unnamed x6 -> x58, local copies, waits for them, and re-layouts: 0.01 us -> 30.6 us
  transfers between devices with their start and end apart: 3 -> 18, of which waited for: 3 -> 4; matrix products, arithmetic and copies ran while one was open for 0% -> 1% of each run, Pallas kernels for 0% -> 31%
where the time goes in v4:
time: 442 us; the launch traced here: 441 us
  waiting for transfers between devices  225 us (51%)
  Pallas kernels  161 us (36%)
  local copies, waits for them, and re-layouts  30.7 us (7%)
  between operations  16.4 us (4%)
  starting transfers between devices  4.91 us (1%)
    all_gather x4, waiting for transfers between devices, gathered(): return lax.all_gather(block, 'batch', axis=0, tiled=True)  224 us
    pallas_call x6, Pallas kernels, corr_half(): pl.pallas_call(functools.partial(corr_kernel, samples, diag_at, acc is No...  106 us
    unnamed x58, local copies, waits for them, and re-layouts  30.6 us
    pallas_call x4, Pallas kernels, norm_half(): pl.pallas_call(functools.partial(norm_kernel, rows, turned), grid_spec=pl...  27.7 us
    pallas_call x6, Pallas kernels, place_two(): pl.pallas_call(place_kernel, grid_spec=pltpu.PrefetchScalarGridSpec(num_s...  19.2 us
  transfers between devices with their start and end apart: 18, of which 4 were waited for; matrix products, arithmetic and copies ran while one was open for 1% of the time, Pallas kernels for 31%

profile of v4, /device:TPU:1, one launch (start us, length us, event | category | flops | bytes accessed | tf_op | source)
XLA Modules:
  0.0 440.8 jit_solution(13697801721990071496)
XLA Ops:
  9.5 131.2 %all-gather.5.cloned.1.call-done.raw_ref = bf16[3072,4096]{1,0:T(8,128)(2,1)} async-done(((bf16[192,4096]{1,0:T(8,128)(2,1)}), bf16[3072,4096]{1,0:T(8,128)(2,1)}) %all-gather.5.cloned.1.call-update) | async-done | bytes 25165840 | tf_op jit(solution)/shard_map/all_gather | solution.py:396
  141.8 12.4 %norm_one.1 = (bf16[2048,3072]{1,0:T(8,128)(2,1)S(1)}, bf16[400,2048]{1,0:T(8,128)(2,1)S(1)}, f32[8,2048]{1,0:T(8,128)S(1)}) custom-call(s32[2]{0:T(128)S(1)} %pad_add_fusion.place_ref.refs_0_.side_ref, bf16[3072,4096]{1,0:T(8,128)(2,1)} %all-gather.5.cloned.1.call-done.raw_ref), custom_call_target="tpu_custom_call" | custom-call | flops 62914560 | bytes 25165824 | tf_op jit(solution)/shard_map/norm_one/pallas_call | solution.py:152
  156.0 4.6 %copy-done.17 = bf16[2048,3072]{1,0:T(8,128)(2,1)} copy-done((bf16[2048,3072]{1,0:T(8,128)(2,1)}, bf16[2048,3072]{1,0:T(8,128)(2,1)S(1)}, u32[]{:S(2)}) %copy-start.17) | copy-done | bytes 12582936
  160.5 64.5 %all-gather.7.cloned.1.call-done.raw_ref = bf16[3072,1536]{1,0:T(8,128)(2,1)} async-done(((bf16[192,1536]{1,0:T(8,128)(2,1)}), bf16[3072,1536]{1,0:T(8,128)(2,1)}) %all-gather.7.cloned.1.call-update) | async-done | bytes 9437200 | tf_op jit(solution)/shard_map/all_gather | solution.py:396
  225.1 3.7 copy-done
  228.8 5.8 %norm_two.3 = (bf16[3072,768]{1,0:T(8,128)(2,1)}, f32[8,768]{1,0:T(8,128)S(1)}) custom-call(s32[2]{0:T(128)S(1)} %pad_add_fusion.place_ref.refs_0_.side_ref, bf16[3072,1536]{1,0:T(8,128)(2,1)S(1)} %copy-done), custom_call_target="tpu_custom_call" | custom-call | flops 23592960 | bytes 9437184 | tf_op jit(solution)/shard_map/norm_two/pallas_call | solution.py:152
  237.4 20.5 %corr_half.6 = (f32[400,2048]{1,0:T(8,128)S(1)}, f32[8,128]{1,0:T(8,128)S(1)}, f32[192,768]{1,0:T(8,128)S(1)}, f32[192,768]{1,0:T(8,128)}) custom-call(s32[2]{0:T(128)S(1)} %pad_add_fusion.place_ref.refs_0_.side_ref, bf16[2048,3072]{1,0:T(8,128)(2,1)} %copy-done.17, bf16[400,2048]{1,0:T(8,128)(2,1)S(1)} %copy-done.5, ...), custom_call_target="tpu_custom_call" | custom-call | flops 12180258816 | bytes 17301504 | tf_op jit(solution)/shard_map/corr_half/pallas_call | solution.py:263
  258.7 19.2 %corr_half.7 = (f32[400,2048]{1,0:T(8,128)S(1)}, f32[8,128]{1,0:T(8,128)S(1)}, f32[192,768]{1,0:T(8,128)S(1)}, f32[192,768]{1,0:T(8,128)S(1)}) custom-call(s32[2]{0:T(128)S(1)} %pad_add_fusion.place_ref.refs_0_.side_ref, bf16[2048,3072]{1,0:T(8,128)(2,1)} %copy-done.17, ...), custom_call_target="tpu_custom_call", output_to_operand_aliasing={{0}: (5, {}), {1}: (6, {})} | custom-call | flops 12180258816 | bytes 17301504 | tf_op jit(solution)/shard_map/corr_half/pallas_call | solution.py:263
  279.5 28.0 %all-gather.9.cloned.1.call-done.raw_ref = bf16[3072,1536]{1,0:T(8,128)(2,1)} async-done(((bf16[192,1536]{1,0:T(8,128)(2,1)}), bf16[3072,1536]{1,0:T(8,128)(2,1)}) %all-gather.9.cloned.1.call-update) | async-done | bytes 9437200 | tf_op jit(solution)/shard_map/all_gather | solution.py:396
  307.6 3.7 copy-done.1
  311.2 5.8 %norm_two.4 = (bf16[3072,768]{1,0:T(8,128)(2,1)}, f32[8,768]{1,0:T(8,128)S(1)}) custom-call(s32[2]{0:T(128)S(1)} %pad_add_fusion.place_ref.refs_0_.side_ref, bf16[3072,1536]{1,0:T(8,128)(2,1)S(1)} %copy-done.1), custom_call_target="tpu_custom_call" | custom-call | flops 23592960 | bytes 9437184 | tf_op jit(solution)/shard_map/norm_two/pallas_call | solution.py:152
  318.0 20.6 %corr_half.8 = (f32[400,2048]{1,0:T(8,128)S(1)}, f32[8,128]{1,0:T(8,128)S(1)}, f32[192,768]{1,0:T(8,128)S(1)}, f32[192,768]{1,0:T(8,128)}) custom-call(s32[2]{0:T(128)S(1)} %pad_add_fusion.place_ref.refs_0_.side_ref, bf16[2048,3072]{1,0:T(8,128)(2,1)} %copy-done.17, bf16[400,2048]{1,0:T(8,128)(2,1)S(1)} %copy-done.6, ...), custom_call_target="tpu_custom_call", output_to_operand_aliasing={{0}: (5, {}), {1}: (6, {})} | custom-call | flops 12180258816 | bytes 17301504 | tf_op jit(solution)/shard_map/corr_half/pallas_call | solution.py:263
  339.6 18.7 %corr_half.9 = (f32[400,2048]{1,0:T(8,128)S(1)}, f32[8,128]{1,0:T(8,128)S(1)}, f32[192,768]{1,0:T(8,128)S(1)}, f32[192,768]{1,0:T(8,128)}) custom-call(s32[2]{0:T(128)S(1)} %pad_add_fusion.place_ref.refs_0_.side_ref, bf16[2048,3072]{1,0:T(8,128)(2,1)} %copy-done.17, bf16[400,2048]{1,0:T(8,128)(2,1)S(1)} %copy-done.6, ...), custom_call_target="tpu_custom_call", output_to_operand_aliasing={{0}: (5, {}), {1}: (6, {})} | custom-call | flops 12180258816 | bytes 17301504 | tf_op jit(solution)/shard_map/corr_half/pallas_call | solution.py:263
  360.5 3.5 place_two.6.refs_0_
  364.0 3.5 place_two.7.refs_0_
  367.4 3.5 place_two.8.refs_0_
  370.9 3.6 place_two.9.refs_0_
  374.6 2.8 copy-done.2
  377.4 3.7 norm_two.5
  381.6 14.2 %corr_half.10 = (f32[400,2048]{1,0:T(8,128)S(1)}, f32[8,128]{1,0:T(8,128)S(1)}, f32[192,512]{1,0:T(8,128)S(1)}, f32[192,512]{1,0:T(8,128)S(1)}) custom-call(s32[2]{0:T(128)S(1)} %copy-done.15, bf16[2048,3072]{1,0:T(8,128)(2,1)} %copy-done.17, bf16[400,2048]{1,0:T(8,128)(2,1)S(1)} %copy-done.7, ...), custom_call_target="tpu_custom_call", output_to_operand_aliasing={{0}: (5, {}), {1}: (6, {})} | custom-call | flops 8120172544 | bytes 15728640 | tf_op jit(solution)/shard_map/corr_half/pallas_call | solution.py:263
  397.3 12.8 %corr_half.11 = (f32[400,2048]{1,0:T(8,128)S(1)}, f32[8,128]{1,0:T(8,128)S(1)}, f32[192,512]{1,0:T(8,128)S(1)}, f32[192,512]{1,0:T(8,128)S(1)}) custom-call(s32[2]{0:T(128)S(1)} %copy-done.15, bf16[2048,3072]{1,0:T(8,128)(2,1)} %copy-done.17, bf16[400,2048]{1,0:T(8,128)(2,1)S(1)} %copy-done.7, ...), custom_call_target="tpu_custom_call", output_to_operand_aliasing={{0}: (5, {}), {1}: (6, {})} | custom-call | flops 8120172544 | bytes 15728640 | tf_op jit(solution)/shard_map/corr_half/pallas_call | solution.py:263
  413.3 4.8 %finish_one.1 = (bf16[192,2048]{1,0:T(8,128)(2,1)}, bf16[192,2048]{1,0:T(8,128)(2,1)}) custom-call(s32[2]{0:T(128)} %copy-done.14, f32[400,2048]{1,0:T(8,128)} %copy-done.3, bf16[400,2048]{1,0:T(8,128)(2,1)} %copy-done.4, f32[8,2048]{1,0:T(8,128)} %copy-done.16), custom_call_target="tpu_custom_call" | custom-call | flops 3932160 | bytes 6291456 | tf_op jit(solution)/shard_map/finish_one/pallas_call | solution.py:339
  426.4 2.6 place_two.11
  429.9 3.3 join_one.1
  (99 shorter events, 27.6 us)
Async XLA Ops:
  7.2 133.6 %all-gather.5.cloned.1.call-start = ((), (), s32[]{:S(2)}) async-start(), calls=%async_computation | async-start | bytes 26738688 | tf_op jit(solution)/shard_map/all_gather | solution.py:396
  7.9 217.1 %all-gather.7.cloned.1.call-start = ((), (), s32[]{:S(2)}) async-start(), calls=%async_computation.1 | async-start | bytes 10027008 | tf_op jit(solution)/shard_map/all_gather | solution.py:396
  140.8 166.8 %all-gather.9.cloned.1.call-start = ((), (), s32[]{:S(2)}) async-start(), calls=%async_computation.2 | async-start | bytes 10027008 | tf_op jit(solution)/shard_map/all_gather | solution.py:396
  140.9 198.6 %copy-start.14 = (s32[2]{0:T(128)}, s32[2]{0:T(128)S(1)}, u32[]{:S(2)}) copy-start(s32[2]{0:T(128)S(1)} %pad_add_fusion.place_ref.refs_0_.side_ref) | copy-start | bytes 28
  156.0 4.6 %copy-start.17 = (bf16[2048,3072]{1,0:T(8,128)(2,1)}, bf16[2048,3072]{1,0:T(8,128)(2,1)S(1)}, u32[]{:S(2)}) copy-start(bf16[2048,3072]{1,0:T(8,128)(2,1)S(1)} %get-tuple-element.58.refs_1_) | copy-start | bytes 37748740
  225.1 149.5 %all-gather.11.cloned.1.call-start = ((), (), s32[]{:S(2)}) async-start(), calls=%async_computation.3 | async-start | bytes 6684672 | tf_op jit(solution)/shard_map/all_gather | solution.py:396
  234.6 24.1 %collective-permute-start = (bf16[3072,768]{1,0:T(8,128)(2,1)}, bf16[3072,768]{1,0:T(8,128)(2,1)}, u32[]{:S(2)}, u32[]{:S(2)}) collective-permute-start(bf16[3072,768]{1,0:T(8,128)(2,1)} %get-tuple-element.62.refs_3_), channel_id=1, source_target_pairs={{0,1},{1,0},{2,3},{3,2},{4,5},{5,4},{6,7},{7,6},{8,9},{9,8},{10,11... | collective-permute-start | bytes 14155784 | tf_op jit(solution)/shard_map/ppermute | solution.py:393
  235.7 23.0 %collective-permute-start.1 = (f32[8,768]{1,0:T(8,128)S(1)}, f32[8,768]{1,0:T(8,128)S(1)}, u32[]{:S(2)}, u32[]{:S(2)}) collective-permute-start(f32[8,768]{1,0:T(8,128)S(1)} %get-tuple-element.63.refs_4_), channel_id=1, source_target_pairs={{0,1},{1,0},{2,3},{3,2},{4,5},{5,4},{6,7},{7,6},{8,9},{9,8},{10,11... | collective-permute-start | bytes 73736 | tf_op jit(solution)/shard_map/ppermute | solution.py:393
  311.2 6.3 %copy-start.19 = (f32[192,768]{1,0:T(8,128)S(1)}, f32[192,768]{1,0:T(8,128)}, u32[]{:S(2)}) copy-start(f32[192,768]{1,0:T(8,128)} %copy-done.18) | copy-start | bytes 1769476
  311.2 6.8 %copy-start.6 = (bf16[400,2048]{1,0:T(8,128)(2,1)S(1)}, bf16[400,2048]{1,0:T(8,128)(2,1)}, u32[]{:S(2)}) copy-start(bf16[400,2048]{1,0:T(8,128)(2,1)} %copy-done.4) | copy-start | bytes 4915204
  317.0 22.5 %collective-permute-start.2 = (bf16[3072,768]{1,0:T(8,128)(2,1)}, bf16[3072,768]{1,0:T(8,128)(2,1)S(1)}, u32[]{:S(2)}, u32[]{:S(2)}) collective-permute-start(bf16[3072,768]{1,0:T(8,128)(2,1)} %get-tuple-element.70.refs_3_), channel_id=1, source_target_pairs={{0,1},{1,0},{2,3},{3,2},{4,5},{5,4},{6,7},{7,6},{8,9},{9,8},{10,11... | collective-permute-start | bytes 14155784 | tf_op jit(solution)/shard_map/ppermute | solution.py:393
  317.3 46.7 %collective-permute-start.6 = (f32[192,768]{1,0:T(8,128)}, f32[192,768]{1,0:T(8,128)}, u32[]{:S(2)}, u32[]{:S(2)}) collective-permute-start(f32[192,768]{1,0:T(8,128)} %get-tuple-element.81), channel_id=1, source_target_pairs={{0,1},{1,0},{2,3},{3,2},{4,5},{5,4},{6,7},{7,6},{8,9},{9,8},{10,11... | collective-permute-start | bytes 1769480 | tf_op jit(solution)/shard_map/ppermute | solution.py:393
  317.5 42.1 %collective-permute-start.7 = (f32[192,768]{1,0:T(8,128)S(1)}, f32[192,768]{1,0:T(8,128)S(1)}, u32[]{:S(2)}, u32[]{:S(2)}) collective-permute-start(f32[192,768]{1,0:T(8,128)S(1)} %copy-done.19), channel_id=1, source_target_pairs={{0,1},{1,0},{2,3},{3,2},{4,5},{5,4},{6,7},{7,6},{8,9},{9,8},{10,11... | collective-permute-start | bytes 1769480 | tf_op jit(solution)/shard_map/ppermute | solution.py:393
  317.8 21.8 %collective-permute-start.3 = (f32[8,768]{1,0:T(8,128)S(1)}, f32[8,768]{1,0:T(8,128)S(1)}, u32[]{:S(2)}, u32[]{:S(2)}) collective-permute-start(f32[8,768]{1,0:T(8,128)S(1)} %get-tuple-element.71.refs_4_), channel_id=1, source_target_pairs={{0,1},{1,0},{2,3},{3,2},{4,5},{5,4},{6,7},{7,6},{8,9},{9,8},{10,11... | collective-permute-start | bytes 73736 | tf_op jit(solution)/shard_map/ppermute | solution.py:393
  359.1 8.3 %collective-permute-start.5 = (f32[192,768]{1,0:T(8,128)}, f32[192,768]{1,0:T(8,128)}, u32[]{:S(2)}, u32[]{:S(2)}) collective-permute-start(f32[192,768]{1,0:T(8,128)} %get-tuple-element.79), channel_id=1, source_target_pairs={{0,1},{1,0},{2,3},{3,2},{4,5},{5,4},{6,7},{7,6},{8,9},{9,8},{10,11... | collective-permute-start | bytes 1769480 | tf_op jit(solution)/shard_map/ppermute | solution.py:393
  359.4 11.6 %collective-permute-start.4 = (f32[192,768]{1,0:T(8,128)}, f32[192,768]{1,0:T(8,128)}, u32[]{:S(2)}, u32[]{:S(2)}) collective-permute-start(f32[192,768]{1,0:T(8,128)} %get-tuple-element.77), channel_id=1, source_target_pairs={{0,1},{1,0},{2,3},{3,2},{4,5},{5,4},{6,7},{7,6},{8,9},{9,8},{10,11... | collective-permute-start | bytes 1769480 | tf_op jit(solution)/shard_map/ppermute | solution.py:393
  381.1 16.3 %collective-permute-start.8 = (bf16[3072,512]{1,0:T(8,128)(2,1)S(1)}, bf16[3072,512]{1,0:T(8,128)(2,1)S(1)}, u32[]{:S(2)}, u32[]{:S(2)}) collective-permute-start(bf16[3072,512]{1,0:T(8,128)(2,1)S(1)} %get-tuple-element.87.refs_3_), channel_id=1, source_target_pairs={{0,1},{1,0},{2,3},{3,2},{4,5},{5,4},{6,7},{7,6},{8,9},{9,8},{10,11... | collective-permute-start | bytes 9437192 | tf_op jit(solution)/shard_map/ppermute | solution.py:393
  381.4 16.0 %collective-permute-start.9 = (f32[8,512]{1,0:T(8,128)S(1)}, f32[8,512]{1,0:T(8,128)S(1)}, u32[]{:S(2)}, u32[]{:S(2)}) collective-permute-start(f32[8,512]{1,0:T(8,128)S(1)} %get-tuple-element.88.refs_4_), channel_id=1, source_target_pairs={{0,1},{1,0},{2,3},{3,2},{4,5},{5,4},{6,7},{7,6},{8,9},{9,8},{10,11... | collective-permute-start | bytes 49160 | tf_op jit(solution)/shard_map/ppermute | solution.py:393
  413.3 5.1 %copy-start.23 = (f32[192,512]{1,0:T(8,128)S(1)}, f32[192,512]{1,0:T(8,128)}, u32[]{:S(2)}) copy-start(f32[192,512]{1,0:T(8,128)} %copy-done.22) | copy-start | bytes 1179652
  413.3 5.4 %copy-start.21 = (f32[192,512]{1,0:T(8,128)S(1)}, f32[192,512]{1,0:T(8,128)}, u32[]{:S(2)}) copy-start(f32[192,512]{1,0:T(8,128)} %copy-done.20) | copy-start | bytes 1179652
  418.2 10.8 %collective-permute-start.10 = (bf16[192,2048]{1,0:T(8,128)(2,1)}, bf16[192,2048]{1,0:T(8,128)(2,1)S(1)}, u32[]{:S(2)}, u32[]{:S(2)}) collective-permute-start(bf16[192,2048]{1,0:T(8,128)(2,1)} %get-tuple-element.96), channel_id=1, source_target_pairs={{0,1},{1,0},{2,3},{3,2},{4,5},{5,4},{6,7},{7,6},{8,9},{9,8},{10,11... | collective-permute-start | bytes 2359304 | tf_op jit(solution)/shard_map/ppermute | solution.py:393
  418.4 3.9 collective-permute-start.12
  418.7 7.0 %collective-permute-start.11 = (f32[192,512]{1,0:T(8,128)S(1)}, f32[192,512]{1,0:T(8,128)S(1)}, u32[]{:S(2)}, u32[]{:S(2)}) collective-permute-start(f32[192,512]{1,0:T(8,128)S(1)} %copy-done.21), channel_id=1, source_target_pairs={{0,1},{1,0},{2,3},{3,2},{4,5},{5,4},{6,7},{7,6},{8,9},{9,8},{10,11... | collective-permute-start | bytes 1179656 | tf_op jit(solution)/shard_map/ppermute | solution.py:393
  420.2 1.5 collective-permute-start.13
  (23 other events, 34.8 us)
Sparse Core Ops, SparseCore 0:
  9.6 131.0 all-gather.4
  143.6 81.4 all-gather.6
  227.9 79.5 all-gather.8
  309.7 60.1 all-gather.10

commit v5 on v0

--- a/solution.py
+++ b/solution.py
@@ -1,9 +1,15 @@
+import functools
+
 import jax
 import jax.numpy as jnp
 from jax import lax
+from jax.experimental import pallas as pl
+from jax.experimental.pallas import tpu as pltpu
 from jax.sharding import PartitionSpec as P
 
 off_weight = 0.0051
+tiles = 4
+vmem = 56 * 1024 * 1024
 
 
 def local_term(columns, full_two):
@@ -86,10 +92,263 @@
     return (grad_one, grad_two, jnp.reshape(loss, (1,)))
 
 
+def attend_kernel(count, begins, ends, *refs):
+    q_one, q_two, stat_ref = refs[:3]
+    blocks_one = refs[3 : 3 + count]
+    blocks_two = refs[3 + count : 3 + 2 * count]
+    rest = list(refs[3 + 2 * count :])
+    loss_in = rest.pop(0)
+    acc_in = None if begins else (rest.pop(0), rest.pop(0))
+    held_one, held_two, gram_one, gram_two, round_one, round_two = rest[-6:]
+    loss_out, *outs = rest[:-6]
+    step = pl.program_id(0)
+    tile = lax.rem(step, tiles)
+
+    @pl.when(step == 0)
+    def _():
+        gram_one[...] = jnp.zeros_like(gram_one)
+        gram_two[...] = jnp.zeros_like(gram_two)
+
+    @pl.when(step < tiles)
+    def _():
+        for blocks, held, mean in ((blocks_one, held_one, 0), (blocks_two, held_two, 2)):
+            start = 0
+            for block in blocks:
+                size = block.shape[0]
+                normal = (block[...].astype(jnp.float32) - stat_ref[mean : mean + 1, :]) * stat_ref[
+                    mean + 1 : mean + 2, :
+                ]
+                held[tile, start : start + size, :] = normal.astype(jnp.bfloat16)
+                start += size
+        for gram, queries, held in ((gram_one, q_one, held_one), (gram_two, q_two, held_two)):
+            gram[...] += lax.dot_general(
+                queries[...], held[tile], (((1,), (1,)), ((), ())), preferred_element_type=jnp.float32
+            )
+
+    @pl.when(step == tiles)
+    def _():
+        both = gram_one[...] * gram_two[...]
+        height, width = both.shape
+        folded = jnp.sum(both.reshape(height // 8, 8, width), axis=0)
+        loss_out[...] = loss_in[...]
+        for start in range(0, width, 128):
+            loss_out[...] += folded[:, start : start + 128]
+        round_one[...] = gram_one[...].astype(jnp.bfloat16)
+        round_two[...] = gram_two[...].astype(jnp.bfloat16)
+
+    @pl.when(step >= tiles)
+    def _():
+        for index, (gram, held) in enumerate(((round_two, held_one), (round_one, held_two))):
+            total = jnp.dot(gram[...], held[tile], preferred_element_type=jnp.float32)
+            if not begins:
+                total += acc_in[index][...]
+            if ends:
+                share = total.shape[0] // 2
+                outs[2 * index][...] = total[:share]
+                outs[2 * index + 1][...] = total[share:].astype(jnp.bfloat16)
+            else:
+                outs[index][...] = total
+
+
+def attend(q_one, q_two, stat, blocks_one, blocks_two, loss, acc, ends):
+    rows, width = q_one.shape
+    lanes = width // tiles
+    keys = sum(block.shape[0] for block in blocks_one)
+    count = len(blocks_one)
+    begins = acc is None
+    early = lambda step: (0, jnp.minimum(step, tiles - 1))
+    late = lambda step: (0, jnp.maximum(step - tiles, 0))
+    fixed = pl.BlockSpec((8, 128), lambda step: (0, 0))
+    operands = [q_one, q_two, stat, *blocks_one, *blocks_two, loss]
+    in_specs = [pl.BlockSpec((rows, lanes), early)] * 2 + [pl.BlockSpec((4, lanes), early)]
+    in_specs += [pl.BlockSpec((block.shape[0], lanes), early) for block in blocks_one] * 2
+    in_specs.append(fixed)
+    out_specs = [fixed]
+    out_shape = [jax.ShapeDtypeStruct((8, 128), jnp.float32)]
+    aliases = {3 + 2 * count: 0}
+    if not begins:
+        operands += list(acc)
+        in_specs += [pl.BlockSpec((rows, lanes), late)] * 2
+    if ends:
+        out_specs += [pl.BlockSpec((rows // 2, lanes), late)] * 4
+        out_shape += [
+            jax.ShapeDtypeStruct((rows // 2, width), jnp.float32),
+            jax.ShapeDtypeStruct((rows // 2, width), jnp.bfloat16),
+        ] * 2
+    else:
+        if not begins:
+            aliases.update({4 + 2 * count: 1, 5 + 2 * count: 2})
+        out_specs += [pl.BlockSpec((rows, lanes), late)] * 2
+        out_shape += [jax.ShapeDtypeStruct((rows, width), jnp.float32)] * 2
+    return pl.pallas_call(
+        functools.partial(attend_kernel, count, begins, ends),
+        grid=(2 * tiles,),
+        in_specs=in_specs,
+        out_specs=out_specs,
+        out_shape=out_shape,
+        scratch_shapes=[pltpu.VMEM((tiles, keys, lanes), jnp.bfloat16)] * 2
+        + [pltpu.VMEM((rows, keys), jnp.float32)] * 2
+        + [pltpu.VMEM((rows, keys), jnp.bfloat16)] * 2,
+        input_output_aliases=aliases,
+        compiler_params=pltpu.CompilerParams(vmem_limit_bytes=vmem),
+        cost_estimate=pl.CostEstimate(flops=width, bytes_accessed=width, transcendentals=0),
+        name="attend",
+    )(*operands)
+
+
+def totals_kernel(own_one, get_one, own_two, get_two, norm_one, norm_two, loss_ref, out_ref):
+    acc_one = own_one[...] + get_one[...].astype(jnp.float32)
+    acc_two = own_two[...] + get_two[...].astype(jnp.float32)
+    one = norm_one[...].astype(jnp.float32)
+    two = norm_two[...].astype(jnp.float32)
+    loss = jnp.full((1, one.shape[1]), jnp.sum(loss_ref[...]), jnp.float32)
+    for row, value in enumerate(
+        (acc_one, acc_one * one, acc_two, acc_two * two, one, two, one * two)
+    ):
+        out_ref[row : row + 1, :] = jnp.sum(value, axis=0, keepdims=True)
+    out_ref[7:8, :] = loss
+
+
+def finish_kernel(
+    samples, own_one, get_one, own_two, get_two, norm_one, norm_two, total_ref, stat_ref, *outs
+):
+    scale = 2.0 * off_weight / samples
+    one = norm_one[...].astype(jnp.float32)
+    two = norm_two[...].astype(jnp.float32)
+    mixed = total_ref[6:7, :]
+    corr = mixed / samples
+    diag = (-2.0 * (1.0 - corr)).astype(jnp.bfloat16).astype(jnp.float32) - 2.0 * off_weight * corr
+    for index, (own, get, mine, other, inv) in enumerate(
+        ((own_one, get_one, one, two, 1), (own_two, get_two, two, one, 3))
+    ):
+        back = scale * (own[...] + get[...].astype(jnp.float32)) + other * diag
+        sum_back = scale * total_ref[2 * index : 2 * index + 1, :]
+        sum_back += total_ref[5 - index : 6 - index, :] * diag
+        sum_prod = scale * total_ref[2 * index + 1 : 2 * index + 2, :] + mixed * diag
+        grad = back - sum_back / samples - mine * (sum_prod / samples)
+        outs[index][...] = (stat_ref[inv : inv + 1, :] * grad).astype(jnp.bfloat16)
+
+
+def by_features(kernel, operands, heights, loss, out_heights, dtype, name):
+    width = operands[0].shape[1]
+    lanes = width // tiles
+    place = lambda step: (0, step)
+    in_specs = [pl.BlockSpec((height, lanes), place) for height in heights]
+    if loss is not None:
+        operands = (*operands, loss)
+        in_specs.append(pl.BlockSpec(loss.shape, lambda step: (0, 0)))
+    return pl.pallas_call(
+        kernel,
+        grid=(tiles,),
+        in_specs=in_specs,
+        out_specs=[pl.BlockSpec((height, lanes), place) for height in out_heights],
+        out_shape=[jax.ShapeDtypeStruct((height, width), dtype) for height in out_heights],
+        compiler_params=pltpu.CompilerParams(vmem_limit_bytes=vmem),
+        cost_estimate=pl.CostEstimate(flops=width, bytes_accessed=width, transcendentals=0),
+        name=name,
+    )(*operands)
+
+
+def ring_shards(view_one, view_two):
+    rows, width = view_one.shape
+    batches = lax.axis_size("batch")
+    samples = rows * batches
+    chips = batches // 2
+    hops = chips // 2
+    line = chips // 2
+    order = [2 * r for r in range(line)] + [2 * r + 1 for r in reversed(range(line))]
+    ahead = [
+        (2 * order[r] + c, 2 * order[(r + 1) % chips] + c) for r in range(chips) for c in range(2)
+    ]
+    behind = [(there, here) for here, there in ahead]
+
+    def swapped(value, bit):
+        return lax.ppermute(value, "batch", [(i, i ^ bit) for i in range(batches)])
+
+    values_one = view_one.astype(jnp.float32)
+    values_two = view_two.astype(jnp.float32)
+    sums = jnp.stack(
+        [
+            jnp.sum(values_one, axis=0),
+            jnp.sum(values_one * values_one, axis=0),
+            jnp.sum(values_two, axis=0),
+            jnp.sum(values_two * values_two, axis=0),
+        ]
+    )
+    sums = jnp.sum(lax.all_gather(sums, "batch", axis=0), axis=0) / samples
+    mean_one, mean_two = sums[0], sums[2]
+    inv_one = 1.0 / jnp.sqrt(sums[1] - mean_one * mean_one + 1e-05)
+    inv_two = 1.0 / jnp.sqrt(sums[3] - mean_two * mean_two + 1e-05)
+    stat = jnp.stack([mean_one, inv_one, mean_two, inv_two])
+
+    def normed(view, mean, inv):
+        both = jnp.concatenate([view, swapped(view, 1)], axis=0).astype(jnp.float32)
+        return ((both - mean) * inv).astype(jnp.bfloat16)
+
+    q_one = normed(view_one, mean_one, inv_one)
+    q_two = normed(view_two, mean_two, inv_two)
+    loss = jnp.zeros((8, 128), jnp.float32)
+    acc = None
+    ends = [[view_one, view_one], [view_two, view_two]]
+    waiting = []
+    for hop in range(hops):
+        last = hop == hops - 1
+        if hop > 1:
+            blocks = waiting.pop(0)
+            loss, *acc = attend(q_one, q_two, stat, *blocks, loss, acc, False)
+            ends[0][0], ends[0][1], ends[1][0], ends[1][1], loss = lax.optimization_barrier(
+                (*ends[0], *ends[1], loss)
+            )
+            if waiting:
+                waiting[0] = (list(ends[0]), list(ends[1]))
+        for pair in ends:
+            up, down = pair
+            if last:
+                up, down = up[: rows // 2], down[rows // 2 :]
+            pair[0] = lax.ppermute(up, "batch", ahead)
+            pair[1] = lax.ppermute(down, "batch", behind)
+        waiting.append((list(ends[0]), list(ends[1])))
+    while len(waiting) > 1:
+        blocks = waiting.pop(0)
+        loss, *acc = attend(q_one, q_two, stat, *blocks, loss, acc, False)
+    blocks = ([view_one, *waiting[0][0]], [view_two, *waiting[0][1]])
+    loss, own_one, send_one, own_two, send_two = attend(
+        q_one, q_two, stat, *blocks, loss, acc, True
+    )
+    get_one, get_two = swapped(send_one, 1), swapped(send_two, 1)
+    parts = (own_one, get_one, own_two, get_two, q_one, q_two)
+    heights = (rows,) * 6
+    (total,) = by_features(totals_kernel, parts, heights, loss, (8,), jnp.float32, "totals")
+    size = 1
+    while size < batches:
+        if size * 4 <= batches:
+            near, far, both = (swapped(total, size * step) for step in (1, 2, 3))
+            total = (total + near) + (far + both)
+            size *= 4
+        else:
+            total = total + swapped(total, size)
+            size *= 2
+    grad_one, grad_two = by_features(
+        functools.partial(finish_kernel, samples),
+        (*parts, total, stat),
+        (*heights, 8, 4),
+        None,
+        (rows, rows),
+        jnp.bfloat16,
+        "finish",
+    )
+    corr = total[6] / samples
+    squares = total[7, 0] / (samples * samples)
+    loss = jnp.sum((1.0 - corr) ** 2 - off_weight * corr * corr) + off_weight * squares
+    return (grad_one, grad_two, jnp.reshape(loss / width, (1,)))
+
+
 def solution(mesh):
     placed = (P(("groups", "batch"), "feat"), P(("groups", "batch"), "feat"))
+    batches = mesh.shape["batch"]
+    ringed = mesh.shape["feat"] == 1 and batches >= 8 and batches & (batches - 1) == 0
     return jax.shard_map(
-        shards,
+        ring_shards if ringed else shards,
         mesh=mesh,
         in_specs=placed,
         out_specs=(P(("groups", "batch"), "feat"), P(("groups", "batch"), "feat"), P("groups")),

time: 1040 us -> 343 us (0.33)
  waiting for transfers between devices: 863 us -> 200 us
  blocking collectives: 86.7 us -> 0 us
  Pallas kernels: 0 us -> 80.1 us
  matrix products: 57.4 us -> 0 us
  starting transfers between devices: 0.12 us -> 23.8 us
    reduce_scatter x1 -> x0, waiting for transfers between devices: 639 us -> none  [shards(): lax.psum_scatter(local_term(norm_one, full_two), 'batch', scatter_dimensi...]
    ppermute x0 -> x26, waiting for transfers between devices: none -> 160 us  [the longest x8 127 us: ring_shards(): pair[0] = lax.ppermute(up, 'batch', ahead)]
    all_gather x1, waiting for transfers between devices: 136 us -> 39.4 us  [ring_shards(): sums = jnp.sum(lax.all_gather(sums, 'batch', axis=0), axis=0) / samples]
    psum x1 -> x0, waiting for transfers between devices: 87.6 us -> none  [shards(): lax.psum((jnp.sum(values_one, axis=0), jnp.sum(values_one * values_one, a...]
    psum x2 -> x0, blocking collectives: 86.7 us -> none  [the longest x1 56 us: shards(): lax.psum(jnp.sum(back_one * norm_one_f, axis=0).astype(jnp.bfloat16), 'ba...]
    pallas_call x0 -> x6, Pallas kernels: none -> 80.1 us  [the longest x4 66.3 us: attend(): pl.pallas_call(functools.partial(attend_kernel, count, begins, ends), gri...]
    dot_general x3 -> x0, matrix products: 57.4 us -> none  [the longest x1 23.2 us: local_term(): lax.dot_general(columns, full_two, (((0,), (0,)), ((), ())), preferred_el...]
    ppermute x0 -> x26, starting transfers between devices: none -> 23.8 us  [the longest x8 12.1 us: ring_shards(): pair[0] = lax.ppermute(up, 'batch', ahead)]
  transfers between devices with their start and end apart: 3 -> 27, of which waited for: 3 -> 19; matrix products, arithmetic and copies ran while one was open for 0% -> 3% of each run, Pallas kernels for 0% -> 14%
where the time goes in v5:
time: 343 us; the launch traced here: 341 us
  waiting for transfers between devices  200 us (58%)
  Pallas kernels  80.1 us (23%)
  starting transfers between devices  23.8 us (7%)
  between operations  16.6 us (5%)
  other arithmetic  14.8 us (4%)
  local copies, waits for them, and re-layouts  6.48 us (2%)
    ppermute x8, waiting for transfers between devices, ring_shards(): pair[0] = lax.ppermute(up, 'batch', ahead)  127 us
    pallas_call x4, Pallas kernels, attend(): pl.pallas_call(functools.partial(attend_kernel, count, begins, ends), gri...  66.3 us
    all_gather x1, waiting for transfers between devices, ring_shards(): sums = jnp.sum(lax.all_gather(sums, 'batch', axis=0), axis=0) / samples  39.4 us
    ppermute x10, waiting for transfers between devices, swapped(): return lax.ppermute(value, 'batch', [(i, i ^ bit) for i in range(batches)])  21.2 us
    pallas_call x2, Pallas kernels, by_features(): pl.pallas_call(kernel, grid=(tiles,), in_specs=in_specs, out_specs=[pl.Bl...  13.8 us
    ppermute x8, waiting for transfers between devices, ring_shards(): pair[1] = lax.ppermute(down, 'batch', behind)  12.4 us
    ppermute x8, starting transfers between devices, ring_shards(): pair[0] = lax.ppermute(up, 'batch', ahead)  12.1 us
    ppermute x10, starting transfers between devices, swapped(): return lax.ppermute(value, 'batch', [(i, i ^ bit) for i in range(batches)])  10.4 us
  transfers between devices with their start and end apart: 27, of which 19 were waited for; matrix products, arithmetic and copies ran while one was open for 3% of the time, Pallas kernels for 14%

profile of v5, /device:TPU:1, one launch (start us, length us, event | category | flops | bytes accessed | tf_op | source)
XLA Modules:
  0.0 341.5 jit_solution(11874444079480753760)
XLA Ops:
  16.5 39.4 %all-gather.4.cloned.1.call-done = f32[16,4,4096]{2,1,0:T(4,128)} async-done(((f32[1,4,4096]{2,1,0:T(4,128)}), f32[16,4,4096]{2,1,0:T(4,128)}) %all-gather.4.cloned.1.call-update) | async-done | bytes 1048592 | tf_op jit(solution)/shard_map/all_gather | solution.py:278
  59.2 27.9 %collective-permute-done.6.refs_5_ = bf16[192,4096]{1,0:T(8,128)(2,1)} collective-permute-done((bf16[192,4096]{1,0:T(8,128)(2,1)S(1)}, bf16[192,4096]{1,0:T(8,128)(2,1)}, u32[]{:S(2)}, u32[]{:S(2)}) %collective-permute-start.6) | collective-permute-done | bytes 1572896 | tf_op jit(solution)/shard_map/ppermute | solution.py:308
  87.1 2.3 collective-permute-start.7
  91.2 3.9 %multiply_convert_fusion.1.refs_0_.norm_one = bf16[384,4096]{1,0:T(8,128)(2,1)} fusion(bf16[192,4096]{1,0:T(8,128)(2,1)} %collective-permute-done, bf16[192,4096]{1,0:T(8,128)(2,1)S(1)} %copy-done, f32[4096]{0:T(1024)S(1)} %bitcast.14, f32[4096]{0:T(1024)S(1)} %bitcast.15), kind=kLoop, calls=%fused_computation.1 | loop fusion | flops 11010048 | bytes 6324224 | tf_op jit(solution)/shard_map/convert_element_type | solution.py:286
  95.8 2.5 multiply_convert_fusion.refs_1_.norm_two
  98.9 14.2 %attend.4 = (f32[8,128]{1,0:T(8,128)}, f32[384,4096]{1,0:T(8,128)}, f32[384,4096]{1,0:T(8,128)}) custom-call(bf16[384,4096]{1,0:T(8,128)(2,1)} %multiply_convert_fusion.1.refs_0_.norm_one, bf16[384,4096]{1,0:T(8,128)(2,1)} %multiply_convert_fusion.refs_1_.norm_two, f32[4,4096]{1,0:T(4,128)} %pad_maximum_fusion.refs_2_.stat_ref, ...), custom_call_target="tpu_custom_call", output_to_operand_aliasing={{0}: (7, {})} | custom-call | flops 4096 | bytes 4096 | tf_op jit(solution)/shard_map/attend/pallas_call | solution.py:183
  113.1 7.9 %collective-permute-done.3.refs_3_ = bf16[192,4096]{1,0:T(8,128)(2,1)} collective-permute-done((bf16[192,4096]{1,0:T(8,128)(2,1)}, bf16[192,4096]{1,0:T(8,128)(2,1)}, u32[]{:S(2)}, u32[]{:S(2)}) %collective-permute-start.3) | collective-permute-done | bytes 1572896 | tf_op jit(solution)/shard_map/ppermute | solution.py:308
  120.9 3.9 %collective-permute-done.5.refs_4_ = bf16[192,4096]{1,0:T(8,128)(2,1)} collective-permute-done((bf16[192,4096]{1,0:T(8,128)(2,1)}, bf16[192,4096]{1,0:T(8,128)(2,1)}, u32[]{:S(2)}, u32[]{:S(2)}) %collective-permute-start.5) | collective-permute-done | bytes 1572896 | tf_op jit(solution)/shard_map/ppermute | solution.py:309
  124.9 29.8 %collective-permute-done.7.refs_5_ = bf16[192,4096]{1,0:T(8,128)(2,1)S(1)} collective-permute-done((bf16[192,4096]{1,0:T(8,128)(2,1)}, bf16[192,4096]{1,0:T(8,128)(2,1)S(1)}, u32[]{:S(2)}, u32[]{:S(2)}) %collective-permute-start.7) | collective-permute-done | bytes 1572896 | tf_op jit(solution)/shard_map/ppermute | solution.py:308
  154.7 3.8 %collective-permute-done.9.refs_6_ = bf16[192,4096]{1,0:T(8,128)(2,1)S(1)} collective-permute-done((bf16[192,4096]{1,0:T(8,128)(2,1)}, bf16[192,4096]{1,0:T(8,128)(2,1)S(1)}, u32[]{:S(2)}, u32[]{:S(2)}) %collective-permute-start.9) | collective-permute-done | bytes 1572896 | tf_op jit(solution)/shard_map/ppermute | solution.py:309
  162.5 17.6 %attend.5 = (f32[8,128]{1,0:T(8,128)}, f32[384,4096]{1,0:T(8,128)}, f32[384,4096]{1,0:T(8,128)}) custom-call(bf16[384,4096]{1,0:T(8,128)(2,1)} %multiply_convert_fusion.1.refs_0_.norm_one, bf16[384,4096]{1,0:T(8,128)(2,1)} %multiply_convert_fusion.refs_1_.norm_two, ...), custom_call_target="tpu_custom_call", output_to_operand_aliasing={{0}: (7, {}), {1}: (8, {}), {2}: (9, {})} | custom-call | flops 4096 | bytes 4096 | tf_op jit(solution)/shard_map/attend/pallas_call | solution.py:183
  180.2 14.8 %collective-permute-done.10.refs_3_ = bf16[192,4096]{1,0:T(8,128)(2,1)S(1)} collective-permute-done((bf16[192,4096]{1,0:T(8,128)(2,1)}, bf16[192,4096]{1,0:T(8,128)(2,1)S(1)}, u32[]{:S(2)}, u32[]{:S(2)}) %collective-permute-start.10) | collective-permute-done | bytes 1572896 | tf_op jit(solution)/shard_map/ppermute | solution.py:308
  195.9 32.7 %collective-permute-done.12.refs_5_ = bf16[192,4096]{1,0:T(8,128)(2,1)S(1)} collective-permute-done((bf16[192,4096]{1,0:T(8,128)(2,1)}, bf16[192,4096]{1,0:T(8,128)(2,1)S(1)}, u32[]{:S(2)}, u32[]{:S(2)}) %collective-permute-start.12) | collective-permute-done | bytes 1572896 | tf_op jit(solution)/shard_map/ppermute | solution.py:308
  234.8 17.6 %attend.6 = (f32[8,128]{1,0:T(8,128)}, f32[384,4096]{1,0:T(8,128)}, f32[384,4096]{1,0:T(8,128)}) custom-call(bf16[384,4096]{1,0:T(8,128)(2,1)} %multiply_convert_fusion.1.refs_0_.norm_one, bf16[384,4096]{1,0:T(8,128)(2,1)} %multiply_convert_fusion.refs_1_.norm_two, ...), custom_call_target="tpu_custom_call", output_to_operand_aliasing={{0}: (7, {}), {1}: (8, {}), {2}: (9, {})} | custom-call | flops 4096 | bytes 4096 | tf_op jit(solution)/shard_map/attend/pallas_call | solution.py:183
  252.5 13.5 %collective-permute-done.16.refs_7_ = bf16[96,4096]{1,0:T(8,128)(2,1)S(1)} collective-permute-done((bf16[96,4096]{1,0:T(8,128)(2,1)S(1)}, bf16[96,4096]{1,0:T(8,128)(2,1)S(1)}, u32[]{:S(2)}, u32[]{:S(2)}) %collective-permute-start.16) | collective-permute-done | bytes 786464 | tf_op jit(solution)/shard_map/ppermute | solution.py:308
  267.9 16.9 %attend.7 = (f32[8,128]{1,0:T(8,128)}, f32[192,4096]{1,0:T(8,128)}, bf16[192,4096]{1,0:T(8,128)(2,1)}, f32[192,4096]{1,0:T(8,128)}, bf16[192,4096]{1,0:T(8,128)(2,1)}) custom-call(bf16[384,4096]{1,0:T(8,128)(2,1)} %multiply_convert_fusion.1.refs_0_.norm_one, ...), custom_call_target="tpu_custom_call", output_to_operand_aliasing={{0}: (9, {})} | custom-call | flops 4096 | bytes 4096 | tf_op jit(solution)/shard_map/attend/pallas_call | solution.py:183
  284.8 3.3 collective-permute-start.18
  288.1 3.2 collective-permute-done.18.get_one
  294.7 6.6 %totals.1 = f32[8,4096]{1,0:T(8,128)} custom-call(f32[192,4096]{1,0:T(8,128)} %get-tuple-element.48.own_one, bf16[192,4096]{1,0:T(8,128)(2,1)} %copy-done.2, f32[192,4096]{1,0:T(8,128)} %get-tuple-element.50.own_two, bf16[192,4096]{1,0:T(8,128)(2,1)} %copy-done.3, bf16[384,4096]{1,0:T(8,128)(2,1)} %multiply_convert_fusion.1.refs_0_.norm_one, ...), custom_call_target="tpu_custom_call" | custom-call | flops 4096 | bytes 4096 | tf_op jit(solution)/shard_map/totals/pallas_call | solution.py:240
  303.4 3.8 %collective-permute-done.22 = f32[8,4096]{1,0:T(8,128)S(1)} collective-permute-done((f32[8,4096]{1,0:T(8,128)}, f32[8,4096]{1,0:T(8,128)S(1)}, u32[]{:S(2)}, u32[]{:S(2)}) %collective-permute-start.22) | collective-permute-done | bytes 131104 | tf_op jit(solution)/shard_map/ppermute | solution.py:266
  307.3 2.5 collective-permute-done.21
  314.3 2.7 collective-permute-done.25
  317.0 6.8 %collective-permute-done.24 = f32[8,4096]{1,0:T(8,128)S(1)} collective-permute-done((f32[8,4096]{1,0:T(8,128)S(1)}, f32[8,4096]{1,0:T(8,128)S(1)}, u32[]{:S(2)}, u32[]{:S(2)}) %collective-permute-start.24) | collective-permute-done | bytes 131104 | tf_op jit(solution)/shard_map/ppermute | solution.py:266
  326.3 7.2 %finish.1 = (bf16[192,4096]{1,0:T(8,128)(2,1)}, bf16[192,4096]{1,0:T(8,128)(2,1)}) custom-call(f32[192,4096]{1,0:T(8,128)} %get-tuple-element.48.own_one, bf16[192,4096]{1,0:T(8,128)(2,1)} %copy-done.2, f32[192,4096]{1,0:T(8,128)} %get-tuple-element.50.own_two, bf16[192,4096]{1,0:T(8,128)(2,1)} %copy-done.3, ...), custom_call_target="tpu_custom_call" | custom-call | flops 4096 | bytes 4096 | tf_op jit(solution)/shard_map/finish/pallas_call | solution.py:240
  (83 shorter events, 40.1 us)
Async XLA Ops:
  7.2 48.7 %all-gather.4.cloned.1.call-start = ((), (), s32[]{:S(2)}) async-start(), calls=%async_computation | async-start | bytes 1114112 | tf_op jit(solution)/shard_map/all_gather | solution.py:278
  11.9 45.4 %collective-permute-start.2 = (bf16[192,4096]{1,0:T(8,128)(2,1)S(1)}, bf16[192,4096]{1,0:T(8,128)(2,1)}, u32[]{:S(2)}, u32[]{:S(2)}) collective-permute-start(bf16[192,4096]{1,0:T(8,128)(2,1)S(1)} %copy-done), channel_id=1, source_target_pairs={{0,4},{1,5},{4,8},{5,9},{8,12},{9,13},{12,14},{13,15},{14,10},{15,... | collective-permute-start | bytes 4718600 | tf_op jit(solution)/shard_map/ppermute | solution.py:308
  14.0 43.6 %collective-permute-start = (bf16[192,4096]{1,0:T(8,128)(2,1)S(1)}, bf16[192,4096]{1,0:T(8,128)(2,1)}, u32[]{:S(2)}, u32[]{:S(2)}) collective-permute-start(bf16[192,4096]{1,0:T(8,128)(2,1)S(1)} %copy-done), channel_id=1, source_target_pairs={{0,1},{1,0},{2,3},{3,2},{4,5},{5,4},{6,7},{7,6},{8,9},{9,8},{10,11... | collective-permute-start | bytes 4718600 | tf_op jit(solution)/shard_map/ppermute | solution.py:266
  15.0 43.6 %collective-permute-start.4 = (bf16[192,4096]{1,0:T(8,128)(2,1)S(1)}, bf16[192,4096]{1,0:T(8,128)(2,1)}, u32[]{:S(2)}, u32[]{:S(2)}) collective-permute-start(bf16[192,4096]{1,0:T(8,128)(2,1)S(1)} %copy-done), channel_id=1, source_target_pairs={{4,0},{5,1},{8,4},{9,5},{12,8},{13,9},{14,12},{15,13},{10,14},{11,... | collective-permute-start | bytes 4718600 | tf_op jit(solution)/shard_map/ppermute | solution.py:309
  15.0 72.1 %collective-permute-start.6 = (bf16[192,4096]{1,0:T(8,128)(2,1)S(1)}, bf16[192,4096]{1,0:T(8,128)(2,1)}, u32[]{:S(2)}, u32[]{:S(2)}) collective-permute-start(bf16[192,4096]{1,0:T(8,128)(2,1)S(1)} %copy-done.1), channel_id=1, source_target_pairs={{0,4},{1,5},{4,8},{5,9},{8,12},{9,13},{12,14},{13,15},{14,10},{15,... | collective-permute-start | bytes 4718600 | tf_op jit(solution)/shard_map/ppermute | solution.py:308
  16.5 74.7 %collective-permute-start.8 = (bf16[192,4096]{1,0:T(8,128)(2,1)S(1)}, bf16[192,4096]{1,0:T(8,128)(2,1)}, u32[]{:S(2)}, u32[]{:S(2)}) collective-permute-start(bf16[192,4096]{1,0:T(8,128)(2,1)S(1)} %copy-done.1), channel_id=1, source_target_pairs={{4,0},{5,1},{8,4},{9,5},{12,8},{13,9},{14,12},{15,13},{10,14},{11,... | collective-permute-start | bytes 4718600 | tf_op jit(solution)/shard_map/ppermute | solution.py:309
  57.3 38.5 %collective-permute-start.1 = (bf16[192,4096]{1,0:T(8,128)(2,1)S(1)}, bf16[192,4096]{1,0:T(8,128)(2,1)S(1)}, u32[]{:S(2)}, u32[]{:S(2)}) collective-permute-start(bf16[192,4096]{1,0:T(8,128)(2,1)S(1)} %copy-done.1), channel_id=1, source_target_pairs={{0,1},{1,0},{2,3},{3,2},{4,5},{5,4},{6,7},{7,6},{8,9},{9,8},{10,11... | collective-permute-start | bytes 4718600 | tf_op jit(solution)/shard_map/ppermute | solution.py:266
  57.7 63.2 %collective-permute-start.3 = (bf16[192,4096]{1,0:T(8,128)(2,1)}, bf16[192,4096]{1,0:T(8,128)(2,1)}, u32[]{:S(2)}, u32[]{:S(2)}) collective-permute-start(bf16[192,4096]{1,0:T(8,128)(2,1)} %collective-permute-done.2.refs_3_), channel_id=1, source_target_pairs={{0,4},{1,5},{4,8},{5,9},{8,12},{9,13},{12,14},{13,15},{14,10},{15,... | collective-permute-start | bytes 4718600 | tf_op jit(solution)/shard_map/ppermute | solution.py:308
  58.6 66.3 %collective-permute-start.5 = (bf16[192,4096]{1,0:T(8,128)(2,1)}, bf16[192,4096]{1,0:T(8,128)(2,1)}, u32[]{:S(2)}, u32[]{:S(2)}) collective-permute-start(bf16[192,4096]{1,0:T(8,128)(2,1)} %collective-permute-done.4.refs_4_), channel_id=1, source_target_pairs={{4,0},{5,1},{8,4},{9,5},{12,8},{13,9},{14,12},{15,13},{10,14},{11,... | collective-permute-start | bytes 4718600 | tf_op jit(solution)/shard_map/ppermute | solution.py:309
  87.1 67.5 %collective-permute-start.7 = (bf16[192,4096]{1,0:T(8,128)(2,1)}, bf16[192,4096]{1,0:T(8,128)(2,1)S(1)}, u32[]{:S(2)}, u32[]{:S(2)}) collective-permute-start(bf16[192,4096]{1,0:T(8,128)(2,1)} %collective-permute-done.6.refs_5_), channel_id=1, source_target_pairs={{0,4},{1,5},{4,8},{5,9},{8,12},{9,13},{12,14},{13,15},{14,10},{15,... | collective-permute-start | bytes 4718600 | tf_op jit(solution)/shard_map/ppermute | solution.py:308
  91.2 67.3 %collective-permute-start.9 = (bf16[192,4096]{1,0:T(8,128)(2,1)}, bf16[192,4096]{1,0:T(8,128)(2,1)S(1)}, u32[]{:S(2)}, u32[]{:S(2)}) collective-permute-start(bf16[192,4096]{1,0:T(8,128)(2,1)} %collective-permute-done.8.refs_6_), channel_id=1, source_target_pairs={{4,0},{5,1},{8,4},{9,5},{12,8},{13,9},{14,12},{15,13},{10,14},{11,... | collective-permute-start | bytes 4718600 | tf_op jit(solution)/shard_map/ppermute | solution.py:309
  159.6 35.3 %collective-permute-start.10 = (bf16[192,4096]{1,0:T(8,128)(2,1)}, bf16[192,4096]{1,0:T(8,128)(2,1)S(1)}, u32[]{:S(2)}, u32[]{:S(2)}) collective-permute-start(bf16[192,4096]{1,0:T(8,128)(2,1)} %collective-permute-done.3.refs_3_), channel_id=1, source_target_pairs={{0,4},{1,5},{4,8},{5,9},{8,12},{9,13},{12,14},{13,15},{14,10},{15,... | collective-permute-start | bytes 4718600 | tf_op jit(solution)/shard_map/ppermute | solution.py:308
  160.9 35.0 %collective-permute-start.11 = (bf16[192,4096]{1,0:T(8,128)(2,1)}, bf16[192,4096]{1,0:T(8,128)(2,1)S(1)}, u32[]{:S(2)}, u32[]{:S(2)}) collective-permute-start(bf16[192,4096]{1,0:T(8,128)(2,1)} %collective-permute-done.5.refs_4_), channel_id=1, source_target_pairs={{4,0},{5,1},{8,4},{9,5},{12,8},{13,9},{14,12},{15,13},{10,14},{11,... | collective-permute-start | bytes 4718600 | tf_op jit(solution)/shard_map/ppermute | solution.py:309
  161.1 67.6 %collective-permute-start.12 = (bf16[192,4096]{1,0:T(8,128)(2,1)}, bf16[192,4096]{1,0:T(8,128)(2,1)S(1)}, u32[]{:S(2)}, u32[]{:S(2)}) collective-permute-start(bf16[192,4096]{1,0:T(8,128)(2,1)} %copy-done.8), channel_id=1, source_target_pairs={{0,4},{1,5},{4,8},{5,9},{8,12},{9,13},{12,14},{13,15},{14,10},{15,... | collective-permute-start | bytes 4718600 | tf_op jit(solution)/shard_map/ppermute | solution.py:308
  162.4 67.3 %collective-permute-start.13 = (bf16[192,4096]{1,0:T(8,128)(2,1)}, bf16[192,4096]{1,0:T(8,128)(2,1)S(1)}, u32[]{:S(2)}, u32[]{:S(2)}) collective-permute-start(bf16[192,4096]{1,0:T(8,128)(2,1)} %copy-done.9), channel_id=1, source_target_pairs={{4,0},{5,1},{8,4},{9,5},{12,8},{13,9},{14,12},{15,13},{10,14},{11,... | collective-permute-start | bytes 4718600 | tf_op jit(solution)/shard_map/ppermute | solution.py:309
  231.9 20.6 %collective-permute-start.14 = (bf16[96,4096]{1,0:T(8,128)(2,1)}, bf16[96,4096]{1,0:T(8,128)(2,1)}, u32[]{:S(2)}, u32[]{:S(2)}) collective-permute-start(bf16[96,4096]{1,0:T(8,128)(2,1)} %slice.34), channel_id=1, source_target_pairs={{0,4},{1,5},{4,8},{5,9},{8,12},{9,13},{12,14},{13,15},{14,10},{15,... | collective-permute-start | bytes 2359304 | tf_op jit(solution)/shard_map/ppermute | solution.py:308
  233.2 19.3 %collective-permute-start.15 = (bf16[96,4096]{1,0:T(8,128)(2,1)}, bf16[96,4096]{1,0:T(8,128)(2,1)S(1)}, u32[]{:S(2)}, u32[]{:S(2)}) collective-permute-start(bf16[96,4096]{1,0:T(8,128)(2,1)} %slice.35), channel_id=1, source_target_pairs={{4,0},{5,1},{8,4},{9,5},{12,8},{13,9},{14,12},{15,13},{10,14},{11,... | collective-permute-start | bytes 2359304 | tf_op jit(solution)/shard_map/ppermute | solution.py:309
  233.4 32.6 %collective-permute-start.16 = (bf16[96,4096]{1,0:T(8,128)(2,1)S(1)}, bf16[96,4096]{1,0:T(8,128)(2,1)S(1)}, u32[]{:S(2)}, u32[]{:S(2)}) collective-permute-start(bf16[96,4096]{1,0:T(8,128)(2,1)S(1)} %slice.36), channel_id=1, source_target_pairs={{0,4},{1,5},{4,8},{5,9},{8,12},{9,13},{12,14},{13,15},{14,10},{15,... | collective-permute-start | bytes 2359304 | tf_op jit(solution)/shard_map/ppermute | solution.py:308
  234.7 32.4 %collective-permute-start.17 = (bf16[96,4096]{1,0:T(8,128)(2,1)S(1)}, bf16[96,4096]{1,0:T(8,128)(2,1)S(1)}, u32[]{:S(2)}, u32[]{:S(2)}) collective-permute-start(bf16[96,4096]{1,0:T(8,128)(2,1)S(1)} %slice.37), channel_id=1, source_target_pairs={{4,0},{5,1},{8,4},{9,5},{12,8},{13,9},{14,12},{15,13},{10,14},{11,... | collective-permute-start | bytes 2359304 | tf_op jit(solution)/shard_map/ppermute | solution.py:309
  284.8 6.5 %collective-permute-start.18 = (bf16[192,4096]{1,0:T(8,128)(2,1)}, bf16[192,4096]{1,0:T(8,128)(2,1)S(1)}, u32[]{:S(2)}, u32[]{:S(2)}) collective-permute-start(bf16[192,4096]{1,0:T(8,128)(2,1)} %get-tuple-element.49), channel_id=1, source_target_pairs={{0,1},{1,0},{2,3},{3,2},{4,5},{5,4},{6,7},{7,6},{8,9},{9,8},{10,11... | collective-permute-start | bytes 4718600 | tf_op jit(solution)/shard_map/ppermute | solution.py:266
  301.7 8.1 %collective-permute-start.21 = (f32[8,4096]{1,0:T(8,128)}, f32[8,4096]{1,0:T(8,128)S(1)}, u32[]{:S(2)}, u32[]{:S(2)}) collective-permute-start(f32[8,4096]{1,0:T(8,128)} %totals.1), channel_id=1, source_target_pairs={{0,2},{1,3},{2,0},{3,1},{4,6},{5,7},{6,4},{7,5},{8,10},{9,11},{10,... | collective-permute-start | bytes 393224 | tf_op jit(solution)/shard_map/ppermute | solution.py:266
  303.0 6.8 %collective-permute-start.20 = (f32[8,4096]{1,0:T(8,128)}, f32[8,4096]{1,0:T(8,128)S(1)}, u32[]{:S(2)}, u32[]{:S(2)}) collective-permute-start(f32[8,4096]{1,0:T(8,128)} %totals.1), channel_id=1, source_target_pairs={{0,1},{1,0},{2,3},{3,2},{4,5},{5,4},{6,7},{7,6},{8,9},{9,8},{10,11... | collective-permute-start | bytes 393224 | tf_op jit(solution)/shard_map/ppermute | solution.py:266
  311.9 11.8 %collective-permute-start.24 = (f32[8,4096]{1,0:T(8,128)S(1)}, f32[8,4096]{1,0:T(8,128)S(1)}, u32[]{:S(2)}, u32[]{:S(2)}) collective-permute-start(f32[8,4096]{1,0:T(8,128)S(1)} %add_add_fusion.1), channel_id=1, source_target_pairs={{0,8},{1,9},{2,10},{3,11},{4,12},{5,13},{6,14},{7,15},{8,0},{9,1},... | collective-permute-start | bytes 393224 | tf_op jit(solution)/shard_map/ppermute | solution.py:266
  312.3 11.4 %collective-permute-start.23 = (f32[8,4096]{1,0:T(8,128)S(1)}, f32[8,4096]{1,0:T(8,128)S(1)}, u32[]{:S(2)}, u32[]{:S(2)}) collective-permute-start(f32[8,4096]{1,0:T(8,128)S(1)} %add_add_fusion.1), channel_id=1, source_target_pairs={{0,4},{1,5},{2,6},{3,7},{4,0},{5,1},{6,2},{7,3},{8,12},{9,13},{10,... | collective-permute-start | bytes 393224 | tf_op jit(solution)/shard_map/ppermute | solution.py:266
  (17 other events, 135.8 us)
Sparse Core Ops, SparseCore 0:
  12.0 43.8 all-gather.3

commit v6 on v5

--- a/solution.py
+++ b/solution.py
@@ -92,6 +92,30 @@
     return (grad_one, grad_two, jnp.reshape(loss, (1,)))
 
 
+def eight_rows(sums, loss):
+    lanes = sums[0].shape[1]
+    row = lax.broadcasted_iota(jnp.int32, (8, lanes), 0)
+    loss = jnp.zeros((1, lanes), jnp.float32) + loss
+    values = list(sums)
+    for _ in range(3):
+        part = loss.astype(jnp.bfloat16).astype(jnp.float32)
+        values.append(part)
+        loss = loss - part
+    out = jnp.zeros((8, lanes), jnp.float32)
+    for index, value in enumerate(values):
+        out = jnp.where(row == index, value, out)
+    return out.astype(jnp.bfloat16)
+
+
+def add_kernel(*refs):
+    terms = [ref[...].astype(jnp.float32) for ref in refs[:-1]]
+    while len(terms) > 1:
+        terms = [terms[k] + terms[k + 1] for k in range(0, len(terms), 2)]
+    total = terms[0]
+    loss = (total[4:5] + total[5:6]) + total[6:7]
+    refs[-1][...] = eight_rows([total[k : k + 1] for k in range(4)], loss)
+
+
 def attend_kernel(count, begins, ends, *refs):
     q_one, q_two, stat_ref = refs[:3]
     blocks_one = refs[3 : 3 + count]
@@ -99,6 +123,7 @@
     rest = list(refs[3 + 2 * count :])
     loss_in = rest.pop(0)
     acc_in = None if begins else (rest.pop(0), rest.pop(0))
+    late = (rest.pop(0), rest.pop(0)) if ends else None
     held_one, held_two, gram_one, gram_two, round_one, round_two = rest[-6:]
     loss_out, *outs = rest[:-6]
     step = pl.program_id(0)
@@ -130,14 +155,13 @@
         both = gram_one[...] * gram_two[...]
         height, width = both.shape
         folded = jnp.sum(both.reshape(height // 8, 8, width), axis=0)
-        loss_out[...] = loss_in[...]
-        for start in range(0, width, 128):
-            loss_out[...] += folded[:, start : start + 128]
+        loss_out[...] = loss_in[...] + jnp.sum(folded) * (1.0 / 1024)
         round_one[...] = gram_one[...].astype(jnp.bfloat16)
         round_two[...] = gram_two[...].astype(jnp.bfloat16)
 
     @pl.when(step >= tiles)
     def _():
+        sums = []
         for index, (gram, held) in enumerate(((round_two, held_one), (round_one, held_two))):
             total = jnp.dot(gram[...], held[tile], preferred_element_type=jnp.float32)
             if not begins:
@@ -146,8 +170,13 @@
                 share = total.shape[0] // 2
                 outs[2 * index][...] = total[:share]
                 outs[2 * index + 1][...] = total[share:].astype(jnp.bfloat16)
+                prod = total * late[index][...].astype(jnp.float32)
+                sums.append(jnp.sum(total, axis=0, keepdims=True))
+                sums.append(jnp.sum(prod, axis=0, keepdims=True))
             else:
                 outs[index][...] = total
+        if ends:
+            outs[4][...] = eight_rows(sums, jnp.sum(loss_out[...]))
 
 
 def attend(q_one, q_two, stat, blocks_one, blocks_two, loss, acc, ends):
@@ -170,11 +199,15 @@
         operands += list(acc)
         in_specs += [pl.BlockSpec((rows, lanes), late)] * 2
     if ends:
+        operands += [q_one, q_two]
+        in_specs += [pl.BlockSpec((rows, lanes), late)] * 2
         out_specs += [pl.BlockSpec((rows // 2, lanes), late)] * 4
         out_shape += [
             jax.ShapeDtypeStruct((rows // 2, width), jnp.float32),
             jax.ShapeDtypeStruct((rows // 2, width), jnp.bfloat16),
         ] * 2
+        out_specs.append(pl.BlockSpec((8, lanes), late))
+        out_shape.append(jax.ShapeDtypeStruct((8, width), jnp.bfloat16))
     else:
         if not begins:
             aliases.update({4 + 2 * count: 1, 5 + 2 * count: 2})
@@ -196,47 +229,32 @@
     )(*operands)
 
 
-def totals_kernel(own_one, get_one, own_two, get_two, norm_one, norm_two, loss_ref, out_ref):
-    acc_one = own_one[...] + get_one[...].astype(jnp.float32)
-    acc_two = own_two[...] + get_two[...].astype(jnp.float32)
-    one = norm_one[...].astype(jnp.float32)
-    two = norm_two[...].astype(jnp.float32)
-    loss = jnp.full((1, one.shape[1]), jnp.sum(loss_ref[...]), jnp.float32)
-    for row, value in enumerate(
-        (acc_one, acc_one * one, acc_two, acc_two * two, one, two, one * two)
-    ):
-        out_ref[row : row + 1, :] = jnp.sum(value, axis=0, keepdims=True)
-    out_ref[7:8, :] = loss
-
-
 def finish_kernel(
-    samples, own_one, get_one, own_two, get_two, norm_one, norm_two, total_ref, stat_ref, *outs
+    samples, own_one, get_one, own_two, get_two, norm_one, norm_two, total_ref, norm_ref, stat_ref, *outs
 ):
     scale = 2.0 * off_weight / samples
     one = norm_one[...].astype(jnp.float32)
     two = norm_two[...].astype(jnp.float32)
-    mixed = total_ref[6:7, :]
+    mixed = norm_ref[2:3, :]
+    total = total_ref[...].astype(jnp.float32)
     corr = mixed / samples
     diag = (-2.0 * (1.0 - corr)).astype(jnp.bfloat16).astype(jnp.float32) - 2.0 * off_weight * corr
     for index, (own, get, mine, other, inv) in enumerate(
         ((own_one, get_one, one, two, 1), (own_two, get_two, two, one, 3))
     ):
         back = scale * (own[...] + get[...].astype(jnp.float32)) + other * diag
-        sum_back = scale * total_ref[2 * index : 2 * index + 1, :]
-        sum_back += total_ref[5 - index : 6 - index, :] * diag
-        sum_prod = scale * total_ref[2 * index + 1 : 2 * index + 2, :] + mixed * diag
+        sum_back = scale * total[2 * index : 2 * index + 1, :]
+        sum_back += norm_ref[1 - index : 2 - index, :] * diag
+        sum_prod = scale * total[2 * index + 1 : 2 * index + 2, :] + mixed * diag
         grad = back - sum_back / samples - mine * (sum_prod / samples)
         outs[index][...] = (stat_ref[inv : inv + 1, :] * grad).astype(jnp.bfloat16)
 
 
-def by_features(kernel, operands, heights, loss, out_heights, dtype, name):
+def by_features(kernel, operands, heights, out_heights, dtype, name):
     width = operands[0].shape[1]
     lanes = width // tiles
     place = lambda step: (0, step)
     in_specs = [pl.BlockSpec((height, lanes), place) for height in heights]
-    if loss is not None:
-        operands = (*operands, loss)
-        in_specs.append(pl.BlockSpec(loss.shape, lambda step: (0, 0)))
     return pl.pallas_call(
         kernel,
         grid=(tiles,),
@@ -265,9 +283,16 @@
     def swapped(value, bit):
         return lax.ppermute(value, "batch", [(i, i ^ bit) for i in range(batches)])
 
-    values_one = view_one.astype(jnp.float32)
-    values_two = view_two.astype(jnp.float32)
-    sums = jnp.stack(
+    def summed(rows_of_sums):
+        return jnp.sum(lax.all_gather(jnp.stack(rows_of_sums), "batch", axis=0), axis=0)
+
+    far_one, far_two = swapped(view_one, 1), swapped(view_two, 1)
+    here_one, here_two, far_one, far_two = lax.optimization_barrier(
+        (view_one, view_two, far_one, far_two)
+    )
+    values_one = here_one.astype(jnp.float32)
+    values_two = here_two.astype(jnp.float32)
+    sums = summed(
         [
             jnp.sum(values_one, axis=0),
             jnp.sum(values_one * values_one, axis=0),
@@ -275,70 +300,64 @@
             jnp.sum(values_two * values_two, axis=0),
         ]
     )
-    sums = jnp.sum(lax.all_gather(sums, "batch", axis=0), axis=0) / samples
+    sums = sums / samples
     mean_one, mean_two = sums[0], sums[2]
     inv_one = 1.0 / jnp.sqrt(sums[1] - mean_one * mean_one + 1e-05)
     inv_two = 1.0 / jnp.sqrt(sums[3] - mean_two * mean_two + 1e-05)
     stat = jnp.stack([mean_one, inv_one, mean_two, inv_two])
 
-    def normed(view, mean, inv):
-        both = jnp.concatenate([view, swapped(view, 1)], axis=0).astype(jnp.float32)
+    def normed(view, far, mean, inv):
+        both = jnp.concatenate([view, far], axis=0).astype(jnp.float32)
         return ((both - mean) * inv).astype(jnp.bfloat16)
 
-    q_one = normed(view_one, mean_one, inv_one)
-    q_two = normed(view_two, mean_two, inv_two)
+    q_one = normed(here_one, far_one, mean_one, inv_one)
+    q_two = normed(here_two, far_two, mean_two, inv_two)
     loss = jnp.zeros((8, 128), jnp.float32)
-    acc = None
-    ends = [[view_one, view_one], [view_two, view_two]]
-    waiting = []
+    loss, *acc = attend(q_one, q_two, stat, [here_one], [here_two], loss, None, False)
+    mine_one = q_one[:rows].astype(jnp.float32)
+    mine_two = q_two[:rows].astype(jnp.float32)
+    norm_sums = summed(
+        [jnp.sum(mine_one, axis=0), jnp.sum(mine_two, axis=0), jnp.sum(mine_one * mine_two, axis=0)]
+    )
+    flows = [[view_one, view_one], [view_two, view_two]]
+    arrived = []
     for hop in range(hops):
-        last = hop == hops - 1
         if hop > 1:
-            blocks = waiting.pop(0)
-            loss, *acc = attend(q_one, q_two, stat, *blocks, loss, acc, False)
-            ends[0][0], ends[0][1], ends[1][0], ends[1][1], loss = lax.optimization_barrier(
-                (*ends[0], *ends[1], loss)
-            )
-            if waiting:
-                waiting[0] = (list(ends[0]), list(ends[1]))
-        for pair in ends:
+            loss, *acc = attend(q_one, q_two, stat, *arrived[hop - 2], loss, acc, False)
+        arrived.append([])
+        for view, pair in enumerate(flows):
+            if hop > 1 and view == 1:
+                *pair, loss, norm_sums = lax.optimization_barrier((*pair, loss, norm_sums))
+                arrived[hop - 1][1] = list(pair)
             up, down = pair
-            if last:
+            if hop == hops - 1:
                 up, down = up[: rows // 2], down[rows // 2 :]
-            pair[0] = lax.ppermute(up, "batch", ahead)
-            pair[1] = lax.ppermute(down, "batch", behind)
-        waiting.append((list(ends[0]), list(ends[1])))
-    while len(waiting) > 1:
-        blocks = waiting.pop(0)
-        loss, *acc = attend(q_one, q_two, stat, *blocks, loss, acc, False)
-    blocks = ([view_one, *waiting[0][0]], [view_two, *waiting[0][1]])
-    loss, own_one, send_one, own_two, send_two = attend(
-        q_one, q_two, stat, *blocks, loss, acc, True
+            flows[view] = [lax.ppermute(up, "batch", ahead), lax.ppermute(down, "batch", behind)]
+            arrived[hop].append(list(flows[view]))
+    loss, *acc = attend(q_one, q_two, stat, *arrived[hops - 2], loss, acc, False)
+    arrived[-1][1][0], loss = lax.optimization_barrier((arrived[-1][1][0], loss))
+    loss, own_one, send_one, own_two, send_two, total = attend(
+        q_one, q_two, stat, *arrived[hops - 1], loss, acc, True
     )
     get_one, get_two = swapped(send_one, 1), swapped(send_two, 1)
-    parts = (own_one, get_one, own_two, get_two, q_one, q_two)
-    heights = (rows,) * 6
-    (total,) = by_features(totals_kernel, parts, heights, loss, (8,), jnp.float32, "totals")
     size = 1
     while size < batches:
-        if size * 4 <= batches:
-            near, far, both = (swapped(total, size * step) for step in (1, 2, 3))
-            total = (total + near) + (far + both)
-            size *= 4
-        else:
-            total = total + swapped(total, size)
-            size *= 2
+        steps = (1, 2, 3) if size * 4 <= batches else (1,)
+        terms = (total, *(swapped(total, size * step) for step in steps))
+        (total,) = by_features(
+            add_kernel, terms, (8,) * len(terms), (8,), jnp.bfloat16, "add_totals"
+        )
+        size *= len(terms)
     grad_one, grad_two = by_features(
         functools.partial(finish_kernel, samples),
-        (*parts, total, stat),
-        (*heights, 8, 4),
-        None,
+        (own_one, get_one, own_two, get_two, q_one, q_two, total, norm_sums, stat),
+        (*((rows,) * 6), 8, 3, 4),
         (rows, rows),
         jnp.bfloat16,
         "finish",
     )
-    corr = total[6] / samples
-    squares = total[7, 0] / (samples * samples)
+    corr = norm_sums[2] / samples
+    squares = jnp.sum(total[4:7, 0].astype(jnp.float32)) / (samples * samples)
     loss = jnp.sum((1.0 - corr) ** 2 - off_weight * corr * corr) + off_weight * squares
     return (grad_one, grad_two, jnp.reshape(loss / width, (1,)))
 

time: 343 us -> 373 us (1.087)
  blocking collectives: 0 us -> 47.3 us
  waiting for transfers between devices: 200 us -> 164 us
  Pallas kernels: 80.1 us -> 95.6 us
    all_gather x0 -> x1, blocking collectives: none -> 47.3 us  [summed(): lax.all_gather(jnp.stack(rows_of_sums), 'batch', axis=0)]
    all_gather x1, waiting for transfers between devices: 39.4 us -> 0.01 us  [summed(): lax.all_gather(jnp.stack(rows_of_sums), 'batch', axis=0)]
    pallas_call x4 -> x5, Pallas kernels: 66.3 us -> 82.8 us  [attend(): pl.pallas_call(functools.partial(attend_kernel, count, begins, ends), gri...]
    ppermute x16, waiting for transfers between devices: 139 us -> 155 us  [the longest x8 95.9 us: ring_shards(): lax.ppermute(up, 'batch', ahead)]
    ppermute x10, waiting for transfers between devices: 21.2 us -> 9.22 us  [swapped(): return lax.ppermute(value, 'batch', [(i, i ^ bit) for i in range(batches)])]
    ppermute x16, starting transfers between devices: 13.4 us -> 17.7 us  [the longest x8 13.1 us: ring_shards(): lax.ppermute(up, 'batch', ahead)]
    pallas_call x2 -> x3, Pallas kernels: 13.8 us -> 12.9 us  [by_features(): pl.pallas_call(kernel, grid=(tiles,), in_specs=in_specs, out_specs=[pl.Bl...]
  transfers between devices with their start and end apart: 27 -> 27, of which waited for: 19 -> 14; matrix products, arithmetic and copies ran while one was open for 3% -> 4% of each run, Pallas kernels for 14% -> 19%
where the time goes in v6:
time: 373 us; the launch traced here: 369 us
  waiting for transfers between devices  164 us (44%)
  Pallas kernels  95.6 us (26%)
  blocking collectives  47.3 us (13%)
  starting transfers between devices  25.9 us (7%)
  between operations  16.7 us (4%)
  other arithmetic  14.6 us (4%)
  local copies, waits for them, and re-layouts  5.06 us (1%)
    ppermute x8, waiting for transfers between devices, ring_shards(): lax.ppermute(up, 'batch', ahead)  95.9 us
    pallas_call x5, Pallas kernels, attend(): pl.pallas_call(functools.partial(attend_kernel, count, begins, ends), gri...  82.8 us
    ppermute x8, waiting for transfers between devices, ring_shards(): lax.ppermute(down, 'batch', behind)  59.1 us
    all_gather x1, blocking collectives, summed(): lax.all_gather(jnp.stack(rows_of_sums), 'batch', axis=0)  47.3 us
    ppermute x8, starting transfers between devices, ring_shards(): lax.ppermute(up, 'batch', ahead)  13.1 us
    pallas_call x3, Pallas kernels, by_features(): pl.pallas_call(kernel, grid=(tiles,), in_specs=in_specs, out_specs=[pl.Bl...  12.9 us
    ppermute x10, waiting for transfers between devices, swapped(): return lax.ppermute(value, 'batch', [(i, i ^ bit) for i in range(batches)])  9.22 us
    ppermute x10, starting transfers between devices, swapped(): return lax.ppermute(value, 'batch', [(i, i ^ bit) for i in range(batches)])  8.17 us
  transfers between devices with their start and end apart: 27, of which 14 were waited for; matrix products, arithmetic and copies ran while one was open for 4% of the time, Pallas kernels for 19%

profile of v6, /device:TPU:1, one launch (start us, length us, event | category | flops | bytes accessed | tf_op | source)
XLA Modules:
  0.0 369.5 jit_solution(12661555435393181432)
XLA Ops:
  7.8 2.4 collective-permute-start.2
  11.1 2.2 collective-permute-done.1
  17.8 2.5 collective-permute-start.10
  21.7 24.8 %collective-permute-done.2.refs_3_ = bf16[192,4096]{1,0:T(8,128)(2,1)} collective-permute-done((bf16[192,4096]{1,0:T(8,128)(2,1)}, bf16[192,4096]{1,0:T(8,128)(2,1)}, u32[]{:S(2)}, u32[]{:S(2)}) %collective-permute-start.2) | collective-permute-done | bytes 1572896 | tf_op jit(solution)/shard_map/ppermute | solution.py:335
  46.5 2.2 collective-permute-start.3
  48.7 35.0 %collective-permute-done.10.refs_5_ = bf16[192,4096]{1,0:T(8,128)(2,1)} collective-permute-done((bf16[192,4096]{1,0:T(8,128)(2,1)S(1)}, bf16[192,4096]{1,0:T(8,128)(2,1)}, u32[]{:S(2)}, u32[]{:S(2)}) %collective-permute-start.10) | collective-permute-done | bytes 1572896 | tf_op jit(solution)/shard_map/ppermute | solution.py:335
  83.8 2.3 collective-permute-start.11
  86.1 9.6 %collective-permute-done.6.refs_4_ = bf16[192,4096]{1,0:T(8,128)(2,1)} collective-permute-done((bf16[192,4096]{1,0:T(8,128)(2,1)S(1)}, bf16[192,4096]{1,0:T(8,128)(2,1)}, u32[]{:S(2)}, u32[]{:S(2)}) %collective-permute-start.6) | collective-permute-done | bytes 1572896 | tf_op jit(solution)/shard_map/ppermute | solution.py:335
  95.7 21.9 %collective-permute-done.3.refs_3_ = bf16[192,4096]{1,0:T(8,128)(2,1)} collective-permute-done((bf16[192,4096]{1,0:T(8,128)(2,1)}, bf16[192,4096]{1,0:T(8,128)(2,1)}, u32[]{:S(2)}, u32[]{:S(2)}) %collective-permute-start.3) | collective-permute-done | bytes 1572896 | tf_op jit(solution)/shard_map/ppermute | solution.py:335
  121.3 5.1 %multiply_convert_fusion = (bf16[384,4096]{1,0:T(8,128)(2,1)}, bf16[384,4096]{1,0:T(8,128)(2,1)}) fusion(bf16[192,4096]{1,0:T(8,128)(2,1)} %collective-permute-done.1, bf16[192,4096]{1,0:T(8,128)(2,1)S(1)} %copy-done.2, f32[4096]{0:T(1024)S(1)} %bitcast.17, f32[4096]{0:T(1024)S(1)} %bitcast.16, f32[4096]{0:T(1024)S(1)} %bitcast.18, f32[4096]{0:T(1024)S(1)} %bitcast.19, ...), kind=kLoop, calls=%fused_computation | loop fusion | flops 22020096 | bytes 12648448 | tf_op jit(solution)/shard_map/convert_element_type | solution.py:311
  127.6 11.6 %attend.5 = (f32[8,128]{1,0:T(8,128)}, f32[384,4096]{1,0:T(8,128)}, f32[384,4096]{1,0:T(8,128)}) custom-call(bf16[384,4096]{1,0:T(8,128)(2,1)} %get-tuple-element.81.refs_0_.refs_10_.norm_one, bf16[384,4096]{1,0:T(8,128)(2,1)} %get-tuple-element.80.refs_1_.refs_11_.norm_two, ...), custom_call_target="tpu_custom_call", output_to_operand_aliasing={{0}: (5, {})} | custom-call | flops 4096 | bytes 4096 | tf_op jit(solution)/shard_map/attend/pallas_call | solution.py:216
  139.3 17.9 %attend.6 = (f32[8,128]{1,0:T(8,128)}, f32[384,4096]{1,0:T(8,128)}, f32[384,4096]{1,0:T(8,128)}) custom-call(bf16[384,4096]{1,0:T(8,128)(2,1)} %get-tuple-element.81.refs_0_.refs_10_.norm_one, bf16[384,4096]{1,0:T(8,128)(2,1)} %get-tuple-element.80.refs_1_.refs_11_.norm_two, ...), custom_call_target="tpu_custom_call", output_to_operand_aliasing={{0}: (7, {}), {1}: (8, {}), {2}: (9, {})} | custom-call | flops 4096 | bytes 4096 | tf_op jit(solution)/shard_map/attend/pallas_call | solution.py:216
  158.0 47.3 %all-gather.3 = f32[16,3,4096]{2,1,0:T(4,128)S(1)} all-gather(f32[1,3,4096]{2,1,0:T(4,128)S(1)} %maximum_bitcast_fusion.1), channel_id=3, replica_groups=mesh['groups'=2,'batch'=16,'feat'=1] {'batch'}, dimensions={0}, use_global_device_ids=true | all-gather | bytes 835584 | tf_op jit(solution)/shard_map/all_gather | solution.py:287
  207.2 17.8 %attend.7 = (f32[8,128]{1,0:T(8,128)}, f32[384,4096]{1,0:T(8,128)}, f32[384,4096]{1,0:T(8,128)}) custom-call(bf16[384,4096]{1,0:T(8,128)(2,1)} %get-tuple-element.81.refs_0_.refs_10_.norm_one, bf16[384,4096]{1,0:T(8,128)(2,1)} %get-tuple-element.80.refs_1_.refs_11_.norm_two, ...), custom_call_target="tpu_custom_call", output_to_operand_aliasing={{0}: (7, {}), {1}: (8, {}), {2}: (9, {})} | custom-call | flops 4096 | bytes 4096 | tf_op jit(solution)/shard_map/attend/pallas_call | solution.py:216
  227.4 14.2 %collective-permute-done.14.refs_5_ = bf16[192,4096]{1,0:T(8,128)(2,1)S(1)} collective-permute-done((bf16[192,4096]{1,0:T(8,128)(2,1)}, bf16[192,4096]{1,0:T(8,128)(2,1)S(1)}, u32[]{:S(2)}, u32[]{:S(2)}) %collective-permute-start.14) | collective-permute-done | bytes 1572896 | tf_op jit(solution)/shard_map/ppermute | solution.py:335
  241.9 33.5 %collective-permute-done.8.refs_4_ = bf16[192,4096]{1,0:T(8,128)(2,1)S(1)} collective-permute-done((bf16[192,4096]{1,0:T(8,128)(2,1)}, bf16[192,4096]{1,0:T(8,128)(2,1)S(1)}, u32[]{:S(2)}, u32[]{:S(2)}) %collective-permute-start.8) | collective-permute-done | bytes 1572896 | tf_op jit(solution)/shard_map/ppermute | solution.py:335
  277.0 17.7 %attend.8 = (f32[8,128]{1,0:T(8,128)}, f32[384,4096]{1,0:T(8,128)}, f32[384,4096]{1,0:T(8,128)}) custom-call(bf16[384,4096]{1,0:T(8,128)(2,1)} %get-tuple-element.81.refs_0_.refs_10_.norm_one, bf16[384,4096]{1,0:T(8,128)(2,1)} %get-tuple-element.80.refs_1_.refs_11_.norm_two, ...), custom_call_target="tpu_custom_call", output_to_operand_aliasing={{0}: (7, {}), {1}: (8, {}), {2}: (9, {})} | custom-call | flops 4096 | bytes 4096 | tf_op jit(solution)/shard_map/attend/pallas_call | solution.py:216
  294.8 15.9 %collective-permute-done.17.refs_6_ = bf16[96,4096]{1,0:T(8,128)(2,1)} collective-permute-done((bf16[96,4096]{1,0:T(8,128)(2,1)S(1)}, bf16[96,4096]{1,0:T(8,128)(2,1)}, u32[]{:S(2)}, u32[]{:S(2)}) %collective-permute-start.17) | collective-permute-done | bytes 786464 | tf_op jit(solution)/shard_map/ppermute | solution.py:335
  310.7 17.7 %attend.9 = (f32[8,128]{1,0:T(8,128)}, f32[192,4096]{1,0:T(8,128)}, bf16[192,4096]{1,0:T(8,128)(2,1)}, f32[192,4096]{1,0:T(8,128)}, bf16[192,4096]{1,0:T(8,128)(2,1)}, /*index=5*/bf16[8,4096]{1,0:T(8,128)(2,1)}) custom-call(bf16[384,4096]{1,0:T(8,128)(2,1)} %get-tuple-element.81.refs_0_.refs_10_.norm_one, ...), custom_call_target="tpu_custom_call", output_to_operand_aliasing={{0}: (7, {})} | custom-call | flops 4096 | bytes 4096 | tf_op jit(solution)/shard_map/attend/pallas_call | solution.py:216
  332.4 3.4 collective-permute-done.20.refs_1_
  337.1 2.8 add_totals.2.refs_0_
  340.1 3.3 collective-permute-start.25
  347.1 2.8 add_totals.3.total_ref
  354.2 7.3 %finish.1 = (bf16[192,4096]{1,0:T(8,128)(2,1)}, bf16[192,4096]{1,0:T(8,128)(2,1)}) custom-call(f32[192,4096]{1,0:T(8,128)} %get-tuple-element.61.own_one, bf16[192,4096]{1,0:T(8,128)(2,1)} %copy-done.7, f32[192,4096]{1,0:T(8,128)} %get-tuple-element.63.own_two, bf16[192,4096]{1,0:T(8,128)(2,1)} %copy-done.8, ...), custom_call_target="tpu_custom_call" | custom-call | flops 4096 | bytes 4096 | tf_op jit(solution)/shard_map/finish/pallas_call | solution.py:258
  (90 shorter events, 31.5 us)
Async XLA Ops:
  7.2 112.6 %all-gather.6.cloned.1.call-start = ((), (), s32[]{:S(2)}) async-start(), calls=%async_computation | async-start | bytes 1114112 | tf_op jit(solution)/shard_map/all_gather | solution.py:287
  7.4 5.9 %collective-permute-start.1 = (bf16[192,4096]{1,0:T(8,128)(2,1)}, bf16[192,4096]{1,0:T(8,128)(2,1)}, u32[]{:S(2)}, u32[]{:S(2)}) collective-permute-start(bf16[192,4096]{1,0:T(8,128)(2,1)} %refs_4_), channel_id=1, source_target_pairs={{0,1},{1,0},{2,3},{3,2},{4,5},{5,4},{6,7},{7,6},{8,9},{9,8},{10,11... | collective-permute-start | bytes 4718600 | tf_op jit(solution)/shard_map/ppermute | solution.py:284
  7.8 38.7 %collective-permute-start.2 = (bf16[192,4096]{1,0:T(8,128)(2,1)}, bf16[192,4096]{1,0:T(8,128)(2,1)}, u32[]{:S(2)}, u32[]{:S(2)}) collective-permute-start(bf16[192,4096]{1,0:T(8,128)(2,1)} %refs_3_), channel_id=1, source_target_pairs={{0,4},{1,5},{4,8},{5,9},{8,12},{9,13},{12,14},{13,15},{14,10},{15,... | collective-permute-start | bytes 4718600 | tf_op jit(solution)/shard_map/ppermute | solution.py:335
  17.8 66.0 %collective-permute-start.10 = (bf16[192,4096]{1,0:T(8,128)(2,1)S(1)}, bf16[192,4096]{1,0:T(8,128)(2,1)}, u32[]{:S(2)}, u32[]{:S(2)}) collective-permute-start(bf16[192,4096]{1,0:T(8,128)(2,1)S(1)} %copy-done.2), channel_id=1, source_target_pairs={{0,4},{1,5},{4,8},{5,9},{8,12},{9,13},{12,14},{13,15},{14,10},{15,... | collective-permute-start | bytes 4718600 | tf_op jit(solution)/shard_map/ppermute | solution.py:335
  20.3 65.8 %collective-permute-start.12 = (bf16[192,4096]{1,0:T(8,128)(2,1)S(1)}, bf16[192,4096]{1,0:T(8,128)(2,1)}, u32[]{:S(2)}, u32[]{:S(2)}) collective-permute-start(bf16[192,4096]{1,0:T(8,128)(2,1)S(1)} %copy-done.2), channel_id=1, source_target_pairs={{4,0},{5,1},{8,4},{9,5},{12,8},{13,9},{14,12},{15,13},{10,14},{11,... | collective-permute-start | bytes 4718600 | tf_op jit(solution)/shard_map/ppermute | solution.py:335
  20.3 75.4 %collective-permute-start.6 = (bf16[192,4096]{1,0:T(8,128)(2,1)S(1)}, bf16[192,4096]{1,0:T(8,128)(2,1)}, u32[]{:S(2)}, u32[]{:S(2)}) collective-permute-start(bf16[192,4096]{1,0:T(8,128)(2,1)S(1)} %copy-done.3), channel_id=1, source_target_pairs={{4,0},{5,1},{8,4},{9,5},{12,8},{13,9},{14,12},{15,13},{10,14},{11,... | collective-permute-start | bytes 4718600 | tf_op jit(solution)/shard_map/ppermute | solution.py:335
  46.5 71.0 %collective-permute-start.3 = (bf16[192,4096]{1,0:T(8,128)(2,1)}, bf16[192,4096]{1,0:T(8,128)(2,1)}, u32[]{:S(2)}, u32[]{:S(2)}) collective-permute-start(bf16[192,4096]{1,0:T(8,128)(2,1)} %collective-permute-done.2.refs_3_), channel_id=1, source_target_pairs={{0,4},{1,5},{4,8},{5,9},{8,12},{9,13},{12,14},{13,15},{14,10},{15,... | collective-permute-start | bytes 4718600 | tf_op jit(solution)/shard_map/ppermute | solution.py:335
  83.8 121.6 %collective-permute-start.11 = (bf16[192,4096]{1,0:T(8,128)(2,1)}, bf16[192,4096]{1,0:T(8,128)(2,1)}, u32[]{:S(2)}, u32[]{:S(2)}) collective-permute-start(bf16[192,4096]{1,0:T(8,128)(2,1)} %collective-permute-done.10.refs_5_), channel_id=1, source_target_pairs={{0,4},{1,5},{4,8},{5,9},{8,12},{9,13},{12,14},{13,15},{14,10},{15,... | collective-permute-start | bytes 4718600 | tf_op jit(solution)/shard_map/ppermute | solution.py:335
  86.1 119.3 %collective-permute-start.13 = (bf16[192,4096]{1,0:T(8,128)(2,1)}, bf16[192,4096]{1,0:T(8,128)(2,1)}, u32[]{:S(2)}, u32[]{:S(2)}) collective-permute-start(bf16[192,4096]{1,0:T(8,128)(2,1)} %collective-permute-done.12.refs_6_), channel_id=1, source_target_pairs={{4,0},{5,1},{8,4},{9,5},{12,8},{13,9},{14,12},{15,13},{10,14},{11,... | collective-permute-start | bytes 4718600 | tf_op jit(solution)/shard_map/ppermute | solution.py:335
  95.7 111.3 %collective-permute-start.7 = (bf16[192,4096]{1,0:T(8,128)(2,1)}, bf16[192,4096]{1,0:T(8,128)(2,1)}, u32[]{:S(2)}, u32[]{:S(2)}) collective-permute-start(bf16[192,4096]{1,0:T(8,128)(2,1)} %collective-permute-done.6.refs_4_), channel_id=1, source_target_pairs={{4,0},{5,1},{8,4},{9,5},{12,8},{13,9},{14,12},{15,13},{10,14},{11,... | collective-permute-start | bytes 4718600 | tf_op jit(solution)/shard_map/ppermute | solution.py:335
  117.6 107.4 %collective-permute-start.4 = (bf16[192,4096]{1,0:T(8,128)(2,1)}, bf16[192,4096]{1,0:T(8,128)(2,1)}, u32[]{:S(2)}, u32[]{:S(2)}) collective-permute-start(bf16[192,4096]{1,0:T(8,128)(2,1)} %collective-permute-done.3.refs_3_), channel_id=1, source_target_pairs={{0,4},{1,5},{4,8},{5,9},{8,12},{9,13},{12,14},{13,15},{14,10},{15,... | collective-permute-start | bytes 4718600 | tf_op jit(solution)/shard_map/ppermute | solution.py:335
  205.4 36.1 %collective-permute-start.14 = (bf16[192,4096]{1,0:T(8,128)(2,1)}, bf16[192,4096]{1,0:T(8,128)(2,1)S(1)}, u32[]{:S(2)}, u32[]{:S(2)}) collective-permute-start(bf16[192,4096]{1,0:T(8,128)(2,1)} %collective-permute-done.11.refs_5_), channel_id=1, source_target_pairs={{0,4},{1,5},{4,8},{5,9},{8,12},{9,13},{12,14},{13,15},{14,10},{15,... | collective-permute-start | bytes 4718600 | tf_op jit(solution)/shard_map/ppermute | solution.py:335
  205.5 36.1 %collective-permute-start.15 = (bf16[192,4096]{1,0:T(8,128)(2,1)}, bf16[192,4096]{1,0:T(8,128)(2,1)S(1)}, u32[]{:S(2)}, u32[]{:S(2)}) collective-permute-start(bf16[192,4096]{1,0:T(8,128)(2,1)} %collective-permute-done.13.refs_6_), channel_id=1, source_target_pairs={{4,0},{5,1},{8,4},{9,5},{12,8},{13,9},{14,12},{15,13},{10,14},{11,... | collective-permute-start | bytes 4718600 | tf_op jit(solution)/shard_map/ppermute | solution.py:335
  206.9 68.5 %collective-permute-start.8 = (bf16[192,4096]{1,0:T(8,128)(2,1)}, bf16[192,4096]{1,0:T(8,128)(2,1)S(1)}, u32[]{:S(2)}, u32[]{:S(2)}) collective-permute-start(bf16[192,4096]{1,0:T(8,128)(2,1)} %collective-permute-done.7.refs_4_), channel_id=1, source_target_pairs={{4,0},{5,1},{8,4},{9,5},{12,8},{13,9},{14,12},{15,13},{10,14},{11,... | collective-permute-start | bytes 4718600 | tf_op jit(solution)/shard_map/ppermute | solution.py:335
  226.1 68.7 %collective-permute-start.5 = (bf16[96,4096]{1,0:T(8,128)(2,1)S(1)}, bf16[96,4096]{1,0:T(8,128)(2,1)}, u32[]{:S(2)}, u32[]{:S(2)}) collective-permute-start(bf16[96,4096]{1,0:T(8,128)(2,1)S(1)} %slice.52), channel_id=1, source_target_pairs={{0,4},{1,5},{4,8},{5,9},{8,12},{9,13},{12,14},{13,15},{14,10},{15,... | collective-permute-start | bytes 2359304 | tf_op jit(solution)/shard_map/ppermute | solution.py:335
  241.7 53.1 %collective-permute-start.16 = (bf16[96,4096]{1,0:T(8,128)(2,1)S(1)}, bf16[96,4096]{1,0:T(8,128)(2,1)}, u32[]{:S(2)}, u32[]{:S(2)}) collective-permute-start(bf16[96,4096]{1,0:T(8,128)(2,1)S(1)} %slice.44), channel_id=1, source_target_pairs={{0,4},{1,5},{4,8},{5,9},{8,12},{9,13},{12,14},{13,15},{14,10},{15,... | collective-permute-start | bytes 2359304 | tf_op jit(solution)/shard_map/ppermute | solution.py:335
  275.5 19.3 %collective-permute-start.9 = (bf16[96,4096]{1,0:T(8,128)(2,1)S(1)}, bf16[96,4096]{1,0:T(8,128)(2,1)}, u32[]{:S(2)}, u32[]{:S(2)}) collective-permute-start(bf16[96,4096]{1,0:T(8,128)(2,1)S(1)} %slice.53), channel_id=1, source_target_pairs={{4,0},{5,1},{8,4},{9,5},{12,8},{13,9},{14,12},{15,13},{10,14},{11,... | collective-permute-start | bytes 2359304 | tf_op jit(solution)/shard_map/ppermute | solution.py:335
  276.6 34.1 %collective-permute-start.17 = (bf16[96,4096]{1,0:T(8,128)(2,1)S(1)}, bf16[96,4096]{1,0:T(8,128)(2,1)}, u32[]{:S(2)}, u32[]{:S(2)}) collective-permute-start(bf16[96,4096]{1,0:T(8,128)(2,1)S(1)} %slice.45), channel_id=1, source_target_pairs={{4,0},{5,1},{8,4},{9,5},{12,8},{13,9},{14,12},{15,13},{10,14},{11,... | collective-permute-start | bytes 2359304 | tf_op jit(solution)/shard_map/ppermute | solution.py:335
  328.4 24.2 %collective-permute-start.18 = (bf16[192,4096]{1,0:T(8,128)(2,1)}, bf16[192,4096]{1,0:T(8,128)(2,1)S(1)}, u32[]{:S(2)}, u32[]{:S(2)}) collective-permute-start(bf16[192,4096]{1,0:T(8,128)(2,1)} %get-tuple-element.62), channel_id=1, source_target_pairs={{0,1},{1,0},{2,3},{3,2},{4,5},{5,4},{6,7},{7,6},{8,9},{9,8},{10,11... | collective-permute-start | bytes 4718600 | tf_op jit(solution)/shard_map/ppermute | solution.py:284
  330.2 22.4 %collective-permute-start.19 = (bf16[192,4096]{1,0:T(8,128)(2,1)}, bf16[192,4096]{1,0:T(8,128)(2,1)S(1)}, u32[]{:S(2)}, u32[]{:S(2)}) collective-permute-start(bf16[192,4096]{1,0:T(8,128)(2,1)} %get-tuple-element.64), channel_id=1, source_target_pairs={{0,1},{1,0},{2,3},{3,2},{4,5},{5,4},{6,7},{7,6},{8,9},{9,8},{10,11... | collective-permute-start | bytes 4718600 | tf_op jit(solution)/shard_map/ppermute | solution.py:284
  330.3 5.5 %collective-permute-start.20 = (bf16[8,4096]{1,0:T(8,128)(2,1)}, bf16[8,4096]{1,0:T(8,128)(2,1)S(1)}, u32[]{:S(2)}, u32[]{:S(2)}) collective-permute-start(bf16[8,4096]{1,0:T(8,128)(2,1)} %get-tuple-element.65.refs_0_), channel_id=1, source_target_pairs={{0,1},{1,0},{2,3},{3,2},{4,5},{5,4},{6,7},{7,6},{8,9},{9,8},{10,11... | collective-permute-start | bytes 196616 | tf_op jit(solution)/shard_map/ppermute | solution.py:284
  330.7 5.1 %collective-permute-start.21 = (bf16[8,4096]{1,0:T(8,128)(2,1)}, bf16[8,4096]{1,0:T(8,128)(2,1)S(1)}, u32[]{:S(2)}, u32[]{:S(2)}) collective-permute-start(bf16[8,4096]{1,0:T(8,128)(2,1)} %get-tuple-element.65.refs_0_), channel_id=1, source_target_pairs={{0,2},{1,3},{2,0},{3,1},{4,6},{5,7},{6,4},{7,5},{8,10},{9,11},{10,... | collective-permute-start | bytes 196616 | tf_op jit(solution)/shard_map/ppermute | solution.py:284
  331.7 4.5 %collective-permute-start.22 = (bf16[8,4096]{1,0:T(8,128)(2,1)}, bf16[8,4096]{1,0:T(8,128)(2,1)S(1)}, u32[]{:S(2)}, u32[]{:S(2)}) collective-permute-start(bf16[8,4096]{1,0:T(8,128)(2,1)} %get-tuple-element.65.refs_0_), channel_id=1, source_target_pairs={{0,3},{1,2},{2,1},{3,0},{4,7},{5,6},{6,5},{7,4},{8,11},{9,10},{10,... | collective-permute-start | bytes 196616 | tf_op jit(solution)/shard_map/ppermute | solution.py:284
  340.1 6.3 %collective-permute-start.25 = (bf16[8,4096]{1,0:T(8,128)(2,1)}, bf16[8,4096]{1,0:T(8,128)(2,1)S(1)}, u32[]{:S(2)}, u32[]{:S(2)}) collective-permute-start(bf16[8,4096]{1,0:T(8,128)(2,1)} %add_totals.2.refs_0_), channel_id=1, source_target_pairs={{0,12},{1,13},{2,14},{3,15},{4,8},{5,9},{6,10},{7,11},{8,4},{9,5},... | collective-permute-start | bytes 196616 | tf_op jit(solution)/shard_map/ppermute | solution.py:284
  (19 other events, 292.4 us)
Sparse Core Ops, SparseCore 0:
  17.9 43.8 all-gather.5

commit v7 on v6

--- a/solution.py
+++ b/solution.py
@@ -168,7 +168,7 @@
                 total += acc_in[index][...]
             if ends:
                 share = total.shape[0] // 2
-                outs[2 * index][...] = total[:share]
+                outs[2 * index][...] = total[:share].astype(jnp.bfloat16)
                 outs[2 * index + 1][...] = total[share:].astype(jnp.bfloat16)
                 prod = total * late[index][...].astype(jnp.float32)
                 sums.append(jnp.sum(total, axis=0, keepdims=True))
@@ -203,7 +203,7 @@
         in_specs += [pl.BlockSpec((rows, lanes), late)] * 2
         out_specs += [pl.BlockSpec((rows // 2, lanes), late)] * 4
         out_shape += [
-            jax.ShapeDtypeStruct((rows // 2, width), jnp.float32),
+            jax.ShapeDtypeStruct((rows // 2, width), jnp.bfloat16),
             jax.ShapeDtypeStruct((rows // 2, width), jnp.bfloat16),
         ] * 2
         out_specs.append(pl.BlockSpec((8, lanes), late))
@@ -242,12 +242,21 @@
     for index, (own, get, mine, other, inv) in enumerate(
         ((own_one, get_one, one, two, 1), (own_two, get_two, two, one, 3))
     ):
-        back = scale * (own[...] + get[...].astype(jnp.float32)) + other * diag
+        back = scale * (own[...].astype(jnp.float32) + get[...].astype(jnp.float32)) + other * diag
         sum_back = scale * total[2 * index : 2 * index + 1, :]
         sum_back += norm_ref[1 - index : 2 - index, :] * diag
         sum_prod = scale * total[2 * index + 1 : 2 * index + 2, :] + mixed * diag
         grad = back - sum_back / samples - mine * (sum_prod / samples)
         outs[index][...] = (stat_ref[inv : inv + 1, :] * grad).astype(jnp.bfloat16)
+
+
+def add_totals(terms):
+    return pl.pallas_call(
+        add_kernel,
+        out_shape=jax.ShapeDtypeStruct(terms[0].shape, jnp.bfloat16),
+        cost_estimate=pl.CostEstimate(flops=1, bytes_accessed=1, transcendentals=0),
+        name="add_totals",
+    )(*terms)
 
 
 def by_features(kernel, operands, heights, out_heights, dtype, name):
@@ -283,6 +292,18 @@
     def swapped(value, bit):
         return lax.ppermute(value, "batch", [(i, i ^ bit) for i in range(batches)])
 
+    def reduced(total, add):
+        size = 1
+        while size < batches:
+            steps = (1, 2, 3) if size * 4 <= batches else (1,)
+            total = add([total, *(swapped(total, size * step) for step in steps)])
+            size *= len(steps) + 1
+        return total
+
+    def norm_totals(q_one, q_two):
+        one, two = (q[:rows].astype(jnp.float32) for q in (q_one, q_two))
+        return summed([jnp.sum(one, axis=0), jnp.sum(two, axis=0), jnp.sum(one * two, axis=0)])
+
     def summed(rows_of_sums):
         return jnp.sum(lax.all_gather(jnp.stack(rows_of_sums), "batch", axis=0), axis=0)
 
@@ -313,41 +334,33 @@
     q_one = normed(here_one, far_one, mean_one, inv_one)
     q_two = normed(here_two, far_two, mean_two, inv_two)
     loss = jnp.zeros((8, 128), jnp.float32)
-    loss, *acc = attend(q_one, q_two, stat, [here_one], [here_two], loss, None, False)
-    mine_one = q_one[:rows].astype(jnp.float32)
-    mine_two = q_two[:rows].astype(jnp.float32)
-    norm_sums = summed(
-        [jnp.sum(mine_one, axis=0), jnp.sum(mine_two, axis=0), jnp.sum(mine_one * mine_two, axis=0)]
-    )
-    flows = [[view_one, view_one], [view_two, view_two]]
+    acc = None
+    ends = [[view_one, view_one], [view_two, view_two]]
     arrived = []
+    norm_sums = None
     for hop in range(hops):
         if hop > 1:
+            if hop == 2:
+                loss, *acc = attend(q_one, q_two, stat, [here_one], [here_two], loss, acc, False)
             loss, *acc = attend(q_one, q_two, stat, *arrived[hop - 2], loss, acc, False)
-        arrived.append([])
-        for view, pair in enumerate(flows):
-            if hop > 1 and view == 1:
-                *pair, loss, norm_sums = lax.optimization_barrier((*pair, loss, norm_sums))
-                arrived[hop - 1][1] = list(pair)
-            up, down = pair
+            tied = (q_one, q_two) if norm_sums is None else (q_one, q_two, norm_sums)
+            *flat, loss = lax.optimization_barrier((*ends[0], *ends[1], *tied, loss))
+            ends = [flat[:2], flat[2:4]]
+            q_one, q_two, *rest = flat[4:]
+            arrived[-1] = [list(pair) for pair in ends]
+            norm_sums = rest[0] if rest else norm_totals(q_one, q_two)
+        for view, (up, down) in enumerate(ends):
             if hop == hops - 1:
                 up, down = up[: rows // 2], down[rows // 2 :]
-            flows[view] = [lax.ppermute(up, "batch", ahead), lax.ppermute(down, "batch", behind)]
-            arrived[hop].append(list(flows[view]))
+            ends[view] = [lax.ppermute(up, "batch", ahead), lax.ppermute(down, "batch", behind)]
+        arrived.append([list(pair) for pair in ends])
     loss, *acc = attend(q_one, q_two, stat, *arrived[hops - 2], loss, acc, False)
     arrived[-1][1][0], loss = lax.optimization_barrier((arrived[-1][1][0], loss))
     loss, own_one, send_one, own_two, send_two, total = attend(
         q_one, q_two, stat, *arrived[hops - 1], loss, acc, True
     )
     get_one, get_two = swapped(send_one, 1), swapped(send_two, 1)
-    size = 1
-    while size < batches:
-        steps = (1, 2, 3) if size * 4 <= batches else (1,)
-        terms = (total, *(swapped(total, size * step) for step in steps))
-        (total,) = by_features(
-            add_kernel, terms, (8,) * len(terms), (8,), jnp.bfloat16, "add_totals"
-        )
-        size *= len(terms)
+    total = reduced(total, add_totals)
     grad_one, grad_two = by_features(
         functools.partial(finish_kernel, samples),
         (own_one, get_one, own_two, get_two, q_one, q_two, total, norm_sums, stat),

time: 373 us -> 353 us (0.946)
  waiting for transfers between devices: 164 us -> 126 us
  blocking collectives: 47.3 us -> 68 us
  local copies, waits for them, and re-layouts: 5.06 us -> 9.21 us
  Pallas kernels: 95.6 us -> 91.7 us
    ppermute x8, waiting for transfers between devices: 59.1 us -> 3.93 us  [ring_shards(): lax.ppermute(down, 'batch', behind)]
    all_gather x1, blocking collectives: 47.3 us -> 68 us  [summed(): lax.all_gather(jnp.stack(rows_of_sums), 'batch', axis=0)]
    ppermute x8, waiting for transfers between devices: 95.9 us -> 109 us  [ring_shards(): lax.ppermute(up, 'batch', ahead)]
    pallas_call x3 -> x1, Pallas kernels: 12.9 us -> 6.59 us  [by_features(): pl.pallas_call(kernel, grid=(tiles,), in_specs=in_specs, out_specs=[pl.Bl...]
    ppermute x10, waiting for transfers between devices: 9.22 us -> 13.4 us  [swapped(): return lax.ppermute(value, 'batch', [(i, i ^ bit) for i in range(batches)])]
  transfers between devices with their start and end apart: 27 -> 27, of which waited for: 14 -> 12; matrix products, arithmetic and copies ran while one was open for 4% -> 4% of each run, Pallas kernels for 19% -> 20%
where the time goes in v7:
time: 353 us; the launch traced here: 349 us
  waiting for transfers between devices  126 us (36%)
  Pallas kernels  91.7 us (26%)
  blocking collectives  68 us (19%)
  starting transfers between devices  22.7 us (6%)
  between operations  16.7 us (5%)
  other arithmetic  14.6 us (4%)
  local copies, waits for them, and re-layouts  9.21 us (3%)
    ppermute x8, waiting for transfers between devices, ring_shards(): lax.ppermute(up, 'batch', ahead)  109 us
    pallas_call x5, Pallas kernels, attend(): pl.pallas_call(functools.partial(attend_kernel, count, begins, ends), gri...  81.7 us
    all_gather x1, blocking collectives, summed(): lax.all_gather(jnp.stack(rows_of_sums), 'batch', axis=0)  68 us
    ppermute x10, waiting for transfers between devices, swapped(): return lax.ppermute(value, 'batch', [(i, i ^ bit) for i in range(batches)])  13.4 us
    ppermute x8, starting transfers between devices, ring_shards(): lax.ppermute(up, 'batch', ahead)  11.3 us
    ppermute x10, starting transfers between devices, swapped(): return lax.ppermute(value, 'batch', [(i, i ^ bit) for i in range(batches)])  7.84 us
  transfers between devices with their start and end apart: 27, of which 12 were waited for; matrix products, arithmetic and copies ran while one was open for 4% of the time, Pallas kernels for 20%

profile of v7, /device:TPU:1, one launch (start us, length us, event | category | flops | bytes accessed | tf_op | source)
XLA Modules:
  0.0 349.0 jit_solution(6731710895680659123)
XLA Ops:
  7.8 3.2 collective-permute-done.8
  11.1 2.2 collective-permute-done.9
  13.3 1.9 convert_reduce_fusion.3
  15.2 1.9 convert_reduce_fusion.2
  17.8 2.5 collective-permute-start
  21.7 38.2 %collective-permute-done.refs_3_ = bf16[192,4096]{1,0:T(8,128)(2,1)} collective-permute-done((bf16[192,4096]{1,0:T(8,128)(2,1)S(1)}, bf16[192,4096]{1,0:T(8,128)(2,1)}, u32[]{:S(2)}, u32[]{:S(2)}) %collective-permute-start) | collective-permute-done | bytes 1572896 | tf_op jit(solution)/shard_map/ppermute | solution.py:355
  60.0 2.3 collective-permute-start.1
  62.3 31.4 %collective-permute-done.4.refs_5_ = bf16[192,4096]{1,0:T(8,128)(2,1)} collective-permute-done((bf16[192,4096]{1,0:T(8,128)(2,1)S(1)}, bf16[192,4096]{1,0:T(8,128)(2,1)}, u32[]{:S(2)}, u32[]{:S(2)}) %collective-permute-start.4) | collective-permute-done | bytes 1572896 | tf_op jit(solution)/shard_map/ppermute | solution.py:355
  93.7 2.3 collective-permute-start.5
  98.2 5.1 %multiply_convert_fusion = (bf16[384,4096]{1,0:T(8,128)(2,1)}, bf16[384,4096]{1,0:T(8,128)(2,1)}) fusion(bf16[192,4096]{1,0:T(8,128)(2,1)} %collective-permute-done.9, bf16[192,4096]{1,0:T(8,128)(2,1)S(1)} %copy-done.2, f32[4096]{0:T(1024)S(1)} %bitcast.17, f32[4096]{0:T(1024)S(1)} %bitcast.16, f32[4096]{0:T(1024)S(1)} %bitcast.18, f32[4096]{0:T(1024)S(1)} %bitcast.19, ...), kind=kLoop, calls=%fused_computation | loop fusion | flops 22020096 | bytes 12648448 | tf_op jit(solution)/shard_map/convert_element_type | solution.py:332
  103.9 11.7 %attend.5 = (f32[8,128]{1,0:T(8,128)}, f32[384,4096]{1,0:T(8,128)}, f32[384,4096]{1,0:T(8,128)}) custom-call(bf16[384,4096]{1,0:T(8,128)(2,1)} %get-tuple-element.61.refs_0_.refs_10_.norm_one, bf16[384,4096]{1,0:T(8,128)(2,1)} %get-tuple-element.62.refs_1_.refs_11_.norm_two, ...), custom_call_target="tpu_custom_call", output_to_operand_aliasing={{0}: (5, {})} | custom-call | flops 4096 | bytes 4096 | tf_op jit(solution)/shard_map/attend/pallas_call | solution.py:216
  115.6 17.7 %attend.6 = (f32[8,128]{1,0:T(8,128)}, f32[384,4096]{1,0:T(8,128)}, f32[384,4096]{1,0:T(8,128)}) custom-call(bf16[384,4096]{1,0:T(8,128)(2,1)} %get-tuple-element.61.refs_0_.refs_10_.norm_one, bf16[384,4096]{1,0:T(8,128)(2,1)} %get-tuple-element.62.refs_1_.refs_11_.norm_two, ...), custom_call_target="tpu_custom_call", output_to_operand_aliasing={{0}: (7, {}), {1}: (8, {}), {2}: (9, {})} | custom-call | flops 4096 | bytes 4096 | tf_op jit(solution)/shard_map/attend/pallas_call | solution.py:216
  133.4 27.9 %collective-permute-done.5.refs_5_ = bf16[192,4096]{1,0:T(8,128)(2,1)} collective-permute-done((bf16[192,4096]{1,0:T(8,128)(2,1)}, bf16[192,4096]{1,0:T(8,128)(2,1)}, u32[]{:S(2)}, u32[]{:S(2)}) %collective-permute-start.5) | collective-permute-done | bytes 1572896 | tf_op jit(solution)/shard_map/ppermute | solution.py:355
  161.2 1.9 collective-permute-done.7.refs_6_
  166.0 17.9 %attend.7 = (f32[8,128]{1,0:T(8,128)}, f32[384,4096]{1,0:T(8,128)}, f32[384,4096]{1,0:T(8,128)}) custom-call(bf16[384,4096]{1,0:T(8,128)(2,1)} %get-tuple-element.61.refs_0_.refs_10_.norm_one, bf16[384,4096]{1,0:T(8,128)(2,1)} %get-tuple-element.62.refs_1_.refs_11_.norm_two, ...), custom_call_target="tpu_custom_call", output_to_operand_aliasing={{0}: (7, {}), {1}: (8, {}), {2}: (9, {})} | custom-call | flops 4096 | bytes 4096 | tf_op jit(solution)/shard_map/attend/pallas_call | solution.py:216
  184.7 68.0 %all-gather.3 = f32[16,3,4096]{2,1,0:T(4,128)S(1)} all-gather(f32[1,3,4096]{2,1,0:T(4,128)S(1)} %maximum_bitcast_fusion.1), channel_id=3, replica_groups=mesh['groups'=2,'batch'=16,'feat'=1] {'batch'}, dimensions={0}, use_global_device_ids=true | all-gather | bytes 835584 | tf_op jit(solution)/shard_map/all_gather | solution.py:308
  261.0 17.7 %attend.8 = (f32[8,128]{1,0:T(8,128)}, f32[384,4096]{1,0:T(8,128)}, f32[384,4096]{1,0:T(8,128)}) custom-call(bf16[384,4096]{1,0:T(8,128)(2,1)} %get-tuple-element.61.refs_0_.refs_10_.norm_one, bf16[384,4096]{1,0:T(8,128)(2,1)} %get-tuple-element.62.refs_1_.refs_11_.norm_two, ...), custom_call_target="tpu_custom_call", output_to_operand_aliasing={{0}: (7, {}), {1}: (8, {}), {2}: (9, {})} | custom-call | flops 4096 | bytes 4096 | tf_op jit(solution)/shard_map/attend/pallas_call | solution.py:216
  278.7 11.3 %collective-permute-done.14.refs_3_ = bf16[96,4096]{1,0:T(8,128)(2,1)S(1)} collective-permute-done((bf16[96,4096]{1,0:T(8,128)(2,1)S(1)}, bf16[96,4096]{1,0:T(8,128)(2,1)S(1)}, u32[]{:S(2)}, u32[]{:S(2)}) %collective-permute-start.14) | collective-permute-done | bytes 786464 | tf_op jit(solution)/shard_map/ppermute | solution.py:355
  290.0 2.0 collective-permute-done.17.refs_6_
  293.0 16.6 %attend.9 = (f32[8,128]{1,0:T(8,128)}, bf16[192,4096]{1,0:T(8,128)(2,1)}, bf16[192,4096]{1,0:T(8,128)(2,1)}, bf16[192,4096]{1,0:T(8,128)(2,1)}, bf16[192,4096]{1,0:T(8,128)(2,1)}, /*index=5*/bf16[8,4096]{1,0:T(8,128)(2,1)}) custom-call(bf16[384,4096]{1,0:T(8,128)(2,1)} %get-tuple-element.61.refs_0_.refs_10_.norm_one, ...), custom_call_target="tpu_custom_call", output_to_operand_aliasing={{0}: (7, {})} | custom-call | flops 4096 | bytes 4096 | tf_op jit(solution)/shard_map/attend/pallas_call | solution.py:216
  313.4 3.4 collective-permute-done.20.refs_1_
  324.0 2.3 collective-permute-done.24.refs_2_
  328.5 1.7 add_totals.3.total_ref
  334.5 6.6 %finish.1 = (bf16[192,4096]{1,0:T(8,128)(2,1)}, bf16[192,4096]{1,0:T(8,128)(2,1)}) custom-call(bf16[192,4096]{1,0:T(8,128)(2,1)} %get-tuple-element.75.own_one, bf16[192,4096]{1,0:T(8,128)(2,1)} %copy-done.4, bf16[192,4096]{1,0:T(8,128)(2,1)} %get-tuple-element.77.own_two, bf16[192,4096]{1,0:T(8,128)(2,1)} %copy-done.5, ...), custom_call_target="tpu_custom_call" | custom-call | flops 4096 | bytes 4096 | tf_op jit(solution)/shard_map/finish/pallas_call | solution.py:267
  (92 shorter events, 34.6 us)
Async XLA Ops:
  7.2 88.8 %all-gather.6.cloned.1.call-start = ((), (), s32[]{:S(2)}) async-start(), calls=%async_computation | async-start | bytes 1114112 | tf_op jit(solution)/shard_map/all_gather | solution.py:308
  7.4 5.9 %collective-permute-start.9 = (bf16[192,4096]{1,0:T(8,128)(2,1)}, bf16[192,4096]{1,0:T(8,128)(2,1)}, u32[]{:S(2)}, u32[]{:S(2)}) collective-permute-start(bf16[192,4096]{1,0:T(8,128)(2,1)} %refs_4_), channel_id=1, source_target_pairs={{0,1},{1,0},{2,3},{3,2},{4,5},{5,4},{6,7},{7,6},{8,9},{9,8},{10,11... | collective-permute-start | bytes 4718600 | tf_op jit(solution)/shard_map/ppermute | solution.py:293
  17.8 42.2 %collective-permute-start = (bf16[192,4096]{1,0:T(8,128)(2,1)S(1)}, bf16[192,4096]{1,0:T(8,128)(2,1)}, u32[]{:S(2)}, u32[]{:S(2)}) collective-permute-start(bf16[192,4096]{1,0:T(8,128)(2,1)S(1)} %copy-done.3), channel_id=1, source_target_pairs={{0,4},{1,5},{4,8},{5,9},{8,12},{9,13},{12,14},{13,15},{14,10},{15,... | collective-permute-start | bytes 4718600 | tf_op jit(solution)/shard_map/ppermute | solution.py:355
  20.3 42.0 %collective-permute-start.2 = (bf16[192,4096]{1,0:T(8,128)(2,1)S(1)}, bf16[192,4096]{1,0:T(8,128)(2,1)}, u32[]{:S(2)}, u32[]{:S(2)}) collective-permute-start(bf16[192,4096]{1,0:T(8,128)(2,1)S(1)} %copy-done.3), channel_id=1, source_target_pairs={{4,0},{5,1},{8,4},{9,5},{12,8},{13,9},{14,12},{15,13},{10,14},{11,... | collective-permute-start | bytes 4718600 | tf_op jit(solution)/shard_map/ppermute | solution.py:355
  20.3 73.4 %collective-permute-start.4 = (bf16[192,4096]{1,0:T(8,128)(2,1)S(1)}, bf16[192,4096]{1,0:T(8,128)(2,1)}, u32[]{:S(2)}, u32[]{:S(2)}) collective-permute-start(bf16[192,4096]{1,0:T(8,128)(2,1)S(1)} %copy-done.2), channel_id=1, source_target_pairs={{0,4},{1,5},{4,8},{5,9},{8,12},{9,13},{12,14},{13,15},{14,10},{15,... | collective-permute-start | bytes 4718600 | tf_op jit(solution)/shard_map/ppermute | solution.py:355
  21.7 74.3 %collective-permute-start.6 = (bf16[192,4096]{1,0:T(8,128)(2,1)S(1)}, bf16[192,4096]{1,0:T(8,128)(2,1)}, u32[]{:S(2)}, u32[]{:S(2)}) collective-permute-start(bf16[192,4096]{1,0:T(8,128)(2,1)S(1)} %copy-done.2), channel_id=1, source_target_pairs={{4,0},{5,1},{8,4},{9,5},{12,8},{13,9},{14,12},{15,13},{10,14},{11,... | collective-permute-start | bytes 4718600 | tf_op jit(solution)/shard_map/ppermute | solution.py:355
  60.0 73.4 %collective-permute-start.1 = (bf16[192,4096]{1,0:T(8,128)(2,1)}, bf16[192,4096]{1,0:T(8,128)(2,1)}, u32[]{:S(2)}, u32[]{:S(2)}) collective-permute-start(bf16[192,4096]{1,0:T(8,128)(2,1)} %collective-permute-done.refs_3_), channel_id=1, source_target_pairs={{0,4},{1,5},{4,8},{5,9},{8,12},{9,13},{12,14},{13,15},{14,10},{15,... | collective-permute-start | bytes 4718600 | tf_op jit(solution)/shard_map/ppermute | solution.py:355
  62.3 71.1 %collective-permute-start.3 = (bf16[192,4096]{1,0:T(8,128)(2,1)}, bf16[192,4096]{1,0:T(8,128)(2,1)}, u32[]{:S(2)}, u32[]{:S(2)}) collective-permute-start(bf16[192,4096]{1,0:T(8,128)(2,1)} %collective-permute-done.2.refs_4_), channel_id=1, source_target_pairs={{4,0},{5,1},{8,4},{9,5},{12,8},{13,9},{14,12},{15,13},{10,14},{11,... | collective-permute-start | bytes 4718600 | tf_op jit(solution)/shard_map/ppermute | solution.py:355
  93.7 67.5 %collective-permute-start.5 = (bf16[192,4096]{1,0:T(8,128)(2,1)}, bf16[192,4096]{1,0:T(8,128)(2,1)}, u32[]{:S(2)}, u32[]{:S(2)}) collective-permute-start(bf16[192,4096]{1,0:T(8,128)(2,1)} %collective-permute-done.4.refs_5_), channel_id=1, source_target_pairs={{0,4},{1,5},{4,8},{5,9},{8,12},{9,13},{12,14},{13,15},{14,10},{15,... | collective-permute-start | bytes 4718600 | tf_op jit(solution)/shard_map/ppermute | solution.py:355
  96.0 67.1 %collective-permute-start.7 = (bf16[192,4096]{1,0:T(8,128)(2,1)}, bf16[192,4096]{1,0:T(8,128)(2,1)}, u32[]{:S(2)}, u32[]{:S(2)}) collective-permute-start(bf16[192,4096]{1,0:T(8,128)(2,1)} %collective-permute-done.6.refs_6_), channel_id=1, source_target_pairs={{4,0},{5,1},{8,4},{9,5},{12,8},{13,9},{14,12},{15,13},{10,14},{11,... | collective-permute-start | bytes 4718600 | tf_op jit(solution)/shard_map/ppermute | solution.py:355
  163.1 89.8 %collective-permute-start.10 = (bf16[192,4096]{1,0:T(8,128)(2,1)}, bf16[192,4096]{1,0:T(8,128)(2,1)}, u32[]{:S(2)}, u32[]{:S(2)}) collective-permute-start(bf16[192,4096]{1,0:T(8,128)(2,1)} %collective-permute-done.1.refs_3_), channel_id=1, source_target_pairs={{0,4},{1,5},{4,8},{5,9},{8,12},{9,13},{12,14},{13,15},{14,10},{15,... | collective-permute-start | bytes 4718600 | tf_op jit(solution)/shard_map/ppermute | solution.py:355
  164.4 88.5 %collective-permute-start.11 = (bf16[192,4096]{1,0:T(8,128)(2,1)}, bf16[192,4096]{1,0:T(8,128)(2,1)}, u32[]{:S(2)}, u32[]{:S(2)}) collective-permute-start(bf16[192,4096]{1,0:T(8,128)(2,1)} %collective-permute-done.3.refs_4_), channel_id=1, source_target_pairs={{4,0},{5,1},{8,4},{9,5},{12,8},{13,9},{14,12},{15,13},{10,14},{11,... | collective-permute-start | bytes 4718600 | tf_op jit(solution)/shard_map/ppermute | solution.py:355
  164.6 88.3 %collective-permute-start.12 = (bf16[192,4096]{1,0:T(8,128)(2,1)}, bf16[192,4096]{1,0:T(8,128)(2,1)}, u32[]{:S(2)}, u32[]{:S(2)}) collective-permute-start(bf16[192,4096]{1,0:T(8,128)(2,1)} %collective-permute-done.5.refs_5_), channel_id=1, source_target_pairs={{0,4},{1,5},{4,8},{5,9},{8,12},{9,13},{12,14},{13,15},{14,10},{15,... | collective-permute-start | bytes 4718600 | tf_op jit(solution)/shard_map/ppermute | solution.py:355
  165.9 87.1 %collective-permute-start.13 = (bf16[192,4096]{1,0:T(8,128)(2,1)}, bf16[192,4096]{1,0:T(8,128)(2,1)}, u32[]{:S(2)}, u32[]{:S(2)}) collective-permute-start(bf16[192,4096]{1,0:T(8,128)(2,1)} %collective-permute-done.7.refs_6_), channel_id=1, source_target_pairs={{4,0},{5,1},{8,4},{9,5},{12,8},{13,9},{14,12},{15,13},{10,14},{11,... | collective-permute-start | bytes 4718600 | tf_op jit(solution)/shard_map/ppermute | solution.py:355
  254.1 24.6 %collective-permute-start.16 = (bf16[96,4096]{1,0:T(8,128)(2,1)S(1)}, bf16[96,4096]{1,0:T(8,128)(2,1)S(1)}, u32[]{:S(2)}, u32[]{:S(2)}) collective-permute-start(bf16[96,4096]{1,0:T(8,128)(2,1)S(1)} %slice.44), channel_id=1, source_target_pairs={{0,4},{1,5},{4,8},{5,9},{8,12},{9,13},{12,14},{13,15},{14,10},{15,... | collective-permute-start | bytes 2359304 | tf_op jit(solution)/shard_map/ppermute | solution.py:355
  255.4 34.6 %collective-permute-start.14 = (bf16[96,4096]{1,0:T(8,128)(2,1)S(1)}, bf16[96,4096]{1,0:T(8,128)(2,1)S(1)}, u32[]{:S(2)}, u32[]{:S(2)}) collective-permute-start(bf16[96,4096]{1,0:T(8,128)(2,1)S(1)} %slice.42), channel_id=1, source_target_pairs={{0,4},{1,5},{4,8},{5,9},{8,12},{9,13},{12,14},{13,15},{14,10},{15,... | collective-permute-start | bytes 2359304 | tf_op jit(solution)/shard_map/ppermute | solution.py:355
  256.6 33.4 %collective-permute-start.15 = (bf16[96,4096]{1,0:T(8,128)(2,1)S(1)}, bf16[96,4096]{1,0:T(8,128)(2,1)S(1)}, u32[]{:S(2)}, u32[]{:S(2)}) collective-permute-start(bf16[96,4096]{1,0:T(8,128)(2,1)S(1)} %slice.43), channel_id=1, source_target_pairs={{4,0},{5,1},{8,4},{9,5},{12,8},{13,9},{14,12},{15,13},{10,14},{11,... | collective-permute-start | bytes 2359304 | tf_op jit(solution)/shard_map/ppermute | solution.py:355
  259.3 32.8 %collective-permute-start.17 = (bf16[96,4096]{1,0:T(8,128)(2,1)S(1)}, bf16[96,4096]{1,0:T(8,128)(2,1)S(1)}, u32[]{:S(2)}, u32[]{:S(2)}) collective-permute-start(bf16[96,4096]{1,0:T(8,128)(2,1)S(1)} %slice.45), channel_id=1, source_target_pairs={{4,0},{5,1},{8,4},{9,5},{12,8},{13,9},{14,12},{15,13},{10,14},{11,... | collective-permute-start | bytes 2359304 | tf_op jit(solution)/shard_map/ppermute | solution.py:355
  309.7 23.1 %collective-permute-start.18 = (bf16[192,4096]{1,0:T(8,128)(2,1)}, bf16[192,4096]{1,0:T(8,128)(2,1)S(1)}, u32[]{:S(2)}, u32[]{:S(2)}) collective-permute-start(bf16[192,4096]{1,0:T(8,128)(2,1)} %get-tuple-element.76), channel_id=1, source_target_pairs={{0,1},{1,0},{2,3},{3,2},{4,5},{5,4},{6,7},{7,6},{8,9},{9,8},{10,11... | collective-permute-start | bytes 4718600 | tf_op jit(solution)/shard_map/ppermute | solution.py:293
  311.2 21.7 %collective-permute-start.19 = (bf16[192,4096]{1,0:T(8,128)(2,1)}, bf16[192,4096]{1,0:T(8,128)(2,1)S(1)}, u32[]{:S(2)}, u32[]{:S(2)}) collective-permute-start(bf16[192,4096]{1,0:T(8,128)(2,1)} %get-tuple-element.78), channel_id=1, source_target_pairs={{0,1},{1,0},{2,3},{3,2},{4,5},{5,4},{6,7},{7,6},{8,9},{9,8},{10,11... | collective-permute-start | bytes 4718600 | tf_op jit(solution)/shard_map/ppermute | solution.py:293
  311.3 5.5 %collective-permute-start.20 = (bf16[8,4096]{1,0:T(8,128)(2,1)}, bf16[8,4096]{1,0:T(8,128)(2,1)S(1)}, u32[]{:S(2)}, u32[]{:S(2)}) collective-permute-start(bf16[8,4096]{1,0:T(8,128)(2,1)} %get-tuple-element.79.refs_0_), channel_id=1, source_target_pairs={{0,1},{1,0},{2,3},{3,2},{4,5},{5,4},{6,7},{7,6},{8,9},{9,8},{10,11... | collective-permute-start | bytes 196616 | tf_op jit(solution)/shard_map/ppermute | solution.py:293
  311.7 5.1 %collective-permute-start.21 = (bf16[8,4096]{1,0:T(8,128)(2,1)}, bf16[8,4096]{1,0:T(8,128)(2,1)S(1)}, u32[]{:S(2)}, u32[]{:S(2)}) collective-permute-start(bf16[8,4096]{1,0:T(8,128)(2,1)} %get-tuple-element.79.refs_0_), channel_id=1, source_target_pairs={{0,2},{1,3},{2,0},{3,1},{4,6},{5,7},{6,4},{7,5},{8,10},{9,11},{10,... | collective-permute-start | bytes 196616 | tf_op jit(solution)/shard_map/ppermute | solution.py:293
  321.2 5.0 %collective-permute-start.24 = (bf16[8,4096]{1,0:T(8,128)(2,1)}, bf16[8,4096]{1,0:T(8,128)(2,1)S(1)}, u32[]{:S(2)}, u32[]{:S(2)}) collective-permute-start(bf16[8,4096]{1,0:T(8,128)(2,1)} %add_totals.2.refs_0_), channel_id=1, source_target_pairs={{0,8},{1,9},{2,10},{3,11},{4,12},{5,13},{6,14},{7,15},{8,0},{9,1},... | collective-permute-start | bytes 196616 | tf_op jit(solution)/shard_map/ppermute | solution.py:293
  322.1 5.8 %collective-permute-start.25 = (bf16[8,4096]{1,0:T(8,128)(2,1)}, bf16[8,4096]{1,0:T(8,128)(2,1)S(1)}, u32[]{:S(2)}, u32[]{:S(2)}) collective-permute-start(bf16[8,4096]{1,0:T(8,128)(2,1)} %add_totals.2.refs_0_), channel_id=1, source_target_pairs={{0,12},{1,13},{2,14},{3,15},{4,8},{5,9},{6,10},{7,11},{8,4},{9,5},... | collective-permute-start | bytes 196616 | tf_op jit(solution)/shard_map/ppermute | solution.py:293
  (20 other events, 171.6 us)
Sparse Core Ops, SparseCore 0:
  17.9 43.8 all-gather.5

commit v8 on v7

--- a/solution.py
+++ b/solution.py
@@ -123,9 +123,9 @@
     rest = list(refs[3 + 2 * count :])
     loss_in = rest.pop(0)
     acc_in = None if begins else (rest.pop(0), rest.pop(0))
-    late = (rest.pop(0), rest.pop(0)) if ends else None
+    late = rest[-8:-6] if ends else ()
     held_one, held_two, gram_one, gram_two, round_one, round_two = rest[-6:]
-    loss_out, *outs = rest[:-6]
+    loss_out, *outs = rest[: -8 if ends else -6]
     step = pl.program_id(0)
     tile = lax.rem(step, tiles)
 
@@ -136,6 +136,8 @@
 
     @pl.when(step < tiles)
     def _():
+        for kept, queries in zip(late, (q_one, q_two)):
+            kept[tile] = queries[...]
         for blocks, held, mean in ((blocks_one, held_one, 0), (blocks_two, held_two, 2)):
             start = 0
             for block in blocks:
@@ -165,21 +167,23 @@
         for index, (gram, held) in enumerate(((round_two, held_one), (round_one, held_two))):
             total = jnp.dot(gram[...], held[tile], preferred_element_type=jnp.float32)
             if not begins:
-                total += acc_in[index][...]
+                total += acc_in[index][...].astype(jnp.float32)
             if ends:
                 share = total.shape[0] // 2
                 outs[2 * index][...] = total[:share].astype(jnp.bfloat16)
                 outs[2 * index + 1][...] = total[share:].astype(jnp.bfloat16)
-                prod = total * late[index][...].astype(jnp.float32)
+                prod = total * late[index][tile].astype(jnp.float32)
                 sums.append(jnp.sum(total, axis=0, keepdims=True))
                 sums.append(jnp.sum(prod, axis=0, keepdims=True))
             else:
-                outs[index][...] = total
+                outs[index][...] = total.astype(outs[index].dtype)
         if ends:
             outs[4][...] = eight_rows(sums, jnp.sum(loss_out[...]))
 
 
-def attend(q_one, q_two, stat, blocks_one, blocks_two, loss, acc, ends):
+def attend(
+    q_one, q_two, stat, blocks_one, blocks_two, loss, acc, ends, dtype=jnp.float32
+):
     rows, width = q_one.shape
     lanes = width // tiles
     keys = sum(block.shape[0] for block in blocks_one)
@@ -199,8 +203,6 @@
         operands += list(acc)
         in_specs += [pl.BlockSpec((rows, lanes), late)] * 2
     if ends:
-        operands += [q_one, q_two]
-        in_specs += [pl.BlockSpec((rows, lanes), late)] * 2
         out_specs += [pl.BlockSpec((rows // 2, lanes), late)] * 4
         out_shape += [
             jax.ShapeDtypeStruct((rows // 2, width), jnp.bfloat16),
@@ -209,17 +211,18 @@
         out_specs.append(pl.BlockSpec((8, lanes), late))
         out_shape.append(jax.ShapeDtypeStruct((8, width), jnp.bfloat16))
     else:
-        if not begins:
+        if not begins and dtype == jnp.float32:
             aliases.update({4 + 2 * count: 1, 5 + 2 * count: 2})
         out_specs += [pl.BlockSpec((rows, lanes), late)] * 2
-        out_shape += [jax.ShapeDtypeStruct((rows, width), jnp.float32)] * 2
+        out_shape += [jax.ShapeDtypeStruct((rows, width), dtype)] * 2
     return pl.pallas_call(
         functools.partial(attend_kernel, count, begins, ends),
         grid=(2 * tiles,),
         in_specs=in_specs,
         out_specs=out_specs,
         out_shape=out_shape,
-        scratch_shapes=[pltpu.VMEM((tiles, keys, lanes), jnp.bfloat16)] * 2
+        scratch_shapes=[pltpu.VMEM((tiles, rows, lanes), jnp.bfloat16)] * (2 if ends else 0)
+        + [pltpu.VMEM((tiles, keys, lanes), jnp.bfloat16)] * 2
         + [pltpu.VMEM((rows, keys), jnp.float32)] * 2
         + [pltpu.VMEM((rows, keys), jnp.bfloat16)] * 2,
         input_output_aliases=aliases,
@@ -239,6 +242,14 @@
     total = total_ref[...].astype(jnp.float32)
     corr = mixed / samples
     diag = (-2.0 * (1.0 - corr)).astype(jnp.bfloat16).astype(jnp.float32) - 2.0 * off_weight * corr
+    squares = (total[4:5, :1] + total[5:6, :1]) + total[6:7, :1]
+    part = jnp.sum((1.0 - corr) ** 2 - off_weight * corr * corr)
+
+    @pl.when(pl.program_id(0) == 0)
+    def _():
+        outs[2][...] = jnp.zeros_like(outs[2]) + squares * (off_weight / (samples * samples))
+
+    outs[2][...] += part
     for index, (own, get, mine, other, inv) in enumerate(
         ((own_one, get_one, one, two, 1), (own_two, get_two, two, one, 3))
     ):
@@ -259,20 +270,22 @@
     )(*terms)
 
 
-def by_features(kernel, operands, heights, out_heights, dtype, name):
+def finish_grads(samples, operands, rows):
     width = operands[0].shape[1]
     lanes = width // tiles
+    heights = (*((rows,) * 6), 8, 4, 4)
     place = lambda step: (0, step)
-    in_specs = [pl.BlockSpec((height, lanes), place) for height in heights]
     return pl.pallas_call(
-        kernel,
+        functools.partial(finish_kernel, samples),
         grid=(tiles,),
-        in_specs=in_specs,
-        out_specs=[pl.BlockSpec((height, lanes), place) for height in out_heights],
-        out_shape=[jax.ShapeDtypeStruct((height, width), dtype) for height in out_heights],
+        in_specs=[pl.BlockSpec((height, lanes), place) for height in heights],
+        out_specs=[pl.BlockSpec((rows, lanes), place)] * 2
+        + [pl.BlockSpec((8, 128), lambda step: (0, 0))],
+        out_shape=[jax.ShapeDtypeStruct((rows, width), jnp.bfloat16)] * 2
+        + [jax.ShapeDtypeStruct((8, 128), jnp.float32)],
         compiler_params=pltpu.CompilerParams(vmem_limit_bytes=vmem),
         cost_estimate=pl.CostEstimate(flops=width, bytes_accessed=width, transcendentals=0),
-        name=name,
+        name="finish",
     )(*operands)
 
 
@@ -302,77 +315,76 @@
 
     def norm_totals(q_one, q_two):
         one, two = (q[:rows].astype(jnp.float32) for q in (q_one, q_two))
-        return summed([jnp.sum(one, axis=0), jnp.sum(two, axis=0), jnp.sum(one * two, axis=0)])
+        sums = [jnp.sum(one, axis=0), jnp.sum(two, axis=0), jnp.sum(one * two, axis=0)]
+        return summed([*sums, jnp.zeros_like(sums[0])])
 
     def summed(rows_of_sums):
         return jnp.sum(lax.all_gather(jnp.stack(rows_of_sums), "batch", axis=0), axis=0)
 
-    far_one, far_two = swapped(view_one, 1), swapped(view_two, 1)
-    here_one, here_two, far_one, far_two = lax.optimization_barrier(
-        (view_one, view_two, far_one, far_two)
-    )
-    values_one = here_one.astype(jnp.float32)
-    values_two = here_two.astype(jnp.float32)
-    sums = summed(
-        [
-            jnp.sum(values_one, axis=0),
-            jnp.sum(values_one * values_one, axis=0),
-            jnp.sum(values_two, axis=0),
-            jnp.sum(values_two * values_two, axis=0),
-        ]
-    )
-    sums = sums / samples
-    mean_one, mean_two = sums[0], sums[2]
-    inv_one = 1.0 / jnp.sqrt(sums[1] - mean_one * mean_one + 1e-05)
-    inv_two = 1.0 / jnp.sqrt(sums[3] - mean_two * mean_two + 1e-05)
-    stat = jnp.stack([mean_one, inv_one, mean_two, inv_two])
+    def statistics(one, two):
+        one, two = one.astype(jnp.float32), two.astype(jnp.float32)
+        sums = summed(
+            [
+                jnp.sum(one, axis=0),
+                jnp.sum(one * one, axis=0),
+                jnp.sum(two, axis=0),
+                jnp.sum(two * two, axis=0),
+            ]
+        )
+        sums = sums / samples
+        inv_one = 1.0 / jnp.sqrt(sums[1] - sums[0] * sums[0] + 1e-05)
+        inv_two = 1.0 / jnp.sqrt(sums[3] - sums[2] * sums[2] + 1e-05)
+        return jnp.stack([sums[0], inv_one, sums[2], inv_two])
 
     def normed(view, far, mean, inv):
         both = jnp.concatenate([view, far], axis=0).astype(jnp.float32)
         return ((both - mean) * inv).astype(jnp.bfloat16)
 
-    q_one = normed(here_one, far_one, mean_one, inv_one)
-    q_two = normed(here_two, far_two, mean_two, inv_two)
-    loss = jnp.zeros((8, 128), jnp.float32)
-    acc = None
+    here_one, here_two = view_one, view_two
+    far_one, far_two = swapped(view_one, 1), swapped(view_two, 1)
     ends = [[view_one, view_one], [view_two, view_two]]
     arrived = []
-    norm_sums = None
+    acc = None
+    loss = jnp.zeros((8, 128), jnp.float32)
     for hop in range(hops):
-        if hop > 1:
-            if hop == 2:
-                loss, *acc = attend(q_one, q_two, stat, [here_one], [here_two], loss, acc, False)
+        if hop == 1:
+            *ends[0], here_one, here_two, far_one, far_two = lax.optimization_barrier(
+                (*ends[0], here_one, here_two, far_one, far_two)
+            )
+            arrived[0][0] = list(ends[0])
+            stat = statistics(here_one, here_two)
+        if hop == 2:
+            *flat, stat = lax.optimization_barrier((*ends[0], *ends[1], stat))
+            ends = [flat[:2], flat[2:]]
+            arrived[1] = [list(pair) for pair in ends]
+            q_one = normed(here_one, far_one, stat[0], stat[1])
+            q_two = normed(here_two, far_two, stat[2], stat[3])
+            norm_sums = norm_totals(q_one, q_two)
+            loss, *acc = attend(q_one, q_two, stat, [here_one], [here_two], loss, acc, False)
+            loss, *acc = attend(q_one, q_two, stat, *arrived[0], loss, acc, False)
+        if hop > 2:
             loss, *acc = attend(q_one, q_two, stat, *arrived[hop - 2], loss, acc, False)
-            tied = (q_one, q_two) if norm_sums is None else (q_one, q_two, norm_sums)
-            *flat, loss = lax.optimization_barrier((*ends[0], *ends[1], *tied, loss))
-            ends = [flat[:2], flat[2:4]]
-            q_one, q_two, *rest = flat[4:]
+            *flat, norm_sums, loss = lax.optimization_barrier((*ends[0], *ends[1], norm_sums, loss))
+            ends = [flat[:2], flat[2:]]
             arrived[-1] = [list(pair) for pair in ends]
-            norm_sums = rest[0] if rest else norm_totals(q_one, q_two)
         for view, (up, down) in enumerate(ends):
             if hop == hops - 1:
                 up, down = up[: rows // 2], down[rows // 2 :]
             ends[view] = [lax.ppermute(up, "batch", ahead), lax.ppermute(down, "batch", behind)]
         arrived.append([list(pair) for pair in ends])
-    loss, *acc = attend(q_one, q_two, stat, *arrived[hops - 2], loss, acc, False)
+    loss, *acc = attend(
+        q_one, q_two, stat, *arrived[hops - 2], loss, acc, False, dtype=jnp.bfloat16
+    )
     arrived[-1][1][0], loss = lax.optimization_barrier((arrived[-1][1][0], loss))
     loss, own_one, send_one, own_two, send_two, total = attend(
         q_one, q_two, stat, *arrived[hops - 1], loss, acc, True
     )
     get_one, get_two = swapped(send_one, 1), swapped(send_two, 1)
     total = reduced(total, add_totals)
-    grad_one, grad_two = by_features(
-        functools.partial(finish_kernel, samples),
-        (own_one, get_one, own_two, get_two, q_one, q_two, total, norm_sums, stat),
-        (*((rows,) * 6), 8, 3, 4),
-        (rows, rows),
-        jnp.bfloat16,
-        "finish",
-    )
-    corr = norm_sums[2] / samples
-    squares = jnp.sum(total[4:7, 0].astype(jnp.float32)) / (samples * samples)
-    loss = jnp.sum((1.0 - corr) ** 2 - off_weight * corr * corr) + off_weight * squares
-    return (grad_one, grad_two, jnp.reshape(loss / width, (1,)))
+    grad_one, grad_two, loss = finish_grads(
+        samples, (own_one, get_one, own_two, get_two, q_one, q_two, total, norm_sums, stat), rows
+    )
+    return (grad_one, grad_two, jnp.reshape(loss[0, :1] / width, (1,)))
 
 
 def solution(mesh):

time: 353 us -> 337 us (0.955)
  blocking collectives: 68 us -> 0 us
  waiting for transfers between devices: 126 us -> 178 us
  Pallas kernels: 91.7 us -> 86.9 us
  local copies, waits for them, and re-layouts: 9.21 us -> 13.4 us
    all_gather x1 -> x0, blocking collectives: 68 us -> none  [summed(): lax.all_gather(jnp.stack(rows_of_sums), 'batch', axis=0)]
    ppermute x8, waiting for transfers between devices: 109 us -> 158 us  [ring_shards(): lax.ppermute(up, 'batch', ahead)]
    ppermute x8, waiting for transfers between devices: 3.93 us -> 10.4 us  [ring_shards(): lax.ppermute(down, 'batch', behind)]
    ppermute x10, waiting for transfers between devices: 13.4 us -> 7.88 us  [swapped(): return lax.ppermute(value, 'batch', [(i, i ^ bit) for i in range(batches)])]
    pallas_call x5, Pallas kernels: 81.7 us -> 76.5 us  [attend(): pl.pallas_call(functools.partial(attend_kernel, count, begins, ends), gri...]
    ppermute x10, starting transfers between devices: 7.84 us -> 12.3 us  [swapped(): return lax.ppermute(value, 'batch', [(i, i ^ bit) for i in range(batches)])]
  transfers between devices with their start and end apart: 27 -> 28, of which waited for: 12 -> 16; matrix products, arithmetic and copies ran while one was open for 4% -> 2% of each run, Pallas kernels for 20% -> 20%
where the time goes in v8:
time: 337 us; the launch traced here: 334 us
  waiting for transfers between devices  178 us (53%)
  Pallas kernels  86.9 us (26%)
  starting transfers between devices  26.1 us (8%)
  between operations  16 us (5%)
  local copies, waits for them, and re-layouts  13.4 us (4%)
  other arithmetic  13 us (4%)
    ppermute x8, waiting for transfers between devices, ring_shards(): lax.ppermute(up, 'batch', ahead)  158 us
    pallas_call x5, Pallas kernels, attend(): pl.pallas_call(functools.partial(attend_kernel, count, begins, ends), gri...  76.5 us
    ppermute x10, starting transfers between devices, swapped(): return lax.ppermute(value, 'batch', [(i, i ^ bit) for i in range(batches)])  12.3 us
    ppermute x8, starting transfers between devices, ring_shards(): lax.ppermute(up, 'batch', ahead)  11.8 us
    ppermute x8, waiting for transfers between devices, ring_shards(): lax.ppermute(down, 'batch', behind)  10.4 us
    ppermute x10, waiting for transfers between devices, swapped(): return lax.ppermute(value, 'batch', [(i, i ^ bit) for i in range(batches)])  7.88 us
    pallas_call x1, Pallas kernels, finish_grads(): pl.pallas_call(functools.partial(finish_kernel, samples), grid=(tiles,),...  7.02 us
  transfers between devices with their start and end apart: 28, of which 16 were waited for; matrix products, arithmetic and copies ran while one was open for 2% of the time, Pallas kernels for 20%

profile of v8, /device:TPU:1, one launch (start us, length us, event | category | flops | bytes accessed | tf_op | source)
XLA Modules:
  0.0 333.7 jit_solution(2355908688507492298)
XLA Ops:
  7.2 2.2 collective-permute-start
  10.4 33.4 %collective-permute-done.refs_3_ = bf16[192,4096]{1,0:T(8,128)(2,1)S(1)} collective-permute-done((bf16[192,4096]{1,0:T(8,128)(2,1)}, bf16[192,4096]{1,0:T(8,128)(2,1)S(1)}, u32[]{:S(2)}, u32[]{:S(2)}) %collective-permute-start) | collective-permute-done | bytes 1572896 | tf_op jit(solution)/shard_map/ppermute | solution.py:373
  44.7 1.9 convert_reduce_fusion.3
  46.5 1.9 convert_reduce_fusion.2
  52.3 36.4 %collective-permute-done.6.refs_5_ = bf16[192,4096]{1,0:T(8,128)(2,1)} collective-permute-done((bf16[192,4096]{1,0:T(8,128)(2,1)S(1)}, bf16[192,4096]{1,0:T(8,128)(2,1)}, u32[]{:S(2)}, u32[]{:S(2)}) %collective-permute-start.6) | collective-permute-done | bytes 1572896 | tf_op jit(solution)/shard_map/ppermute | solution.py:373
  88.7 2.3 collective-permute-start.7
  94.3 28.1 %collective-permute-done.4.refs_3_ = bf16[192,4096]{1,0:T(8,128)(2,1)} collective-permute-done((bf16[192,4096]{1,0:T(8,128)(2,1)S(1)}, bf16[192,4096]{1,0:T(8,128)(2,1)}, u32[]{:S(2)}, u32[]{:S(2)}) %collective-permute-start.4) | collective-permute-done | bytes 1572896 | tf_op jit(solution)/shard_map/ppermute | solution.py:373
  122.4 2.0 collective-permute-done.5.refs_4_
  124.4 31.8 %collective-permute-done.7.refs_5_ = bf16[192,4096]{1,0:T(8,128)(2,1)} collective-permute-done((bf16[192,4096]{1,0:T(8,128)(2,1)}, bf16[192,4096]{1,0:T(8,128)(2,1)}, u32[]{:S(2)}, u32[]{:S(2)}) %collective-permute-start.7) | collective-permute-done | bytes 1572896 | tf_op jit(solution)/shard_map/ppermute | solution.py:373
  159.2 3.6 %multiply_convert_fusion = (bf16[384,4096]{1,0:T(8,128)(2,1)S(1)}, bf16[384,4096]{1,0:T(8,128)(2,1)S(1)}) fusion(bf16[192,4096]{1,0:T(8,128)(2,1)} %collective-permute-done.3, bf16[192,4096]{1,0:T(8,128)(2,1)} %refs_4_, f32[4096]{0:T(1024)S(1)} %bitcast.21, f32[4096]{0:T(1024)S(1)} %bitcast.20, f32[4096]{0:T(1024)S(1)} %bitcast.22, f32[4096]{0:T(1024)S(1)} %bitcast.23, ...), kind=kLoop, calls=%fused_computation | loop fusion | flops 22020096 | bytes 12648448 | tf_op jit(solution)/shard_map/convert_element_type | solution.py:341
  169.5 11.6 %attend.5 = (f32[8,128]{1,0:T(8,128)}, f32[384,4096]{1,0:T(8,128)}, f32[384,4096]{1,0:T(8,128)}) custom-call(bf16[384,4096]{1,0:T(8,128)(2,1)} %copy-done.1, bf16[384,4096]{1,0:T(8,128)(2,1)} %copy-done, f32[4,4096]{1,0:T(4,128)} %copy-done.3, bf16[192,4096]{1,0:T(8,128)(2,1)} %refs_3_, bf16[192,4096]{1,0:T(8,128)(2,1)} %refs_4_, ...), custom_call_target="tpu_custom_call", output_to_operand_aliasing={{0}: (5, {})} | custom-call | flops 4096 | bytes 4096 | tf_op jit(solution)/shard_map/attend/pallas_call | solution.py:218
  181.0 17.7 %attend.6 = (f32[8,128]{1,0:T(8,128)}, f32[384,4096]{1,0:T(8,128)}, f32[384,4096]{1,0:T(8,128)}) custom-call(bf16[384,4096]{1,0:T(8,128)(2,1)} %copy-done.1, bf16[384,4096]{1,0:T(8,128)(2,1)} %copy-done, f32[4,4096]{1,0:T(4,128)} %copy-done.3, bf16[192,4096]{1,0:T(8,128)(2,1)} %copy-done.6, ...), custom_call_target="tpu_custom_call", output_to_operand_aliasing={{0}: (7, {}), {1}: (8, {}), {2}: (9, {})} | custom-call | flops 4096 | bytes 4096 | tf_op jit(solution)/shard_map/attend/pallas_call | solution.py:218
  198.8 17.7 %attend.7 = (f32[8,128]{1,0:T(8,128)}, f32[384,4096]{1,0:T(8,128)}, f32[384,4096]{1,0:T(8,128)}) custom-call(bf16[384,4096]{1,0:T(8,128)(2,1)} %copy-done.1, bf16[384,4096]{1,0:T(8,128)(2,1)} %copy-done, f32[4,4096]{1,0:T(4,128)} %copy-done.3, ...), custom_call_target="tpu_custom_call", output_to_operand_aliasing={{0}: (7, {}), {1}: (8, {}), {2}: (9, {})} | custom-call | flops 4096 | bytes 4096 | tf_op jit(solution)/shard_map/attend/pallas_call | solution.py:218
  216.5 2.0 reduce_sum.89.norm_ref
  218.5 19.9 %collective-permute-done.12.refs_5_ = bf16[192,4096]{1,0:T(8,128)(2,1)} collective-permute-done((bf16[192,4096]{1,0:T(8,128)(2,1)}, bf16[192,4096]{1,0:T(8,128)(2,1)}, u32[]{:S(2)}, u32[]{:S(2)}) %collective-permute-start.12) | collective-permute-done | bytes 1572896 | tf_op jit(solution)/shard_map/ppermute | solution.py:373
  238.4 1.9 collective-permute-done.13.refs_6_
  248.4 16.4 %attend.8 = (f32[8,128]{1,0:T(8,128)}, bf16[384,4096]{1,0:T(8,128)(2,1)}, bf16[384,4096]{1,0:T(8,128)(2,1)}) custom-call(bf16[384,4096]{1,0:T(8,128)(2,1)} %copy-done.1, bf16[384,4096]{1,0:T(8,128)(2,1)} %copy-done, f32[4,4096]{1,0:T(4,128)} %copy-done.3, bf16[192,4096]{1,0:T(8,128)(2,1)} %collective-permute-done.10.refs_3_, ...), custom_call_target="tpu_custom_call", output_to_operand_aliasing={{0}: (7, {})} | custom-call | flops 4096 | bytes 4096 | tf_op jit(solution)/shard_map/attend/pallas_call | solution.py:218
  264.8 8.5 %collective-permute-done.14.refs_3_ = bf16[96,4096]{1,0:T(8,128)(2,1)S(1)} collective-permute-done((bf16[96,4096]{1,0:T(8,128)(2,1)S(1)}, bf16[96,4096]{1,0:T(8,128)(2,1)S(1)}, u32[]{:S(2)}, u32[]{:S(2)}) %collective-permute-start.14) | collective-permute-done | bytes 786464 | tf_op jit(solution)/shard_map/ppermute | solution.py:373
  273.3 3.8 %collective-permute-done.17.refs_6_ = bf16[96,4096]{1,0:T(8,128)(2,1)S(1)} collective-permute-done((bf16[96,4096]{1,0:T(8,128)(2,1)S(1)}, bf16[96,4096]{1,0:T(8,128)(2,1)S(1)}, u32[]{:S(2)}, u32[]{:S(2)}) %collective-permute-start.17) | collective-permute-done | bytes 786464 | tf_op jit(solution)/shard_map/ppermute | solution.py:373
  278.0 13.1 %attend.9 = (f32[8,128]{1,0:T(8,128)}, bf16[192,4096]{1,0:T(8,128)(2,1)}, bf16[192,4096]{1,0:T(8,128)(2,1)}, bf16[192,4096]{1,0:T(8,128)(2,1)}, bf16[192,4096]{1,0:T(8,128)(2,1)}, /*index=5*/bf16[8,4096]{1,0:T(8,128)(2,1)}) custom-call(bf16[384,4096]{1,0:T(8,128)(2,1)} %copy-done.1, bf16[384,4096]{1,0:T(8,128)(2,1)} %copy-done, ...), custom_call_target="tpu_custom_call", output_to_operand_aliasing={{0}: (7, {})} | custom-call | flops 4096 | bytes 4096 | tf_op jit(solution)/shard_map/attend/pallas_call | solution.py:218
  291.1 5.5 %collective-permute-start.18 = (bf16[192,4096]{1,0:T(8,128)(2,1)}, bf16[192,4096]{1,0:T(8,128)(2,1)S(1)}, u32[]{:S(2)}, u32[]{:S(2)}) collective-permute-start(bf16[192,4096]{1,0:T(8,128)(2,1)} %get-tuple-element.73), channel_id=1, source_target_pairs={{0,1},{1,0},{2,3},{3,2},{4,5},{5,4},{6,7},{7,6},{8,9},{9,8},{10,11... | collective-permute-start | bytes 4718600 | tf_op jit(solution)/shard_map/ppermute | solution.py:306
  298.9 3.4 %collective-permute-done.20.refs_1_ = bf16[8,4096]{1,0:T(8,128)(2,1)S(1)} collective-permute-done((bf16[8,4096]{1,0:T(8,128)(2,1)}, bf16[8,4096]{1,0:T(8,128)(2,1)S(1)}, u32[]{:S(2)}, u32[]{:S(2)}) %collective-permute-start.20) | collective-permute-done | bytes 65568 | tf_op jit(solution)/shard_map/ppermute | solution.py:306
  310.0 2.9 collective-permute-done.25.refs_3_
  316.8 7.0 %finish.1 = (bf16[192,4096]{1,0:T(8,128)(2,1)}, bf16[192,4096]{1,0:T(8,128)(2,1)}, f32[8,128]{1,0:T(8,128)}) custom-call(bf16[192,4096]{1,0:T(8,128)(2,1)} %get-tuple-element.72.own_one, bf16[192,4096]{1,0:T(8,128)(2,1)} %copy-done.4, bf16[192,4096]{1,0:T(8,128)(2,1)} %get-tuple-element.74.own_two, bf16[192,4096]{1,0:T(8,128)(2,1)} %copy-done.5, ...), custom_call_target="tpu_custom_call" | custom-call | flops 4096 | bytes 4096 | tf_op jit(solution)/shard_map/finish/pallas_call | solution.py:278
  (97 shorter events, 42.6 us)
Async XLA Ops:
  7.2 85.5 %all-gather.7.cloned.1.call-start = ((), (), s32[]{:S(2)}) async-start(), calls=%async_computation | async-start | bytes 1114112 | tf_op jit(solution)/shard_map/all_gather | solution.py:322
  7.2 36.6 %collective-permute-start = (bf16[192,4096]{1,0:T(8,128)(2,1)}, bf16[192,4096]{1,0:T(8,128)(2,1)S(1)}, u32[]{:S(2)}, u32[]{:S(2)}) collective-permute-start(bf16[192,4096]{1,0:T(8,128)(2,1)} %refs_3_), channel_id=1, source_target_pairs={{0,4},{1,5},{4,8},{5,9},{8,12},{9,13},{12,14},{13,15},{14,10},{15,... | collective-permute-start | bytes 4718600 | tf_op jit(solution)/shard_map/ppermute | solution.py:373
  9.4 35.3 %collective-permute-start.1 = (bf16[192,4096]{1,0:T(8,128)(2,1)}, bf16[192,4096]{1,0:T(8,128)(2,1)}, u32[]{:S(2)}, u32[]{:S(2)}) collective-permute-start(bf16[192,4096]{1,0:T(8,128)(2,1)} %refs_3_), channel_id=1, source_target_pairs={{4,0},{5,1},{8,4},{9,5},{12,8},{13,9},{14,12},{15,13},{10,14},{11,... | collective-permute-start | bytes 4718600 | tf_op jit(solution)/shard_map/ppermute | solution.py:373
  9.4 35.3 %collective-permute-start.2 = (bf16[192,4096]{1,0:T(8,128)(2,1)}, bf16[192,4096]{1,0:T(8,128)(2,1)}, u32[]{:S(2)}, u32[]{:S(2)}) collective-permute-start(bf16[192,4096]{1,0:T(8,128)(2,1)} %refs_3_), channel_id=1, source_target_pairs={{0,1},{1,0},{2,3},{3,2},{4,5},{5,4},{6,7},{7,6},{8,9},{9,8},{10,11... | collective-permute-start | bytes 4718600 | tf_op jit(solution)/shard_map/ppermute | solution.py:306
  10.4 34.3 %collective-permute-start.3 = (bf16[192,4096]{1,0:T(8,128)(2,1)}, bf16[192,4096]{1,0:T(8,128)(2,1)}, u32[]{:S(2)}, u32[]{:S(2)}) collective-permute-start(bf16[192,4096]{1,0:T(8,128)(2,1)} %refs_4_), channel_id=1, source_target_pairs={{0,1},{1,0},{2,3},{3,2},{4,5},{5,4},{6,7},{7,6},{8,9},{9,8},{10,11... | collective-permute-start | bytes 4718600 | tf_op jit(solution)/shard_map/ppermute | solution.py:306
  49.1 167.4 %all-gather.9.cloned.1.call-start = ((), (), s32[]{:S(2)}) async-start(), calls=%async_computation.1 | async-start | bytes 1114112 | tf_op jit(solution)/shard_map/all_gather | solution.py:322
  49.2 39.5 %collective-permute-start.6 = (bf16[192,4096]{1,0:T(8,128)(2,1)S(1)}, bf16[192,4096]{1,0:T(8,128)(2,1)}, u32[]{:S(2)}, u32[]{:S(2)}) collective-permute-start(bf16[192,4096]{1,0:T(8,128)(2,1)S(1)} %copy-done.2), channel_id=1, source_target_pairs={{0,4},{1,5},{4,8},{5,9},{8,12},{9,13},{12,14},{13,15},{14,10},{15,... | collective-permute-start | bytes 4718600 | tf_op jit(solution)/shard_map/ppermute | solution.py:373
  50.6 40.5 %collective-permute-start.8 = (bf16[192,4096]{1,0:T(8,128)(2,1)S(1)}, bf16[192,4096]{1,0:T(8,128)(2,1)}, u32[]{:S(2)}, u32[]{:S(2)}) collective-permute-start(bf16[192,4096]{1,0:T(8,128)(2,1)S(1)} %copy-done.2), channel_id=1, source_target_pairs={{4,0},{5,1},{8,4},{9,5},{12,8},{13,9},{14,12},{15,13},{10,14},{11,... | collective-permute-start | bytes 4718600 | tf_op jit(solution)/shard_map/ppermute | solution.py:373
  50.8 71.6 %collective-permute-start.4 = (bf16[192,4096]{1,0:T(8,128)(2,1)S(1)}, bf16[192,4096]{1,0:T(8,128)(2,1)}, u32[]{:S(2)}, u32[]{:S(2)}) collective-permute-start(bf16[192,4096]{1,0:T(8,128)(2,1)S(1)} %collective-permute-done.refs_3_), channel_id=1, source_target_pairs={{0,4},{1,5},{4,8},{5,9},{8,12},{9,13},{12,14},{13,15},{14,10},{15,... | collective-permute-start | bytes 4718600 | tf_op jit(solution)/shard_map/ppermute | solution.py:373
  52.1 72.3 %collective-permute-start.5 = (bf16[192,4096]{1,0:T(8,128)(2,1)}, bf16[192,4096]{1,0:T(8,128)(2,1)}, u32[]{:S(2)}, u32[]{:S(2)}) collective-permute-start(bf16[192,4096]{1,0:T(8,128)(2,1)} %collective-permute-done.1.refs_4_), channel_id=1, source_target_pairs={{4,0},{5,1},{8,4},{9,5},{12,8},{13,9},{14,12},{15,13},{10,14},{11,... | collective-permute-start | bytes 4718600 | tf_op jit(solution)/shard_map/ppermute | solution.py:373
  88.7 67.5 %collective-permute-start.7 = (bf16[192,4096]{1,0:T(8,128)(2,1)}, bf16[192,4096]{1,0:T(8,128)(2,1)}, u32[]{:S(2)}, u32[]{:S(2)}) collective-permute-start(bf16[192,4096]{1,0:T(8,128)(2,1)} %collective-permute-done.6.refs_5_), channel_id=1, source_target_pairs={{0,4},{1,5},{4,8},{5,9},{8,12},{9,13},{12,14},{13,15},{14,10},{15,... | collective-permute-start | bytes 4718600 | tf_op jit(solution)/shard_map/ppermute | solution.py:373
  91.0 67.0 %collective-permute-start.9 = (bf16[192,4096]{1,0:T(8,128)(2,1)}, bf16[192,4096]{1,0:T(8,128)(2,1)S(1)}, u32[]{:S(2)}, u32[]{:S(2)}) collective-permute-start(bf16[192,4096]{1,0:T(8,128)(2,1)} %collective-permute-done.8.refs_6_), channel_id=1, source_target_pairs={{4,0},{5,1},{8,4},{9,5},{12,8},{13,9},{14,12},{15,13},{10,14},{11,... | collective-permute-start | bytes 4718600 | tf_op jit(solution)/shard_map/ppermute | solution.py:373
  165.9 52.6 %collective-permute-start.10 = (bf16[192,4096]{1,0:T(8,128)(2,1)}, bf16[192,4096]{1,0:T(8,128)(2,1)}, u32[]{:S(2)}, u32[]{:S(2)}) collective-permute-start(bf16[192,4096]{1,0:T(8,128)(2,1)} %collective-permute-done.4.refs_3_), channel_id=1, source_target_pairs={{0,4},{1,5},{4,8},{5,9},{8,12},{9,13},{12,14},{13,15},{14,10},{15,... | collective-permute-start | bytes 4718600 | tf_op jit(solution)/shard_map/ppermute | solution.py:373
  167.3 51.2 %collective-permute-start.11 = (bf16[192,4096]{1,0:T(8,128)(2,1)}, bf16[192,4096]{1,0:T(8,128)(2,1)}, u32[]{:S(2)}, u32[]{:S(2)}) collective-permute-start(bf16[192,4096]{1,0:T(8,128)(2,1)} %collective-permute-done.5.refs_4_), channel_id=1, source_target_pairs={{4,0},{5,1},{8,4},{9,5},{12,8},{13,9},{14,12},{15,13},{10,14},{11,... | collective-permute-start | bytes 4718600 | tf_op jit(solution)/shard_map/ppermute | solution.py:373
  167.4 71.0 %collective-permute-start.12 = (bf16[192,4096]{1,0:T(8,128)(2,1)}, bf16[192,4096]{1,0:T(8,128)(2,1)}, u32[]{:S(2)}, u32[]{:S(2)}) collective-permute-start(bf16[192,4096]{1,0:T(8,128)(2,1)} %collective-permute-done.7.refs_5_), channel_id=1, source_target_pairs={{0,4},{1,5},{4,8},{5,9},{8,12},{9,13},{12,14},{13,15},{14,10},{15,... | collective-permute-start | bytes 4718600 | tf_op jit(solution)/shard_map/ppermute | solution.py:373
  168.8 71.5 %collective-permute-start.13 = (bf16[192,4096]{1,0:T(8,128)(2,1)}, bf16[192,4096]{1,0:T(8,128)(2,1)}, u32[]{:S(2)}, u32[]{:S(2)}) collective-permute-start(bf16[192,4096]{1,0:T(8,128)(2,1)} %copy-done.7), channel_id=1, source_target_pairs={{4,0},{5,1},{8,4},{9,5},{12,8},{13,9},{14,12},{15,13},{10,14},{11,... | collective-permute-start | bytes 4718600 | tf_op jit(solution)/shard_map/ppermute | solution.py:373
  241.5 23.2 %collective-permute-start.16 = (bf16[96,4096]{1,0:T(8,128)(2,1)S(1)}, bf16[96,4096]{1,0:T(8,128)(2,1)S(1)}, u32[]{:S(2)}, u32[]{:S(2)}) collective-permute-start(bf16[96,4096]{1,0:T(8,128)(2,1)S(1)} %slice.61), channel_id=1, source_target_pairs={{0,4},{1,5},{4,8},{5,9},{8,12},{9,13},{12,14},{13,15},{14,10},{15,... | collective-permute-start | bytes 2359304 | tf_op jit(solution)/shard_map/ppermute | solution.py:373
  244.0 29.3 %collective-permute-start.14 = (bf16[96,4096]{1,0:T(8,128)(2,1)S(1)}, bf16[96,4096]{1,0:T(8,128)(2,1)S(1)}, u32[]{:S(2)}, u32[]{:S(2)}) collective-permute-start(bf16[96,4096]{1,0:T(8,128)(2,1)S(1)} %slice.59), channel_id=1, source_target_pairs={{0,4},{1,5},{4,8},{5,9},{8,12},{9,13},{12,14},{13,15},{14,10},{15,... | collective-permute-start | bytes 2359304 | tf_op jit(solution)/shard_map/ppermute | solution.py:373
  245.7 27.6 %collective-permute-start.15 = (bf16[96,4096]{1,0:T(8,128)(2,1)S(1)}, bf16[96,4096]{1,0:T(8,128)(2,1)S(1)}, u32[]{:S(2)}, u32[]{:S(2)}) collective-permute-start(bf16[96,4096]{1,0:T(8,128)(2,1)S(1)} %slice.60), channel_id=1, source_target_pairs={{4,0},{5,1},{8,4},{9,5},{12,8},{13,9},{14,12},{15,13},{10,14},{11,... | collective-permute-start | bytes 2359304 | tf_op jit(solution)/shard_map/ppermute | solution.py:373
  247.9 29.1 %collective-permute-start.17 = (bf16[96,4096]{1,0:T(8,128)(2,1)S(1)}, bf16[96,4096]{1,0:T(8,128)(2,1)S(1)}, u32[]{:S(2)}, u32[]{:S(2)}) collective-permute-start(bf16[96,4096]{1,0:T(8,128)(2,1)S(1)} %slice.62), channel_id=1, source_target_pairs={{4,0},{5,1},{8,4},{9,5},{12,8},{13,9},{14,12},{15,13},{10,14},{11,... | collective-permute-start | bytes 2359304 | tf_op jit(solution)/shard_map/ppermute | solution.py:373
  291.1 24.0 %collective-permute-start.18 = (bf16[192,4096]{1,0:T(8,128)(2,1)}, bf16[192,4096]{1,0:T(8,128)(2,1)S(1)}, u32[]{:S(2)}, u32[]{:S(2)}) collective-permute-start(bf16[192,4096]{1,0:T(8,128)(2,1)} %get-tuple-element.73), channel_id=1, source_target_pairs={{0,1},{1,0},{2,3},{3,2},{4,5},{5,4},{6,7},{7,6},{8,9},{9,8},{10,11... | collective-permute-start | bytes 4718600 | tf_op jit(solution)/shard_map/ppermute | solution.py:306
  296.7 18.5 %collective-permute-start.19 = (bf16[192,4096]{1,0:T(8,128)(2,1)}, bf16[192,4096]{1,0:T(8,128)(2,1)S(1)}, u32[]{:S(2)}, u32[]{:S(2)}) collective-permute-start(bf16[192,4096]{1,0:T(8,128)(2,1)} %get-tuple-element.75), channel_id=1, source_target_pairs={{0,1},{1,0},{2,3},{3,2},{4,5},{5,4},{6,7},{7,6},{8,9},{9,8},{10,11... | collective-permute-start | bytes 4718600 | tf_op jit(solution)/shard_map/ppermute | solution.py:306
  296.7 5.5 %collective-permute-start.20 = (bf16[8,4096]{1,0:T(8,128)(2,1)}, bf16[8,4096]{1,0:T(8,128)(2,1)S(1)}, u32[]{:S(2)}, u32[]{:S(2)}) collective-permute-start(bf16[8,4096]{1,0:T(8,128)(2,1)} %get-tuple-element.76.refs_0_), channel_id=1, source_target_pairs={{0,1},{1,0},{2,3},{3,2},{4,5},{5,4},{6,7},{7,6},{8,9},{9,8},{10,11... | collective-permute-start | bytes 196616 | tf_op jit(solution)/shard_map/ppermute | solution.py:306
  307.1 5.7 %collective-permute-start.25 = (bf16[8,4096]{1,0:T(8,128)(2,1)}, bf16[8,4096]{1,0:T(8,128)(2,1)S(1)}, u32[]{:S(2)}, u32[]{:S(2)}) collective-permute-start(bf16[8,4096]{1,0:T(8,128)(2,1)} %add_totals.2.refs_0_), channel_id=1, source_target_pairs={{0,12},{1,13},{2,14},{3,15},{4,8},{5,9},{6,10},{7,11},{8,4},{9,5},... | collective-permute-start | bytes 196616 | tf_op jit(solution)/shard_map/ppermute | solution.py:306
  (22 other events, 284.9 us)
Sparse Core Ops, SparseCore 0:
  49.3 43.3 all-gather.6
  166.0 43.8 all-gather.8

commit v9 on v8

--- a/solution.py
+++ b/solution.py
@@ -107,11 +107,37 @@
     return out.astype(jnp.bfloat16)
 
 
-def add_kernel(*refs):
-    terms = [ref[...].astype(jnp.float32) for ref in refs[:-1]]
+def added(refs):
+    terms = [ref[...].astype(jnp.float32) for ref in refs]
     while len(terms) > 1:
         terms = [terms[k] + terms[k + 1] for k in range(0, len(terms), 2)]
-    total = terms[0]
+    return terms[0]
+
+
+def sums_kernel(one_ref, two_ref, out_ref):
+    for index, ref in enumerate((one_ref, two_ref)):
+        values = ref[...].astype(jnp.float32)
+        out_ref[2 * index : 2 * index + 1, :] = jnp.sum(values, axis=0, keepdims=True)
+        out_ref[2 * index + 1 : 2 * index + 2, :] = jnp.sum(values * values, axis=0, keepdims=True)
+
+
+def first_sums(one, two):
+    rows, width = one.shape
+    lanes = width // tiles
+    place = lambda step: (0, step)
+    return pl.pallas_call(
+        sums_kernel,
+        grid=(tiles,),
+        in_specs=[pl.BlockSpec((rows, lanes), place)] * 2,
+        out_specs=pl.BlockSpec((4, lanes), place),
+        out_shape=jax.ShapeDtypeStruct((4, width), jnp.float32),
+        cost_estimate=pl.CostEstimate(flops=width, bytes_accessed=width, transcendentals=0),
+        name="first_sums",
+    )(one, two)
+
+
+def add_kernel(*refs):
+    total = added(refs[:-1])
     loss = (total[4:5] + total[5:6]) + total[6:7]
     refs[-1][...] = eight_rows([total[k : k + 1] for k in range(4)], loss)
 
@@ -233,23 +259,24 @@
 
 
 def finish_kernel(
-    samples, own_one, get_one, own_two, get_two, norm_one, norm_two, total_ref, norm_ref, stat_ref, *outs
+    samples, full, own_one, get_one, own_two, get_two, norm_one, norm_two, norm_ref, stat_ref, *rest
 ):
+    outs = rest[-3:]
     scale = 2.0 * off_weight / samples
     one = norm_one[...].astype(jnp.float32)
     two = norm_two[...].astype(jnp.float32)
     mixed = norm_ref[2:3, :]
-    total = total_ref[...].astype(jnp.float32)
+    total = added(rest[:-3])
     corr = mixed / samples
     diag = (-2.0 * (1.0 - corr)).astype(jnp.bfloat16).astype(jnp.float32) - 2.0 * off_weight * corr
-    squares = (total[4:5, :1] + total[5:6, :1]) + total[6:7, :1]
+    squares = jnp.max((total[4:5, :128] + total[5:6, :128]) + total[6:7, :128])
     part = jnp.sum((1.0 - corr) ** 2 - off_weight * corr * corr)
 
     @pl.when(pl.program_id(0) == 0)
     def _():
-        outs[2][...] = jnp.zeros_like(outs[2]) + squares * (off_weight / (samples * samples))
-
-    outs[2][...] += part
+        outs[2][0] = squares * (off_weight / (samples * samples * full))
+
+    outs[2][0] += part / full
     for index, (own, get, mine, other, inv) in enumerate(
         ((own_one, get_one, one, two, 1), (own_two, get_two, two, one, 3))
     ):
@@ -273,16 +300,16 @@
 def finish_grads(samples, operands, rows):
     width = operands[0].shape[1]
     lanes = width // tiles
-    heights = (*((rows,) * 6), 8, 4, 4)
+    heights = (*((rows,) * 6), 4, 4) + (8,) * (len(operands) - 8)
     place = lambda step: (0, step)
     return pl.pallas_call(
-        functools.partial(finish_kernel, samples),
+        functools.partial(finish_kernel, samples, width),
         grid=(tiles,),
         in_specs=[pl.BlockSpec((height, lanes), place) for height in heights],
         out_specs=[pl.BlockSpec((rows, lanes), place)] * 2
-        + [pl.BlockSpec((8, 128), lambda step: (0, 0))],
+        + [pl.BlockSpec(memory_space=pltpu.SMEM)],
         out_shape=[jax.ShapeDtypeStruct((rows, width), jnp.bfloat16)] * 2
-        + [jax.ShapeDtypeStruct((8, 128), jnp.float32)],
+        + [jax.ShapeDtypeStruct((1,), jnp.float32)],
         compiler_params=pltpu.CompilerParams(vmem_limit_bytes=vmem),
         cost_estimate=pl.CostEstimate(flops=width, bytes_accessed=width, transcendentals=0),
         name="finish",
@@ -309,9 +336,10 @@
         size = 1
         while size < batches:
             steps = (1, 2, 3) if size * 4 <= batches else (1,)
-            total = add([total, *(swapped(total, size * step) for step in steps)])
+            terms = [total, *(swapped(total, size * step) for step in steps)]
             size *= len(steps) + 1
-        return total
+            total = add(terms) if size < batches else None
+        return terms
 
     def norm_totals(q_one, q_two):
         one, two = (q[:rows].astype(jnp.float32) for q in (q_one, q_two))
@@ -322,16 +350,8 @@
         return jnp.sum(lax.all_gather(jnp.stack(rows_of_sums), "batch", axis=0), axis=0)
 
     def statistics(one, two):
-        one, two = one.astype(jnp.float32), two.astype(jnp.float32)
-        sums = summed(
-            [
-                jnp.sum(one, axis=0),
-                jnp.sum(one * one, axis=0),
-                jnp.sum(two, axis=0),
-                jnp.sum(two * two, axis=0),
-            ]
-        )
-        sums = sums / samples
+        sums = first_sums(one, two)
+        sums = jnp.sum(lax.all_gather(sums, "batch", axis=0), axis=0) / samples
         inv_one = 1.0 / jnp.sqrt(sums[1] - sums[0] * sums[0] + 1e-05)
         inv_two = 1.0 / jnp.sqrt(sums[3] - sums[2] * sums[2] + 1e-05)
         return jnp.stack([sums[0], inv_one, sums[2], inv_two])
@@ -340,51 +360,48 @@
         both = jnp.concatenate([view, far], axis=0).astype(jnp.float32)
         return ((both - mean) * inv).astype(jnp.bfloat16)
 
-    here_one, here_two = view_one, view_two
+    stat = statistics(view_one, view_two)
     far_one, far_two = swapped(view_one, 1), swapped(view_two, 1)
+    q_one = normed(view_one, far_one, stat[0], stat[1])
+    q_two = normed(view_two, far_two, stat[2], stat[3])
     ends = [[view_one, view_one], [view_two, view_two]]
     arrived = []
-    acc = None
     loss = jnp.zeros((8, 128), jnp.float32)
+    loss, *acc = attend(q_one, q_two, stat, [view_one], [view_two], loss, None, False)
     for hop in range(hops):
-        if hop == 1:
-            *ends[0], here_one, here_two, far_one, far_two = lax.optimization_barrier(
-                (*ends[0], here_one, here_two, far_one, far_two)
-            )
-            arrived[0][0] = list(ends[0])
-            stat = statistics(here_one, here_two)
-        if hop == 2:
-            *flat, stat = lax.optimization_barrier((*ends[0], *ends[1], stat))
-            ends = [flat[:2], flat[2:]]
-            arrived[1] = [list(pair) for pair in ends]
-            q_one = normed(here_one, far_one, stat[0], stat[1])
-            q_two = normed(here_two, far_two, stat[2], stat[3])
-            norm_sums = norm_totals(q_one, q_two)
-            loss, *acc = attend(q_one, q_two, stat, [here_one], [here_two], loss, acc, False)
-            loss, *acc = attend(q_one, q_two, stat, *arrived[0], loss, acc, False)
-        if hop > 2:
+        if hop > 1:
             loss, *acc = attend(q_one, q_two, stat, *arrived[hop - 2], loss, acc, False)
-            *flat, norm_sums, loss = lax.optimization_barrier((*ends[0], *ends[1], norm_sums, loss))
-            ends = [flat[:2], flat[2:]]
+            tied = (q_one, q_two) if hop == 2 else (norm_sums,)
+            *flat, loss = lax.optimization_barrier((*ends[0], *ends[1], *tied, loss))
+            ends = [flat[:2], flat[2:4]]
             arrived[-1] = [list(pair) for pair in ends]
-        for view, (up, down) in enumerate(ends):
-            if hop == hops - 1:
-                up, down = up[: rows // 2], down[rows // 2 :]
-            ends[view] = [lax.ppermute(up, "batch", ahead), lax.ppermute(down, "batch", behind)]
-        arrived.append([list(pair) for pair in ends])
+            if hop == 2:
+                q_one, q_two = flat[4:]
+                norm_sums = norm_totals(q_one, q_two)
+            else:
+                norm_sums = flat[4]
+        if hop < hops - 1:
+            ends = [
+                [lax.ppermute(up, "batch", ahead), lax.ppermute(down, "batch", behind)]
+                for up, down in ends
+            ]
+            arrived.append([list(pair) for pair in ends])
+        else:
+            last_one = lax.ppermute(ends[0][0], "batch", ahead)
+            last_two = lax.ppermute(ends[1][1], "batch", behind)
     loss, *acc = attend(
         q_one, q_two, stat, *arrived[hops - 2], loss, acc, False, dtype=jnp.bfloat16
     )
-    arrived[-1][1][0], loss = lax.optimization_barrier((arrived[-1][1][0], loss))
+    last_one, last_two, loss = lax.optimization_barrier((last_one, last_two, loss))
     loss, own_one, send_one, own_two, send_two, total = attend(
-        q_one, q_two, stat, *arrived[hops - 1], loss, acc, True
+        q_one, q_two, stat, [last_one], [last_two], loss, acc, True
     )
     get_one, get_two = swapped(send_one, 1), swapped(send_two, 1)
-    total = reduced(total, add_totals)
+    terms = reduced(total, add_totals)
     grad_one, grad_two, loss = finish_grads(
-        samples, (own_one, get_one, own_two, get_two, q_one, q_two, total, norm_sums, stat), rows
-    )
-    return (grad_one, grad_two, jnp.reshape(loss[0, :1] / width, (1,)))
+        samples, (own_one, get_one, own_two, get_two, q_one, q_two, norm_sums, stat, *terms), rows
+    )
+    return (grad_one, grad_two, loss)
 
 
 def solution(mesh):

time: 337 us -> 323 us (0.958)
  local copies, waits for them, and re-layouts: 13.4 us -> 4.38 us
  starting transfers between devices: 26.1 us -> 22.3 us
  Pallas kernels: 86.9 us -> 90.6 us
    ppermute x8 -> x6, waiting for transfers between devices: 158 us -> 86.9 us  [ring_shards(): lax.ppermute(up, 'batch', ahead)]
    all_gather x0 -> x1, waiting for transfers between devices: none -> 39.5 us  [statistics(): sums = jnp.sum(lax.all_gather(sums, 'batch', axis=0), axis=0) / samples]
    all_gather x2 -> x1, waiting for transfers between devices: 1.67 us -> 21.8 us  [summed(): lax.all_gather(jnp.stack(rows_of_sums), 'batch', axis=0)]
    ppermute x0 -> x2, waiting for transfers between devices: none -> 16.9 us  [the longest x1 15.7 us: ring_shards(): last_one = lax.ppermute(ends[0][0], 'batch', ahead)]
    ppermute x8 -> x6, waiting for transfers between devices: 10.4 us -> 3.71 us  [ring_shards(): lax.ppermute(down, 'batch', behind)]
    slice x6 -> x0, local copies, waits for them, and re-layouts: 5.97 us -> none  [the longest x4 4.74 us: ring_shards(): up, down = (up[:rows // 2], down[rows // 2:])]
    pallas_call x1 -> x2, Pallas kernels: 7.02 us -> 12.1 us  [the longest x1 8.13 us: finish_grads(): pl.pallas_call(functools.partial(finish_kernel, samples, width), grid=(ti...]
    ppermute x8 -> x6, starting transfers between devices: 11.8 us -> 9.83 us  [ring_shards(): lax.ppermute(up, 'batch', ahead)]
  transfers between devices with their start and end apart: 28 -> 26, of which waited for: 16 -> 13; matrix products, arithmetic and copies ran while one was open for 2% -> 4% of each run, Pallas kernels for 20% -> 20%
where the time goes in v9:
time: 323 us; the launch traced here: 320 us
  waiting for transfers between devices  176 us (54%)
  Pallas kernels  90.6 us (28%)
  starting transfers between devices  22.3 us (7%)
  between operations  14.2 us (4%)
  other arithmetic  12 us (4%)
  local copies, waits for them, and re-layouts  4.38 us (1%)
    ppermute x6, waiting for transfers between devices, ring_shards(): lax.ppermute(up, 'batch', ahead)  86.9 us
    pallas_call x5, Pallas kernels, attend(): pl.pallas_call(functools.partial(attend_kernel, count, begins, ends), gri...  76.7 us
    all_gather x1, waiting for transfers between devices, statistics(): sums = jnp.sum(lax.all_gather(sums, 'batch', axis=0), axis=0) / samples  39.5 us
    all_gather x1, waiting for transfers between devices, summed(): lax.all_gather(jnp.stack(rows_of_sums), 'batch', axis=0)  21.8 us
    ppermute x1, waiting for transfers between devices, ring_shards(): last_one = lax.ppermute(ends[0][0], 'batch', ahead)  15.7 us
    ppermute x6, starting transfers between devices, ring_shards(): lax.ppermute(up, 'batch', ahead)  9.83 us
    ppermute x10, starting transfers between devices, swapped(): return lax.ppermute(value, 'batch', [(i, i ^ bit) for i in range(batches)])  9.74 us
    pallas_call x1, Pallas kernels, finish_grads(): pl.pallas_call(functools.partial(finish_kernel, samples, width), grid=(ti...  8.13 us
  transfers between devices with their start and end apart: 26, of which 13 were waited for; matrix products, arithmetic and copies ran while one was open for 4% of the time, Pallas kernels for 20%

profile of v9, /device:TPU:1, one launch (start us, length us, event | category | flops | bytes accessed | tf_op | source)
XLA Modules:
  0.0 319.8 jit_solution(13769052674230420695)
XLA Ops:
  7.2 4.0 %first_sums.1 = f32[4,4096]{1,0:T(4,128)} custom-call(bf16[192,4096]{1,0:T(8,128)(2,1)} %refs_3_.1, bf16[192,4096]{1,0:T(8,128)(2,1)} %refs_4_.1), custom_call_target="tpu_custom_call" | custom-call | flops 4096 | bytes 4096 | tf_op jit(solution)/shard_map/first_sums/pallas_call | solution.py:128
  11.5 2.7 collective-permute-start
  15.7 39.5 %all-gather.7.cloned.1.call-done = f32[16,4,4096]{2,1,0:T(4,128)} async-done(((f32[1,4,4096]{2,1,0:T(4,128)}), f32[16,4,4096]{2,1,0:T(4,128)}) %all-gather.7.cloned.1.call-update) | async-done | bytes 1048592 | tf_op jit(solution)/shard_map/all_gather | solution.py:354
  58.6 29.3 %collective-permute-done.4.refs_5_ = bf16[192,4096]{1,0:T(8,128)(2,1)} collective-permute-done((bf16[192,4096]{1,0:T(8,128)(2,1)S(1)}, bf16[192,4096]{1,0:T(8,128)(2,1)}, u32[]{:S(2)}, u32[]{:S(2)}) %collective-permute-start.4) | collective-permute-done | bytes 1572896 | tf_op jit(solution)/shard_map/ppermute | solution.py:385
  88.0 2.3 collective-permute-start.5
  90.3 3.9 %multiply_convert_fusion.refs_1_.norm_two = bf16[384,4096]{1,0:T(8,128)(2,1)} fusion(bf16[192,4096]{1,0:T(8,128)(2,1)} %collective-permute-done.9, bf16[192,4096]{1,0:T(8,128)(2,1)S(1)} %copy-done.3, f32[4096]{0:T(1024)S(1)} %bitcast.15, f32[4096]{0:T(1024)S(1)} %bitcast.14), kind=kLoop, calls=%fused_computation | loop fusion | flops 11010048 | bytes 6324224 | tf_op jit(solution)/shard_map/convert_element_type | solution.py:361
  94.9 2.5 multiply_convert_fusion.1.refs_0_.norm_one
  98.0 11.6 %attend.5 = (f32[8,128]{1,0:T(8,128)}, f32[384,4096]{1,0:T(8,128)}, f32[384,4096]{1,0:T(8,128)}) custom-call(bf16[384,4096]{1,0:T(8,128)(2,1)} %multiply_convert_fusion.1.refs_0_.norm_one, bf16[384,4096]{1,0:T(8,128)(2,1)} %multiply_convert_fusion.refs_1_.norm_two, f32[4,4096]{1,0:T(4,128)} %pad_maximum_fusion.refs_2_.stat_ref, ...), custom_call_target="tpu_custom_call", output_to_operand_aliasing={{0}: (5, {})} | custom-call | flops 4096 | bytes 4096 | tf_op jit(solution)/shard_map/attend/pallas_call | solution.py:244
  109.6 17.9 %attend.6 = (f32[8,128]{1,0:T(8,128)}, f32[384,4096]{1,0:T(8,128)}, f32[384,4096]{1,0:T(8,128)}) custom-call(bf16[384,4096]{1,0:T(8,128)(2,1)} %multiply_convert_fusion.1.refs_0_.norm_one, bf16[384,4096]{1,0:T(8,128)(2,1)} %multiply_convert_fusion.refs_1_.norm_two, ...), custom_call_target="tpu_custom_call", output_to_operand_aliasing={{0}: (7, {}), {1}: (8, {}), {2}: (9, {})} | custom-call | flops 4096 | bytes 4096 | tf_op jit(solution)/shard_map/attend/pallas_call | solution.py:244
  127.5 28.0 %collective-permute-done.5.refs_5_ = bf16[192,4096]{1,0:T(8,128)(2,1)} collective-permute-done((bf16[192,4096]{1,0:T(8,128)(2,1)}, bf16[192,4096]{1,0:T(8,128)(2,1)}, u32[]{:S(2)}, u32[]{:S(2)}) %collective-permute-start.5) | collective-permute-done | bytes 1572896 | tf_op jit(solution)/shard_map/ppermute | solution.py:385
  155.5 1.9 collective-permute-done.7.refs_6_
  161.8 17.7 %attend.7 = (f32[8,128]{1,0:T(8,128)}, f32[384,4096]{1,0:T(8,128)}, f32[384,4096]{1,0:T(8,128)}) custom-call(bf16[384,4096]{1,0:T(8,128)(2,1)} %multiply_convert_fusion.1.refs_0_.norm_one, bf16[384,4096]{1,0:T(8,128)(2,1)} %multiply_convert_fusion.refs_1_.norm_two, ...), custom_call_target="tpu_custom_call", output_to_operand_aliasing={{0}: (7, {}), {1}: (8, {}), {2}: (9, {})} | custom-call | flops 4096 | bytes 4096 | tf_op jit(solution)/shard_map/attend/pallas_call | solution.py:244
  179.5 21.8 %all-gather.9.cloned.1.call-done = f32[16,4,4096]{2,1,0:T(4,128)} async-done(((f32[1,4,4096]{2,1,0:T(4,128)}), f32[16,4,4096]{2,1,0:T(4,128)}) %all-gather.9.cloned.1.call-update) | async-done | bytes 1048592 | tf_op jit(solution)/shard_map/all_gather | solution.py:350
  201.4 2.0 reduce_sum.49.norm_ref
  203.4 29.6 %collective-permute-done.12.refs_5_ = bf16[192,4096]{1,0:T(8,128)(2,1)} collective-permute-done((bf16[192,4096]{1,0:T(8,128)(2,1)}, bf16[192,4096]{1,0:T(8,128)(2,1)}, u32[]{:S(2)}, u32[]{:S(2)}) %collective-permute-start.12) | collective-permute-done | bytes 1572896 | tf_op jit(solution)/shard_map/ppermute | solution.py:385
  233.0 1.8 collective-permute-done.13.refs_6_
  236.3 16.4 %attend.8 = (f32[8,128]{1,0:T(8,128)}, bf16[384,4096]{1,0:T(8,128)(2,1)}, bf16[384,4096]{1,0:T(8,128)(2,1)}) custom-call(bf16[384,4096]{1,0:T(8,128)(2,1)} %multiply_convert_fusion.1.refs_0_.norm_one, bf16[384,4096]{1,0:T(8,128)(2,1)} %multiply_convert_fusion.refs_1_.norm_two, ...), custom_call_target="tpu_custom_call", output_to_operand_aliasing={{0}: (7, {})} | custom-call | flops 4096 | bytes 4096 | tf_op jit(solution)/shard_map/attend/pallas_call | solution.py:244
  252.6 15.7 %collective-permute-done.14.refs_3_ = bf16[192,4096]{1,0:T(8,128)(2,1)S(1)} collective-permute-done((bf16[192,4096]{1,0:T(8,128)(2,1)S(1)}, bf16[192,4096]{1,0:T(8,128)(2,1)S(1)}, u32[]{:S(2)}, u32[]{:S(2)}) %collective-permute-start.14) | collective-permute-done | bytes 1572896 | tf_op jit(solution)/shard_map/ppermute | solution.py:390
  270.7 13.2 %attend.9 = (f32[8,128]{1,0:T(8,128)}, bf16[192,4096]{1,0:T(8,128)(2,1)}, bf16[192,4096]{1,0:T(8,128)(2,1)}, bf16[192,4096]{1,0:T(8,128)(2,1)}, bf16[192,4096]{1,0:T(8,128)(2,1)}, /*index=5*/bf16[8,4096]{1,0:T(8,128)(2,1)}) custom-call(bf16[384,4096]{1,0:T(8,128)(2,1)} %multiply_convert_fusion.1.refs_0_.norm_one, ...), custom_call_target="tpu_custom_call", output_to_operand_aliasing={{0}: (5, {})} | custom-call | flops 4096 | bytes 4096 | tf_op jit(solution)/shard_map/attend/pallas_call | solution.py:244
  283.9 3.5 %collective-permute-start.16 = (bf16[192,4096]{1,0:T(8,128)(2,1)}, bf16[192,4096]{1,0:T(8,128)(2,1)S(1)}, u32[]{:S(2)}, u32[]{:S(2)}) collective-permute-start(bf16[192,4096]{1,0:T(8,128)(2,1)} %get-tuple-element.64), channel_id=1, source_target_pairs={{0,1},{1,0},{2,3},{3,2},{4,5},{5,4},{6,7},{7,6},{8,9},{9,8},{10,11... | collective-permute-start | bytes 4718600 | tf_op jit(solution)/shard_map/ppermute | solution.py:333
  289.6 3.4 %collective-permute-done.18.refs_1_ = bf16[8,4096]{1,0:T(8,128)(2,1)S(1)} collective-permute-done((bf16[8,4096]{1,0:T(8,128)(2,1)}, bf16[8,4096]{1,0:T(8,128)(2,1)S(1)}, u32[]{:S(2)}, u32[]{:S(2)}) %collective-permute-start.18) | collective-permute-done | bytes 65568 | tf_op jit(solution)/shard_map/ppermute | solution.py:333
  297.5 2.0 collective-permute-start.23
  299.5 2.4 collective-permute-done.22.rest_2_
  304.9 8.1 %finish.1 = (bf16[192,4096]{1,0:T(8,128)(2,1)}, bf16[192,4096]{1,0:T(8,128)(2,1)}, f32[1]{0:T(128)}) custom-call(bf16[192,4096]{1,0:T(8,128)(2,1)} %get-tuple-element.63.own_one, bf16[192,4096]{1,0:T(8,128)(2,1)} %copy-done.4, bf16[192,4096]{1,0:T(8,128)(2,1)} %get-tuple-element.65.own_two, bf16[192,4096]{1,0:T(8,128)(2,1)} %copy-done.5, ...), custom_call_target="tpu_custom_call" | custom-call | flops 4096 | bytes 4096 | tf_op jit(solution)/shard_map/finish/pallas_call | solution.py:305
  (81 shorter events, 24.3 us)
Async XLA Ops:
  7.2 48.1 %all-gather.7.cloned.1.call-start = ((), (), s32[]{:S(2)}) async-start(), calls=%async_computation | async-start | bytes 1114112 | tf_op jit(solution)/shard_map/all_gather | solution.py:354
  11.3 190.1 %all-gather.9.cloned.1.call-start = ((), (), s32[]{:S(2)}) async-start(), calls=%async_computation.1 | async-start | bytes 1114112 | tf_op jit(solution)/shard_map/all_gather | solution.py:350
  11.3 45.4 %collective-permute-start.9 = (bf16[192,4096]{1,0:T(8,128)(2,1)S(1)}, bf16[192,4096]{1,0:T(8,128)(2,1)}, u32[]{:S(2)}, u32[]{:S(2)}) collective-permute-start(bf16[192,4096]{1,0:T(8,128)(2,1)S(1)} %copy-done.3), channel_id=1, source_target_pairs={{0,1},{1,0},{2,3},{3,2},{4,5},{5,4},{6,7},{7,6},{8,9},{9,8},{10,11... | collective-permute-start | bytes 4718600 | tf_op jit(solution)/shard_map/ppermute | solution.py:333
  11.5 45.6 %collective-permute-start = (bf16[192,4096]{1,0:T(8,128)(2,1)S(1)}, bf16[192,4096]{1,0:T(8,128)(2,1)}, u32[]{:S(2)}, u32[]{:S(2)}) collective-permute-start(bf16[192,4096]{1,0:T(8,128)(2,1)S(1)} %copy-done.2), channel_id=1, source_target_pairs={{0,4},{1,5},{4,8},{5,9},{8,12},{9,13},{12,14},{13,15},{14,10},{15,... | collective-permute-start | bytes 4718600 | tf_op jit(solution)/shard_map/ppermute | solution.py:385
  14.2 43.6 %collective-permute-start.2 = (bf16[192,4096]{1,0:T(8,128)(2,1)S(1)}, bf16[192,4096]{1,0:T(8,128)(2,1)}, u32[]{:S(2)}, u32[]{:S(2)}) collective-permute-start(bf16[192,4096]{1,0:T(8,128)(2,1)S(1)} %copy-done.2), channel_id=1, source_target_pairs={{4,0},{5,1},{8,4},{9,5},{12,8},{13,9},{14,12},{15,13},{10,14},{11,... | collective-permute-start | bytes 4718600 | tf_op jit(solution)/shard_map/ppermute | solution.py:385
  14.2 73.8 %collective-permute-start.4 = (bf16[192,4096]{1,0:T(8,128)(2,1)S(1)}, bf16[192,4096]{1,0:T(8,128)(2,1)}, u32[]{:S(2)}, u32[]{:S(2)}) collective-permute-start(bf16[192,4096]{1,0:T(8,128)(2,1)S(1)} %copy-done.3), channel_id=1, source_target_pairs={{0,4},{1,5},{4,8},{5,9},{8,12},{9,13},{12,14},{13,15},{14,10},{15,... | collective-permute-start | bytes 4718600 | tf_op jit(solution)/shard_map/ppermute | solution.py:385
  15.7 74.6 %collective-permute-start.6 = (bf16[192,4096]{1,0:T(8,128)(2,1)S(1)}, bf16[192,4096]{1,0:T(8,128)(2,1)}, u32[]{:S(2)}, u32[]{:S(2)}) collective-permute-start(bf16[192,4096]{1,0:T(8,128)(2,1)S(1)} %copy-done.3), channel_id=1, source_target_pairs={{4,0},{5,1},{8,4},{9,5},{12,8},{13,9},{14,12},{15,13},{10,14},{11,... | collective-permute-start | bytes 4718600 | tf_op jit(solution)/shard_map/ppermute | solution.py:385
  56.7 38.2 %collective-permute-start.8 = (bf16[192,4096]{1,0:T(8,128)(2,1)S(1)}, bf16[192,4096]{1,0:T(8,128)(2,1)S(1)}, u32[]{:S(2)}, u32[]{:S(2)}) collective-permute-start(bf16[192,4096]{1,0:T(8,128)(2,1)S(1)} %copy-done.2), channel_id=1, source_target_pairs={{0,1},{1,0},{2,3},{3,2},{4,5},{5,4},{6,7},{7,6},{8,9},{9,8},{10,11... | collective-permute-start | bytes 4718600 | tf_op jit(solution)/shard_map/ppermute | solution.py:333
  57.1 70.4 %collective-permute-start.1 = (bf16[192,4096]{1,0:T(8,128)(2,1)}, bf16[192,4096]{1,0:T(8,128)(2,1)}, u32[]{:S(2)}, u32[]{:S(2)}) collective-permute-start(bf16[192,4096]{1,0:T(8,128)(2,1)} %collective-permute-done.refs_3_), channel_id=1, source_target_pairs={{0,4},{1,5},{4,8},{5,9},{8,12},{9,13},{12,14},{13,15},{14,10},{15,... | collective-permute-start | bytes 4718600 | tf_op jit(solution)/shard_map/ppermute | solution.py:385
  57.8 69.7 %collective-permute-start.3 = (bf16[192,4096]{1,0:T(8,128)(2,1)}, bf16[192,4096]{1,0:T(8,128)(2,1)}, u32[]{:S(2)}, u32[]{:S(2)}) collective-permute-start(bf16[192,4096]{1,0:T(8,128)(2,1)} %collective-permute-done.2.refs_4_), channel_id=1, source_target_pairs={{4,0},{5,1},{8,4},{9,5},{12,8},{13,9},{14,12},{15,13},{10,14},{11,... | collective-permute-start | bytes 4718600 | tf_op jit(solution)/shard_map/ppermute | solution.py:385
  88.0 67.5 %collective-permute-start.5 = (bf16[192,4096]{1,0:T(8,128)(2,1)}, bf16[192,4096]{1,0:T(8,128)(2,1)}, u32[]{:S(2)}, u32[]{:S(2)}) collective-permute-start(bf16[192,4096]{1,0:T(8,128)(2,1)} %collective-permute-done.4.refs_5_), channel_id=1, source_target_pairs={{0,4},{1,5},{4,8},{5,9},{8,12},{9,13},{12,14},{13,15},{14,10},{15,... | collective-permute-start | bytes 4718600 | tf_op jit(solution)/shard_map/ppermute | solution.py:385
  90.3 67.1 %collective-permute-start.7 = (bf16[192,4096]{1,0:T(8,128)(2,1)}, bf16[192,4096]{1,0:T(8,128)(2,1)}, u32[]{:S(2)}, u32[]{:S(2)}) collective-permute-start(bf16[192,4096]{1,0:T(8,128)(2,1)} %collective-permute-done.6.refs_6_), channel_id=1, source_target_pairs={{4,0},{5,1},{8,4},{9,5},{12,8},{13,9},{14,12},{15,13},{10,14},{11,... | collective-permute-start | bytes 4718600 | tf_op jit(solution)/shard_map/ppermute | solution.py:385
  158.8 44.6 %collective-permute-start.10 = (bf16[192,4096]{1,0:T(8,128)(2,1)}, bf16[192,4096]{1,0:T(8,128)(2,1)S(1)}, u32[]{:S(2)}, u32[]{:S(2)}) collective-permute-start(bf16[192,4096]{1,0:T(8,128)(2,1)} %collective-permute-done.1.refs_3_), channel_id=1, source_target_pairs={{0,4},{1,5},{4,8},{5,9},{8,12},{9,13},{12,14},{13,15},{14,10},{15,... | collective-permute-start | bytes 4718600 | tf_op jit(solution)/shard_map/ppermute | solution.py:385
  160.2 43.2 %collective-permute-start.11 = (bf16[192,4096]{1,0:T(8,128)(2,1)}, bf16[192,4096]{1,0:T(8,128)(2,1)}, u32[]{:S(2)}, u32[]{:S(2)}) collective-permute-start(bf16[192,4096]{1,0:T(8,128)(2,1)} %collective-permute-done.3.refs_4_), channel_id=1, source_target_pairs={{4,0},{5,1},{8,4},{9,5},{12,8},{13,9},{14,12},{15,13},{10,14},{11,... | collective-permute-start | bytes 4718600 | tf_op jit(solution)/shard_map/ppermute | solution.py:385
  160.3 72.7 %collective-permute-start.12 = (bf16[192,4096]{1,0:T(8,128)(2,1)}, bf16[192,4096]{1,0:T(8,128)(2,1)}, u32[]{:S(2)}, u32[]{:S(2)}) collective-permute-start(bf16[192,4096]{1,0:T(8,128)(2,1)} %collective-permute-done.5.refs_5_), channel_id=1, source_target_pairs={{0,4},{1,5},{4,8},{5,9},{8,12},{9,13},{12,14},{13,15},{14,10},{15,... | collective-permute-start | bytes 4718600 | tf_op jit(solution)/shard_map/ppermute | solution.py:385
  161.6 73.2 %collective-permute-start.13 = (bf16[192,4096]{1,0:T(8,128)(2,1)}, bf16[192,4096]{1,0:T(8,128)(2,1)S(1)}, u32[]{:S(2)}, u32[]{:S(2)}) collective-permute-start(bf16[192,4096]{1,0:T(8,128)(2,1)} %collective-permute-done.7.refs_6_), channel_id=1, source_target_pairs={{4,0},{5,1},{8,4},{9,5},{12,8},{13,9},{14,12},{15,13},{10,14},{11,... | collective-permute-start | bytes 4718600 | tf_op jit(solution)/shard_map/ppermute | solution.py:385
  234.8 33.5 %collective-permute-start.14 = (bf16[192,4096]{1,0:T(8,128)(2,1)S(1)}, bf16[192,4096]{1,0:T(8,128)(2,1)S(1)}, u32[]{:S(2)}, u32[]{:S(2)}) collective-permute-start(bf16[192,4096]{1,0:T(8,128)(2,1)S(1)} %collective-permute-done.10.refs_3_), channel_id=1, source_target_pairs={{0,4},{1,5},{4,8},{5,9},{8,12},{9,13},{12,14},{13,15},{14,10},{15,... | collective-permute-start | bytes 4718600 | tf_op jit(solution)/shard_map/ppermute | solution.py:390
  236.2 33.3 %collective-permute-start.15 = (bf16[192,4096]{1,0:T(8,128)(2,1)S(1)}, bf16[192,4096]{1,0:T(8,128)(2,1)S(1)}, u32[]{:S(2)}, u32[]{:S(2)}) collective-permute-start(bf16[192,4096]{1,0:T(8,128)(2,1)S(1)} %collective-permute-done.13.refs_6_), channel_id=1, source_target_pairs={{4,0},{5,1},{8,4},{9,5},{12,8},{13,9},{14,12},{15,13},{10,14},{11,... | collective-permute-start | bytes 4718600 | tf_op jit(solution)/shard_map/ppermute | solution.py:391
  283.9 19.4 %collective-permute-start.16 = (bf16[192,4096]{1,0:T(8,128)(2,1)}, bf16[192,4096]{1,0:T(8,128)(2,1)S(1)}, u32[]{:S(2)}, u32[]{:S(2)}) collective-permute-start(bf16[192,4096]{1,0:T(8,128)(2,1)} %get-tuple-element.64), channel_id=1, source_target_pairs={{0,1},{1,0},{2,3},{3,2},{4,5},{5,4},{6,7},{7,6},{8,9},{9,8},{10,11... | collective-permute-start | bytes 4718600 | tf_op jit(solution)/shard_map/ppermute | solution.py:333
  287.4 15.8 %collective-permute-start.17 = (bf16[192,4096]{1,0:T(8,128)(2,1)}, bf16[192,4096]{1,0:T(8,128)(2,1)S(1)}, u32[]{:S(2)}, u32[]{:S(2)}) collective-permute-start(bf16[192,4096]{1,0:T(8,128)(2,1)} %get-tuple-element.66), channel_id=1, source_target_pairs={{0,1},{1,0},{2,3},{3,2},{4,5},{5,4},{6,7},{7,6},{8,9},{9,8},{10,11... | collective-permute-start | bytes 4718600 | tf_op jit(solution)/shard_map/ppermute | solution.py:333
  287.5 5.5 %collective-permute-start.18 = (bf16[8,4096]{1,0:T(8,128)(2,1)}, bf16[8,4096]{1,0:T(8,128)(2,1)S(1)}, u32[]{:S(2)}, u32[]{:S(2)}) collective-permute-start(bf16[8,4096]{1,0:T(8,128)(2,1)} %get-tuple-element.68.refs_0_), channel_id=1, source_target_pairs={{0,1},{1,0},{2,3},{3,2},{4,5},{5,4},{6,7},{7,6},{8,9},{9,8},{10,11... | collective-permute-start | bytes 196616 | tf_op jit(solution)/shard_map/ppermute | solution.py:333
  288.0 5.4 %collective-permute-start.20 = (bf16[8,4096]{1,0:T(8,128)(2,1)}, bf16[8,4096]{1,0:T(8,128)(2,1)S(1)}, u32[]{:S(2)}, u32[]{:S(2)}) collective-permute-start(bf16[8,4096]{1,0:T(8,128)(2,1)} %get-tuple-element.68.refs_0_), channel_id=1, source_target_pairs={{0,3},{1,2},{2,1},{3,0},{4,7},{5,6},{6,5},{7,4},{8,11},{9,10},{10,... | collective-permute-start | bytes 196616 | tf_op jit(solution)/shard_map/ppermute | solution.py:333
  296.6 5.3 %collective-permute-start.22 = (bf16[8,4096]{1,0:T(8,128)(2,1)}, bf16[8,4096]{1,0:T(8,128)(2,1)S(1)}, u32[]{:S(2)}, u32[]{:S(2)}) collective-permute-start(bf16[8,4096]{1,0:T(8,128)(2,1)} %add_totals.1.rest_0_), channel_id=1, source_target_pairs={{0,8},{1,9},{2,10},{3,11},{4,12},{5,13},{6,14},{7,15},{8,0},{9,1},... | collective-permute-start | bytes 196616 | tf_op jit(solution)/shard_map/ppermute | solution.py:333
  297.5 5.7 %collective-permute-start.23 = (bf16[8,4096]{1,0:T(8,128)(2,1)}, bf16[8,4096]{1,0:T(8,128)(2,1)S(1)}, u32[]{:S(2)}, u32[]{:S(2)}) collective-permute-start(bf16[8,4096]{1,0:T(8,128)(2,1)} %add_totals.1.rest_0_), channel_id=1, source_target_pairs={{0,12},{1,13},{2,14},{3,15},{4,8},{5,9},{6,10},{7,11},{8,4},{9,5},... | collective-permute-start | bytes 196616 | tf_op jit(solution)/shard_map/ppermute | solution.py:333
  (18 other events, 159.8 us)
Sparse Core Ops, SparseCore 0:
  11.4 43.8 all-gather.6
  158.9 42.3 all-gather.8

commit v10 on v9

--- a/solution.py
+++ b/solution.py
@@ -9,7 +9,7 @@
 
 off_weight = 0.0051
 tiles = 4
-vmem = 56 * 1024 * 1024
+vmem = 36 * 1024 * 1024
 
 
 def local_term(columns, full_two):
@@ -122,14 +122,9 @@
 
 
 def first_sums(one, two):
-    rows, width = one.shape
-    lanes = width // tiles
-    place = lambda step: (0, step)
+    width = one.shape[1]
     return pl.pallas_call(
         sums_kernel,
-        grid=(tiles,),
-        in_specs=[pl.BlockSpec((rows, lanes), place)] * 2,
-        out_specs=pl.BlockSpec((4, lanes), place),
         out_shape=jax.ShapeDtypeStruct((4, width), jnp.float32),
         cost_estimate=pl.CostEstimate(flops=width, bytes_accessed=width, transcendentals=0),
         name="first_sums",

time: 323 us -> 325 us (level)
  local copies, waits for them, and re-layouts: 4.38 us -> 24.4 us
  Pallas kernels: 90.6 us -> 79.1 us
  waiting for transfers between devices: 176 us -> 172 us
    unnamed x32 -> x58, local copies, waits for them, and re-layouts: 3.71 us -> 24.4 us
    pallas_call x5, Pallas kernels: 76.7 us -> 66.9 us  [attend(): pl.pallas_call(functools.partial(attend_kernel, count, begins, ends), gri...]
    all_gather x1, waiting for transfers between devices: 21.8 us -> 16 us  [summed(): lax.all_gather(jnp.stack(rows_of_sums), 'batch', axis=0)]
    ppermute x6, waiting for transfers between devices: 86.9 us -> 90.2 us  [ring_shards(): lax.ppermute(up, 'batch', ahead)]
  transfers between devices with their start and end apart: 26 -> 26, of which waited for: 13 -> 13; matrix products, arithmetic and copies ran while one was open for 4% -> 3% of each run, Pallas kernels for 20% -> 18%
where the time goes in v10:
time: 325 us; the launch traced here: 322 us
  waiting for transfers between devices  172 us (53%)
  Pallas kernels  79.1 us (24%)
  local copies, waits for them, and re-layouts  24.4 us (8%)
  starting transfers between devices  22.3 us (7%)
  between operations  14.3 us (4%)
  other arithmetic  10.3 us (3%)
    ppermute x6, waiting for transfers between devices, ring_shards(): lax.ppermute(up, 'batch', ahead)  90.2 us
    pallas_call x5, Pallas kernels, attend(): pl.pallas_call(functools.partial(attend_kernel, count, begins, ends), gri...  66.9 us
    all_gather x1, waiting for transfers between devices, statistics(): sums = jnp.sum(lax.all_gather(sums, 'batch', axis=0), axis=0) / samples  39.6 us
    unnamed x58, local copies, waits for them, and re-layouts  24.4 us
    all_gather x1, waiting for transfers between devices, summed(): lax.all_gather(jnp.stack(rows_of_sums), 'batch', axis=0)  16 us
    ppermute x1, waiting for transfers between devices, ring_shards(): last_one = lax.ppermute(ends[0][0], 'batch', ahead)  13 us
    ppermute x6, starting transfers between devices, ring_shards(): lax.ppermute(up, 'batch', ahead)  9.83 us
    ppermute x10, starting transfers between devices, swapped(): return lax.ppermute(value, 'batch', [(i, i ^ bit) for i in range(batches)])  9.71 us
  transfers between devices with their start and end apart: 26, of which 13 were waited for; matrix products, arithmetic and copies ran while one was open for 3% of the time, Pallas kernels for 18%

profile of v10, /device:TPU:1, one launch (start us, length us, event | category | flops | bytes accessed | tf_op | source)
XLA Modules:
  0.0 322.2 jit_solution(15867351559389347801)
XLA Ops:
  7.2 3.3 %first_sums.1 = f32[4,4096]{1,0:T(4,128)} custom-call(bf16[192,4096]{1,0:T(8,128)(2,1)} %refs_3_.1, bf16[192,4096]{1,0:T(8,128)(2,1)} %refs_4_.1), custom_call_target="tpu_custom_call" | custom-call | flops 4096 | bytes 4096 | tf_op jit(solution)/shard_map/first_sums/pallas_call | solution.py:126
  10.7 2.7 collective-permute-start
  15.0 39.6 %all-gather.7.cloned.1.call-done = f32[16,4,4096]{2,1,0:T(4,128)} async-done(((f32[1,4,4096]{2,1,0:T(4,128)}), f32[16,4,4096]{2,1,0:T(4,128)}) %all-gather.7.cloned.1.call-update) | async-done | bytes 1048592 | tf_op jit(solution)/shard_map/all_gather | solution.py:349
  58.0 29.4 %collective-permute-done.4.refs_5_ = bf16[192,4096]{1,0:T(8,128)(2,1)} collective-permute-done((bf16[192,4096]{1,0:T(8,128)(2,1)S(1)}, bf16[192,4096]{1,0:T(8,128)(2,1)}, u32[]{:S(2)}, u32[]{:S(2)}) %collective-permute-start.4) | collective-permute-done | bytes 1572896 | tf_op jit(solution)/shard_map/ppermute | solution.py:380
  87.4 2.3 collective-permute-start.5
  89.8 2.7 multiply_convert_fusion.refs_1_.norm_two
  92.5 3.3 %multiply_convert_fusion.1.refs_0_.norm_one = bf16[384,4096]{1,0:T(8,128)(2,1)S(1)} fusion(bf16[192,4096]{1,0:T(8,128)(2,1)S(1)} %collective-permute-done.8, bf16[192,4096]{1,0:T(8,128)(2,1)} %refs_3_.1, f32[4096]{0:T(1024)S(1)} %bitcast.12, f32[4096]{0:T(1024)S(1)} %bitcast.13), kind=kLoop, calls=%fused_computation.1 | loop fusion | flops 11010048 | bytes 6324224 | tf_op jit(solution)/shard_map/convert_element_type | solution.py:356
  95.9 9.3 %attend.5 = (f32[8,128]{1,0:T(8,128)S(1)}, f32[384,4096]{1,0:T(8,128)S(1)}, f32[384,4096]{1,0:T(8,128)}) custom-call(bf16[384,4096]{1,0:T(8,128)(2,1)S(1)} %multiply_convert_fusion.1.refs_0_.norm_one, bf16[384,4096]{1,0:T(8,128)(2,1)S(1)} %multiply_convert_fusion.refs_1_.norm_two, ...), custom_call_target="tpu_custom_call", output_to_operand_aliasing={{0}: (5, {})} | custom-call | flops 4096 | bytes 4096 | tf_op jit(solution)/shard_map/attend/pallas_call | solution.py:239
  105.2 2.7 copy-done.6
  107.9 16.5 %attend.6 = (f32[8,128]{1,0:T(8,128)S(1)}, f32[384,4096]{1,0:T(8,128)}, f32[384,4096]{1,0:T(8,128)}) custom-call(bf16[384,4096]{1,0:T(8,128)(2,1)S(1)} %multiply_convert_fusion.1.refs_0_.norm_one, bf16[384,4096]{1,0:T(8,128)(2,1)S(1)} %multiply_convert_fusion.refs_1_.norm_two, ...), custom_call_target="tpu_custom_call", output_to_operand_aliasing={{0}: (7, {}), {1}: (8, {}), {2}: (9, {})} | custom-call | flops 4096 | bytes 4096 | tf_op jit(solution)/shard_map/attend/pallas_call | solution.py:239
  124.4 30.5 %collective-permute-done.5.refs_5_ = bf16[192,4096]{1,0:T(8,128)(2,1)S(1)} collective-permute-done((bf16[192,4096]{1,0:T(8,128)(2,1)}, bf16[192,4096]{1,0:T(8,128)(2,1)S(1)}, u32[]{:S(2)}, u32[]{:S(2)}) %collective-permute-start.5) | collective-permute-done | bytes 1572896 | tf_op jit(solution)/shard_map/ppermute | solution.py:380
  161.6 1.9 copy-done.3
  169.1 16.0 %attend.7 = (f32[8,128]{1,0:T(8,128)S(1)}, f32[384,4096]{1,0:T(8,128)}, f32[384,4096]{1,0:T(8,128)}) custom-call(bf16[384,4096]{1,0:T(8,128)(2,1)S(1)} %copy-done.3, bf16[384,4096]{1,0:T(8,128)(2,1)S(1)} %multiply_convert_fusion.refs_1_.norm_two, ...), custom_call_target="tpu_custom_call", output_to_operand_aliasing={{0}: (7, {}), {1}: (8, {}), {2}: (9, {})} | custom-call | flops 4096 | bytes 4096 | tf_op jit(solution)/shard_map/attend/pallas_call | solution.py:239
  185.1 16.0 %all-gather.9.cloned.1.call-done = f32[16,4,4096]{2,1,0:T(4,128)} async-done(((f32[1,4,4096]{2,1,0:T(4,128)}), f32[16,4,4096]{2,1,0:T(4,128)}) %all-gather.9.cloned.1.call-update) | async-done | bytes 1048592 | tf_op jit(solution)/shard_map/all_gather | solution.py:345
  202.6 30.2 %collective-permute-done.12.refs_5_ = bf16[192,4096]{1,0:T(8,128)(2,1)} collective-permute-done((bf16[192,4096]{1,0:T(8,128)(2,1)}, bf16[192,4096]{1,0:T(8,128)(2,1)}, u32[]{:S(2)}, u32[]{:S(2)}) %collective-permute-start.12) | collective-permute-done | bytes 1572896 | tf_op jit(solution)/shard_map/ppermute | solution.py:380
  232.8 1.9 collective-permute-done.13.refs_6_
  236.2 1.9 copy-done.4
  238.1 14.0 %attend.8 = (f32[8,128]{1,0:T(8,128)S(1)}, bf16[384,4096]{1,0:T(8,128)(2,1)S(1)}, bf16[384,4096]{1,0:T(8,128)(2,1)S(1)}) custom-call(bf16[384,4096]{1,0:T(8,128)(2,1)S(1)} %copy-done.4, bf16[384,4096]{1,0:T(8,128)(2,1)} %copy-done, f32[4,4096]{1,0:T(4,128)S(1)} %pad_maximum_fusion.refs_2_.stat_ref, ...), custom_call_target="tpu_custom_call", output_to_operand_aliasing={{0}: (7, {})} | custom-call | flops 4096 | bytes 4096 | tf_op jit(solution)/shard_map/attend/pallas_call | solution.py:239
  255.4 13.0 %collective-permute-done.14.refs_3_ = bf16[192,4096]{1,0:T(8,128)(2,1)S(1)} collective-permute-done((bf16[192,4096]{1,0:T(8,128)(2,1)}, bf16[192,4096]{1,0:T(8,128)(2,1)S(1)}, u32[]{:S(2)}, u32[]{:S(2)}) %collective-permute-start.14) | collective-permute-done | bytes 1572896 | tf_op jit(solution)/shard_map/ppermute | solution.py:385
  269.5 11.0 %attend.9 = (f32[8,128]{1,0:T(8,128)S(1)}, bf16[192,4096]{1,0:T(8,128)(2,1)S(1)}, bf16[192,4096]{1,0:T(8,128)(2,1)}, bf16[192,4096]{1,0:T(8,128)(2,1)S(1)}, bf16...) custom-call(bf16[384,4096]{1,0:T(8,128)(2,1)S(1)} %copy-done.4, ...), custom_call_target="tpu_custom_call", output_to_operand_aliasing={{0}: (5, {})} | custom-call | flops 4096 | bytes 4096 | tf_op jit(solution)/shard_map/attend/pallas_call | solution.py:239
  282.8 3.6 %collective-permute-start.16 = (bf16[192,4096]{1,0:T(8,128)(2,1)}, bf16[192,4096]{1,0:T(8,128)(2,1)}, u32[]{:S(2)}, u32[]{:S(2)}) collective-permute-start(bf16[192,4096]{1,0:T(8,128)(2,1)} %get-tuple-element.64), channel_id=1, source_target_pairs={{0,1},{1,0},{2,3},{3,2},{4,5},{5,4},{6,7},{7,6},{8,9},{9,8},{10,11... | collective-permute-start | bytes 4718600 | tf_op jit(solution)/shard_map/ppermute | solution.py:328
  298.0 4.6 %collective-permute-done.22.rest_2_ = bf16[8,4096]{1,0:T(8,128)(2,1)S(1)} collective-permute-done((bf16[8,4096]{1,0:T(8,128)(2,1)}, bf16[8,4096]{1,0:T(8,128)(2,1)S(1)}, u32[]{:S(2)}, u32[]{:S(2)}) %collective-permute-start.22) | collective-permute-done | bytes 65568 | tf_op jit(solution)/shard_map/ppermute | solution.py:328
  302.6 1.9 copy-done.5
  308.2 7.2 %finish.1 = (bf16[192,4096]{1,0:T(8,128)(2,1)}, bf16[192,4096]{1,0:T(8,128)(2,1)}, f32[1]{0:T(128)}) custom-call(bf16[192,4096]{1,0:T(8,128)(2,1)S(1)} %copy-done.12, bf16[192,4096]{1,0:T(8,128)(2,1)} %collective-permute-done.16.get_one, bf16[192,4096]{1,0:T(8,128)(2,1)S(1)} %copy-done.14, bf16[192,4096]{1,0:T(8,128)(2,1)} %collective-permute-done.17.get_two, ...), custom_call_target="tpu_custom_call" | custom-call | flops 4096 | bytes 4096 | tf_op jit(solution)/shard_map/finish/pallas_call | solution.py:300
  (107 shorter events, 42.2 us)
Async XLA Ops:
  7.2 47.5 %all-gather.7.cloned.1.call-start = ((), (), s32[]{:S(2)}) async-start(), calls=%async_computation | async-start | bytes 1114112 | tf_op jit(solution)/shard_map/all_gather | solution.py:349
  10.5 190.6 %all-gather.9.cloned.1.call-start = ((), (), s32[]{:S(2)}) async-start(), calls=%async_computation.1 | async-start | bytes 1114112 | tf_op jit(solution)/shard_map/all_gather | solution.py:345
  10.6 45.5 %collective-permute-start.9 = (bf16[192,4096]{1,0:T(8,128)(2,1)S(1)}, bf16[192,4096]{1,0:T(8,128)(2,1)S(1)}, u32[]{:S(2)}, u32[]{:S(2)}) collective-permute-start(bf16[192,4096]{1,0:T(8,128)(2,1)S(1)} %copy-done.7), channel_id=1, source_target_pairs={{0,1},{1,0},{2,3},{3,2},{4,5},{5,4},{6,7},{7,6},{8,9},{9,8},{10,11... | collective-permute-start | bytes 4718600 | tf_op jit(solution)/shard_map/ppermute | solution.py:328
  10.7 45.8 %collective-permute-start = (bf16[192,4096]{1,0:T(8,128)(2,1)}, bf16[192,4096]{1,0:T(8,128)(2,1)}, u32[]{:S(2)}, u32[]{:S(2)}) collective-permute-start(bf16[192,4096]{1,0:T(8,128)(2,1)} %refs_3_.1), channel_id=1, source_target_pairs={{0,4},{1,5},{4,8},{5,9},{8,12},{9,13},{12,14},{13,15},{14,10},{15,... | collective-permute-start | bytes 4718600 | tf_op jit(solution)/shard_map/ppermute | solution.py:380
  13.5 43.7 %collective-permute-start.2 = (bf16[192,4096]{1,0:T(8,128)(2,1)}, bf16[192,4096]{1,0:T(8,128)(2,1)}, u32[]{:S(2)}, u32[]{:S(2)}) collective-permute-start(bf16[192,4096]{1,0:T(8,128)(2,1)} %refs_3_.1), channel_id=1, source_target_pairs={{4,0},{5,1},{8,4},{9,5},{12,8},{13,9},{14,12},{15,13},{10,14},{11,... | collective-permute-start | bytes 4718600 | tf_op jit(solution)/shard_map/ppermute | solution.py:380
  13.5 74.0 %collective-permute-start.4 = (bf16[192,4096]{1,0:T(8,128)(2,1)S(1)}, bf16[192,4096]{1,0:T(8,128)(2,1)}, u32[]{:S(2)}, u32[]{:S(2)}) collective-permute-start(bf16[192,4096]{1,0:T(8,128)(2,1)S(1)} %copy-done.7), channel_id=1, source_target_pairs={{0,4},{1,5},{4,8},{5,9},{8,12},{9,13},{12,14},{13,15},{14,10},{15,... | collective-permute-start | bytes 4718600 | tf_op jit(solution)/shard_map/ppermute | solution.py:380
  14.9 74.8 %collective-permute-start.6 = (bf16[192,4096]{1,0:T(8,128)(2,1)S(1)}, bf16[192,4096]{1,0:T(8,128)(2,1)}, u32[]{:S(2)}, u32[]{:S(2)}) collective-permute-start(bf16[192,4096]{1,0:T(8,128)(2,1)S(1)} %copy-done.7), channel_id=1, source_target_pairs={{4,0},{5,1},{8,4},{9,5},{12,8},{13,9},{14,12},{15,13},{10,14},{11,... | collective-permute-start | bytes 4718600 | tf_op jit(solution)/shard_map/ppermute | solution.py:380
  56.1 36.5 %collective-permute-start.8 = (bf16[192,4096]{1,0:T(8,128)(2,1)}, bf16[192,4096]{1,0:T(8,128)(2,1)S(1)}, u32[]{:S(2)}, u32[]{:S(2)}) collective-permute-start(bf16[192,4096]{1,0:T(8,128)(2,1)} %refs_3_.1), channel_id=1, source_target_pairs={{0,1},{1,0},{2,3},{3,2},{4,5},{5,4},{6,7},{7,6},{8,9},{9,8},{10,11... | collective-permute-start | bytes 4718600 | tf_op jit(solution)/shard_map/ppermute | solution.py:328
  56.5 67.9 %collective-permute-start.1 = (bf16[192,4096]{1,0:T(8,128)(2,1)}, bf16[192,4096]{1,0:T(8,128)(2,1)S(1)}, u32[]{:S(2)}, u32[]{:S(2)}) collective-permute-start(bf16[192,4096]{1,0:T(8,128)(2,1)} %collective-permute-done.refs_3_), channel_id=1, source_target_pairs={{0,4},{1,5},{4,8},{5,9},{8,12},{9,13},{12,14},{13,15},{14,10},{15,... | collective-permute-start | bytes 4718600 | tf_op jit(solution)/shard_map/ppermute | solution.py:380
  57.2 67.3 %collective-permute-start.3 = (bf16[192,4096]{1,0:T(8,128)(2,1)}, bf16[192,4096]{1,0:T(8,128)(2,1)S(1)}, u32[]{:S(2)}, u32[]{:S(2)}) collective-permute-start(bf16[192,4096]{1,0:T(8,128)(2,1)} %collective-permute-done.2.refs_4_), channel_id=1, source_target_pairs={{4,0},{5,1},{8,4},{9,5},{12,8},{13,9},{14,12},{15,13},{10,14},{11,... | collective-permute-start | bytes 4718600 | tf_op jit(solution)/shard_map/ppermute | solution.py:380
  87.4 67.5 %collective-permute-start.5 = (bf16[192,4096]{1,0:T(8,128)(2,1)}, bf16[192,4096]{1,0:T(8,128)(2,1)S(1)}, u32[]{:S(2)}, u32[]{:S(2)}) collective-permute-start(bf16[192,4096]{1,0:T(8,128)(2,1)} %collective-permute-done.4.refs_5_), channel_id=1, source_target_pairs={{0,4},{1,5},{4,8},{5,9},{8,12},{9,13},{12,14},{13,15},{14,10},{15,... | collective-permute-start | bytes 4718600 | tf_op jit(solution)/shard_map/ppermute | solution.py:380
  89.8 67.0 %collective-permute-start.7 = (bf16[192,4096]{1,0:T(8,128)(2,1)}, bf16[192,4096]{1,0:T(8,128)(2,1)S(1)}, u32[]{:S(2)}, u32[]{:S(2)}) collective-permute-start(bf16[192,4096]{1,0:T(8,128)(2,1)} %collective-permute-done.6.refs_6_), channel_id=1, source_target_pairs={{4,0},{5,1},{8,4},{9,5},{12,8},{13,9},{14,12},{15,13},{10,14},{11,... | collective-permute-start | bytes 4718600 | tf_op jit(solution)/shard_map/ppermute | solution.py:380
  158.6 44.0 %collective-permute-start.10 = (bf16[192,4096]{1,0:T(8,128)(2,1)}, bf16[192,4096]{1,0:T(8,128)(2,1)}, u32[]{:S(2)}, u32[]{:S(2)}) collective-permute-start(bf16[192,4096]{1,0:T(8,128)(2,1)} %copy-done.15), channel_id=1, source_target_pairs={{0,4},{1,5},{4,8},{5,9},{8,12},{9,13},{12,14},{13,15},{14,10},{15,... | collective-permute-start | bytes 4718600 | tf_op jit(solution)/shard_map/ppermute | solution.py:380
  159.9 42.6 %collective-permute-start.11 = (bf16[192,4096]{1,0:T(8,128)(2,1)}, bf16[192,4096]{1,0:T(8,128)(2,1)}, u32[]{:S(2)}, u32[]{:S(2)}) collective-permute-start(bf16[192,4096]{1,0:T(8,128)(2,1)} %copy-done.17), channel_id=1, source_target_pairs={{4,0},{5,1},{8,4},{9,5},{12,8},{13,9},{14,12},{15,13},{10,14},{11,... | collective-permute-start | bytes 4718600 | tf_op jit(solution)/shard_map/ppermute | solution.py:380
  160.1 72.7 %collective-permute-start.12 = (bf16[192,4096]{1,0:T(8,128)(2,1)}, bf16[192,4096]{1,0:T(8,128)(2,1)}, u32[]{:S(2)}, u32[]{:S(2)}) collective-permute-start(bf16[192,4096]{1,0:T(8,128)(2,1)} %copy-done.19), channel_id=1, source_target_pairs={{0,4},{1,5},{4,8},{5,9},{8,12},{9,13},{12,14},{13,15},{14,10},{15,... | collective-permute-start | bytes 4718600 | tf_op jit(solution)/shard_map/ppermute | solution.py:380
  161.4 73.3 %collective-permute-start.13 = (bf16[192,4096]{1,0:T(8,128)(2,1)}, bf16[192,4096]{1,0:T(8,128)(2,1)}, u32[]{:S(2)}, u32[]{:S(2)}) collective-permute-start(bf16[192,4096]{1,0:T(8,128)(2,1)} %copy-done.21), channel_id=1, source_target_pairs={{4,0},{5,1},{8,4},{9,5},{12,8},{13,9},{14,12},{15,13},{10,14},{11,... | collective-permute-start | bytes 4718600 | tf_op jit(solution)/shard_map/ppermute | solution.py:380
  234.7 33.7 %collective-permute-start.14 = (bf16[192,4096]{1,0:T(8,128)(2,1)}, bf16[192,4096]{1,0:T(8,128)(2,1)S(1)}, u32[]{:S(2)}, u32[]{:S(2)}) collective-permute-start(bf16[192,4096]{1,0:T(8,128)(2,1)} %collective-permute-done.10.refs_3_), channel_id=1, source_target_pairs={{0,4},{1,5},{4,8},{5,9},{8,12},{9,13},{12,14},{13,15},{14,10},{15,... | collective-permute-start | bytes 4718600 | tf_op jit(solution)/shard_map/ppermute | solution.py:385
  236.0 33.4 %collective-permute-start.15 = (bf16[192,4096]{1,0:T(8,128)(2,1)}, bf16[192,4096]{1,0:T(8,128)(2,1)S(1)}, u32[]{:S(2)}, u32[]{:S(2)}) collective-permute-start(bf16[192,4096]{1,0:T(8,128)(2,1)} %collective-permute-done.13.refs_6_), channel_id=1, source_target_pairs={{4,0},{5,1},{8,4},{9,5},{12,8},{13,9},{14,12},{15,13},{10,14},{11,... | collective-permute-start | bytes 4718600 | tf_op jit(solution)/shard_map/ppermute | solution.py:386
  282.8 19.8 %collective-permute-start.16 = (bf16[192,4096]{1,0:T(8,128)(2,1)}, bf16[192,4096]{1,0:T(8,128)(2,1)}, u32[]{:S(2)}, u32[]{:S(2)}) collective-permute-start(bf16[192,4096]{1,0:T(8,128)(2,1)} %get-tuple-element.64), channel_id=1, source_target_pairs={{0,1},{1,0},{2,3},{3,2},{4,5},{5,4},{6,7},{7,6},{8,9},{9,8},{10,11... | collective-permute-start | bytes 4718600 | tf_op jit(solution)/shard_map/ppermute | solution.py:328
  286.4 16.2 %collective-permute-start.17 = (bf16[192,4096]{1,0:T(8,128)(2,1)}, bf16[192,4096]{1,0:T(8,128)(2,1)}, u32[]{:S(2)}, u32[]{:S(2)}) collective-permute-start(bf16[192,4096]{1,0:T(8,128)(2,1)} %get-tuple-element.66), channel_id=1, source_target_pairs={{0,1},{1,0},{2,3},{3,2},{4,5},{5,4},{6,7},{7,6},{8,9},{9,8},{10,11... | collective-permute-start | bytes 4718600 | tf_op jit(solution)/shard_map/ppermute | solution.py:328
  286.9 3.7 %collective-permute-start.19 = (bf16[8,4096]{1,0:T(8,128)(2,1)S(1)}, bf16[8,4096]{1,0:T(8,128)(2,1)S(1)}, u32[]{:S(2)}, u32[]{:S(2)}) collective-permute-start(bf16[8,4096]{1,0:T(8,128)(2,1)S(1)} %get-tuple-element.68.refs_0_), channel_id=1, source_target_pairs={{0,2},{1,3},{2,0},{3,1},{4,6},{5,7},{6,4},{7,5},{8,10},{9,11},{10,... | collective-permute-start | bytes 196616 | tf_op jit(solution)/shard_map/ppermute | solution.py:328
  287.1 5.1 %collective-permute-start.20 = (bf16[8,4096]{1,0:T(8,128)(2,1)S(1)}, bf16[8,4096]{1,0:T(8,128)(2,1)S(1)}, u32[]{:S(2)}, u32[]{:S(2)}) collective-permute-start(bf16[8,4096]{1,0:T(8,128)(2,1)S(1)} %get-tuple-element.68.refs_0_), channel_id=1, source_target_pairs={{0,3},{1,2},{2,1},{3,0},{4,7},{5,6},{6,5},{7,4},{8,11},{9,10},{10,... | collective-permute-start | bytes 196616 | tf_op jit(solution)/shard_map/ppermute | solution.py:328
  295.6 7.0 %collective-permute-start.22 = (bf16[8,4096]{1,0:T(8,128)(2,1)}, bf16[8,4096]{1,0:T(8,128)(2,1)S(1)}, u32[]{:S(2)}, u32[]{:S(2)}) collective-permute-start(bf16[8,4096]{1,0:T(8,128)(2,1)} %add_totals.1.rest_0_), channel_id=1, source_target_pairs={{0,8},{1,9},{2,10},{3,11},{4,12},{5,13},{6,14},{7,15},{8,0},{9,1},... | collective-permute-start | bytes 196616 | tf_op jit(solution)/shard_map/ppermute | solution.py:328
  296.7 5.9 %collective-permute-start.23 = (bf16[8,4096]{1,0:T(8,128)(2,1)}, bf16[8,4096]{1,0:T(8,128)(2,1)S(1)}, u32[]{:S(2)}, u32[]{:S(2)}) collective-permute-start(bf16[8,4096]{1,0:T(8,128)(2,1)} %add_totals.1.rest_0_), channel_id=1, source_target_pairs={{0,12},{1,13},{2,14},{3,15},{4,8},{5,9},{6,10},{7,11},{8,4},{9,5},... | collective-permute-start | bytes 196616 | tf_op jit(solution)/shard_map/ppermute | solution.py:328
  (31 other events, 315.6 us)
Sparse Core Ops, SparseCore 0:
  10.7 43.8 all-gather.6
  158.7 42.3 all-gather.8

commit v11 on v10

--- a/solution.py
+++ b/solution.py
@@ -9,7 +9,8 @@
 
 off_weight = 0.0051
 tiles = 4
-vmem = 36 * 1024 * 1024
+vmem = 56 * 1024 * 1024
+strip = 16
 
 
 def local_term(columns, full_two):
@@ -146,7 +147,8 @@
     acc_in = None if begins else (rest.pop(0), rest.pop(0))
     late = rest[-8:-6] if ends else ()
     held_one, held_two, gram_one, gram_two, round_one, round_two = rest[-6:]
-    loss_out, *outs = rest[: -8 if ends else -6]
+    fresh = rest[-9] if ends else None
+    loss_out, *outs = rest[: -9 if ends else -6]
     step = pl.program_id(0)
     tile = lax.rem(step, tiles)
 
@@ -186,18 +188,28 @@
     def _():
         sums = []
         for index, (gram, held) in enumerate(((round_two, held_one), (round_one, held_two))):
-            total = jnp.dot(gram[...], held[tile], preferred_element_type=jnp.float32)
-            if not begins:
-                total += acc_in[index][...].astype(jnp.float32)
-            if ends:
-                share = total.shape[0] // 2
-                outs[2 * index][...] = total[:share].astype(jnp.bfloat16)
-                outs[2 * index + 1][...] = total[share:].astype(jnp.bfloat16)
-                prod = total * late[index][tile].astype(jnp.float32)
-                sums.append(jnp.sum(total, axis=0, keepdims=True))
-                sums.append(jnp.sum(prod, axis=0, keepdims=True))
-            else:
+            if not ends:
+                total = jnp.dot(gram[...], held[tile], preferred_element_type=jnp.float32)
+                if not begins:
+                    total += acc_in[index][...].astype(jnp.float32)
                 outs[index][...] = total.astype(outs[index].dtype)
+                continue
+            fresh[...] = jnp.dot(gram[...], held[tile], preferred_element_type=jnp.float32)
+            height, lanes = fresh.shape
+            share = height // 2
+            plain = jnp.zeros((8, lanes), jnp.float32)
+            prods = jnp.zeros((8, lanes), jnp.float32)
+            for start in range(0, height, strip):
+                rows = slice(start, start + strip)
+                total = fresh[rows, :] + acc_in[index][rows, :].astype(jnp.float32)
+                prod = total * late[index][tile, rows, :].astype(jnp.float32)
+                plain += jnp.sum(total.reshape(strip // 8, 8, lanes), axis=0)
+                prods += jnp.sum(prod.reshape(strip // 8, 8, lanes), axis=0)
+                place = start % share
+                out = outs[2 * index + start // share]
+                out[place : place + strip, :] = total.astype(jnp.bfloat16)
+            sums.append(jnp.sum(plain, axis=0, keepdims=True))
+            sums.append(jnp.sum(prods, axis=0, keepdims=True))
         if ends:
             outs[4][...] = eight_rows(sums, jnp.sum(loss_out[...]))
 
@@ -242,7 +254,8 @@
         in_specs=in_specs,
         out_specs=out_specs,
         out_shape=out_shape,
-        scratch_shapes=[pltpu.VMEM((tiles, rows, lanes), jnp.bfloat16)] * (2 if ends else 0)
+        scratch_shapes=[pltpu.VMEM((rows, lanes), jnp.float32)] * (1 if ends else 0)
+        + [pltpu.VMEM((tiles, rows, lanes), jnp.bfloat16)] * (2 if ends else 0)
         + [pltpu.VMEM((tiles, keys, lanes), jnp.bfloat16)] * 2
         + [pltpu.VMEM((rows, keys), jnp.float32)] * 2
         + [pltpu.VMEM((rows, keys), jnp.bfloat16)] * 2,
@@ -258,8 +271,6 @@
 ):
     outs = rest[-3:]
     scale = 2.0 * off_weight / samples
-    one = norm_one[...].astype(jnp.float32)
-    two = norm_two[...].astype(jnp.float32)
     mixed = norm_ref[2:3, :]
     total = added(rest[:-3])
     corr = mixed / samples
@@ -272,15 +283,21 @@
         outs[2][0] = squares * (off_weight / (samples * samples * full))
 
     outs[2][0] += part / full
-    for index, (own, get, mine, other, inv) in enumerate(
-        ((own_one, get_one, one, two, 1), (own_two, get_two, two, one, 3))
+    for index, (own, get, mine, other, inv_row) in enumerate(
+        ((own_one, get_one, norm_one, norm_two, 1), (own_two, get_two, norm_two, norm_one, 3))
     ):
-        back = scale * (own[...].astype(jnp.float32) + get[...].astype(jnp.float32)) + other * diag
+        inv = stat_ref[inv_row : inv_row + 1, :]
         sum_back = scale * total[2 * index : 2 * index + 1, :]
         sum_back += norm_ref[1 - index : 2 - index, :] * diag
         sum_prod = scale * total[2 * index + 1 : 2 * index + 2, :] + mixed * diag
-        grad = back - sum_back / samples - mine * (sum_prod / samples)
-        outs[index][...] = (stat_ref[inv : inv + 1, :] * grad).astype(jnp.bfloat16)
+        by_acc, by_other = inv * scale, inv * diag
+        minus, by_mine = inv * sum_back / samples, inv * sum_prod / samples
+        for start in range(0, own.shape[0], strip):
+            rows = slice(start, start + strip)
+            grad = by_acc * (own[rows, :].astype(jnp.float32) + get[rows, :].astype(jnp.float32))
+            grad += by_other * other[rows, :].astype(jnp.float32) - minus
+            grad -= by_mine * mine[rows, :].astype(jnp.float32)
+            outs[index][rows, :] = grad.astype(jnp.bfloat16)
 
 
 def add_totals(terms):

time: 325 us -> 321 us (0.988)
  local copies, waits for them, and re-layouts: 24.4 us -> 4.38 us
  Pallas kernels: 79.1 us -> 88.4 us
  waiting for transfers between devices: 172 us -> 176 us
    unnamed x58 -> x32, local copies, waits for them, and re-layouts: 24.4 us -> 3.71 us
    pallas_call x5, Pallas kernels: 66.9 us -> 76.7 us  [attend(): pl.pallas_call(functools.partial(attend_kernel, count, begins, ends), gri...]
    all_gather x1, waiting for transfers between devices: 16 us -> 21.8 us  [summed(): lax.all_gather(jnp.stack(rows_of_sums), 'batch', axis=0)]
    ppermute x6, waiting for transfers between devices: 90.2 us -> 86.9 us  [ring_shards(): lax.ppermute(up, 'batch', ahead)]
  transfers between devices with their start and end apart: 26 -> 26, of which waited for: 13 -> 13; matrix products, arithmetic and copies ran while one was open for 3% -> 4% of each run, Pallas kernels for 18% -> 21%
where the time goes in v11:
time: 321 us; the launch traced here: 318 us
  waiting for transfers between devices  176 us (55%)
  Pallas kernels  88.4 us (28%)
  starting transfers between devices  22.3 us (7%)
  between operations  14.2 us (4%)
  other arithmetic  12 us (4%)
  local copies, waits for them, and re-layouts  4.38 us (1%)
    ppermute x6, waiting for transfers between devices, ring_shards(): lax.ppermute(up, 'batch', ahead)  86.9 us
    pallas_call x5, Pallas kernels, attend(): pl.pallas_call(functools.partial(attend_kernel, count, begins, ends), gri...  76.7 us
    all_gather x1, waiting for transfers between devices, statistics(): sums = jnp.sum(lax.all_gather(sums, 'batch', axis=0), axis=0) / samples  39.6 us
    all_gather x1, waiting for transfers between devices, summed(): lax.all_gather(jnp.stack(rows_of_sums), 'batch', axis=0)  21.8 us
    ppermute x1, waiting for transfers between devices, ring_shards(): last_one = lax.ppermute(ends[0][0], 'batch', ahead)  15.7 us
    ppermute x6, starting transfers between devices, ring_shards(): lax.ppermute(up, 'batch', ahead)  9.83 us
    ppermute x10, starting transfers between devices, swapped(): return lax.ppermute(value, 'batch', [(i, i ^ bit) for i in range(batches)])  9.74 us
    ppermute x10, waiting for transfers between devices, swapped(): return lax.ppermute(value, 'batch', [(i, i ^ bit) for i in range(batches)])  7.42 us
  transfers between devices with their start and end apart: 26, of which 13 were waited for; matrix products, arithmetic and copies ran while one was open for 4% of the time, Pallas kernels for 21%

profile of v11, /device:TPU:1, one launch (start us, length us, event | category | flops | bytes accessed | tf_op | source)
XLA Modules:
  0.0 317.7 jit_solution(15856872034390797211)
XLA Ops:
  7.2 3.3 %first_sums.1 = f32[4,4096]{1,0:T(4,128)} custom-call(bf16[192,4096]{1,0:T(8,128)(2,1)} %refs_3_.1, bf16[192,4096]{1,0:T(8,128)(2,1)} %refs_4_.1), custom_call_target="tpu_custom_call" | custom-call | flops 4096 | bytes 4096 | tf_op jit(solution)/shard_map/first_sums/pallas_call | solution.py:127
  10.8 2.7 collective-permute-start
  15.1 39.6 %all-gather.7.cloned.1.call-done = f32[16,4,4096]{2,1,0:T(4,128)} async-done(((f32[1,4,4096]{2,1,0:T(4,128)}), f32[16,4,4096]{2,1,0:T(4,128)}) %all-gather.7.cloned.1.call-update) | async-done | bytes 1048592 | tf_op jit(solution)/shard_map/all_gather | solution.py:366
  58.0 29.3 %collective-permute-done.4.refs_5_ = bf16[192,4096]{1,0:T(8,128)(2,1)} collective-permute-done((bf16[192,4096]{1,0:T(8,128)(2,1)S(1)}, bf16[192,4096]{1,0:T(8,128)(2,1)}, u32[]{:S(2)}, u32[]{:S(2)}) %collective-permute-start.4) | collective-permute-done | bytes 1572896 | tf_op jit(solution)/shard_map/ppermute | solution.py:397
  87.3 2.3 collective-permute-start.5
  89.6 3.9 %multiply_convert_fusion.refs_1_.norm_two = bf16[384,4096]{1,0:T(8,128)(2,1)} fusion(bf16[192,4096]{1,0:T(8,128)(2,1)} %collective-permute-done.9, bf16[192,4096]{1,0:T(8,128)(2,1)S(1)} %copy-done.3, f32[4096]{0:T(1024)S(1)} %bitcast.15, f32[4096]{0:T(1024)S(1)} %bitcast.14), kind=kLoop, calls=%fused_computation | loop fusion | flops 11010048 | bytes 6324224 | tf_op jit(solution)/shard_map/convert_element_type | solution.py:373
  94.2 2.5 multiply_convert_fusion.1.refs_0_.norm_one
  97.3 11.6 %attend.5 = (f32[8,128]{1,0:T(8,128)}, f32[384,4096]{1,0:T(8,128)}, f32[384,4096]{1,0:T(8,128)}) custom-call(bf16[384,4096]{1,0:T(8,128)(2,1)} %multiply_convert_fusion.1.refs_0_.norm_one, bf16[384,4096]{1,0:T(8,128)(2,1)} %multiply_convert_fusion.refs_1_.norm_two, f32[4,4096]{1,0:T(4,128)} %pad_maximum_fusion.refs_2_.stat_ref, ...), custom_call_target="tpu_custom_call", output_to_operand_aliasing={{0}: (5, {})} | custom-call | flops 4096 | bytes 4096 | tf_op jit(solution)/shard_map/attend/pallas_call | solution.py:251
  108.9 17.9 %attend.6 = (f32[8,128]{1,0:T(8,128)}, f32[384,4096]{1,0:T(8,128)}, f32[384,4096]{1,0:T(8,128)}) custom-call(bf16[384,4096]{1,0:T(8,128)(2,1)} %multiply_convert_fusion.1.refs_0_.norm_one, bf16[384,4096]{1,0:T(8,128)(2,1)} %multiply_convert_fusion.refs_1_.norm_two, ...), custom_call_target="tpu_custom_call", output_to_operand_aliasing={{0}: (7, {}), {1}: (8, {}), {2}: (9, {})} | custom-call | flops 4096 | bytes 4096 | tf_op jit(solution)/shard_map/attend/pallas_call | solution.py:251
  126.8 28.0 %collective-permute-done.5.refs_5_ = bf16[192,4096]{1,0:T(8,128)(2,1)} collective-permute-done((bf16[192,4096]{1,0:T(8,128)(2,1)}, bf16[192,4096]{1,0:T(8,128)(2,1)}, u32[]{:S(2)}, u32[]{:S(2)}) %collective-permute-start.5) | collective-permute-done | bytes 1572896 | tf_op jit(solution)/shard_map/ppermute | solution.py:397
  154.8 1.9 collective-permute-done.7.refs_6_
  161.1 17.8 %attend.7 = (f32[8,128]{1,0:T(8,128)}, f32[384,4096]{1,0:T(8,128)}, f32[384,4096]{1,0:T(8,128)}) custom-call(bf16[384,4096]{1,0:T(8,128)(2,1)} %multiply_convert_fusion.1.refs_0_.norm_one, bf16[384,4096]{1,0:T(8,128)(2,1)} %multiply_convert_fusion.refs_1_.norm_two, ...), custom_call_target="tpu_custom_call", output_to_operand_aliasing={{0}: (7, {}), {1}: (8, {}), {2}: (9, {})} | custom-call | flops 4096 | bytes 4096 | tf_op jit(solution)/shard_map/attend/pallas_call | solution.py:251
  178.9 21.8 %all-gather.9.cloned.1.call-done = f32[16,4,4096]{2,1,0:T(4,128)} async-done(((f32[1,4,4096]{2,1,0:T(4,128)}), f32[16,4,4096]{2,1,0:T(4,128)}) %all-gather.9.cloned.1.call-update) | async-done | bytes 1048592 | tf_op jit(solution)/shard_map/all_gather | solution.py:362
  200.7 2.0 reduce_sum.49.norm_ref
  202.7 29.6 %collective-permute-done.12.refs_5_ = bf16[192,4096]{1,0:T(8,128)(2,1)} collective-permute-done((bf16[192,4096]{1,0:T(8,128)(2,1)}, bf16[192,4096]{1,0:T(8,128)(2,1)}, u32[]{:S(2)}, u32[]{:S(2)}) %collective-permute-start.12) | collective-permute-done | bytes 1572896 | tf_op jit(solution)/shard_map/ppermute | solution.py:397
  232.3 1.8 collective-permute-done.13.refs_6_
  235.6 16.4 %attend.8 = (f32[8,128]{1,0:T(8,128)}, bf16[384,4096]{1,0:T(8,128)(2,1)}, bf16[384,4096]{1,0:T(8,128)(2,1)}) custom-call(bf16[384,4096]{1,0:T(8,128)(2,1)} %multiply_convert_fusion.1.refs_0_.norm_one, bf16[384,4096]{1,0:T(8,128)(2,1)} %multiply_convert_fusion.refs_1_.norm_two, ...), custom_call_target="tpu_custom_call", output_to_operand_aliasing={{0}: (7, {})} | custom-call | flops 4096 | bytes 4096 | tf_op jit(solution)/shard_map/attend/pallas_call | solution.py:251
  252.0 15.7 %collective-permute-done.14.refs_3_ = bf16[192,4096]{1,0:T(8,128)(2,1)S(1)} collective-permute-done((bf16[192,4096]{1,0:T(8,128)(2,1)S(1)}, bf16[192,4096]{1,0:T(8,128)(2,1)S(1)}, u32[]{:S(2)}, u32[]{:S(2)}) %collective-permute-start.14) | collective-permute-done | bytes 1572896 | tf_op jit(solution)/shard_map/ppermute | solution.py:402
  270.0 13.2 %attend.9 = (f32[8,128]{1,0:T(8,128)}, bf16[192,4096]{1,0:T(8,128)(2,1)}, bf16[192,4096]{1,0:T(8,128)(2,1)}, bf16[192,4096]{1,0:T(8,128)(2,1)}, bf16[192,4096]{1,0:T(8,128)(2,1)}, /*index=5*/bf16[8,4096]{1,0:T(8,128)(2,1)}) custom-call(bf16[384,4096]{1,0:T(8,128)(2,1)} %multiply_convert_fusion.1.refs_0_.norm_one, ...), custom_call_target="tpu_custom_call", output_to_operand_aliasing={{0}: (5, {})} | custom-call | flops 4096 | bytes 4096 | tf_op jit(solution)/shard_map/attend/pallas_call | solution.py:251
  283.2 3.5 %collective-permute-start.16 = (bf16[192,4096]{1,0:T(8,128)(2,1)}, bf16[192,4096]{1,0:T(8,128)(2,1)S(1)}, u32[]{:S(2)}, u32[]{:S(2)}) collective-permute-start(bf16[192,4096]{1,0:T(8,128)(2,1)} %get-tuple-element.64), channel_id=1, source_target_pairs={{0,1},{1,0},{2,3},{3,2},{4,5},{5,4},{6,7},{7,6},{8,9},{9,8},{10,11... | collective-permute-start | bytes 4718600 | tf_op jit(solution)/shard_map/ppermute | solution.py:345
  288.9 3.4 %collective-permute-done.18.refs_1_ = bf16[8,4096]{1,0:T(8,128)(2,1)S(1)} collective-permute-done((bf16[8,4096]{1,0:T(8,128)(2,1)}, bf16[8,4096]{1,0:T(8,128)(2,1)S(1)}, u32[]{:S(2)}, u32[]{:S(2)}) %collective-permute-start.18) | collective-permute-done | bytes 65568 | tf_op jit(solution)/shard_map/ppermute | solution.py:345
  296.8 2.1 collective-permute-start.23
  298.9 2.4 collective-permute-done.22.rest_2_
  304.2 6.6 %finish.1 = (bf16[192,4096]{1,0:T(8,128)(2,1)}, bf16[192,4096]{1,0:T(8,128)(2,1)}, f32[1]{0:T(128)}) custom-call(bf16[192,4096]{1,0:T(8,128)(2,1)} %get-tuple-element.63.own_one, bf16[192,4096]{1,0:T(8,128)(2,1)} %copy-done.4, bf16[192,4096]{1,0:T(8,128)(2,1)} %get-tuple-element.65.own_two, bf16[192,4096]{1,0:T(8,128)(2,1)} %copy-done.5, ...), custom_call_target="tpu_custom_call" | custom-call | flops 4096 | bytes 4096 | tf_op jit(solution)/shard_map/finish/pallas_call | solution.py:317
  (81 shorter events, 24.3 us)
Async XLA Ops:
  7.2 47.5 %all-gather.7.cloned.1.call-start = ((), (), s32[]{:S(2)}) async-start(), calls=%async_computation | async-start | bytes 1114112 | tf_op jit(solution)/shard_map/all_gather | solution.py:366
  10.6 190.1 %all-gather.9.cloned.1.call-start = ((), (), s32[]{:S(2)}) async-start(), calls=%async_computation.1 | async-start | bytes 1114112 | tf_op jit(solution)/shard_map/all_gather | solution.py:362
  10.6 45.4 %collective-permute-start.9 = (bf16[192,4096]{1,0:T(8,128)(2,1)S(1)}, bf16[192,4096]{1,0:T(8,128)(2,1)}, u32[]{:S(2)}, u32[]{:S(2)}) collective-permute-start(bf16[192,4096]{1,0:T(8,128)(2,1)S(1)} %copy-done.3), channel_id=1, source_target_pairs={{0,1},{1,0},{2,3},{3,2},{4,5},{5,4},{6,7},{7,6},{8,9},{9,8},{10,11... | collective-permute-start | bytes 4718600 | tf_op jit(solution)/shard_map/ppermute | solution.py:345
  10.8 45.7 %collective-permute-start = (bf16[192,4096]{1,0:T(8,128)(2,1)S(1)}, bf16[192,4096]{1,0:T(8,128)(2,1)}, u32[]{:S(2)}, u32[]{:S(2)}) collective-permute-start(bf16[192,4096]{1,0:T(8,128)(2,1)S(1)} %copy-done.2), channel_id=1, source_target_pairs={{0,4},{1,5},{4,8},{5,9},{8,12},{9,13},{12,14},{13,15},{14,10},{15,... | collective-permute-start | bytes 4718600 | tf_op jit(solution)/shard_map/ppermute | solution.py:397
  13.5 43.6 %collective-permute-start.2 = (bf16[192,4096]{1,0:T(8,128)(2,1)S(1)}, bf16[192,4096]{1,0:T(8,128)(2,1)}, u32[]{:S(2)}, u32[]{:S(2)}) collective-permute-start(bf16[192,4096]{1,0:T(8,128)(2,1)S(1)} %copy-done.2), channel_id=1, source_target_pairs={{4,0},{5,1},{8,4},{9,5},{12,8},{13,9},{14,12},{15,13},{10,14},{11,... | collective-permute-start | bytes 4718600 | tf_op jit(solution)/shard_map/ppermute | solution.py:397
  13.5 73.8 %collective-permute-start.4 = (bf16[192,4096]{1,0:T(8,128)(2,1)S(1)}, bf16[192,4096]{1,0:T(8,128)(2,1)}, u32[]{:S(2)}, u32[]{:S(2)}) collective-permute-start(bf16[192,4096]{1,0:T(8,128)(2,1)S(1)} %copy-done.3), channel_id=1, source_target_pairs={{0,4},{1,5},{4,8},{5,9},{8,12},{9,13},{12,14},{13,15},{14,10},{15,... | collective-permute-start | bytes 4718600 | tf_op jit(solution)/shard_map/ppermute | solution.py:397
  15.0 74.6 %collective-permute-start.6 = (bf16[192,4096]{1,0:T(8,128)(2,1)S(1)}, bf16[192,4096]{1,0:T(8,128)(2,1)}, u32[]{:S(2)}, u32[]{:S(2)}) collective-permute-start(bf16[192,4096]{1,0:T(8,128)(2,1)S(1)} %copy-done.3), channel_id=1, source_target_pairs={{4,0},{5,1},{8,4},{9,5},{12,8},{13,9},{14,12},{15,13},{10,14},{11,... | collective-permute-start | bytes 4718600 | tf_op jit(solution)/shard_map/ppermute | solution.py:397
  56.1 38.1 %collective-permute-start.8 = (bf16[192,4096]{1,0:T(8,128)(2,1)S(1)}, bf16[192,4096]{1,0:T(8,128)(2,1)S(1)}, u32[]{:S(2)}, u32[]{:S(2)}) collective-permute-start(bf16[192,4096]{1,0:T(8,128)(2,1)S(1)} %copy-done.2), channel_id=1, source_target_pairs={{0,1},{1,0},{2,3},{3,2},{4,5},{5,4},{6,7},{7,6},{8,9},{9,8},{10,11... | collective-permute-start | bytes 4718600 | tf_op jit(solution)/shard_map/ppermute | solution.py:345
  56.5 70.3 %collective-permute-start.1 = (bf16[192,4096]{1,0:T(8,128)(2,1)}, bf16[192,4096]{1,0:T(8,128)(2,1)}, u32[]{:S(2)}, u32[]{:S(2)}) collective-permute-start(bf16[192,4096]{1,0:T(8,128)(2,1)} %collective-permute-done.refs_3_), channel_id=1, source_target_pairs={{0,4},{1,5},{4,8},{5,9},{8,12},{9,13},{12,14},{13,15},{14,10},{15,... | collective-permute-start | bytes 4718600 | tf_op jit(solution)/shard_map/ppermute | solution.py:397
  57.1 69.7 %collective-permute-start.3 = (bf16[192,4096]{1,0:T(8,128)(2,1)}, bf16[192,4096]{1,0:T(8,128)(2,1)}, u32[]{:S(2)}, u32[]{:S(2)}) collective-permute-start(bf16[192,4096]{1,0:T(8,128)(2,1)} %collective-permute-done.2.refs_4_), channel_id=1, source_target_pairs={{4,0},{5,1},{8,4},{9,5},{12,8},{13,9},{14,12},{15,13},{10,14},{11,... | collective-permute-start | bytes 4718600 | tf_op jit(solution)/shard_map/ppermute | solution.py:397
  87.3 67.5 %collective-permute-start.5 = (bf16[192,4096]{1,0:T(8,128)(2,1)}, bf16[192,4096]{1,0:T(8,128)(2,1)}, u32[]{:S(2)}, u32[]{:S(2)}) collective-permute-start(bf16[192,4096]{1,0:T(8,128)(2,1)} %collective-permute-done.4.refs_5_), channel_id=1, source_target_pairs={{0,4},{1,5},{4,8},{5,9},{8,12},{9,13},{12,14},{13,15},{14,10},{15,... | collective-permute-start | bytes 4718600 | tf_op jit(solution)/shard_map/ppermute | solution.py:397
  89.6 67.1 %collective-permute-start.7 = (bf16[192,4096]{1,0:T(8,128)(2,1)}, bf16[192,4096]{1,0:T(8,128)(2,1)}, u32[]{:S(2)}, u32[]{:S(2)}) collective-permute-start(bf16[192,4096]{1,0:T(8,128)(2,1)} %collective-permute-done.6.refs_6_), channel_id=1, source_target_pairs={{4,0},{5,1},{8,4},{9,5},{12,8},{13,9},{14,12},{15,13},{10,14},{11,... | collective-permute-start | bytes 4718600 | tf_op jit(solution)/shard_map/ppermute | solution.py:397
  158.1 44.6 %collective-permute-start.10 = (bf16[192,4096]{1,0:T(8,128)(2,1)}, bf16[192,4096]{1,0:T(8,128)(2,1)S(1)}, u32[]{:S(2)}, u32[]{:S(2)}) collective-permute-start(bf16[192,4096]{1,0:T(8,128)(2,1)} %collective-permute-done.1.refs_3_), channel_id=1, source_target_pairs={{0,4},{1,5},{4,8},{5,9},{8,12},{9,13},{12,14},{13,15},{14,10},{15,... | collective-permute-start | bytes 4718600 | tf_op jit(solution)/shard_map/ppermute | solution.py:397
  159.5 43.2 %collective-permute-start.11 = (bf16[192,4096]{1,0:T(8,128)(2,1)}, bf16[192,4096]{1,0:T(8,128)(2,1)}, u32[]{:S(2)}, u32[]{:S(2)}) collective-permute-start(bf16[192,4096]{1,0:T(8,128)(2,1)} %collective-permute-done.3.refs_4_), channel_id=1, source_target_pairs={{4,0},{5,1},{8,4},{9,5},{12,8},{13,9},{14,12},{15,13},{10,14},{11,... | collective-permute-start | bytes 4718600 | tf_op jit(solution)/shard_map/ppermute | solution.py:397
  159.6 72.7 %collective-permute-start.12 = (bf16[192,4096]{1,0:T(8,128)(2,1)}, bf16[192,4096]{1,0:T(8,128)(2,1)}, u32[]{:S(2)}, u32[]{:S(2)}) collective-permute-start(bf16[192,4096]{1,0:T(8,128)(2,1)} %collective-permute-done.5.refs_5_), channel_id=1, source_target_pairs={{0,4},{1,5},{4,8},{5,9},{8,12},{9,13},{12,14},{13,15},{14,10},{15,... | collective-permute-start | bytes 4718600 | tf_op jit(solution)/shard_map/ppermute | solution.py:397
  160.9 73.2 %collective-permute-start.13 = (bf16[192,4096]{1,0:T(8,128)(2,1)}, bf16[192,4096]{1,0:T(8,128)(2,1)S(1)}, u32[]{:S(2)}, u32[]{:S(2)}) collective-permute-start(bf16[192,4096]{1,0:T(8,128)(2,1)} %collective-permute-done.7.refs_6_), channel_id=1, source_target_pairs={{4,0},{5,1},{8,4},{9,5},{12,8},{13,9},{14,12},{15,13},{10,14},{11,... | collective-permute-start | bytes 4718600 | tf_op jit(solution)/shard_map/ppermute | solution.py:397
  234.1 33.5 %collective-permute-start.14 = (bf16[192,4096]{1,0:T(8,128)(2,1)S(1)}, bf16[192,4096]{1,0:T(8,128)(2,1)S(1)}, u32[]{:S(2)}, u32[]{:S(2)}) collective-permute-start(bf16[192,4096]{1,0:T(8,128)(2,1)S(1)} %collective-permute-done.10.refs_3_), channel_id=1, source_target_pairs={{0,4},{1,5},{4,8},{5,9},{8,12},{9,13},{12,14},{13,15},{14,10},{15,... | collective-permute-start | bytes 4718600 | tf_op jit(solution)/shard_map/ppermute | solution.py:402
  235.5 33.3 %collective-permute-start.15 = (bf16[192,4096]{1,0:T(8,128)(2,1)S(1)}, bf16[192,4096]{1,0:T(8,128)(2,1)S(1)}, u32[]{:S(2)}, u32[]{:S(2)}) collective-permute-start(bf16[192,4096]{1,0:T(8,128)(2,1)S(1)} %collective-permute-done.13.refs_6_), channel_id=1, source_target_pairs={{4,0},{5,1},{8,4},{9,5},{12,8},{13,9},{14,12},{15,13},{10,14},{11,... | collective-permute-start | bytes 4718600 | tf_op jit(solution)/shard_map/ppermute | solution.py:403
  283.2 19.4 %collective-permute-start.16 = (bf16[192,4096]{1,0:T(8,128)(2,1)}, bf16[192,4096]{1,0:T(8,128)(2,1)S(1)}, u32[]{:S(2)}, u32[]{:S(2)}) collective-permute-start(bf16[192,4096]{1,0:T(8,128)(2,1)} %get-tuple-element.64), channel_id=1, source_target_pairs={{0,1},{1,0},{2,3},{3,2},{4,5},{5,4},{6,7},{7,6},{8,9},{9,8},{10,11... | collective-permute-start | bytes 4718600 | tf_op jit(solution)/shard_map/ppermute | solution.py:345
  286.7 15.8 %collective-permute-start.17 = (bf16[192,4096]{1,0:T(8,128)(2,1)}, bf16[192,4096]{1,0:T(8,128)(2,1)S(1)}, u32[]{:S(2)}, u32[]{:S(2)}) collective-permute-start(bf16[192,4096]{1,0:T(8,128)(2,1)} %get-tuple-element.66), channel_id=1, source_target_pairs={{0,1},{1,0},{2,3},{3,2},{4,5},{5,4},{6,7},{7,6},{8,9},{9,8},{10,11... | collective-permute-start | bytes 4718600 | tf_op jit(solution)/shard_map/ppermute | solution.py:345
  286.8 5.5 %collective-permute-start.18 = (bf16[8,4096]{1,0:T(8,128)(2,1)}, bf16[8,4096]{1,0:T(8,128)(2,1)S(1)}, u32[]{:S(2)}, u32[]{:S(2)}) collective-permute-start(bf16[8,4096]{1,0:T(8,128)(2,1)} %get-tuple-element.68.refs_0_), channel_id=1, source_target_pairs={{0,1},{1,0},{2,3},{3,2},{4,5},{5,4},{6,7},{7,6},{8,9},{9,8},{10,11... | collective-permute-start | bytes 196616 | tf_op jit(solution)/shard_map/ppermute | solution.py:345
  287.3 5.4 %collective-permute-start.20 = (bf16[8,4096]{1,0:T(8,128)(2,1)}, bf16[8,4096]{1,0:T(8,128)(2,1)S(1)}, u32[]{:S(2)}, u32[]{:S(2)}) collective-permute-start(bf16[8,4096]{1,0:T(8,128)(2,1)} %get-tuple-element.68.refs_0_), channel_id=1, source_target_pairs={{0,3},{1,2},{2,1},{3,0},{4,7},{5,6},{6,5},{7,4},{8,11},{9,10},{10,... | collective-permute-start | bytes 196616 | tf_op jit(solution)/shard_map/ppermute | solution.py:345
  295.9 5.3 %collective-permute-start.22 = (bf16[8,4096]{1,0:T(8,128)(2,1)}, bf16[8,4096]{1,0:T(8,128)(2,1)S(1)}, u32[]{:S(2)}, u32[]{:S(2)}) collective-permute-start(bf16[8,4096]{1,0:T(8,128)(2,1)} %add_totals.1.rest_0_), channel_id=1, source_target_pairs={{0,8},{1,9},{2,10},{3,11},{4,12},{5,13},{6,14},{7,15},{8,0},{9,1},... | collective-permute-start | bytes 196616 | tf_op jit(solution)/shard_map/ppermute | solution.py:345
  296.8 5.7 %collective-permute-start.23 = (bf16[8,4096]{1,0:T(8,128)(2,1)}, bf16[8,4096]{1,0:T(8,128)(2,1)S(1)}, u32[]{:S(2)}, u32[]{:S(2)}) collective-permute-start(bf16[8,4096]{1,0:T(8,128)(2,1)} %add_totals.1.rest_0_), channel_id=1, source_target_pairs={{0,12},{1,13},{2,14},{3,15},{4,8},{5,9},{6,10},{7,11},{8,4},{9,5},... | collective-permute-start | bytes 196616 | tf_op jit(solution)/shard_map/ppermute | solution.py:345
  (18 other events, 158.4 us)
Sparse Core Ops, SparseCore 0:
  10.8 43.8 all-gather.6
  158.2 42.4 all-gather.8

commit v12 on v11

--- a/solution.py
+++ b/solution.py
@@ -116,10 +116,19 @@
 
 
 def sums_kernel(one_ref, two_ref, out_ref):
+    height, width = one_ref.shape
+    lanes = width // tiles
     for index, ref in enumerate((one_ref, two_ref)):
-        values = ref[...].astype(jnp.float32)
-        out_ref[2 * index : 2 * index + 1, :] = jnp.sum(values, axis=0, keepdims=True)
-        out_ref[2 * index + 1 : 2 * index + 2, :] = jnp.sum(values * values, axis=0, keepdims=True)
+        for left in range(0, width, lanes):
+            plain = jnp.zeros((8, lanes), jnp.float32)
+            squares = jnp.zeros((8, lanes), jnp.float32)
+            for start in range(0, height, strip):
+                values = ref[start : start + strip, left : left + lanes].astype(jnp.float32)
+                values = values.reshape(strip // 8, 8, lanes)
+                plain += jnp.sum(values, axis=0)
+                squares += jnp.sum(values * values, axis=0)
+            for row, value in ((2 * index, plain), (2 * index + 1, squares)):
+                out_ref[row : row + 1, left : left + lanes] = jnp.sum(value, axis=0, keepdims=True)
 
 
 def first_sums(one, two):
@@ -145,10 +154,10 @@
     rest = list(refs[3 + 2 * count :])
     loss_in = rest.pop(0)
     acc_in = None if begins else (rest.pop(0), rest.pop(0))
-    late = rest[-8:-6] if ends else ()
+    late = (rest.pop(0), rest.pop(0)) if ends else ()
     held_one, held_two, gram_one, gram_two, round_one, round_two = rest[-6:]
-    fresh = rest[-9] if ends else None
-    loss_out, *outs = rest[: -9 if ends else -6]
+    fresh = rest[-7] if ends else None
+    loss_out, *outs = rest[: -7 if ends else -6]
     step = pl.program_id(0)
     tile = lax.rem(step, tiles)
 
@@ -159,17 +168,14 @@
 
     @pl.when(step < tiles)
     def _():
-        for kept, queries in zip(late, (q_one, q_two)):
-            kept[tile] = queries[...]
         for blocks, held, mean in ((blocks_one, held_one, 0), (blocks_two, held_two, 2)):
             start = 0
             for block in blocks:
-                size = block.shape[0]
-                normal = (block[...].astype(jnp.float32) - stat_ref[mean : mean + 1, :]) * stat_ref[
-                    mean + 1 : mean + 2, :
-                ]
-                held[tile, start : start + size, :] = normal.astype(jnp.bfloat16)
-                start += size
+                for row in range(0, block.shape[0], strip):
+                    normal = block[row : row + strip, :].astype(jnp.float32)
+                    normal = (normal - stat_ref[mean : mean + 1, :]) * stat_ref[mean + 1 : mean + 2, :]
+                    held[tile, start : start + strip, :] = normal.astype(jnp.bfloat16)
+                    start += strip
         for gram, queries, held in ((gram_one, q_one, held_one), (gram_two, q_two, held_two)):
             gram[...] += lax.dot_general(
                 queries[...], held[tile], (((1,), (1,)), ((), ())), preferred_element_type=jnp.float32
@@ -202,7 +208,7 @@
             for start in range(0, height, strip):
                 rows = slice(start, start + strip)
                 total = fresh[rows, :] + acc_in[index][rows, :].astype(jnp.float32)
-                prod = total * late[index][tile, rows, :].astype(jnp.float32)
+                prod = total * late[index][rows, :].astype(jnp.float32)
                 plain += jnp.sum(total.reshape(strip // 8, 8, lanes), axis=0)
                 prods += jnp.sum(prod.reshape(strip // 8, 8, lanes), axis=0)
                 place = start % share
@@ -236,6 +242,8 @@
         operands += list(acc)
         in_specs += [pl.BlockSpec((rows, lanes), late)] * 2
     if ends:
+        operands += [q_one, q_two]
+        in_specs += [pl.BlockSpec((rows, lanes), late)] * 2
         out_specs += [pl.BlockSpec((rows // 2, lanes), late)] * 4
         out_shape += [
             jax.ShapeDtypeStruct((rows // 2, width), jnp.bfloat16),
@@ -255,7 +263,6 @@
         out_specs=out_specs,
         out_shape=out_shape,
         scratch_shapes=[pltpu.VMEM((rows, lanes), jnp.float32)] * (1 if ends else 0)
-        + [pltpu.VMEM((tiles, rows, lanes), jnp.bfloat16)] * (2 if ends else 0)
         + [pltpu.VMEM((tiles, keys, lanes), jnp.bfloat16)] * 2
         + [pltpu.VMEM((rows, keys), jnp.float32)] * 2
         + [pltpu.VMEM((rows, keys), jnp.bfloat16)] * 2,
@@ -356,14 +363,14 @@
     def norm_totals(q_one, q_two):
         one, two = (q[:rows].astype(jnp.float32) for q in (q_one, q_two))
         sums = [jnp.sum(one, axis=0), jnp.sum(two, axis=0), jnp.sum(one * two, axis=0)]
-        return summed([*sums, jnp.zeros_like(sums[0])])
-
-    def summed(rows_of_sums):
-        return jnp.sum(lax.all_gather(jnp.stack(rows_of_sums), "batch", axis=0), axis=0)
+        return jnp.stack([*sums, jnp.zeros_like(sums[0])])
+
+    def summed(sums):
+        return jnp.sum(lax.all_gather(sums, "batch", axis=0), axis=0)
 
     def statistics(one, two):
         sums = first_sums(one, two)
-        sums = jnp.sum(lax.all_gather(sums, "batch", axis=0), axis=0) / samples
+        sums = summed(sums) / samples
         inv_one = 1.0 / jnp.sqrt(sums[1] - sums[0] * sums[0] + 1e-05)
         inv_two = 1.0 / jnp.sqrt(sums[3] - sums[2] * sums[2] + 1e-05)
         return jnp.stack([sums[0], inv_one, sums[2], inv_two])
@@ -383,13 +390,13 @@
     for hop in range(hops):
         if hop > 1:
             loss, *acc = attend(q_one, q_two, stat, *arrived[hop - 2], loss, acc, False)
-            tied = (q_one, q_two) if hop == 2 else (norm_sums,)
+            tied = (q_one, q_two, norm_totals(q_one, q_two)) if hop == 2 else (norm_sums,)
             *flat, loss = lax.optimization_barrier((*ends[0], *ends[1], *tied, loss))
             ends = [flat[:2], flat[2:4]]
             arrived[-1] = [list(pair) for pair in ends]
             if hop == 2:
-                q_one, q_two = flat[4:]
-                norm_sums = norm_totals(q_one, q_two)
+                q_one, q_two = flat[4:6]
+                norm_sums = summed(flat[6])
             else:
                 norm_sums = flat[4]
         if hop < hops - 1:

time: 321 us -> 321 us (level)
  no operation moved by 1% of the time
where the time goes in v12:
time: 321 us; the launch traced here: 318 us
  waiting for transfers between devices  175 us (55%)
  Pallas kernels  90.1 us (28%)
  starting transfers between devices  22.3 us (7%)
  between operations  14.2 us (4%)
  other arithmetic  12 us (4%)
  local copies, waits for them, and re-layouts  4.38 us (1%)
    ppermute x6, waiting for transfers between devices, ring_shards(): lax.ppermute(up, 'batch', ahead)  85.5 us
    pallas_call x5, Pallas kernels, attend(): pl.pallas_call(functools.partial(attend_kernel, count, begins, ends), gri...  78.1 us
    all_gather x2, waiting for transfers between devices, summed(): return jnp.sum(lax.all_gather(sums, 'batch', axis=0), axis=0)  61.4 us
    ppermute x1, waiting for transfers between devices, ring_shards(): last_one = lax.ppermute(ends[0][0], 'batch', ahead)  15.7 us
    ppermute x6, starting transfers between devices, ring_shards(): lax.ppermute(up, 'batch', ahead)  9.83 us
    ppermute x10, starting transfers between devices, swapped(): return lax.ppermute(value, 'batch', [(i, i ^ bit) for i in range(batches)])  9.75 us
    ppermute x10, waiting for transfers between devices, swapped(): return lax.ppermute(value, 'batch', [(i, i ^ bit) for i in range(batches)])  7.41 us
    pallas_call x1, Pallas kernels, finish_grads(): pl.pallas_call(functools.partial(finish_kernel, samples, width), grid=(ti...  6.63 us
  transfers between devices with their start and end apart: 26, of which 13 were waited for; matrix products, arithmetic and copies ran while one was open for 4% of the time, Pallas kernels for 21%

profile of v12, /device:TPU:1, one launch (start us, length us, event | category | flops | bytes accessed | tf_op | source)
XLA Modules:
  0.0 317.9 jit_solution(6095769596124826470)
XLA Ops:
  7.2 3.6 %first_sums.1 = f32[4,4096]{1,0:T(4,128)} custom-call(bf16[192,4096]{1,0:T(8,128)(2,1)} %refs_3_.1, bf16[192,4096]{1,0:T(8,128)(2,1)} %refs_4_.1), custom_call_target="tpu_custom_call" | custom-call | flops 4096 | bytes 4096 | tf_op jit(solution)/shard_map/first_sums/pallas_call | solution.py:136
  11.0 2.7 collective-permute-start
  15.3 39.5 %all-gather.7.cloned.1.call-done = f32[16,4,4096]{2,1,0:T(4,128)} async-done(((f32[1,4,4096]{2,1,0:T(4,128)}), f32[16,4,4096]{2,1,0:T(4,128)}) %all-gather.7.cloned.1.call-update) | async-done | bytes 1048592 | tf_op jit(solution)/shard_map/all_gather | solution.py:369
  58.2 29.3 %collective-permute-done.4.refs_5_ = bf16[192,4096]{1,0:T(8,128)(2,1)} collective-permute-done((bf16[192,4096]{1,0:T(8,128)(2,1)S(1)}, bf16[192,4096]{1,0:T(8,128)(2,1)}, u32[]{:S(2)}, u32[]{:S(2)}) %collective-permute-start.4) | collective-permute-done | bytes 1572896 | tf_op jit(solution)/shard_map/ppermute | solution.py:404
  87.6 2.3 collective-permute-start.5
  89.9 3.9 %multiply_convert_fusion.refs_1_.refs_9_.norm_two = bf16[384,4096]{1,0:T(8,128)(2,1)} fusion(bf16[192,4096]{1,0:T(8,128)(2,1)} %collective-permute-done.9, bf16[192,4096]{1,0:T(8,128)(2,1)S(1)} %copy-done.3, f32[4096]{0:T(1024)S(1)} %bitcast.13, f32[4096]{0:T(1024)S(1)} %bitcast.12), kind=kLoop, calls=%fused_computation | loop fusion | flops 11010048 | bytes 6324224 | tf_op jit(solution)/shard_map/convert_element_type | solution.py:380
  93.8 2.5 multiply_convert_fusion.1.refs_0_.refs_8_.norm_one
  97.6 11.6 %attend.5 = (f32[8,128]{1,0:T(8,128)}, f32[384,4096]{1,0:T(8,128)}, f32[384,4096]{1,0:T(8,128)}) custom-call(bf16[384,4096]{1,0:T(8,128)(2,1)} %multiply_convert_fusion.1.refs_0_.refs_8_.norm_one, bf16[384,4096]{1,0:T(8,128)(2,1)} %multiply_convert_fusion.refs_1_.refs_9_.norm_two, ...), custom_call_target="tpu_custom_call", output_to_operand_aliasing={{0}: (5, {})} | custom-call | flops 4096 | bytes 4096 | tf_op jit(solution)/shard_map/attend/pallas_call | solution.py:259
  109.2 17.9 %attend.6 = (f32[8,128]{1,0:T(8,128)}, f32[384,4096]{1,0:T(8,128)}, f32[384,4096]{1,0:T(8,128)}) custom-call(bf16[384,4096]{1,0:T(8,128)(2,1)} %multiply_convert_fusion.1.refs_0_.refs_8_.norm_one, bf16[384,4096]{1,0:T(8,128)(2,1)} %multiply_convert_fusion.refs_1_.refs_9_.norm_two, ...), custom_call_target="tpu_custom_call", output_to_operand_aliasing={{0}: (7, {}), {1}: (8, {}), {2}: (9, {})} | custom-call | flops 4096 | bytes 4096 | tf_op jit(solution)/shard_map/attend/pallas_call | solution.py:259
  128.5 26.5 %collective-permute-done.5.refs_5_ = bf16[192,4096]{1,0:T(8,128)(2,1)} collective-permute-done((bf16[192,4096]{1,0:T(8,128)(2,1)}, bf16[192,4096]{1,0:T(8,128)(2,1)}, u32[]{:S(2)}, u32[]{:S(2)}) %collective-permute-start.5) | collective-permute-done | bytes 1572896 | tf_op jit(solution)/shard_map/ppermute | solution.py:404
  155.1 1.9 collective-permute-done.7.refs_6_
  160.0 17.8 %attend.7 = (f32[8,128]{1,0:T(8,128)}, f32[384,4096]{1,0:T(8,128)}, f32[384,4096]{1,0:T(8,128)}) custom-call(bf16[384,4096]{1,0:T(8,128)(2,1)} %multiply_convert_fusion.1.refs_0_.refs_8_.norm_one, bf16[384,4096]{1,0:T(8,128)(2,1)} %multiply_convert_fusion.refs_1_.refs_9_.norm_two, ...), custom_call_target="tpu_custom_call", output_to_operand_aliasing={{0}: (7, {}), {1}: (8, {}), {2}: (9, {})} | custom-call | flops 4096 | bytes 4096 | tf_op jit(solution)/shard_map/attend/pallas_call | solution.py:259
  177.7 21.8 %all-gather.9.cloned.1.call-done = f32[16,4,4096]{2,1,0:T(4,128)} async-done(((f32[1,4,4096]{2,1,0:T(4,128)}), f32[16,4,4096]{2,1,0:T(4,128)}) %all-gather.9.cloned.1.call-update) | async-done | bytes 1048592 | tf_op jit(solution)/shard_map/all_gather | solution.py:369
  199.5 2.0 reduce_sum.49.norm_ref
  201.6 29.6 %collective-permute-done.12.refs_5_ = bf16[192,4096]{1,0:T(8,128)(2,1)} collective-permute-done((bf16[192,4096]{1,0:T(8,128)(2,1)}, bf16[192,4096]{1,0:T(8,128)(2,1)}, u32[]{:S(2)}, u32[]{:S(2)}) %collective-permute-start.12) | collective-permute-done | bytes 1572896 | tf_op jit(solution)/shard_map/ppermute | solution.py:404
  231.2 1.8 collective-permute-done.13.refs_6_
  234.5 16.4 %attend.8 = (f32[8,128]{1,0:T(8,128)}, bf16[384,4096]{1,0:T(8,128)(2,1)}, bf16[384,4096]{1,0:T(8,128)(2,1)}) custom-call(bf16[384,4096]{1,0:T(8,128)(2,1)} %multiply_convert_fusion.1.refs_0_.refs_8_.norm_one, bf16[384,4096]{1,0:T(8,128)(2,1)} %multiply_convert_fusion.refs_1_.refs_9_.norm_two, ...), custom_call_target="tpu_custom_call", output_to_operand_aliasing={{0}: (7, {})} | custom-call | flops 4096 | bytes 4096 | tf_op jit(solution)/shard_map/attend/pallas_call | solution.py:259
  250.8 15.7 %collective-permute-done.14.refs_3_ = bf16[192,4096]{1,0:T(8,128)(2,1)S(1)} collective-permute-done((bf16[192,4096]{1,0:T(8,128)(2,1)S(1)}, bf16[192,4096]{1,0:T(8,128)(2,1)S(1)}, u32[]{:S(2)}, u32[]{:S(2)}) %collective-permute-start.14) | collective-permute-done | bytes 1572896 | tf_op jit(solution)/shard_map/ppermute | solution.py:409
  268.9 14.5 %attend.9 = (f32[8,128]{1,0:T(8,128)}, bf16[192,4096]{1,0:T(8,128)(2,1)}, bf16[192,4096]{1,0:T(8,128)(2,1)}, bf16[192,4096]{1,0:T(8,128)(2,1)}, bf16[192,4096]{1,0:T(8,128)(2,1)}, /*index=5*/bf16[8,4096]{1,0:T(8,128)(2,1)}) custom-call(bf16[384,4096]{1,0:T(8,128)(2,1)} %multiply_convert_fusion.1.refs_0_.refs_8_.norm_one, ...), custom_call_target="tpu_custom_call", output_to_operand_aliasing={{0}: (5, {})} | custom-call | flops 4096 | bytes 4096 | tf_op jit(solution)/shard_map/attend/pallas_call | solution.py:259
  283.4 3.6 %collective-permute-start.16 = (bf16[192,4096]{1,0:T(8,128)(2,1)}, bf16[192,4096]{1,0:T(8,128)(2,1)S(1)}, u32[]{:S(2)}, u32[]{:S(2)}) collective-permute-start(bf16[192,4096]{1,0:T(8,128)(2,1)} %get-tuple-element.66), channel_id=1, source_target_pairs={{0,1},{1,0},{2,3},{3,2},{4,5},{5,4},{6,7},{7,6},{8,9},{9,8},{10,11... | collective-permute-start | bytes 4718600 | tf_op jit(solution)/shard_map/ppermute | solution.py:352
  289.2 3.4 %collective-permute-done.18.refs_1_ = bf16[8,4096]{1,0:T(8,128)(2,1)S(1)} collective-permute-done((bf16[8,4096]{1,0:T(8,128)(2,1)}, bf16[8,4096]{1,0:T(8,128)(2,1)S(1)}, u32[]{:S(2)}, u32[]{:S(2)}) %collective-permute-start.18) | collective-permute-done | bytes 65568 | tf_op jit(solution)/shard_map/ppermute | solution.py:352
  297.0 2.1 collective-permute-start.23
  299.1 2.4 collective-permute-done.22.rest_2_
  304.4 6.6 %finish.1 = (bf16[192,4096]{1,0:T(8,128)(2,1)}, bf16[192,4096]{1,0:T(8,128)(2,1)}, f32[1]{0:T(128)}) custom-call(bf16[192,4096]{1,0:T(8,128)(2,1)} %get-tuple-element.65.own_one, bf16[192,4096]{1,0:T(8,128)(2,1)} %copy-done.4, bf16[192,4096]{1,0:T(8,128)(2,1)} %get-tuple-element.67.own_two, bf16[192,4096]{1,0:T(8,128)(2,1)} %copy-done.5, ...), custom_call_target="tpu_custom_call" | custom-call | flops 4096 | bytes 4096 | tf_op jit(solution)/shard_map/finish/pallas_call | solution.py:324
  (81 shorter events, 24.3 us)
Async XLA Ops:
  7.2 47.7 %all-gather.7.cloned.1.call-start = ((), (), s32[]{:S(2)}) async-start(), calls=%async_computation | async-start | bytes 1114112 | tf_op jit(solution)/shard_map/all_gather | solution.py:369
  10.9 188.7 %all-gather.9.cloned.1.call-start = ((), (), s32[]{:S(2)}) async-start(), calls=%async_computation.1 | async-start | bytes 1114112 | tf_op jit(solution)/shard_map/all_gather | solution.py:369
  10.9 45.4 %collective-permute-start.9 = (bf16[192,4096]{1,0:T(8,128)(2,1)S(1)}, bf16[192,4096]{1,0:T(8,128)(2,1)}, u32[]{:S(2)}, u32[]{:S(2)}) collective-permute-start(bf16[192,4096]{1,0:T(8,128)(2,1)S(1)} %copy-done.3), channel_id=1, source_target_pairs={{0,1},{1,0},{2,3},{3,2},{4,5},{5,4},{6,7},{7,6},{8,9},{9,8},{10,11... | collective-permute-start | bytes 4718600 | tf_op jit(solution)/shard_map/ppermute | solution.py:352
  11.0 45.6 %collective-permute-start = (bf16[192,4096]{1,0:T(8,128)(2,1)S(1)}, bf16[192,4096]{1,0:T(8,128)(2,1)}, u32[]{:S(2)}, u32[]{:S(2)}) collective-permute-start(bf16[192,4096]{1,0:T(8,128)(2,1)S(1)} %copy-done.2), channel_id=1, source_target_pairs={{0,4},{1,5},{4,8},{5,9},{8,12},{9,13},{12,14},{13,15},{14,10},{15,... | collective-permute-start | bytes 4718600 | tf_op jit(solution)/shard_map/ppermute | solution.py:404
  13.8 43.6 %collective-permute-start.2 = (bf16[192,4096]{1,0:T(8,128)(2,1)S(1)}, bf16[192,4096]{1,0:T(8,128)(2,1)}, u32[]{:S(2)}, u32[]{:S(2)}) collective-permute-start(bf16[192,4096]{1,0:T(8,128)(2,1)S(1)} %copy-done.2), channel_id=1, source_target_pairs={{4,0},{5,1},{8,4},{9,5},{12,8},{13,9},{14,12},{15,13},{10,14},{11,... | collective-permute-start | bytes 4718600 | tf_op jit(solution)/shard_map/ppermute | solution.py:404
  13.8 73.8 %collective-permute-start.4 = (bf16[192,4096]{1,0:T(8,128)(2,1)S(1)}, bf16[192,4096]{1,0:T(8,128)(2,1)}, u32[]{:S(2)}, u32[]{:S(2)}) collective-permute-start(bf16[192,4096]{1,0:T(8,128)(2,1)S(1)} %copy-done.3), channel_id=1, source_target_pairs={{0,4},{1,5},{4,8},{5,9},{8,12},{9,13},{12,14},{13,15},{14,10},{15,... | collective-permute-start | bytes 4718600 | tf_op jit(solution)/shard_map/ppermute | solution.py:404
  15.3 74.6 %collective-permute-start.6 = (bf16[192,4096]{1,0:T(8,128)(2,1)S(1)}, bf16[192,4096]{1,0:T(8,128)(2,1)}, u32[]{:S(2)}, u32[]{:S(2)}) collective-permute-start(bf16[192,4096]{1,0:T(8,128)(2,1)S(1)} %copy-done.3), channel_id=1, source_target_pairs={{4,0},{5,1},{8,4},{9,5},{12,8},{13,9},{14,12},{15,13},{10,14},{11,... | collective-permute-start | bytes 4718600 | tf_op jit(solution)/shard_map/ppermute | solution.py:404
  56.3 37.5 %collective-permute-start.8 = (bf16[192,4096]{1,0:T(8,128)(2,1)S(1)}, bf16[192,4096]{1,0:T(8,128)(2,1)S(1)}, u32[]{:S(2)}, u32[]{:S(2)}) collective-permute-start(bf16[192,4096]{1,0:T(8,128)(2,1)S(1)} %copy-done.2), channel_id=1, source_target_pairs={{0,1},{1,0},{2,3},{3,2},{4,5},{5,4},{6,7},{7,6},{8,9},{9,8},{10,11... | collective-permute-start | bytes 4718600 | tf_op jit(solution)/shard_map/ppermute | solution.py:352
  56.7 71.8 %collective-permute-start.1 = (bf16[192,4096]{1,0:T(8,128)(2,1)}, bf16[192,4096]{1,0:T(8,128)(2,1)}, u32[]{:S(2)}, u32[]{:S(2)}) collective-permute-start(bf16[192,4096]{1,0:T(8,128)(2,1)} %collective-permute-done.refs_3_), channel_id=1, source_target_pairs={{0,4},{1,5},{4,8},{5,9},{8,12},{9,13},{12,14},{13,15},{14,10},{15,... | collective-permute-start | bytes 4718600 | tf_op jit(solution)/shard_map/ppermute | solution.py:404
  57.4 71.2 %collective-permute-start.3 = (bf16[192,4096]{1,0:T(8,128)(2,1)}, bf16[192,4096]{1,0:T(8,128)(2,1)}, u32[]{:S(2)}, u32[]{:S(2)}) collective-permute-start(bf16[192,4096]{1,0:T(8,128)(2,1)} %collective-permute-done.2.refs_4_), channel_id=1, source_target_pairs={{4,0},{5,1},{8,4},{9,5},{12,8},{13,9},{14,12},{15,13},{10,14},{11,... | collective-permute-start | bytes 4718600 | tf_op jit(solution)/shard_map/ppermute | solution.py:404
  87.6 67.5 %collective-permute-start.5 = (bf16[192,4096]{1,0:T(8,128)(2,1)}, bf16[192,4096]{1,0:T(8,128)(2,1)}, u32[]{:S(2)}, u32[]{:S(2)}) collective-permute-start(bf16[192,4096]{1,0:T(8,128)(2,1)} %collective-permute-done.4.refs_5_), channel_id=1, source_target_pairs={{0,4},{1,5},{4,8},{5,9},{8,12},{9,13},{12,14},{13,15},{14,10},{15,... | collective-permute-start | bytes 4718600 | tf_op jit(solution)/shard_map/ppermute | solution.py:404
  89.9 67.1 %collective-permute-start.7 = (bf16[192,4096]{1,0:T(8,128)(2,1)}, bf16[192,4096]{1,0:T(8,128)(2,1)}, u32[]{:S(2)}, u32[]{:S(2)}) collective-permute-start(bf16[192,4096]{1,0:T(8,128)(2,1)} %collective-permute-done.6.refs_6_), channel_id=1, source_target_pairs={{4,0},{5,1},{8,4},{9,5},{12,8},{13,9},{14,12},{15,13},{10,14},{11,... | collective-permute-start | bytes 4718600 | tf_op jit(solution)/shard_map/ppermute | solution.py:404
  157.0 44.6 %collective-permute-start.10 = (bf16[192,4096]{1,0:T(8,128)(2,1)}, bf16[192,4096]{1,0:T(8,128)(2,1)S(1)}, u32[]{:S(2)}, u32[]{:S(2)}) collective-permute-start(bf16[192,4096]{1,0:T(8,128)(2,1)} %collective-permute-done.1.refs_3_), channel_id=1, source_target_pairs={{0,4},{1,5},{4,8},{5,9},{8,12},{9,13},{12,14},{13,15},{14,10},{15,... | collective-permute-start | bytes 4718600 | tf_op jit(solution)/shard_map/ppermute | solution.py:404
  158.3 43.2 %collective-permute-start.11 = (bf16[192,4096]{1,0:T(8,128)(2,1)}, bf16[192,4096]{1,0:T(8,128)(2,1)}, u32[]{:S(2)}, u32[]{:S(2)}) collective-permute-start(bf16[192,4096]{1,0:T(8,128)(2,1)} %collective-permute-done.3.refs_4_), channel_id=1, source_target_pairs={{4,0},{5,1},{8,4},{9,5},{12,8},{13,9},{14,12},{15,13},{10,14},{11,... | collective-permute-start | bytes 4718600 | tf_op jit(solution)/shard_map/ppermute | solution.py:404
  158.5 72.7 %collective-permute-start.12 = (bf16[192,4096]{1,0:T(8,128)(2,1)}, bf16[192,4096]{1,0:T(8,128)(2,1)}, u32[]{:S(2)}, u32[]{:S(2)}) collective-permute-start(bf16[192,4096]{1,0:T(8,128)(2,1)} %collective-permute-done.5.refs_5_), channel_id=1, source_target_pairs={{0,4},{1,5},{4,8},{5,9},{8,12},{9,13},{12,14},{13,15},{14,10},{15,... | collective-permute-start | bytes 4718600 | tf_op jit(solution)/shard_map/ppermute | solution.py:404
  159.8 73.2 %collective-permute-start.13 = (bf16[192,4096]{1,0:T(8,128)(2,1)}, bf16[192,4096]{1,0:T(8,128)(2,1)S(1)}, u32[]{:S(2)}, u32[]{:S(2)}) collective-permute-start(bf16[192,4096]{1,0:T(8,128)(2,1)} %collective-permute-done.7.refs_6_), channel_id=1, source_target_pairs={{4,0},{5,1},{8,4},{9,5},{12,8},{13,9},{14,12},{15,13},{10,14},{11,... | collective-permute-start | bytes 4718600 | tf_op jit(solution)/shard_map/ppermute | solution.py:404
  233.0 33.5 %collective-permute-start.14 = (bf16[192,4096]{1,0:T(8,128)(2,1)S(1)}, bf16[192,4096]{1,0:T(8,128)(2,1)S(1)}, u32[]{:S(2)}, u32[]{:S(2)}) collective-permute-start(bf16[192,4096]{1,0:T(8,128)(2,1)S(1)} %collective-permute-done.10.refs_3_), channel_id=1, source_target_pairs={{0,4},{1,5},{4,8},{5,9},{8,12},{9,13},{12,14},{13,15},{14,10},{15,... | collective-permute-start | bytes 4718600 | tf_op jit(solution)/shard_map/ppermute | solution.py:409
  234.4 33.3 %collective-permute-start.15 = (bf16[192,4096]{1,0:T(8,128)(2,1)S(1)}, bf16[192,4096]{1,0:T(8,128)(2,1)S(1)}, u32[]{:S(2)}, u32[]{:S(2)}) collective-permute-start(bf16[192,4096]{1,0:T(8,128)(2,1)S(1)} %collective-permute-done.13.refs_6_), channel_id=1, source_target_pairs={{4,0},{5,1},{8,4},{9,5},{12,8},{13,9},{14,12},{15,13},{10,14},{11,... | collective-permute-start | bytes 4718600 | tf_op jit(solution)/shard_map/ppermute | solution.py:410
  283.4 19.4 %collective-permute-start.16 = (bf16[192,4096]{1,0:T(8,128)(2,1)}, bf16[192,4096]{1,0:T(8,128)(2,1)S(1)}, u32[]{:S(2)}, u32[]{:S(2)}) collective-permute-start(bf16[192,4096]{1,0:T(8,128)(2,1)} %get-tuple-element.66), channel_id=1, source_target_pairs={{0,1},{1,0},{2,3},{3,2},{4,5},{5,4},{6,7},{7,6},{8,9},{9,8},{10,11... | collective-permute-start | bytes 4718600 | tf_op jit(solution)/shard_map/ppermute | solution.py:352
  286.9 15.8 %collective-permute-start.17 = (bf16[192,4096]{1,0:T(8,128)(2,1)}, bf16[192,4096]{1,0:T(8,128)(2,1)S(1)}, u32[]{:S(2)}, u32[]{:S(2)}) collective-permute-start(bf16[192,4096]{1,0:T(8,128)(2,1)} %get-tuple-element.68), channel_id=1, source_target_pairs={{0,1},{1,0},{2,3},{3,2},{4,5},{5,4},{6,7},{7,6},{8,9},{9,8},{10,11... | collective-permute-start | bytes 4718600 | tf_op jit(solution)/shard_map/ppermute | solution.py:352
  287.0 5.5 %collective-permute-start.18 = (bf16[8,4096]{1,0:T(8,128)(2,1)}, bf16[8,4096]{1,0:T(8,128)(2,1)S(1)}, u32[]{:S(2)}, u32[]{:S(2)}) collective-permute-start(bf16[8,4096]{1,0:T(8,128)(2,1)} %get-tuple-element.70.refs_0_), channel_id=1, source_target_pairs={{0,1},{1,0},{2,3},{3,2},{4,5},{5,4},{6,7},{7,6},{8,9},{9,8},{10,11... | collective-permute-start | bytes 196616 | tf_op jit(solution)/shard_map/ppermute | solution.py:352
  287.5 5.4 %collective-permute-start.20 = (bf16[8,4096]{1,0:T(8,128)(2,1)}, bf16[8,4096]{1,0:T(8,128)(2,1)S(1)}, u32[]{:S(2)}, u32[]{:S(2)}) collective-permute-start(bf16[8,4096]{1,0:T(8,128)(2,1)} %get-tuple-element.70.refs_0_), channel_id=1, source_target_pairs={{0,3},{1,2},{2,1},{3,0},{4,7},{5,6},{6,5},{7,4},{8,11},{9,10},{10,... | collective-permute-start | bytes 196616 | tf_op jit(solution)/shard_map/ppermute | solution.py:352
  296.2 5.3 %collective-permute-start.22 = (bf16[8,4096]{1,0:T(8,128)(2,1)}, bf16[8,4096]{1,0:T(8,128)(2,1)S(1)}, u32[]{:S(2)}, u32[]{:S(2)}) collective-permute-start(bf16[8,4096]{1,0:T(8,128)(2,1)} %add_totals.1.rest_0_), channel_id=1, source_target_pairs={{0,8},{1,9},{2,10},{3,11},{4,12},{5,13},{6,14},{7,15},{8,0},{9,1},... | collective-permute-start | bytes 196616 | tf_op jit(solution)/shard_map/ppermute | solution.py:352
  297.0 5.7 %collective-permute-start.23 = (bf16[8,4096]{1,0:T(8,128)(2,1)}, bf16[8,4096]{1,0:T(8,128)(2,1)S(1)}, u32[]{:S(2)}, u32[]{:S(2)}) collective-permute-start(bf16[8,4096]{1,0:T(8,128)(2,1)} %add_totals.1.rest_0_), channel_id=1, source_target_pairs={{0,12},{1,13},{2,14},{3,15},{4,8},{5,9},{6,10},{7,11},{8,4},{9,5},... | collective-permute-start | bytes 196616 | tf_op jit(solution)/shard_map/ppermute | solution.py:352
  (18 other events, 99.3 us)
Sparse Core Ops, SparseCore 0:
  11.0 43.8 all-gather.6
  157.1 42.3 all-gather.8

commit v13 on v11

--- a/solution.py
+++ b/solution.py
@@ -356,14 +356,13 @@
     def norm_totals(q_one, q_two):
         one, two = (q[:rows].astype(jnp.float32) for q in (q_one, q_two))
         sums = [jnp.sum(one, axis=0), jnp.sum(two, axis=0), jnp.sum(one * two, axis=0)]
-        return summed([*sums, jnp.zeros_like(sums[0])])
-
-    def summed(rows_of_sums):
-        return jnp.sum(lax.all_gather(jnp.stack(rows_of_sums), "batch", axis=0), axis=0)
-
-    def statistics(one, two):
-        sums = first_sums(one, two)
-        sums = jnp.sum(lax.all_gather(sums, "batch", axis=0), axis=0) / samples
+        return jnp.stack([*sums, jnp.zeros_like(sums[0])])
+
+    def summed(sums):
+        return jnp.sum(lax.all_gather(sums, "batch", axis=0), axis=0)
+
+    def statistics(gathered):
+        sums = jnp.sum(gathered, axis=0) / samples
         inv_one = 1.0 / jnp.sqrt(sums[1] - sums[0] * sums[0] + 1e-05)
         inv_two = 1.0 / jnp.sqrt(sums[3] - sums[2] * sums[2] + 1e-05)
         return jnp.stack([sums[0], inv_one, sums[2], inv_two])
@@ -372,26 +371,28 @@
         both = jnp.concatenate([view, far], axis=0).astype(jnp.float32)
         return ((both - mean) * inv).astype(jnp.bfloat16)
 
-    stat = statistics(view_one, view_two)
+    gathered = lax.all_gather(first_sums(view_one, view_two), "batch", axis=0)
     far_one, far_two = swapped(view_one, 1), swapped(view_two, 1)
-    q_one = normed(view_one, far_one, stat[0], stat[1])
-    q_two = normed(view_two, far_two, stat[2], stat[3])
     ends = [[view_one, view_one], [view_two, view_two]]
     arrived = []
     loss = jnp.zeros((8, 128), jnp.float32)
-    loss, *acc = attend(q_one, q_two, stat, [view_one], [view_two], loss, None, False)
     for hop in range(hops):
+        if hop == 1:
+            *arrived[0][0], gathered = lax.optimization_barrier((*ends[0], gathered))
+            stat = statistics(gathered)
+            q_one = normed(view_one, far_one, stat[0], stat[1])
+            q_two = normed(view_two, far_two, stat[2], stat[3])
+            loss, *acc = attend(q_one, q_two, stat, [view_one], [view_two], loss, None, False)
         if hop > 1:
             loss, *acc = attend(q_one, q_two, stat, *arrived[hop - 2], loss, acc, False)
-            tied = (q_one, q_two) if hop == 2 else (norm_sums,)
-            *flat, loss = lax.optimization_barrier((*ends[0], *ends[1], *tied, loss))
-            ends = [flat[:2], flat[2:4]]
+            tied = (q_one, q_two, norm_totals(q_one, q_two)) if hop == 2 else (norm_sums,)
+            *ends[1], tied, loss = lax.optimization_barrier((*ends[1], tied, loss))
             arrived[-1] = [list(pair) for pair in ends]
             if hop == 2:
-                q_one, q_two = flat[4:]
-                norm_sums = norm_totals(q_one, q_two)
+                q_one, q_two, sums = tied
+                norm_sums = summed(sums)
             else:
-                norm_sums = flat[4]
+                (norm_sums,) = tied
         if hop < hops - 1:
             ends = [
                 [lax.ppermute(up, "batch", ahead), lax.ppermute(down, "batch", behind)]

time: 321 us -> 326 us (1.016)
  starting transfers between devices: 22.3 us -> 28.5 us
  waiting for transfers between devices: 176 us -> 172 us
    all_gather x2, waiting for transfers between devices: 61.4 us -> 0.01 us  [the longest x1 0.01 us: ring_shards(): gathered = lax.all_gather(first_sums(view_one, view_two), 'batch', axis=0)]
    ppermute x6, waiting for transfers between devices: 86.9 us -> 126 us  [ring_shards(): lax.ppermute(up, 'batch', ahead)]
    ppermute x6, waiting for transfers between devices: 3.71 us -> 21.6 us  [ring_shards(): lax.ppermute(down, 'batch', behind)]
    ppermute x1, waiting for transfers between devices: 15.7 us -> 5.58 us  [ring_shards(): last_one = lax.ppermute(ends[0][0], 'batch', ahead)]
    ppermute x1, waiting for transfers between devices: 1.23 us -> 10.6 us  [ring_shards(): last_two = lax.ppermute(ends[1][1], 'batch', behind)]
    ppermute x10, starting transfers between devices: 9.74 us -> 13.4 us  [swapped(): return lax.ppermute(value, 'batch', [(i, i ^ bit) for i in range(batches)])]
  transfers between devices with their start and end apart: 26 -> 26, of which waited for: 13 -> 14; matrix products, arithmetic and copies ran while one was open for 4% -> 4% of each run, Pallas kernels for 21% -> 20%
where the time goes in v13:
time: 326 us; the launch traced here: 323 us
  waiting for transfers between devices  172 us (53%)
  Pallas kernels  88.4 us (27%)
  starting transfers between devices  28.5 us (9%)
  between operations  14.2 us (4%)
  other arithmetic  13.5 us (4%)
  local copies, waits for them, and re-layouts  6.64 us (2%)
    ppermute x6, waiting for transfers between devices, ring_shards(): lax.ppermute(up, 'batch', ahead)  126 us
    pallas_call x5, Pallas kernels, attend(): pl.pallas_call(functools.partial(attend_kernel, count, begins, ends), gri...  76.7 us
    ppermute x6, waiting for transfers between devices, ring_shards(): lax.ppermute(down, 'batch', behind)  21.6 us
    ppermute x10, starting transfers between devices, swapped(): return lax.ppermute(value, 'batch', [(i, i ^ bit) for i in range(batches)])  13.4 us
    ppermute x1, waiting for transfers between devices, ring_shards(): last_two = lax.ppermute(ends[1][1], 'batch', behind)  10.6 us
    ppermute x6, starting transfers between devices, ring_shards(): lax.ppermute(up, 'batch', ahead)  10.6 us
    ppermute x10, waiting for transfers between devices, swapped(): return lax.ppermute(value, 'batch', [(i, i ^ bit) for i in range(batches)])  8.25 us
    convert_element_type x2, other arithmetic, normed(): return ((both - mean) * inv).astype(jnp.bfloat16)  7.91 us
  transfers between devices with their start and end apart: 26, of which 14 were waited for; matrix products, arithmetic and copies ran while one was open for 4% of the time, Pallas kernels for 20%

profile of v13, /device:TPU:1, one launch (start us, length us, event | category | flops | bytes accessed | tf_op | source)
XLA Modules:
  0.0 323.4 jit_solution(14916251776075368978)
XLA Ops:
  7.2 3.3 %first_sums.1 = f32[4,4096]{1,0:T(4,128)} custom-call(bf16[192,4096]{1,0:T(8,128)(2,1)} %refs_3_.1, bf16[192,4096]{1,0:T(8,128)(2,1)} %refs_4_.1), custom_call_target="tpu_custom_call" | custom-call | flops 4096 | bytes 4096 | tf_op jit(solution)/shard_map/first_sums/pallas_call | solution.py:127
  15.9 36.3 %collective-permute-done.5.refs_3_ = bf16[192,4096]{1,0:T(8,128)(2,1)} collective-permute-done((bf16[192,4096]{1,0:T(8,128)(2,1)S(1)}, bf16[192,4096]{1,0:T(8,128)(2,1)}, u32[]{:S(2)}, u32[]{:S(2)}) %collective-permute-start.5) | collective-permute-done | bytes 1572896 | tf_op jit(solution)/shard_map/ppermute | solution.py:398
  52.2 2.7 collective-permute-start.4
  54.9 31.0 %collective-permute-done.refs_5_ = bf16[192,4096]{1,0:T(8,128)(2,1)} collective-permute-done((bf16[192,4096]{1,0:T(8,128)(2,1)S(1)}, bf16[192,4096]{1,0:T(8,128)(2,1)}, u32[]{:S(2)}, u32[]{:S(2)}) %collective-permute-start) | collective-permute-done | bytes 1572896 | tf_op jit(solution)/shard_map/ppermute | solution.py:398
  85.9 2.3 collective-permute-start.1
  92.8 3.9 %multiply_convert_fusion.refs_1_.norm_two = bf16[384,4096]{1,0:T(8,128)(2,1)} fusion(bf16[192,4096]{1,0:T(8,128)(2,1)} %collective-permute-done.7, bf16[192,4096]{1,0:T(8,128)(2,1)S(1)} %copy-done.3, f32[4096]{0:T(1024)S(1)} %bitcast.13, f32[4096]{0:T(1024)S(1)} %bitcast.12), kind=kLoop, calls=%fused_computation | loop fusion | flops 11010048 | bytes 6324224 | tf_op jit(solution)/shard_map/convert_element_type | solution.py:372
  96.7 4.0 %multiply_convert_fusion.1.refs_0_.norm_one = bf16[384,4096]{1,0:T(8,128)(2,1)} fusion(bf16[192,4096]{1,0:T(8,128)(2,1)} %collective-permute-done.4, bf16[192,4096]{1,0:T(8,128)(2,1)S(1)} %copy-done.2, f32[4096]{0:T(1024)S(1)} %bitcast.14, f32[4096]{0:T(1024)S(1)} %bitcast.15), kind=kLoop, calls=%fused_computation.1 | loop fusion | flops 11010048 | bytes 6324224 | tf_op jit(solution)/shard_map/convert_element_type | solution.py:372
  102.0 11.6 %attend.5 = (f32[8,128]{1,0:T(8,128)}, f32[384,4096]{1,0:T(8,128)}, f32[384,4096]{1,0:T(8,128)}) custom-call(bf16[384,4096]{1,0:T(8,128)(2,1)} %multiply_convert_fusion.1.refs_0_.norm_one, bf16[384,4096]{1,0:T(8,128)(2,1)} %multiply_convert_fusion.refs_1_.norm_two, f32[4,4096]{1,0:T(4,128)} %pad_maximum_fusion.refs_2_.stat_ref, ...), custom_call_target="tpu_custom_call", output_to_operand_aliasing={{0}: (5, {})} | custom-call | flops 4096 | bytes 4096 | tf_op jit(solution)/shard_map/attend/pallas_call | solution.py:251
  113.6 17.9 %attend.6 = (f32[8,128]{1,0:T(8,128)}, f32[384,4096]{1,0:T(8,128)}, f32[384,4096]{1,0:T(8,128)}) custom-call(bf16[384,4096]{1,0:T(8,128)(2,1)} %multiply_convert_fusion.1.refs_0_.norm_one, bf16[384,4096]{1,0:T(8,128)(2,1)} %multiply_convert_fusion.refs_1_.norm_two, ...), custom_call_target="tpu_custom_call", output_to_operand_aliasing={{0}: (7, {}), {1}: (8, {}), {2}: (9, {})} | custom-call | flops 4096 | bytes 4096 | tf_op jit(solution)/shard_map/attend/pallas_call | solution.py:251
  133.1 23.3 %collective-permute-done.8.refs_3_ = bf16[192,4096]{1,0:T(8,128)(2,1)} collective-permute-done((bf16[192,4096]{1,0:T(8,128)(2,1)}, bf16[192,4096]{1,0:T(8,128)(2,1)}, u32[]{:S(2)}, u32[]{:S(2)}) %collective-permute-start.8) | collective-permute-done | bytes 1572896 | tf_op jit(solution)/shard_map/ppermute | solution.py:398
  156.5 2.2 collective-permute-start.9
  160.1 12.1 %collective-permute-done.13.refs_4_ = bf16[192,4096]{1,0:T(8,128)(2,1)} collective-permute-done((bf16[192,4096]{1,0:T(8,128)(2,1)S(1)}, bf16[192,4096]{1,0:T(8,128)(2,1)}, u32[]{:S(2)}, u32[]{:S(2)}) %collective-permute-start.13) | collective-permute-done | bytes 1572896 | tf_op jit(solution)/shard_map/ppermute | solution.py:398
  172.2 17.7 %attend.7 = (f32[8,128]{1,0:T(8,128)}, f32[384,4096]{1,0:T(8,128)}, f32[384,4096]{1,0:T(8,128)}) custom-call(bf16[384,4096]{1,0:T(8,128)(2,1)} %multiply_convert_fusion.1.refs_0_.norm_one, bf16[384,4096]{1,0:T(8,128)(2,1)} %multiply_convert_fusion.refs_1_.norm_two, ...), custom_call_target="tpu_custom_call", output_to_operand_aliasing={{0}: (7, {}), {1}: (8, {}), {2}: (9, {})} | custom-call | flops 4096 | bytes 4096 | tf_op jit(solution)/shard_map/attend/pallas_call | solution.py:251
  190.0 5.9 %collective-permute-done.9.refs_3_ = bf16[192,4096]{1,0:T(8,128)(2,1)} collective-permute-done((bf16[192,4096]{1,0:T(8,128)(2,1)}, bf16[192,4096]{1,0:T(8,128)(2,1)}, u32[]{:S(2)}, u32[]{:S(2)}) %collective-permute-start.9) | collective-permute-done | bytes 1572896 | tf_op jit(solution)/shard_map/ppermute | solution.py:398
  200.0 29.5 %collective-permute-done.11.refs_5_ = bf16[192,4096]{1,0:T(8,128)(2,1)} collective-permute-done((bf16[192,4096]{1,0:T(8,128)(2,1)}, bf16[192,4096]{1,0:T(8,128)(2,1)}, u32[]{:S(2)}, u32[]{:S(2)}) %collective-permute-start.11) | collective-permute-done | bytes 1572896 | tf_op jit(solution)/shard_map/ppermute | solution.py:398
  231.2 8.9 %collective-permute-done.15.refs_4_ = bf16[192,4096]{1,0:T(8,128)(2,1)S(1)} collective-permute-done((bf16[192,4096]{1,0:T(8,128)(2,1)}, bf16[192,4096]{1,0:T(8,128)(2,1)S(1)}, u32[]{:S(2)}, u32[]{:S(2)}) %collective-permute-start.15) | collective-permute-done | bytes 1572896 | tf_op jit(solution)/shard_map/ppermute | solution.py:398
  241.3 16.4 %attend.8 = (f32[8,128]{1,0:T(8,128)}, bf16[384,4096]{1,0:T(8,128)(2,1)}, bf16[384,4096]{1,0:T(8,128)(2,1)}) custom-call(bf16[384,4096]{1,0:T(8,128)(2,1)} %multiply_convert_fusion.1.refs_0_.norm_one, bf16[384,4096]{1,0:T(8,128)(2,1)} %multiply_convert_fusion.refs_1_.norm_two, ...), custom_call_target="tpu_custom_call", output_to_operand_aliasing={{0}: (7, {})} | custom-call | flops 4096 | bytes 4096 | tf_op jit(solution)/shard_map/attend/pallas_call | solution.py:251
  257.7 5.6 %collective-permute-done.10.refs_3_ = bf16[192,4096]{1,0:T(8,128)(2,1)S(1)} collective-permute-done((bf16[192,4096]{1,0:T(8,128)(2,1)}, bf16[192,4096]{1,0:T(8,128)(2,1)S(1)}, u32[]{:S(2)}, u32[]{:S(2)}) %collective-permute-start.10) | collective-permute-done | bytes 1572896 | tf_op jit(solution)/shard_map/ppermute | solution.py:403
  263.2 10.6 %collective-permute-done.14.refs_4_ = bf16[192,4096]{1,0:T(8,128)(2,1)S(1)} collective-permute-done((bf16[192,4096]{1,0:T(8,128)(2,1)}, bf16[192,4096]{1,0:T(8,128)(2,1)S(1)}, u32[]{:S(2)}, u32[]{:S(2)}) %collective-permute-start.14) | collective-permute-done | bytes 1572896 | tf_op jit(solution)/shard_map/ppermute | solution.py:404
  275.0 13.2 %attend.9 = (f32[8,128]{1,0:T(8,128)}, bf16[192,4096]{1,0:T(8,128)(2,1)}, bf16[192,4096]{1,0:T(8,128)(2,1)}, bf16[192,4096]{1,0:T(8,128)(2,1)}, bf16[192,4096]{1,0:T(8,128)(2,1)}, /*index=5*/bf16[8,4096]{1,0:T(8,128)(2,1)}) custom-call(bf16[384,4096]{1,0:T(8,128)(2,1)} %multiply_convert_fusion.1.refs_0_.norm_one, ...), custom_call_target="tpu_custom_call", output_to_operand_aliasing={{0}: (5, {})} | custom-call | flops 4096 | bytes 4096 | tf_op jit(solution)/shard_map/attend/pallas_call | solution.py:251
  288.2 3.4 %collective-permute-start.16 = (bf16[192,4096]{1,0:T(8,128)(2,1)}, bf16[192,4096]{1,0:T(8,128)(2,1)S(1)}, u32[]{:S(2)}, u32[]{:S(2)}) collective-permute-start(bf16[192,4096]{1,0:T(8,128)(2,1)} %get-tuple-element.64), channel_id=1, source_target_pairs={{0,1},{1,0},{2,3},{3,2},{4,5},{5,4},{6,7},{7,6},{8,9},{9,8},{10,11... | collective-permute-start | bytes 4718600 | tf_op jit(solution)/shard_map/ppermute | solution.py:345
  293.8 3.4 %collective-permute-done.18.refs_1_ = bf16[8,4096]{1,0:T(8,128)(2,1)S(1)} collective-permute-done((bf16[8,4096]{1,0:T(8,128)(2,1)}, bf16[8,4096]{1,0:T(8,128)(2,1)S(1)}, u32[]{:S(2)}, u32[]{:S(2)}) %collective-permute-start.18) | collective-permute-done | bytes 65568 | tf_op jit(solution)/shard_map/ppermute | solution.py:345
  303.7 3.0 collective-permute-done.22.rest_2_
  309.9 6.6 %finish.1 = (bf16[192,4096]{1,0:T(8,128)(2,1)}, bf16[192,4096]{1,0:T(8,128)(2,1)}, f32[1]{0:T(128)}) custom-call(bf16[192,4096]{1,0:T(8,128)(2,1)} %get-tuple-element.63.own_one, bf16[192,4096]{1,0:T(8,128)(2,1)} %copy-done.4, bf16[192,4096]{1,0:T(8,128)(2,1)} %get-tuple-element.65.own_two, bf16[192,4096]{1,0:T(8,128)(2,1)} %copy-done.5, ...), custom_call_target="tpu_custom_call" | custom-call | flops 4096 | bytes 4096 | tf_op jit(solution)/shard_map/finish/pallas_call | solution.py:317
  (83 shorter events, 34.3 us)
Async XLA Ops:
  7.2 84.0 %all-gather.7.cloned.1.call-start = ((), (), s32[]{:S(2)}) async-start(), calls=%async_computation | async-start | bytes 1114112 | tf_op jit(solution)/shard_map/all_gather | solution.py:374
  10.6 187.5 %all-gather.9.cloned.1.call-start = ((), (), s32[]{:S(2)}) async-start(), calls=%async_computation.1 | async-start | bytes 1114112 | tf_op jit(solution)/shard_map/all_gather | solution.py:362
  10.6 41.6 %collective-permute-start.5 = (bf16[192,4096]{1,0:T(8,128)(2,1)S(1)}, bf16[192,4096]{1,0:T(8,128)(2,1)}, u32[]{:S(2)}, u32[]{:S(2)}) collective-permute-start(bf16[192,4096]{1,0:T(8,128)(2,1)S(1)} %copy-done.2), channel_id=1, source_target_pairs={{0,4},{1,5},{4,8},{5,9},{8,12},{9,13},{12,14},{13,15},{14,10},{15,... | collective-permute-start | bytes 4718600 | tf_op jit(solution)/shard_map/ppermute | solution.py:398
  12.8 73.1 %collective-permute-start = (bf16[192,4096]{1,0:T(8,128)(2,1)S(1)}, bf16[192,4096]{1,0:T(8,128)(2,1)}, u32[]{:S(2)}, u32[]{:S(2)}) collective-permute-start(bf16[192,4096]{1,0:T(8,128)(2,1)S(1)} %copy-done.3), channel_id=1, source_target_pairs={{0,4},{1,5},{4,8},{5,9},{8,12},{9,13},{12,14},{13,15},{14,10},{15,... | collective-permute-start | bytes 4718600 | tf_op jit(solution)/shard_map/ppermute | solution.py:398
  14.1 74.1 %collective-permute-start.2 = (bf16[192,4096]{1,0:T(8,128)(2,1)S(1)}, bf16[192,4096]{1,0:T(8,128)(2,1)}, u32[]{:S(2)}, u32[]{:S(2)}) collective-permute-start(bf16[192,4096]{1,0:T(8,128)(2,1)S(1)} %copy-done.3), channel_id=1, source_target_pairs={{4,0},{5,1},{8,4},{9,5},{12,8},{13,9},{14,12},{15,13},{10,14},{11,... | collective-permute-start | bytes 4718600 | tf_op jit(solution)/shard_map/ppermute | solution.py:398
  14.3 74.5 %collective-permute-start.6 = (bf16[192,4096]{1,0:T(8,128)(2,1)S(1)}, bf16[192,4096]{1,0:T(8,128)(2,1)S(1)}, u32[]{:S(2)}, u32[]{:S(2)}) collective-permute-start(bf16[192,4096]{1,0:T(8,128)(2,1)S(1)} %copy-done.2), channel_id=1, source_target_pairs={{4,0},{5,1},{8,4},{9,5},{12,8},{13,9},{14,12},{15,13},{10,14},{11,... | collective-permute-start | bytes 4718600 | tf_op jit(solution)/shard_map/ppermute | solution.py:398
  14.3 78.4 %collective-permute-start.7 = (bf16[192,4096]{1,0:T(8,128)(2,1)S(1)}, bf16[192,4096]{1,0:T(8,128)(2,1)}, u32[]{:S(2)}, u32[]{:S(2)}) collective-permute-start(bf16[192,4096]{1,0:T(8,128)(2,1)S(1)} %copy-done.3), channel_id=1, source_target_pairs={{0,1},{1,0},{2,3},{3,2},{4,5},{5,4},{6,7},{7,6},{8,9},{9,8},{10,11... | collective-permute-start | bytes 4718600 | tf_op jit(solution)/shard_map/ppermute | solution.py:345
  52.2 44.5 %collective-permute-start.4 = (bf16[192,4096]{1,0:T(8,128)(2,1)S(1)}, bf16[192,4096]{1,0:T(8,128)(2,1)}, u32[]{:S(2)}, u32[]{:S(2)}) collective-permute-start(bf16[192,4096]{1,0:T(8,128)(2,1)S(1)} %copy-done.2), channel_id=1, source_target_pairs={{0,1},{1,0},{2,3},{3,2},{4,5},{5,4},{6,7},{7,6},{8,9},{9,8},{10,11... | collective-permute-start | bytes 4718600 | tf_op jit(solution)/shard_map/ppermute | solution.py:345
  85.9 47.0 %collective-permute-start.1 = (bf16[192,4096]{1,0:T(8,128)(2,1)}, bf16[192,4096]{1,0:T(8,128)(2,1)}, u32[]{:S(2)}, u32[]{:S(2)}) collective-permute-start(bf16[192,4096]{1,0:T(8,128)(2,1)} %collective-permute-done.refs_5_), channel_id=1, source_target_pairs={{0,4},{1,5},{4,8},{5,9},{8,12},{9,13},{12,14},{13,15},{14,10},{15,... | collective-permute-start | bytes 4718600 | tf_op jit(solution)/shard_map/ppermute | solution.py:398
  88.2 44.7 %collective-permute-start.3 = (bf16[192,4096]{1,0:T(8,128)(2,1)}, bf16[192,4096]{1,0:T(8,128)(2,1)}, u32[]{:S(2)}, u32[]{:S(2)}) collective-permute-start(bf16[192,4096]{1,0:T(8,128)(2,1)} %collective-permute-done.2.refs_6_), channel_id=1, source_target_pairs={{4,0},{5,1},{8,4},{9,5},{12,8},{13,9},{14,12},{15,13},{10,14},{11,... | collective-permute-start | bytes 4718600 | tf_op jit(solution)/shard_map/ppermute | solution.py:398
  89.9 66.5 %collective-permute-start.8 = (bf16[192,4096]{1,0:T(8,128)(2,1)}, bf16[192,4096]{1,0:T(8,128)(2,1)}, u32[]{:S(2)}, u32[]{:S(2)}) collective-permute-start(bf16[192,4096]{1,0:T(8,128)(2,1)} %collective-permute-done.5.refs_3_), channel_id=1, source_target_pairs={{0,4},{1,5},{4,8},{5,9},{8,12},{9,13},{12,14},{13,15},{14,10},{15,... | collective-permute-start | bytes 4718600 | tf_op jit(solution)/shard_map/ppermute | solution.py:398
  132.9 39.3 %collective-permute-start.13 = (bf16[192,4096]{1,0:T(8,128)(2,1)S(1)}, bf16[192,4096]{1,0:T(8,128)(2,1)}, u32[]{:S(2)}, u32[]{:S(2)}) collective-permute-start(bf16[192,4096]{1,0:T(8,128)(2,1)S(1)} %copy-done.9), channel_id=1, source_target_pairs={{4,0},{5,1},{8,4},{9,5},{12,8},{13,9},{14,12},{15,13},{10,14},{11,... | collective-permute-start | bytes 4718600 | tf_op jit(solution)/shard_map/ppermute | solution.py:398
  156.5 39.4 %collective-permute-start.9 = (bf16[192,4096]{1,0:T(8,128)(2,1)}, bf16[192,4096]{1,0:T(8,128)(2,1)}, u32[]{:S(2)}, u32[]{:S(2)}) collective-permute-start(bf16[192,4096]{1,0:T(8,128)(2,1)} %collective-permute-done.8.refs_3_), channel_id=1, source_target_pairs={{0,4},{1,5},{4,8},{5,9},{8,12},{9,13},{12,14},{13,15},{14,10},{15,... | collective-permute-start | bytes 4718600 | tf_op jit(solution)/shard_map/ppermute | solution.py:398
  158.7 70.9 %collective-permute-start.11 = (bf16[192,4096]{1,0:T(8,128)(2,1)}, bf16[192,4096]{1,0:T(8,128)(2,1)}, u32[]{:S(2)}, u32[]{:S(2)}) collective-permute-start(bf16[192,4096]{1,0:T(8,128)(2,1)} %collective-permute-done.1.refs_5_), channel_id=1, source_target_pairs={{0,4},{1,5},{4,8},{5,9},{8,12},{9,13},{12,14},{13,15},{14,10},{15,... | collective-permute-start | bytes 4718600 | tf_op jit(solution)/shard_map/ppermute | solution.py:398
  160.0 69.6 %collective-permute-start.12 = (bf16[192,4096]{1,0:T(8,128)(2,1)}, bf16[192,4096]{1,0:T(8,128)(2,1)}, u32[]{:S(2)}, u32[]{:S(2)}) collective-permute-start(bf16[192,4096]{1,0:T(8,128)(2,1)} %collective-permute-done.3.refs_6_), channel_id=1, source_target_pairs={{4,0},{5,1},{8,4},{9,5},{12,8},{13,9},{14,12},{15,13},{10,14},{11,... | collective-permute-start | bytes 4718600 | tf_op jit(solution)/shard_map/ppermute | solution.py:398
  172.2 67.9 %collective-permute-start.15 = (bf16[192,4096]{1,0:T(8,128)(2,1)}, bf16[192,4096]{1,0:T(8,128)(2,1)S(1)}, u32[]{:S(2)}, u32[]{:S(2)}) collective-permute-start(bf16[192,4096]{1,0:T(8,128)(2,1)} %collective-permute-done.13.refs_4_), channel_id=1, source_target_pairs={{4,0},{5,1},{8,4},{9,5},{12,8},{13,9},{14,12},{15,13},{10,14},{11,... | collective-permute-start | bytes 4718600 | tf_op jit(solution)/shard_map/ppermute | solution.py:398
  195.8 67.4 %collective-permute-start.10 = (bf16[192,4096]{1,0:T(8,128)(2,1)}, bf16[192,4096]{1,0:T(8,128)(2,1)S(1)}, u32[]{:S(2)}, u32[]{:S(2)}) collective-permute-start(bf16[192,4096]{1,0:T(8,128)(2,1)} %collective-permute-done.9.refs_3_), channel_id=1, source_target_pairs={{0,4},{1,5},{4,8},{5,9},{8,12},{9,13},{12,14},{13,15},{14,10},{15,... | collective-permute-start | bytes 4718600 | tf_op jit(solution)/shard_map/ppermute | solution.py:403
  229.5 44.3 %collective-permute-start.14 = (bf16[192,4096]{1,0:T(8,128)(2,1)}, bf16[192,4096]{1,0:T(8,128)(2,1)S(1)}, u32[]{:S(2)}, u32[]{:S(2)}) collective-permute-start(bf16[192,4096]{1,0:T(8,128)(2,1)} %collective-permute-done.12.refs_6_), channel_id=1, source_target_pairs={{4,0},{5,1},{8,4},{9,5},{12,8},{13,9},{14,12},{15,13},{10,14},{11,... | collective-permute-start | bytes 4718600 | tf_op jit(solution)/shard_map/ppermute | solution.py:404
  288.2 20.1 %collective-permute-start.16 = (bf16[192,4096]{1,0:T(8,128)(2,1)}, bf16[192,4096]{1,0:T(8,128)(2,1)S(1)}, u32[]{:S(2)}, u32[]{:S(2)}) collective-permute-start(bf16[192,4096]{1,0:T(8,128)(2,1)} %get-tuple-element.64), channel_id=1, source_target_pairs={{0,1},{1,0},{2,3},{3,2},{4,5},{5,4},{6,7},{7,6},{8,9},{9,8},{10,11... | collective-permute-start | bytes 4718600 | tf_op jit(solution)/shard_map/ppermute | solution.py:345
  291.6 16.6 %collective-permute-start.17 = (bf16[192,4096]{1,0:T(8,128)(2,1)}, bf16[192,4096]{1,0:T(8,128)(2,1)S(1)}, u32[]{:S(2)}, u32[]{:S(2)}) collective-permute-start(bf16[192,4096]{1,0:T(8,128)(2,1)} %get-tuple-element.66), channel_id=1, source_target_pairs={{0,1},{1,0},{2,3},{3,2},{4,5},{5,4},{6,7},{7,6},{8,9},{9,8},{10,11... | collective-permute-start | bytes 4718600 | tf_op jit(solution)/shard_map/ppermute | solution.py:345
  291.7 5.5 %collective-permute-start.18 = (bf16[8,4096]{1,0:T(8,128)(2,1)}, bf16[8,4096]{1,0:T(8,128)(2,1)S(1)}, u32[]{:S(2)}, u32[]{:S(2)}) collective-permute-start(bf16[8,4096]{1,0:T(8,128)(2,1)} %get-tuple-element.68.refs_0_), channel_id=1, source_target_pairs={{0,1},{1,0},{2,3},{3,2},{4,5},{5,4},{6,7},{7,6},{8,9},{9,8},{10,11... | collective-permute-start | bytes 196616 | tf_op jit(solution)/shard_map/ppermute | solution.py:345
  292.1 5.4 %collective-permute-start.20 = (bf16[8,4096]{1,0:T(8,128)(2,1)}, bf16[8,4096]{1,0:T(8,128)(2,1)S(1)}, u32[]{:S(2)}, u32[]{:S(2)}) collective-permute-start(bf16[8,4096]{1,0:T(8,128)(2,1)} %get-tuple-element.68.refs_0_), channel_id=1, source_target_pairs={{0,3},{1,2},{2,1},{3,0},{4,7},{5,6},{6,5},{7,4},{8,11},{9,10},{10,... | collective-permute-start | bytes 196616 | tf_op jit(solution)/shard_map/ppermute | solution.py:345
  301.4 5.3 %collective-permute-start.22 = (bf16[8,4096]{1,0:T(8,128)(2,1)}, bf16[8,4096]{1,0:T(8,128)(2,1)S(1)}, u32[]{:S(2)}, u32[]{:S(2)}) collective-permute-start(bf16[8,4096]{1,0:T(8,128)(2,1)} %add_totals.1.rest_0_), channel_id=1, source_target_pairs={{0,8},{1,9},{2,10},{3,11},{4,12},{5,13},{6,14},{7,15},{8,0},{9,1},... | collective-permute-start | bytes 196616 | tf_op jit(solution)/shard_map/ppermute | solution.py:345
  302.1 6.2 %collective-permute-start.23 = (bf16[8,4096]{1,0:T(8,128)(2,1)}, bf16[8,4096]{1,0:T(8,128)(2,1)S(1)}, u32[]{:S(2)}, u32[]{:S(2)}) collective-permute-start(bf16[8,4096]{1,0:T(8,128)(2,1)} %add_totals.1.rest_0_), channel_id=1, source_target_pairs={{0,12},{1,13},{2,14},{3,15},{4,8},{5,9},{6,10},{7,11},{8,4},{9,5},... | collective-permute-start | bytes 196616 | tf_op jit(solution)/shard_map/ppermute | solution.py:345
  (19 other events, 80.5 us)
Sparse Core Ops, SparseCore 0:
  10.8 43.8 all-gather.6
  133.0 43.2 all-gather.8

commit v14 on v13

--- a/solution.py
+++ b/solution.py
@@ -358,11 +358,8 @@
         sums = [jnp.sum(one, axis=0), jnp.sum(two, axis=0), jnp.sum(one * two, axis=0)]
         return jnp.stack([*sums, jnp.zeros_like(sums[0])])
 
-    def summed(sums):
-        return jnp.sum(lax.all_gather(sums, "batch", axis=0), axis=0)
-
-    def statistics(gathered):
-        sums = jnp.sum(gathered, axis=0) / samples
+    def statistics(sums):
+        sums = [value / samples for value in sums]
         inv_one = 1.0 / jnp.sqrt(sums[1] - sums[0] * sums[0] + 1e-05)
         inv_two = 1.0 / jnp.sqrt(sums[3] - sums[2] * sums[2] + 1e-05)
         return jnp.stack([sums[0], inv_one, sums[2], inv_two])
@@ -371,28 +368,31 @@
         both = jnp.concatenate([view, far], axis=0).astype(jnp.float32)
         return ((both - mean) * inv).astype(jnp.bfloat16)
 
-    gathered = lax.all_gather(first_sums(view_one, view_two), "batch", axis=0)
+    sums = first_sums(view_one, view_two)
+    sums = lax.psum(tuple(sums[row] for row in range(4)), "batch")
     far_one, far_two = swapped(view_one, 1), swapped(view_two, 1)
     ends = [[view_one, view_one], [view_two, view_two]]
     arrived = []
     loss = jnp.zeros((8, 128), jnp.float32)
     for hop in range(hops):
-        if hop == 1:
-            *arrived[0][0], gathered = lax.optimization_barrier((*ends[0], gathered))
-            stat = statistics(gathered)
+        if hop == 2:
+            ends[0][0], *sums = lax.optimization_barrier((ends[0][0], *sums))
+            stat = statistics(sums)
             q_one = normed(view_one, far_one, stat[0], stat[1])
             q_two = normed(view_two, far_two, stat[2], stat[3])
+            *flat, q_one, q_two, norm_sums = lax.optimization_barrier(
+                (*ends[0], *ends[1], q_one, q_two, norm_totals(q_one, q_two))
+            )
+            ends = [flat[:2], flat[2:]]
+            arrived[-1] = [list(pair) for pair in ends]
+            norm_sums = jnp.sum(lax.all_gather(norm_sums, "batch", axis=0), axis=0)
             loss, *acc = attend(q_one, q_two, stat, [view_one], [view_two], loss, None, False)
-        if hop > 1:
-            loss, *acc = attend(q_one, q_two, stat, *arrived[hop - 2], loss, acc, False)
-            tied = (q_one, q_two, norm_totals(q_one, q_two)) if hop == 2 else (norm_sums,)
-            *ends[1], tied, loss = lax.optimization_barrier((*ends[1], tied, loss))
+        if hop > 2:
+            for blocks in arrived[:2] if hop == 3 else arrived[hop - 2 : hop - 1]:
+                loss, *acc = attend(q_one, q_two, stat, *blocks, loss, acc, False)
+            *flat, norm_sums, loss = lax.optimization_barrier((*ends[0], *ends[1], norm_sums, loss))
+            ends = [flat[:2], flat[2:]]
             arrived[-1] = [list(pair) for pair in ends]
-            if hop == 2:
-                q_one, q_two, sums = tied
-                norm_sums = summed(sums)
-            else:
-                (norm_sums,) = tied
         if hop < hops - 1:
             ends = [
                 [lax.ppermute(up, "batch", ahead), lax.ppermute(down, "batch", behind)]
@@ -420,7 +420,7 @@
 def solution(mesh):
     placed = (P(("groups", "batch"), "feat"), P(("groups", "batch"), "feat"))
     batches = mesh.shape["batch"]
-    ringed = mesh.shape["feat"] == 1 and batches >= 8 and batches & (batches - 1) == 0
+    ringed = mesh.shape["feat"] == 1 and batches >= 16 and batches & (batches - 1) == 0
     return jax.shard_map(
         ring_shards if ringed else shards,
         mesh=mesh,

time: 326 us -> 313 us (0.960)
  waiting for transfers between devices: 172 us -> 161 us
  other arithmetic: 13.5 us -> 10.2 us
    psum x0 -> x1, waiting for transfers between devices: none -> 28.1 us  [ring_shards(): sums = lax.psum(tuple((sums[row] for row in range(4))), 'batch')]
    ppermute x6, waiting for transfers between devices: 21.6 us -> 0.89 us  [ring_shards(): lax.ppermute(down, 'batch', behind)]
    ppermute x6, waiting for transfers between devices: 126 us -> 109 us  [ring_shards(): lax.ppermute(up, 'batch', ahead)]
    ppermute x1, waiting for transfers between devices: 5.58 us -> 14.8 us  [ring_shards(): last_one = lax.ppermute(ends[0][0], 'batch', ahead)]
    ppermute x1, waiting for transfers between devices: 10.6 us -> 1.92 us  [ring_shards(): last_two = lax.ppermute(ends[1][1], 'batch', behind)]
    ppermute x6, starting transfers between devices: 0.6 us -> 5.48 us  [ring_shards(): lax.ppermute(down, 'batch', behind)]
    ppermute x6, starting transfers between devices: 10.6 us -> 6.75 us  [ring_shards(): lax.ppermute(up, 'batch', ahead)]
    convert_element_type x2, other arithmetic: 7.91 us -> 4.58 us  [normed(): return ((both - mean) * inv).astype(jnp.bfloat16)]
  transfers between devices with their start and end apart: 26 -> 26, of which waited for: 14 -> 12; matrix products, arithmetic and copies ran while one was open for 4% -> 4% of each run, Pallas kernels for 20% -> 22%
where the time goes in v14:
time: 313 us; the launch traced here: 309 us
  waiting for transfers between devices  161 us (51%)
  Pallas kernels  88.4 us (28%)
  starting transfers between devices  27.9 us (9%)
  between operations  14.2 us (5%)
  other arithmetic  10.2 us (3%)
  local copies, waits for them, and re-layouts  6.95 us (2%)
    ppermute x6, waiting for transfers between devices, ring_shards(): lax.ppermute(up, 'batch', ahead)  109 us
    pallas_call x5, Pallas kernels, attend(): pl.pallas_call(functools.partial(attend_kernel, count, begins, ends), gri...  76.9 us
    psum x1, waiting for transfers between devices, ring_shards(): sums = lax.psum(tuple((sums[row] for row in range(4))), 'batch')  28.1 us
    ppermute x1, waiting for transfers between devices, ring_shards(): last_one = lax.ppermute(ends[0][0], 'batch', ahead)  14.8 us
    ppermute x10, starting transfers between devices, swapped(): return lax.ppermute(value, 'batch', [(i, i ^ bit) for i in range(batches)])  12.5 us
    ppermute x6, starting transfers between devices, ring_shards(): lax.ppermute(up, 'batch', ahead)  6.75 us
    ppermute x10, waiting for transfers between devices, swapped(): return lax.ppermute(value, 'batch', [(i, i ^ bit) for i in range(batches)])  6.73 us
    pallas_call x1, Pallas kernels, finish_grads(): pl.pallas_call(functools.partial(finish_kernel, samples, width), grid=(ti...  6.63 us
  transfers between devices with their start and end apart: 26, of which 12 were waited for; matrix products, arithmetic and copies ran while one was open for 4% of the time, Pallas kernels for 22%

profile of v14, /device:TPU:1, one launch (start us, length us, event | category | flops | bytes accessed | tf_op | source)
XLA Modules:
  0.0 308.9 jit_solution(9373235344982161294)
XLA Ops:
  7.2 2.2 collective-permute-start
  10.9 32.9 %collective-permute-done.refs_3_ = bf16[192,4096]{1,0:T(8,128)(2,1)} collective-permute-done((bf16[192,4096]{1,0:T(8,128)(2,1)}, bf16[192,4096]{1,0:T(8,128)(2,1)}, u32[]{:S(2)}, u32[]{:S(2)}) %collective-permute-start) | collective-permute-done | bytes 1572896 | tf_op jit(solution)/shard_map/ppermute | solution.py:398
  45.0 3.0 collective-permute-start.9
  48.0 3.2 %first_sums.1 = f32[4,4096]{1,0:T(4,128)} custom-call(bf16[192,4096]{1,0:T(8,128)(2,1)} %refs_3_.1, bf16[192,4096]{1,0:T(8,128)(2,1)} %refs_4_.1), custom_call_target="tpu_custom_call" | custom-call | flops 4096 | bytes 4096 | tf_op jit(solution)/shard_map/first_sums/pallas_call | solution.py:127
  52.9 24.9 %collective-permute-done.4.refs_5_ = bf16[192,4096]{1,0:T(8,128)(2,1)} collective-permute-done((bf16[192,4096]{1,0:T(8,128)(2,1)}, bf16[192,4096]{1,0:T(8,128)(2,1)}, u32[]{:S(2)}, u32[]{:S(2)}) %collective-permute-start.4) | collective-permute-done | bytes 1572896 | tf_op jit(solution)/shard_map/ppermute | solution.py:398
  80.4 31.5 %collective-permute-done.1.refs_3_ = bf16[192,4096]{1,0:T(8,128)(2,1)} collective-permute-done((bf16[192,4096]{1,0:T(8,128)(2,1)}, bf16[192,4096]{1,0:T(8,128)(2,1)}, u32[]{:S(2)}, u32[]{:S(2)}) %collective-permute-start.1) | collective-permute-done | bytes 1572896 | tf_op jit(solution)/shard_map/ppermute | solution.py:398
  111.8 1.9 collective-permute-start.7
  113.8 28.1 %all-reduce.3.cloned.1.call-done = (f32[4096]{0:T(1024)}, f32[4096]{0:T(1024)}, f32[4096]{0:T(1024)}, f32[4096]{0:T(1024)}) async-done(((f32[4096]{0:T(1024)}, f32[4096]{0:T(1024)}, f32[4096]{0:T(1024)}, f32[4096]{0:T(1024)}), (f32[4096]{0:T(1024)}, f32[4096]{0:T(1024)}, f32[4096]{0:T(1024)}, f32[4096]{0:T(1024)})) %all-reduce.3.cloned.1.call-update) | async-done | bytes 65552 | tf_op jit(solution)/shard_map/psum | solution.py:372
  144.2 3.8 %multiply_convert_fusion.1.refs_0_.norm_one = bf16[384,4096]{1,0:T(8,128)(2,1)S(1)} fusion(bf16[192,4096]{1,0:T(8,128)(2,1)} %collective-permute-done.8, bf16[192,4096]{1,0:T(8,128)(2,1)} %refs_3_.1, f32[4096]{0:T(1024)S(1)} %get-tuple-element.93, f32[4096]{0:T(1024)S(1)} %get-tuple-element.92), kind=kLoop, calls=%fused_computation.1 | loop fusion | flops 11010048 | bytes 6324224 | tf_op jit(solution)/shard_map/convert_element_type | solution.py:369
  154.7 11.7 %attend.5 = (f32[8,128]{1,0:T(8,128)}, f32[384,4096]{1,0:T(8,128)}, f32[384,4096]{1,0:T(8,128)}) custom-call(bf16[384,4096]{1,0:T(8,128)(2,1)} %copy-done.1, bf16[384,4096]{1,0:T(8,128)(2,1)} %copy-done, f32[4,4096]{1,0:T(4,128)} %pad_maximum_fusion.refs_2_.stat_ref, bf16[192,4096]{1,0:T(8,128)(2,1)} %refs_3_.1, ...), custom_call_target="tpu_custom_call", output_to_operand_aliasing={{0}: (5, {})} | custom-call | flops 4096 | bytes 4096 | tf_op jit(solution)/shard_map/attend/pallas_call | solution.py:251
  166.4 17.8 %attend.6 = (f32[8,128]{1,0:T(8,128)}, f32[384,4096]{1,0:T(8,128)}, f32[384,4096]{1,0:T(8,128)}) custom-call(bf16[384,4096]{1,0:T(8,128)(2,1)} %copy-done.1, bf16[384,4096]{1,0:T(8,128)(2,1)} %copy-done, f32[4,4096]{1,0:T(4,128)} %pad_maximum_fusion.refs_2_.stat_ref, ...), custom_call_target="tpu_custom_call", output_to_operand_aliasing={{0}: (7, {}), {1}: (8, {}), {2}: (9, {})} | custom-call | flops 4096 | bytes 4096 | tf_op jit(solution)/shard_map/attend/pallas_call | solution.py:251
  184.2 17.8 %attend.7 = (f32[8,128]{1,0:T(8,128)}, f32[384,4096]{1,0:T(8,128)}, f32[384,4096]{1,0:T(8,128)}) custom-call(bf16[384,4096]{1,0:T(8,128)(2,1)} %copy-done.1, bf16[384,4096]{1,0:T(8,128)(2,1)} %copy-done, f32[4,4096]{1,0:T(4,128)} %pad_maximum_fusion.refs_2_.stat_ref, ...), custom_call_target="tpu_custom_call", output_to_operand_aliasing={{0}: (7, {}), {1}: (8, {}), {2}: (9, {})} | custom-call | flops 4096 | bytes 4096 | tf_op jit(solution)/shard_map/attend/pallas_call | solution.py:251
  202.0 2.0 reduce_sum.39.norm_ref
  204.0 19.4 %collective-permute-done.12.refs_5_ = bf16[192,4096]{1,0:T(8,128)(2,1)} collective-permute-done((bf16[192,4096]{1,0:T(8,128)(2,1)}, bf16[192,4096]{1,0:T(8,128)(2,1)}, u32[]{:S(2)}, u32[]{:S(2)}) %collective-permute-start.12) | collective-permute-done | bytes 1572896 | tf_op jit(solution)/shard_map/ppermute | solution.py:398
  224.3 3.0 collective-permute-start.14
  227.3 16.3 %attend.8 = (f32[8,128]{1,0:T(8,128)}, bf16[384,4096]{1,0:T(8,128)(2,1)}, bf16[384,4096]{1,0:T(8,128)(2,1)}) custom-call(bf16[384,4096]{1,0:T(8,128)(2,1)} %copy-done.1, bf16[384,4096]{1,0:T(8,128)(2,1)} %copy-done, f32[4,4096]{1,0:T(4,128)} %pad_maximum_fusion.refs_2_.stat_ref, bf16[192,4096]{1,0:T(8,128)(2,1)} %copy-done.7, ...), custom_call_target="tpu_custom_call", output_to_operand_aliasing={{0}: (7, {})} | custom-call | flops 4096 | bytes 4096 | tf_op jit(solution)/shard_map/attend/pallas_call | solution.py:251
  243.7 14.8 %collective-permute-done.14.refs_3_ = bf16[192,4096]{1,0:T(8,128)(2,1)S(1)} collective-permute-done((bf16[192,4096]{1,0:T(8,128)(2,1)S(1)}, bf16[192,4096]{1,0:T(8,128)(2,1)S(1)}, u32[]{:S(2)}, u32[]{:S(2)}) %collective-permute-start.14) | collective-permute-done | bytes 1572896 | tf_op jit(solution)/shard_map/ppermute | solution.py:403
  258.5 1.9 collective-permute-done.15.refs_4_
  261.6 13.3 %attend.9 = (f32[8,128]{1,0:T(8,128)}, bf16[192,4096]{1,0:T(8,128)(2,1)}, bf16[192,4096]{1,0:T(8,128)(2,1)}, bf16[192,4096]{1,0:T(8,128)(2,1)}, bf16[192,4096]{1,0:T(8,128)(2,1)}, /*index=5*/bf16[8,4096]{1,0:T(8,128)(2,1)}) custom-call(bf16[384,4096]{1,0:T(8,128)(2,1)} %copy-done.1, bf16[384,4096]{1,0:T(8,128)(2,1)} %copy-done, ...), custom_call_target="tpu_custom_call", output_to_operand_aliasing={{0}: (5, {})} | custom-call | flops 4096 | bytes 4096 | tf_op jit(solution)/shard_map/attend/pallas_call | solution.py:251
  274.9 3.8 %collective-permute-start.16 = (bf16[192,4096]{1,0:T(8,128)(2,1)}, bf16[192,4096]{1,0:T(8,128)(2,1)S(1)}, u32[]{:S(2)}, u32[]{:S(2)}) collective-permute-start(bf16[192,4096]{1,0:T(8,128)(2,1)} %get-tuple-element.74), channel_id=1, source_target_pairs={{0,1},{1,0},{2,3},{3,2},{4,5},{5,4},{6,7},{7,6},{8,9},{9,8},{10,11... | collective-permute-start | bytes 4718600 | tf_op jit(solution)/shard_map/ppermute | solution.py:345
  280.9 3.4 %collective-permute-done.18.refs_1_ = bf16[8,4096]{1,0:T(8,128)(2,1)S(1)} collective-permute-done((bf16[8,4096]{1,0:T(8,128)(2,1)}, bf16[8,4096]{1,0:T(8,128)(2,1)S(1)}, u32[]{:S(2)}, u32[]{:S(2)}) %collective-permute-start.18) | collective-permute-done | bytes 65568 | tf_op jit(solution)/shard_map/ppermute | solution.py:345
  285.5 1.7 add_totals.1.rest_0_
  287.9 2.9 collective-permute-start.23
  295.4 6.6 %finish.1 = (bf16[192,4096]{1,0:T(8,128)(2,1)}, bf16[192,4096]{1,0:T(8,128)(2,1)}, f32[1]{0:T(128)}) custom-call(bf16[192,4096]{1,0:T(8,128)(2,1)} %get-tuple-element.73.own_one, bf16[192,4096]{1,0:T(8,128)(2,1)} %copy-done.3, bf16[192,4096]{1,0:T(8,128)(2,1)} %get-tuple-element.75.own_two, bf16[192,4096]{1,0:T(8,128)(2,1)} %copy-done.4, ...), custom_call_target="tpu_custom_call" | custom-call | flops 4096 | bytes 4096 | tf_op jit(solution)/shard_map/finish/pallas_call | solution.py:317
  (79 shorter events, 26.7 us)
Async XLA Ops:
  7.2 134.7 %all-reduce.3.cloned.1.call-start = ((), (), s32[]{:S(2)}) async-start(), calls=%async_computation.1 | async-start | bytes 131072 | tf_op jit(solution)/shard_map/psum | solution.py:372
  7.2 36.6 %collective-permute-start = (bf16[192,4096]{1,0:T(8,128)(2,1)}, bf16[192,4096]{1,0:T(8,128)(2,1)}, u32[]{:S(2)}, u32[]{:S(2)}) collective-permute-start(bf16[192,4096]{1,0:T(8,128)(2,1)} %refs_3_.1), channel_id=1, source_target_pairs={{0,4},{1,5},{4,8},{5,9},{8,12},{9,13},{12,14},{13,15},{14,10},{15,... | collective-permute-start | bytes 4718600 | tf_op jit(solution)/shard_map/ppermute | solution.py:398
  9.4 41.7 %collective-permute-start.2 = (bf16[192,4096]{1,0:T(8,128)(2,1)}, bf16[192,4096]{1,0:T(8,128)(2,1)}, u32[]{:S(2)}, u32[]{:S(2)}) collective-permute-start(bf16[192,4096]{1,0:T(8,128)(2,1)} %refs_3_.1), channel_id=1, source_target_pairs={{4,0},{5,1},{8,4},{9,5},{12,8},{13,9},{14,12},{15,13},{10,14},{11,... | collective-permute-start | bytes 4718600 | tf_op jit(solution)/shard_map/ppermute | solution.py:398
  9.4 68.5 %collective-permute-start.4 = (bf16[192,4096]{1,0:T(8,128)(2,1)}, bf16[192,4096]{1,0:T(8,128)(2,1)}, u32[]{:S(2)}, u32[]{:S(2)}) collective-permute-start(bf16[192,4096]{1,0:T(8,128)(2,1)} %refs_4_.1), channel_id=1, source_target_pairs={{0,4},{1,5},{4,8},{5,9},{8,12},{9,13},{12,14},{13,15},{14,10},{15,... | collective-permute-start | bytes 4718600 | tf_op jit(solution)/shard_map/ppermute | solution.py:398
  10.9 68.5 %collective-permute-start.6 = (bf16[192,4096]{1,0:T(8,128)(2,1)}, bf16[192,4096]{1,0:T(8,128)(2,1)}, u32[]{:S(2)}, u32[]{:S(2)}) collective-permute-start(bf16[192,4096]{1,0:T(8,128)(2,1)} %refs_4_.1), channel_id=1, source_target_pairs={{4,0},{5,1},{8,4},{9,5},{12,8},{13,9},{14,12},{15,13},{10,14},{11,... | collective-permute-start | bytes 4718600 | tf_op jit(solution)/shard_map/ppermute | solution.py:398
  43.8 68.1 %collective-permute-start.1 = (bf16[192,4096]{1,0:T(8,128)(2,1)}, bf16[192,4096]{1,0:T(8,128)(2,1)}, u32[]{:S(2)}, u32[]{:S(2)}) collective-permute-start(bf16[192,4096]{1,0:T(8,128)(2,1)} %collective-permute-done.refs_3_), channel_id=1, source_target_pairs={{0,4},{1,5},{4,8},{5,9},{8,12},{9,13},{12,14},{13,15},{14,10},{15,... | collective-permute-start | bytes 4718600 | tf_op jit(solution)/shard_map/ppermute | solution.py:398
  45.0 98.4 %collective-permute-start.9 = (bf16[192,4096]{1,0:T(8,128)(2,1)}, bf16[192,4096]{1,0:T(8,128)(2,1)S(1)}, u32[]{:S(2)}, u32[]{:S(2)}) collective-permute-start(bf16[192,4096]{1,0:T(8,128)(2,1)} %refs_4_.1), channel_id=1, source_target_pairs={{0,1},{1,0},{2,3},{3,2},{4,5},{5,4},{6,7},{7,6},{8,9},{9,8},{10,11... | collective-permute-start | bytes 4718600 | tf_op jit(solution)/shard_map/ppermute | solution.py:345
  51.1 93.1 %collective-permute-start.8 = (bf16[192,4096]{1,0:T(8,128)(2,1)}, bf16[192,4096]{1,0:T(8,128)(2,1)}, u32[]{:S(2)}, u32[]{:S(2)}) collective-permute-start(bf16[192,4096]{1,0:T(8,128)(2,1)} %refs_3_.1), channel_id=1, source_target_pairs={{0,1},{1,0},{2,3},{3,2},{4,5},{5,4},{6,7},{7,6},{8,9},{9,8},{10,11... | collective-permute-start | bytes 4718600 | tf_op jit(solution)/shard_map/ppermute | solution.py:345
  52.8 149.2 %all-gather.4.cloned.1.call-start = ((), (), s32[]{:S(2)}) async-start(), calls=%async_computation | async-start | bytes 1114112 | tf_op jit(solution)/shard_map/all_gather | solution.py:388
  77.9 72.5 %collective-permute-start.3 = (bf16[192,4096]{1,0:T(8,128)(2,1)}, bf16[192,4096]{1,0:T(8,128)(2,1)}, u32[]{:S(2)}, u32[]{:S(2)}) collective-permute-start(bf16[192,4096]{1,0:T(8,128)(2,1)} %collective-permute-done.2.refs_4_), channel_id=1, source_target_pairs={{4,0},{5,1},{8,4},{9,5},{12,8},{13,9},{14,12},{15,13},{10,14},{11,... | collective-permute-start | bytes 4718600 | tf_op jit(solution)/shard_map/ppermute | solution.py:398
  79.3 71.1 %collective-permute-start.5 = (bf16[192,4096]{1,0:T(8,128)(2,1)}, bf16[192,4096]{1,0:T(8,128)(2,1)}, u32[]{:S(2)}, u32[]{:S(2)}) collective-permute-start(bf16[192,4096]{1,0:T(8,128)(2,1)} %collective-permute-done.4.refs_5_), channel_id=1, source_target_pairs={{0,4},{1,5},{4,8},{5,9},{8,12},{9,13},{12,14},{13,15},{14,10},{15,... | collective-permute-start | bytes 4718600 | tf_op jit(solution)/shard_map/ppermute | solution.py:398
  111.8 38.6 %collective-permute-start.7 = (bf16[192,4096]{1,0:T(8,128)(2,1)}, bf16[192,4096]{1,0:T(8,128)(2,1)}, u32[]{:S(2)}, u32[]{:S(2)}) collective-permute-start(bf16[192,4096]{1,0:T(8,128)(2,1)} %collective-permute-done.6.refs_6_), channel_id=1, source_target_pairs={{4,0},{5,1},{8,4},{9,5},{12,8},{13,9},{14,12},{15,13},{10,14},{11,... | collective-permute-start | bytes 4718600 | tf_op jit(solution)/shard_map/ppermute | solution.py:398
  150.5 53.6 %collective-permute-start.10 = (bf16[192,4096]{1,0:T(8,128)(2,1)}, bf16[192,4096]{1,0:T(8,128)(2,1)S(1)}, u32[]{:S(2)}, u32[]{:S(2)}) collective-permute-start(bf16[192,4096]{1,0:T(8,128)(2,1)} %collective-permute-done.1.refs_3_), channel_id=1, source_target_pairs={{0,4},{1,5},{4,8},{5,9},{8,12},{9,13},{12,14},{13,15},{14,10},{15,... | collective-permute-start | bytes 4718600 | tf_op jit(solution)/shard_map/ppermute | solution.py:398
  150.5 53.5 %collective-permute-start.11 = (bf16[192,4096]{1,0:T(8,128)(2,1)}, bf16[192,4096]{1,0:T(8,128)(2,1)}, u32[]{:S(2)}, u32[]{:S(2)}) collective-permute-start(bf16[192,4096]{1,0:T(8,128)(2,1)} %collective-permute-done.3.refs_4_), channel_id=1, source_target_pairs={{4,0},{5,1},{8,4},{9,5},{12,8},{13,9},{14,12},{15,13},{10,14},{11,... | collective-permute-start | bytes 4718600 | tf_op jit(solution)/shard_map/ppermute | solution.py:398
  152.0 71.4 %collective-permute-start.12 = (bf16[192,4096]{1,0:T(8,128)(2,1)}, bf16[192,4096]{1,0:T(8,128)(2,1)}, u32[]{:S(2)}, u32[]{:S(2)}) collective-permute-start(bf16[192,4096]{1,0:T(8,128)(2,1)} %collective-permute-done.5.refs_5_), channel_id=1, source_target_pairs={{0,4},{1,5},{4,8},{5,9},{8,12},{9,13},{12,14},{13,15},{14,10},{15,... | collective-permute-start | bytes 4718600 | tf_op jit(solution)/shard_map/ppermute | solution.py:398
  152.8 71.5 %collective-permute-start.13 = (bf16[192,4096]{1,0:T(8,128)(2,1)}, bf16[192,4096]{1,0:T(8,128)(2,1)S(1)}, u32[]{:S(2)}, u32[]{:S(2)}) collective-permute-start(bf16[192,4096]{1,0:T(8,128)(2,1)} %collective-permute-done.7.refs_6_), channel_id=1, source_target_pairs={{4,0},{5,1},{8,4},{9,5},{12,8},{13,9},{14,12},{15,13},{10,14},{11,... | collective-permute-start | bytes 4718600 | tf_op jit(solution)/shard_map/ppermute | solution.py:398
  224.3 34.2 %collective-permute-start.14 = (bf16[192,4096]{1,0:T(8,128)(2,1)S(1)}, bf16[192,4096]{1,0:T(8,128)(2,1)S(1)}, u32[]{:S(2)}, u32[]{:S(2)}) collective-permute-start(bf16[192,4096]{1,0:T(8,128)(2,1)S(1)} %collective-permute-done.10.refs_3_), channel_id=1, source_target_pairs={{0,4},{1,5},{4,8},{5,9},{8,12},{9,13},{12,14},{13,15},{14,10},{15,... | collective-permute-start | bytes 4718600 | tf_op jit(solution)/shard_map/ppermute | solution.py:403
  227.3 33.1 %collective-permute-start.15 = (bf16[192,4096]{1,0:T(8,128)(2,1)S(1)}, bf16[192,4096]{1,0:T(8,128)(2,1)S(1)}, u32[]{:S(2)}, u32[]{:S(2)}) collective-permute-start(bf16[192,4096]{1,0:T(8,128)(2,1)S(1)} %collective-permute-done.13.refs_6_), channel_id=1, source_target_pairs={{4,0},{5,1},{8,4},{9,5},{12,8},{13,9},{14,12},{15,13},{10,14},{11,... | collective-permute-start | bytes 4718600 | tf_op jit(solution)/shard_map/ppermute | solution.py:404
  274.9 18.9 %collective-permute-start.16 = (bf16[192,4096]{1,0:T(8,128)(2,1)}, bf16[192,4096]{1,0:T(8,128)(2,1)S(1)}, u32[]{:S(2)}, u32[]{:S(2)}) collective-permute-start(bf16[192,4096]{1,0:T(8,128)(2,1)} %get-tuple-element.74), channel_id=1, source_target_pairs={{0,1},{1,0},{2,3},{3,2},{4,5},{5,4},{6,7},{7,6},{8,9},{9,8},{10,11... | collective-permute-start | bytes 4718600 | tf_op jit(solution)/shard_map/ppermute | solution.py:345
  278.6 15.1 %collective-permute-start.17 = (bf16[192,4096]{1,0:T(8,128)(2,1)}, bf16[192,4096]{1,0:T(8,128)(2,1)S(1)}, u32[]{:S(2)}, u32[]{:S(2)}) collective-permute-start(bf16[192,4096]{1,0:T(8,128)(2,1)} %get-tuple-element.76), channel_id=1, source_target_pairs={{0,1},{1,0},{2,3},{3,2},{4,5},{5,4},{6,7},{7,6},{8,9},{9,8},{10,11... | collective-permute-start | bytes 4718600 | tf_op jit(solution)/shard_map/ppermute | solution.py:345
  278.7 5.5 %collective-permute-start.18 = (bf16[8,4096]{1,0:T(8,128)(2,1)}, bf16[8,4096]{1,0:T(8,128)(2,1)S(1)}, u32[]{:S(2)}, u32[]{:S(2)}) collective-permute-start(bf16[8,4096]{1,0:T(8,128)(2,1)} %get-tuple-element.78.refs_0_), channel_id=1, source_target_pairs={{0,1},{1,0},{2,3},{3,2},{4,5},{5,4},{6,7},{7,6},{8,9},{9,8},{10,11... | collective-permute-start | bytes 196616 | tf_op jit(solution)/shard_map/ppermute | solution.py:345
  279.1 5.1 %collective-permute-start.19 = (bf16[8,4096]{1,0:T(8,128)(2,1)}, bf16[8,4096]{1,0:T(8,128)(2,1)S(1)}, u32[]{:S(2)}, u32[]{:S(2)}) collective-permute-start(bf16[8,4096]{1,0:T(8,128)(2,1)} %get-tuple-element.78.refs_0_), channel_id=1, source_target_pairs={{0,2},{1,3},{2,0},{3,1},{4,6},{5,7},{6,4},{7,5},{8,10},{9,11},{10,... | collective-permute-start | bytes 196616 | tf_op jit(solution)/shard_map/ppermute | solution.py:345
  279.2 5.4 %collective-permute-start.20 = (bf16[8,4096]{1,0:T(8,128)(2,1)}, bf16[8,4096]{1,0:T(8,128)(2,1)S(1)}, u32[]{:S(2)}, u32[]{:S(2)}) collective-permute-start(bf16[8,4096]{1,0:T(8,128)(2,1)} %get-tuple-element.78.refs_0_), channel_id=1, source_target_pairs={{0,3},{1,2},{2,1},{3,0},{4,7},{5,6},{6,5},{7,4},{8,11},{9,10},{10,... | collective-permute-start | bytes 196616 | tf_op jit(solution)/shard_map/ppermute | solution.py:345
  287.9 5.8 %collective-permute-start.23 = (bf16[8,4096]{1,0:T(8,128)(2,1)}, bf16[8,4096]{1,0:T(8,128)(2,1)S(1)}, u32[]{:S(2)}, u32[]{:S(2)}) collective-permute-start(bf16[8,4096]{1,0:T(8,128)(2,1)} %add_totals.1.rest_0_), channel_id=1, source_target_pairs={{0,12},{1,13},{2,14},{3,15},{4,8},{5,9},{6,10},{7,11},{8,4},{9,5},... | collective-permute-start | bytes 196616 | tf_op jit(solution)/shard_map/ppermute | solution.py:345
  (17 other events, 189.1 us)
Sparse Core Ops, SparseCore 0:
  52.9 88.9 all-reduce.2
  150.6 42.8 all-gather.3

commit v15 on v14

--- a/solution.py
+++ b/solution.py
@@ -93,21 +93,6 @@
     return (grad_one, grad_two, jnp.reshape(loss, (1,)))
 
 
-def eight_rows(sums, loss):
-    lanes = sums[0].shape[1]
-    row = lax.broadcasted_iota(jnp.int32, (8, lanes), 0)
-    loss = jnp.zeros((1, lanes), jnp.float32) + loss
-    values = list(sums)
-    for _ in range(3):
-        part = loss.astype(jnp.bfloat16).astype(jnp.float32)
-        values.append(part)
-        loss = loss - part
-    out = jnp.zeros((8, lanes), jnp.float32)
-    for index, value in enumerate(values):
-        out = jnp.where(row == index, value, out)
-    return out.astype(jnp.bfloat16)
-
-
 def added(refs):
     terms = [ref[...].astype(jnp.float32) for ref in refs]
     while len(terms) > 1:
@@ -132,10 +117,26 @@
     )(one, two)
 
 
+def three_rows(value):
+    rows = []
+    for _ in range(3):
+        part = value.astype(jnp.bfloat16).astype(jnp.float32)
+        rows.append(part)
+        value = value - part
+    row = lax.broadcasted_iota(jnp.int32, (4, 128), 0)
+    out = jnp.where(row == 0, rows[0], jnp.where(row == 1, rows[1], 0.0))
+    return jnp.where(row == 2, rows[2], out).astype(jnp.bfloat16)
+
+
+def loss_of(total):
+    return (total[0:1] + total[1:2]) + total[2:3]
+
+
 def add_kernel(*refs):
     total = added(refs[:-1])
-    loss = (total[4:5] + total[5:6]) + total[6:7]
-    refs[-1][...] = eight_rows([total[k : k + 1] for k in range(4)], loss)
+    width = total.shape[1] - 128
+    refs[-1][:, :width] = total[:, :width].astype(jnp.bfloat16)
+    refs[-1][:, width:] = three_rows(loss_of(total[:, width:]))
 
 
 def attend_kernel(count, begins, ends, *refs):
@@ -211,7 +212,9 @@
             sums.append(jnp.sum(plain, axis=0, keepdims=True))
             sums.append(jnp.sum(prods, axis=0, keepdims=True))
         if ends:
-            outs[4][...] = eight_rows(sums, jnp.sum(loss_out[...]))
+            for index, value in enumerate(sums):
+                outs[4][index : index + 1, :] = value.astype(jnp.bfloat16)
+            outs[5][...] = three_rows(jnp.zeros((1, 128), jnp.float32) + jnp.sum(loss_out[...]))
 
 
 def attend(
@@ -241,8 +244,8 @@
             jax.ShapeDtypeStruct((rows // 2, width), jnp.bfloat16),
             jax.ShapeDtypeStruct((rows // 2, width), jnp.bfloat16),
         ] * 2
-        out_specs.append(pl.BlockSpec((8, lanes), late))
-        out_shape.append(jax.ShapeDtypeStruct((8, width), jnp.bfloat16))
+        out_specs += [pl.BlockSpec((4, lanes), late), pl.BlockSpec((4, 128), lambda step: (0, 0))]
+        out_shape += [jax.ShapeDtypeStruct((4, size), jnp.bfloat16) for size in (width, 128)]
     else:
         if not begins and dtype == jnp.float32:
             aliases.update({4 + 2 * count: 1, 5 + 2 * count: 2})
@@ -270,12 +273,13 @@
     samples, full, own_one, get_one, own_two, get_two, norm_one, norm_two, norm_ref, stat_ref, *rest
 ):
     outs = rest[-3:]
+    count = (len(rest) - 3) // 2
     scale = 2.0 * off_weight / samples
     mixed = norm_ref[2:3, :]
-    total = added(rest[:-3])
+    total = added(rest[:count])
     corr = mixed / samples
     diag = (-2.0 * (1.0 - corr)).astype(jnp.bfloat16).astype(jnp.float32) - 2.0 * off_weight * corr
-    squares = jnp.max((total[4:5, :128] + total[5:6, :128]) + total[6:7, :128])
+    squares = jnp.max(loss_of(added(rest[count:-3])))
     part = jnp.sum((1.0 - corr) ** 2 - off_weight * corr * corr)
 
     @pl.when(pl.program_id(0) == 0)
@@ -312,12 +316,14 @@
 def finish_grads(samples, operands, rows):
     width = operands[0].shape[1]
     lanes = width // tiles
-    heights = (*((rows,) * 6), 4, 4) + (8,) * (len(operands) - 8)
+    count = (len(operands) - 8) // 2
+    heights = (*((rows,) * 6), 4, 4) + (4,) * count
     place = lambda step: (0, step)
     return pl.pallas_call(
         functools.partial(finish_kernel, samples, width),
         grid=(tiles,),
-        in_specs=[pl.BlockSpec((height, lanes), place) for height in heights],
+        in_specs=[pl.BlockSpec((height, lanes), place) for height in heights]
+        + [pl.BlockSpec((4, 128), lambda step: (0, width // 128))] * count,
         out_specs=[pl.BlockSpec((rows, lanes), place)] * 2
         + [pl.BlockSpec(memory_space=pltpu.SMEM)],
         out_shape=[jax.ShapeDtypeStruct((rows, width), jnp.bfloat16)] * 2
@@ -343,15 +349,6 @@
 
     def swapped(value, bit):
         return lax.ppermute(value, "batch", [(i, i ^ bit) for i in range(batches)])
-
-    def reduced(total, add):
-        size = 1
-        while size < batches:
-            steps = (1, 2, 3) if size * 4 <= batches else (1,)
-            terms = [total, *(swapped(total, size * step) for step in steps)]
-            size *= len(steps) + 1
-            total = add(terms) if size < batches else None
-        return terms
 
     def norm_totals(q_one, q_two):
         one, two = (q[:rows].astype(jnp.float32) for q in (q_one, q_two))
@@ -406,13 +403,20 @@
         q_one, q_two, stat, *arrived[hops - 2], loss, acc, False, dtype=jnp.bfloat16
     )
     last_one, last_two, loss = lax.optimization_barrier((last_one, last_two, loss))
-    loss, own_one, send_one, own_two, send_two, total = attend(
+    loss, own_one, send_one, own_two, send_two, total, loss_rows = attend(
         q_one, q_two, stat, [last_one], [last_two], loss, acc, True
     )
     get_one, get_two = swapped(send_one, 1), swapped(send_two, 1)
-    terms = reduced(total, add_totals)
+    total = jnp.concatenate([total, loss_rows], axis=1)
+    size = 1
+    while size < batches:
+        if size > 1:
+            total = add_totals(terms)
+        steps = (1, 2, 3) if size * 4 <= batches else (1,)
+        terms = [total, *(swapped(total, size * step) for step in steps)]
+        size *= len(terms)
     grad_one, grad_two, loss = finish_grads(
-        samples, (own_one, get_one, own_two, get_two, q_one, q_two, norm_sums, stat, *terms), rows
+        samples, (own_one, get_one, own_two, get_two, q_one, q_two, norm_sums, stat, *terms, *terms), rows
     )
     return (grad_one, grad_two, loss)
 

time: 313 us -> 310 us (level)
  transfers between devices with their start and end apart: 26 -> 26, of which waited for: 12 -> 12; matrix products, arithmetic and copies ran while one was open for 4% -> 5% of each run, Pallas kernels for 22% -> 22%
where the time goes in v15:
time: 310 us; the launch traced here: 307 us
  waiting for transfers between devices  159 us (51%)
  Pallas kernels  88.1 us (28%)
  starting transfers between devices  27.9 us (9%)
  between operations  14.2 us (5%)
  other arithmetic  10.2 us (3%)
  local copies, waits for them, and re-layouts  8.09 us (3%)
    ppermute x6, waiting for transfers between devices, ring_shards(): lax.ppermute(up, 'batch', ahead)  109 us
    pallas_call x5, Pallas kernels, attend(): pl.pallas_call(functools.partial(attend_kernel, count, begins, ends), gri...  76.9 us
    psum x1, waiting for transfers between devices, ring_shards(): sums = lax.psum(tuple((sums[row] for row in range(4))), 'batch')  28.1 us
    ppermute x1, waiting for transfers between devices, ring_shards(): last_one = lax.ppermute(ends[0][0], 'batch', ahead)  14.8 us
    ppermute x10, starting transfers between devices, swapped(): return lax.ppermute(value, 'batch', [(i, i ^ bit) for i in range(batches)])  12.5 us
    ppermute x6, starting transfers between devices, ring_shards(): lax.ppermute(up, 'batch', ahead)  6.75 us
    pallas_call x1, Pallas kernels, finish_grads(): pl.pallas_call(functools.partial(finish_kernel, samples, width), grid=(ti...  6.62 us
  transfers between devices with their start and end apart: 26, of which 12 were waited for; matrix products, arithmetic and copies ran while one was open for 5% of the time, Pallas kernels for 22%

profile of v15, /device:TPU:1, one launch (start us, length us, event | category | flops | bytes accessed | tf_op | source)
XLA Modules:
  0.0 307.2 jit_solution(16961730053975792428)
XLA Ops:
  7.2 2.2 collective-permute-start
  10.9 32.9 %collective-permute-done.refs_3_ = bf16[192,4096]{1,0:T(8,128)(2,1)} collective-permute-done((bf16[192,4096]{1,0:T(8,128)(2,1)}, bf16[192,4096]{1,0:T(8,128)(2,1)}, u32[]{:S(2)}, u32[]{:S(2)}) %collective-permute-start) | collective-permute-done | bytes 1572896 | tf_op jit(solution)/shard_map/ppermute | solution.py:395
  45.0 3.0 collective-permute-start.9
  48.0 3.2 %first_sums.1 = f32[4,4096]{1,0:T(4,128)} custom-call(bf16[192,4096]{1,0:T(8,128)(2,1)} %refs_3_.1, bf16[192,4096]{1,0:T(8,128)(2,1)} %refs_4_.1), custom_call_target="tpu_custom_call" | custom-call | flops 4096 | bytes 4096 | tf_op jit(solution)/shard_map/first_sums/pallas_call | solution.py:112
  51.1 1.7 fusion.1
  52.9 24.9 %collective-permute-done.4.refs_5_ = bf16[192,4096]{1,0:T(8,128)(2,1)} collective-permute-done((bf16[192,4096]{1,0:T(8,128)(2,1)}, bf16[192,4096]{1,0:T(8,128)(2,1)}, u32[]{:S(2)}, u32[]{:S(2)}) %collective-permute-start.4) | collective-permute-done | bytes 1572896 | tf_op jit(solution)/shard_map/ppermute | solution.py:395
  80.4 31.5 %collective-permute-done.1.refs_3_ = bf16[192,4096]{1,0:T(8,128)(2,1)} collective-permute-done((bf16[192,4096]{1,0:T(8,128)(2,1)}, bf16[192,4096]{1,0:T(8,128)(2,1)}, u32[]{:S(2)}, u32[]{:S(2)}) %collective-permute-start.1) | collective-permute-done | bytes 1572896 | tf_op jit(solution)/shard_map/ppermute | solution.py:395
  111.8 1.9 collective-permute-start.7
  113.8 28.1 %all-reduce.3.cloned.1.call-done = (f32[4096]{0:T(1024)}, f32[4096]{0:T(1024)}, f32[4096]{0:T(1024)}, f32[4096]{0:T(1024)}) async-done(((f32[4096]{0:T(1024)}, f32[4096]{0:T(1024)}, f32[4096]{0:T(1024)}, f32[4096]{0:T(1024)}), (f32[4096]{0:T(1024)}, f32[4096]{0:T(1024)}, f32[4096]{0:T(1024)}, f32[4096]{0:T(1024)})) %all-reduce.3.cloned.1.call-update) | async-done | bytes 65552 | tf_op jit(solution)/shard_map/psum | solution.py:369
  144.2 3.8 %multiply_convert_fusion.1.refs_0_.norm_one = bf16[384,4096]{1,0:T(8,128)(2,1)S(1)} fusion(bf16[192,4096]{1,0:T(8,128)(2,1)} %collective-permute-done.8, bf16[192,4096]{1,0:T(8,128)(2,1)} %refs_3_.1, f32[4096]{0:T(1024)S(1)} %get-tuple-element.95, f32[4096]{0:T(1024)S(1)} %get-tuple-element.94), kind=kLoop, calls=%fused_computation.1 | loop fusion | flops 11010048 | bytes 6324224 | tf_op jit(solution)/shard_map/convert_element_type | solution.py:366
  154.7 11.7 %attend.5 = (f32[8,128]{1,0:T(8,128)}, f32[384,4096]{1,0:T(8,128)}, f32[384,4096]{1,0:T(8,128)}) custom-call(bf16[384,4096]{1,0:T(8,128)(2,1)} %copy-done.1, bf16[384,4096]{1,0:T(8,128)(2,1)} %copy-done, f32[4,4096]{1,0:T(4,128)} %pad_maximum_fusion.refs_2_.stat_ref, bf16[192,4096]{1,0:T(8,128)(2,1)} %refs_3_.1, ...), custom_call_target="tpu_custom_call", output_to_operand_aliasing={{0}: (5, {})} | custom-call | flops 4096 | bytes 4096 | tf_op jit(solution)/shard_map/attend/pallas_call | solution.py:254
  166.4 17.8 %attend.6 = (f32[8,128]{1,0:T(8,128)}, f32[384,4096]{1,0:T(8,128)}, f32[384,4096]{1,0:T(8,128)}) custom-call(bf16[384,4096]{1,0:T(8,128)(2,1)} %copy-done.1, bf16[384,4096]{1,0:T(8,128)(2,1)} %copy-done, f32[4,4096]{1,0:T(4,128)} %pad_maximum_fusion.refs_2_.stat_ref, ...), custom_call_target="tpu_custom_call", output_to_operand_aliasing={{0}: (7, {}), {1}: (8, {}), {2}: (9, {})} | custom-call | flops 4096 | bytes 4096 | tf_op jit(solution)/shard_map/attend/pallas_call | solution.py:254
  184.2 17.8 %attend.7 = (f32[8,128]{1,0:T(8,128)}, f32[384,4096]{1,0:T(8,128)}, f32[384,4096]{1,0:T(8,128)}) custom-call(bf16[384,4096]{1,0:T(8,128)(2,1)} %copy-done.1, bf16[384,4096]{1,0:T(8,128)(2,1)} %copy-done, f32[4,4096]{1,0:T(4,128)} %pad_maximum_fusion.refs_2_.stat_ref, ...), custom_call_target="tpu_custom_call", output_to_operand_aliasing={{0}: (7, {}), {1}: (8, {}), {2}: (9, {})} | custom-call | flops 4096 | bytes 4096 | tf_op jit(solution)/shard_map/attend/pallas_call | solution.py:254
  202.1 2.0 reduce_sum.39.norm_ref
  204.1 19.3 %collective-permute-done.12.refs_5_ = bf16[192,4096]{1,0:T(8,128)(2,1)} collective-permute-done((bf16[192,4096]{1,0:T(8,128)(2,1)}, bf16[192,4096]{1,0:T(8,128)(2,1)}, u32[]{:S(2)}, u32[]{:S(2)}) %collective-permute-start.12) | collective-permute-done | bytes 1572896 | tf_op jit(solution)/shard_map/ppermute | solution.py:395
  224.3 3.0 collective-permute-start.14
  227.4 16.4 %attend.8 = (f32[8,128]{1,0:T(8,128)}, bf16[384,4096]{1,0:T(8,128)(2,1)}, bf16[384,4096]{1,0:T(8,128)(2,1)}) custom-call(bf16[384,4096]{1,0:T(8,128)(2,1)} %copy-done.1, bf16[384,4096]{1,0:T(8,128)(2,1)} %copy-done, f32[4,4096]{1,0:T(4,128)} %pad_maximum_fusion.refs_2_.stat_ref, bf16[192,4096]{1,0:T(8,128)(2,1)} %copy-done.7, ...), custom_call_target="tpu_custom_call", output_to_operand_aliasing={{0}: (7, {})} | custom-call | flops 4096 | bytes 4096 | tf_op jit(solution)/shard_map/attend/pallas_call | solution.py:254
  243.7 14.8 %collective-permute-done.14.refs_3_ = bf16[192,4096]{1,0:T(8,128)(2,1)S(1)} collective-permute-done((bf16[192,4096]{1,0:T(8,128)(2,1)S(1)}, bf16[192,4096]{1,0:T(8,128)(2,1)S(1)}, u32[]{:S(2)}, u32[]{:S(2)}) %collective-permute-start.14) | collective-permute-done | bytes 1572896 | tf_op jit(solution)/shard_map/ppermute | solution.py:400
  258.5 1.9 collective-permute-done.15.refs_4_
  261.6 13.2 %attend.9 = (f32[8,128]{1,0:T(8,128)}, bf16[192,4096]{1,0:T(8,128)(2,1)}, bf16[192,4096]{1,0:T(8,128)(2,1)}, bf16[192,4096]{1,0:T(8,128)(2,1)}, bf16[192,4096]{1...) custom-call(bf16[384,4096]{1,0:T(8,128)(2,1)} %copy-done.1, ...), custom_call_target="tpu_custom_call", output_to_operand_aliasing={{0}: (5, {})} | custom-call | flops 4096 | bytes 4096 | tf_op jit(solution)/shard_map/attend/pallas_call | solution.py:254
  274.8 3.8 %collective-permute-start.16 = (bf16[192,4096]{1,0:T(8,128)(2,1)}, bf16[192,4096]{1,0:T(8,128)(2,1)S(1)}, u32[]{:S(2)}, u32[]{:S(2)}) collective-permute-start(bf16[192,4096]{1,0:T(8,128)(2,1)} %get-tuple-element.75), channel_id=1, source_target_pairs={{0,1},{1,0},{2,3},{3,2},{4,5},{5,4},{6,7},{7,6},{8,9},{9,8},{10,11... | collective-permute-start | bytes 4718600 | tf_op jit(solution)/shard_map/ppermute | solution.py:351
  280.5 1.7 collective-permute-start.20
  287.3 2.7 collective-permute-start.23
  293.7 6.6 %finish.1 = (bf16[192,4096]{1,0:T(8,128)(2,1)}, bf16[192,4096]{1,0:T(8,128)(2,1)}, f32[1]{0:T(128)}) custom-call(bf16[192,4096]{1,0:T(8,128)(2,1)} %get-tuple-element.74.own_one, bf16[192,4096]{1,0:T(8,128)(2,1)} %copy-done.5, bf16[192,4096]{1,0:T(8,128)(2,1)} %get-tuple-element.76.own_two, bf16[192,4096]{1,0:T(8,128)(2,1)} %copy-done.6, ...), custom_call_target="tpu_custom_call" | custom-call | flops 4096 | bytes 4096 | tf_op jit(solution)/shard_map/finish/pallas_call | solution.py:322
  (83 shorter events, 27.0 us)
Async XLA Ops:
  7.2 134.7 %all-reduce.3.cloned.1.call-start = ((), (), s32[]{:S(2)}) async-start(), calls=%async_computation.1 | async-start | bytes 131072 | tf_op jit(solution)/shard_map/psum | solution.py:369
  7.2 36.6 %collective-permute-start = (bf16[192,4096]{1,0:T(8,128)(2,1)}, bf16[192,4096]{1,0:T(8,128)(2,1)}, u32[]{:S(2)}, u32[]{:S(2)}) collective-permute-start(bf16[192,4096]{1,0:T(8,128)(2,1)} %refs_3_.1), channel_id=1, source_target_pairs={{0,4},{1,5},{4,8},{5,9},{8,12},{9,13},{12,14},{13,15},{14,10},{15,... | collective-permute-start | bytes 4718600 | tf_op jit(solution)/shard_map/ppermute | solution.py:395
  9.4 41.7 %collective-permute-start.2 = (bf16[192,4096]{1,0:T(8,128)(2,1)}, bf16[192,4096]{1,0:T(8,128)(2,1)}, u32[]{:S(2)}, u32[]{:S(2)}) collective-permute-start(bf16[192,4096]{1,0:T(8,128)(2,1)} %refs_3_.1), channel_id=1, source_target_pairs={{4,0},{5,1},{8,4},{9,5},{12,8},{13,9},{14,12},{15,13},{10,14},{11,... | collective-permute-start | bytes 4718600 | tf_op jit(solution)/shard_map/ppermute | solution.py:395
  9.4 68.5 %collective-permute-start.4 = (bf16[192,4096]{1,0:T(8,128)(2,1)}, bf16[192,4096]{1,0:T(8,128)(2,1)}, u32[]{:S(2)}, u32[]{:S(2)}) collective-permute-start(bf16[192,4096]{1,0:T(8,128)(2,1)} %refs_4_.1), channel_id=1, source_target_pairs={{0,4},{1,5},{4,8},{5,9},{8,12},{9,13},{12,14},{13,15},{14,10},{15,... | collective-permute-start | bytes 4718600 | tf_op jit(solution)/shard_map/ppermute | solution.py:395
  10.9 68.5 %collective-permute-start.6 = (bf16[192,4096]{1,0:T(8,128)(2,1)}, bf16[192,4096]{1,0:T(8,128)(2,1)}, u32[]{:S(2)}, u32[]{:S(2)}) collective-permute-start(bf16[192,4096]{1,0:T(8,128)(2,1)} %refs_4_.1), channel_id=1, source_target_pairs={{4,0},{5,1},{8,4},{9,5},{12,8},{13,9},{14,12},{15,13},{10,14},{11,... | collective-permute-start | bytes 4718600 | tf_op jit(solution)/shard_map/ppermute | solution.py:395
  43.8 68.1 %collective-permute-start.1 = (bf16[192,4096]{1,0:T(8,128)(2,1)}, bf16[192,4096]{1,0:T(8,128)(2,1)}, u32[]{:S(2)}, u32[]{:S(2)}) collective-permute-start(bf16[192,4096]{1,0:T(8,128)(2,1)} %collective-permute-done.refs_3_), channel_id=1, source_target_pairs={{0,4},{1,5},{4,8},{5,9},{8,12},{9,13},{12,14},{13,15},{14,10},{15,... | collective-permute-start | bytes 4718600 | tf_op jit(solution)/shard_map/ppermute | solution.py:395
  45.0 98.4 %collective-permute-start.9 = (bf16[192,4096]{1,0:T(8,128)(2,1)}, bf16[192,4096]{1,0:T(8,128)(2,1)S(1)}, u32[]{:S(2)}, u32[]{:S(2)}) collective-permute-start(bf16[192,4096]{1,0:T(8,128)(2,1)} %refs_4_.1), channel_id=1, source_target_pairs={{0,1},{1,0},{2,3},{3,2},{4,5},{5,4},{6,7},{7,6},{8,9},{9,8},{10,11... | collective-permute-start | bytes 4718600 | tf_op jit(solution)/shard_map/ppermute | solution.py:351
  51.1 93.1 %collective-permute-start.8 = (bf16[192,4096]{1,0:T(8,128)(2,1)}, bf16[192,4096]{1,0:T(8,128)(2,1)}, u32[]{:S(2)}, u32[]{:S(2)}) collective-permute-start(bf16[192,4096]{1,0:T(8,128)(2,1)} %refs_3_.1), channel_id=1, source_target_pairs={{0,1},{1,0},{2,3},{3,2},{4,5},{5,4},{6,7},{7,6},{8,9},{9,8},{10,11... | collective-permute-start | bytes 4718600 | tf_op jit(solution)/shard_map/ppermute | solution.py:351
  52.8 149.2 %all-gather.4.cloned.1.call-start = ((), (), s32[]{:S(2)}) async-start(), calls=%async_computation | async-start | bytes 1114112 | tf_op jit(solution)/shard_map/all_gather | solution.py:385
  77.9 72.6 %collective-permute-start.3 = (bf16[192,4096]{1,0:T(8,128)(2,1)}, bf16[192,4096]{1,0:T(8,128)(2,1)}, u32[]{:S(2)}, u32[]{:S(2)}) collective-permute-start(bf16[192,4096]{1,0:T(8,128)(2,1)} %collective-permute-done.2.refs_4_), channel_id=1, source_target_pairs={{4,0},{5,1},{8,4},{9,5},{12,8},{13,9},{14,12},{15,13},{10,14},{11,... | collective-permute-start | bytes 4718600 | tf_op jit(solution)/shard_map/ppermute | solution.py:395
  79.3 71.1 %collective-permute-start.5 = (bf16[192,4096]{1,0:T(8,128)(2,1)}, bf16[192,4096]{1,0:T(8,128)(2,1)}, u32[]{:S(2)}, u32[]{:S(2)}) collective-permute-start(bf16[192,4096]{1,0:T(8,128)(2,1)} %collective-permute-done.4.refs_5_), channel_id=1, source_target_pairs={{0,4},{1,5},{4,8},{5,9},{8,12},{9,13},{12,14},{13,15},{14,10},{15,... | collective-permute-start | bytes 4718600 | tf_op jit(solution)/shard_map/ppermute | solution.py:395
  111.8 38.6 %collective-permute-start.7 = (bf16[192,4096]{1,0:T(8,128)(2,1)}, bf16[192,4096]{1,0:T(8,128)(2,1)}, u32[]{:S(2)}, u32[]{:S(2)}) collective-permute-start(bf16[192,4096]{1,0:T(8,128)(2,1)} %collective-permute-done.6.refs_6_), channel_id=1, source_target_pairs={{4,0},{5,1},{8,4},{9,5},{12,8},{13,9},{14,12},{15,13},{10,14},{11,... | collective-permute-start | bytes 4718600 | tf_op jit(solution)/shard_map/ppermute | solution.py:395
  150.5 53.6 %collective-permute-start.10 = (bf16[192,4096]{1,0:T(8,128)(2,1)}, bf16[192,4096]{1,0:T(8,128)(2,1)S(1)}, u32[]{:S(2)}, u32[]{:S(2)}) collective-permute-start(bf16[192,4096]{1,0:T(8,128)(2,1)} %collective-permute-done.1.refs_3_), channel_id=1, source_target_pairs={{0,4},{1,5},{4,8},{5,9},{8,12},{9,13},{12,14},{13,15},{14,10},{15,... | collective-permute-start | bytes 4718600 | tf_op jit(solution)/shard_map/ppermute | solution.py:395
  150.5 53.6 %collective-permute-start.11 = (bf16[192,4096]{1,0:T(8,128)(2,1)}, bf16[192,4096]{1,0:T(8,128)(2,1)}, u32[]{:S(2)}, u32[]{:S(2)}) collective-permute-start(bf16[192,4096]{1,0:T(8,128)(2,1)} %collective-permute-done.3.refs_4_), channel_id=1, source_target_pairs={{4,0},{5,1},{8,4},{9,5},{12,8},{13,9},{14,12},{15,13},{10,14},{11,... | collective-permute-start | bytes 4718600 | tf_op jit(solution)/shard_map/ppermute | solution.py:395
  152.0 71.5 %collective-permute-start.12 = (bf16[192,4096]{1,0:T(8,128)(2,1)}, bf16[192,4096]{1,0:T(8,128)(2,1)}, u32[]{:S(2)}, u32[]{:S(2)}) collective-permute-start(bf16[192,4096]{1,0:T(8,128)(2,1)} %collective-permute-done.5.refs_5_), channel_id=1, source_target_pairs={{0,4},{1,5},{4,8},{5,9},{8,12},{9,13},{12,14},{13,15},{14,10},{15,... | collective-permute-start | bytes 4718600 | tf_op jit(solution)/shard_map/ppermute | solution.py:395
  152.8 71.5 %collective-permute-start.13 = (bf16[192,4096]{1,0:T(8,128)(2,1)}, bf16[192,4096]{1,0:T(8,128)(2,1)S(1)}, u32[]{:S(2)}, u32[]{:S(2)}) collective-permute-start(bf16[192,4096]{1,0:T(8,128)(2,1)} %collective-permute-done.7.refs_6_), channel_id=1, source_target_pairs={{4,0},{5,1},{8,4},{9,5},{12,8},{13,9},{14,12},{15,13},{10,14},{11,... | collective-permute-start | bytes 4718600 | tf_op jit(solution)/shard_map/ppermute | solution.py:395
  224.3 34.2 %collective-permute-start.14 = (bf16[192,4096]{1,0:T(8,128)(2,1)S(1)}, bf16[192,4096]{1,0:T(8,128)(2,1)S(1)}, u32[]{:S(2)}, u32[]{:S(2)}) collective-permute-start(bf16[192,4096]{1,0:T(8,128)(2,1)S(1)} %collective-permute-done.10.refs_3_), channel_id=1, source_target_pairs={{0,4},{1,5},{4,8},{5,9},{8,12},{9,13},{12,14},{13,15},{14,10},{15,... | collective-permute-start | bytes 4718600 | tf_op jit(solution)/shard_map/ppermute | solution.py:400
  227.4 33.1 %collective-permute-start.15 = (bf16[192,4096]{1,0:T(8,128)(2,1)S(1)}, bf16[192,4096]{1,0:T(8,128)(2,1)S(1)}, u32[]{:S(2)}, u32[]{:S(2)}) collective-permute-start(bf16[192,4096]{1,0:T(8,128)(2,1)S(1)} %collective-permute-done.13.refs_6_), channel_id=1, source_target_pairs={{4,0},{5,1},{8,4},{9,5},{12,8},{13,9},{14,12},{15,13},{10,14},{11,... | collective-permute-start | bytes 4718600 | tf_op jit(solution)/shard_map/ppermute | solution.py:401
  274.8 17.3 %collective-permute-start.16 = (bf16[192,4096]{1,0:T(8,128)(2,1)}, bf16[192,4096]{1,0:T(8,128)(2,1)S(1)}, u32[]{:S(2)}, u32[]{:S(2)}) collective-permute-start(bf16[192,4096]{1,0:T(8,128)(2,1)} %get-tuple-element.75), channel_id=1, source_target_pairs={{0,1},{1,0},{2,3},{3,2},{4,5},{5,4},{6,7},{7,6},{8,9},{9,8},{10,11... | collective-permute-start | bytes 4718600 | tf_op jit(solution)/shard_map/ppermute | solution.py:351
  278.6 13.5 %collective-permute-start.17 = (bf16[192,4096]{1,0:T(8,128)(2,1)}, bf16[192,4096]{1,0:T(8,128)(2,1)S(1)}, u32[]{:S(2)}, u32[]{:S(2)}) collective-permute-start(bf16[192,4096]{1,0:T(8,128)(2,1)} %get-tuple-element.77), channel_id=1, source_target_pairs={{0,1},{1,0},{2,3},{3,2},{4,5},{5,4},{6,7},{7,6},{8,9},{9,8},{10,11... | collective-permute-start | bytes 4718600 | tf_op jit(solution)/shard_map/ppermute | solution.py:351
  280.5 3.9 %collective-permute-start.20 = (bf16[4,4224]{1,0:T(4,128)(2,1)S(1)}, bf16[4,4224]{1,0:T(4,128)(2,1)S(1)}, u32[]{:S(2)}, u32[]{:S(2)}) collective-permute-start(bf16[4,4224]{1,0:T(4,128)(2,1)S(1)} %constant_dynamic-update-slice_fusion.refs_0_), channel_id=1, source_target_pairs={{0,3},{1,2},{2,1},{3,0},{4,7},{5,6},{6,5},{7,4},{8,11},{9,10},{10,... | collective-permute-start | bytes 101384 | tf_op jit(solution)/shard_map/ppermute | solution.py:351
  286.4 3.6 %collective-permute-start.21 = (bf16[4,4224]{1,0:T(4,128)(2,1)}, bf16[4,4224]{1,0:T(4,128)(2,1)S(1)}, u32[]{:S(2)}, u32[]{:S(2)}) collective-permute-start(bf16[4,4224]{1,0:T(4,128)(2,1)} %add_totals.1.rest_0_.rest_4_), channel_id=1, source_target_pairs={{0,4},{1,5},{2,6},{3,7},{4,0},{5,1},{6,2},{7,3},{8,12},{9,13},{10,... | collective-permute-start | bytes 101384 | tf_op jit(solution)/shard_map/ppermute | solution.py:351
  287.0 4.0 %collective-permute-start.22 = (bf16[4,4224]{1,0:T(4,128)(2,1)}, bf16[4,4224]{1,0:T(4,128)(2,1)S(1)}, u32[]{:S(2)}, u32[]{:S(2)}) collective-permute-start(bf16[4,4224]{1,0:T(4,128)(2,1)} %add_totals.1.rest_0_.rest_4_), channel_id=1, source_target_pairs={{0,8},{1,9},{2,10},{3,11},{4,12},{5,13},{6,14},{7,15},{8,0},{9,1},... | collective-permute-start | bytes 101384 | tf_op jit(solution)/shard_map/ppermute | solution.py:351
  287.3 4.8 %collective-permute-start.23 = (bf16[4,4224]{1,0:T(4,128)(2,1)}, bf16[4,4224]{1,0:T(4,128)(2,1)S(1)}, u32[]{:S(2)}, u32[]{:S(2)}) collective-permute-start(bf16[4,4224]{1,0:T(4,128)(2,1)} %add_totals.1.rest_0_.rest_4_), channel_id=1, source_target_pairs={{0,12},{1,13},{2,14},{3,15},{4,8},{5,9},{6,10},{7,11},{8,4},{9,5},... | collective-permute-start | bytes 101384 | tf_op jit(solution)/shard_map/ppermute | solution.py:351
  (18 other events, 190.9 us)
Sparse Core Ops, SparseCore 0:
  52.9 88.9 all-reduce.2
  150.6 42.7 all-gather.3

commit v16 on v15

--- a/solution.py
+++ b/solution.py
@@ -123,20 +123,38 @@
         part = value.astype(jnp.bfloat16).astype(jnp.float32)
         rows.append(part)
         value = value - part
-    row = lax.broadcasted_iota(jnp.int32, (4, 128), 0)
+    row = lax.broadcasted_iota(jnp.int32, (8, 128), 0)
     out = jnp.where(row == 0, rows[0], jnp.where(row == 1, rows[1], 0.0))
     return jnp.where(row == 2, rows[2], out).astype(jnp.bfloat16)
 
 
 def loss_of(total):
     return (total[0:1] + total[1:2]) + total[2:3]
+
+
+def halves(value):
+    high = value.astype(jnp.bfloat16)
+    return (high, (value - high.astype(jnp.float32)).astype(jnp.bfloat16))
+
+
+def split_kernel(sums_ref, out_ref):
+    out_ref[:2, :] = sums_ref[:2, :].astype(jnp.bfloat16)
+    out_ref[2:3, :], out_ref[3:4, :] = halves(sums_ref[2:3, :])
+
+
+def split_rows(sums):
+    return pl.pallas_call(
+        split_kernel, out_shape=jax.ShapeDtypeStruct(sums.shape, jnp.bfloat16), name="split_rows"
+    )(sums)
 
 
 def add_kernel(*refs):
     total = added(refs[:-1])
     width = total.shape[1] - 128
-    refs[-1][:, :width] = total[:, :width].astype(jnp.bfloat16)
-    refs[-1][:, width:] = three_rows(loss_of(total[:, width:]))
+    out_ref = refs[-1]
+    out_ref[:6, :width] = total[:6, :width].astype(jnp.bfloat16)
+    out_ref[6:7, :width], out_ref[7:8, :width] = halves(total[6:7, :width] + total[7:8, :width])
+    out_ref[:, width:] = three_rows(loss_of(total[:, width:]))
 
 
 def attend_kernel(count, begins, ends, *refs):
@@ -146,6 +164,7 @@
     rest = list(refs[3 + 2 * count :])
     loss_in = rest.pop(0)
     acc_in = None if begins else (rest.pop(0), rest.pop(0))
+    norm_rows = rest.pop(0) if ends else None
     late = rest[-8:-6] if ends else ()
     held_one, held_two, gram_one, gram_two, round_one, round_two = rest[-6:]
     fresh = rest[-9] if ends else None
@@ -214,11 +233,12 @@
         if ends:
             for index, value in enumerate(sums):
                 outs[4][index : index + 1, :] = value.astype(jnp.bfloat16)
+            outs[4][4:, :] = norm_rows[...]
             outs[5][...] = three_rows(jnp.zeros((1, 128), jnp.float32) + jnp.sum(loss_out[...]))
 
 
 def attend(
-    q_one, q_two, stat, blocks_one, blocks_two, loss, acc, ends, dtype=jnp.float32
+    q_one, q_two, stat, blocks_one, blocks_two, loss, acc, ends, dtype=jnp.float32, norm_rows=None
 ):
     rows, width = q_one.shape
     lanes = width // tiles
@@ -239,13 +259,15 @@
         operands += list(acc)
         in_specs += [pl.BlockSpec((rows, lanes), late)] * 2
     if ends:
+        operands.append(norm_rows)
+        in_specs.append(pl.BlockSpec((4, lanes), late))
         out_specs += [pl.BlockSpec((rows // 2, lanes), late)] * 4
         out_shape += [
             jax.ShapeDtypeStruct((rows // 2, width), jnp.bfloat16),
             jax.ShapeDtypeStruct((rows // 2, width), jnp.bfloat16),
         ] * 2
-        out_specs += [pl.BlockSpec((4, lanes), late), pl.BlockSpec((4, 128), lambda step: (0, 0))]
-        out_shape += [jax.ShapeDtypeStruct((4, size), jnp.bfloat16) for size in (width, 128)]
+        out_specs += [pl.BlockSpec((8, lanes), late), pl.BlockSpec((8, 128), lambda step: (0, 0))]
+        out_shape += [jax.ShapeDtypeStruct((8, size), jnp.bfloat16) for size in (width, 128)]
     else:
         if not begins and dtype == jnp.float32:
             aliases.update({4 + 2 * count: 1, 5 + 2 * count: 2})
@@ -270,13 +292,13 @@
 
 
 def finish_kernel(
-    samples, full, own_one, get_one, own_two, get_two, norm_one, norm_two, norm_ref, stat_ref, *rest
+    samples, full, own_one, get_one, own_two, get_two, norm_one, norm_two, stat_ref, *rest
 ):
     outs = rest[-3:]
     count = (len(rest) - 3) // 2
     scale = 2.0 * off_weight / samples
-    mixed = norm_ref[2:3, :]
     total = added(rest[:count])
+    mixed = total[6:7] + total[7:8]
     corr = mixed / samples
     diag = (-2.0 * (1.0 - corr)).astype(jnp.bfloat16).astype(jnp.float32) - 2.0 * off_weight * corr
     squares = jnp.max(loss_of(added(rest[count:-3])))
@@ -292,7 +314,7 @@
     ):
         inv = stat_ref[inv_row : inv_row + 1, :]
         sum_back = scale * total[2 * index : 2 * index + 1, :]
-        sum_back += norm_ref[1 - index : 2 - index, :] * diag
+        sum_back += total[5 - index : 6 - index, :] * diag
         sum_prod = scale * total[2 * index + 1 : 2 * index + 2, :] + mixed * diag
         by_acc, by_other = inv * scale, inv * diag
         minus, by_mine = inv * sum_back / samples, inv * sum_prod / samples
@@ -316,14 +338,14 @@
 def finish_grads(samples, operands, rows):
     width = operands[0].shape[1]
     lanes = width // tiles
-    count = (len(operands) - 8) // 2
-    heights = (*((rows,) * 6), 4, 4) + (4,) * count
+    count = (len(operands) - 7) // 2
+    heights = (*((rows,) * 6), 4) + (8,) * count
     place = lambda step: (0, step)
     return pl.pallas_call(
         functools.partial(finish_kernel, samples, width),
         grid=(tiles,),
         in_specs=[pl.BlockSpec((height, lanes), place) for height in heights]
-        + [pl.BlockSpec((4, 128), lambda step: (0, width // 128))] * count,
+        + [pl.BlockSpec((8, 128), lambda step: (0, width // 128))] * count,
         out_specs=[pl.BlockSpec((rows, lanes), place)] * 2
         + [pl.BlockSpec(memory_space=pltpu.SMEM)],
         out_shape=[jax.ShapeDtypeStruct((rows, width), jnp.bfloat16)] * 2
@@ -382,7 +404,7 @@
             )
             ends = [flat[:2], flat[2:]]
             arrived[-1] = [list(pair) for pair in ends]
-            norm_sums = jnp.sum(lax.all_gather(norm_sums, "batch", axis=0), axis=0)
+            norm_sums = split_rows(norm_sums)
             loss, *acc = attend(q_one, q_two, stat, [view_one], [view_two], loss, None, False)
         if hop > 2:
             for blocks in arrived[:2] if hop == 3 else arrived[hop - 2 : hop - 1]:
@@ -404,7 +426,7 @@
     )
     last_one, last_two, loss = lax.optimization_barrier((last_one, last_two, loss))
     loss, own_one, send_one, own_two, send_two, total, loss_rows = attend(
-        q_one, q_two, stat, [last_one], [last_two], loss, acc, True
+        q_one, q_two, stat, [last_one], [last_two], loss, acc, True, norm_rows=norm_sums
     )
     get_one, get_two = swapped(send_one, 1), swapped(send_two, 1)
     total = jnp.concatenate([total, loss_rows], axis=1)
@@ -416,7 +438,7 @@
         terms = [total, *(swapped(total, size * step) for step in steps)]
         size *= len(terms)
     grad_one, grad_two, loss = finish_grads(
-        samples, (own_one, get_one, own_two, get_two, q_one, q_two, norm_sums, stat, *terms, *terms), rows
+        samples, (own_one, get_one, own_two, get_two, q_one, q_two, stat, *terms, *terms), rows
     )
     return (grad_one, grad_two, loss)
 

time: 310 us -> 307 us (level)
    ppermute x6, waiting for transfers between devices: 109 us -> 105 us  [ring_shards(): lax.ppermute(up, 'batch', ahead)]
  transfers between devices with their start and end apart: 26 -> 25, of which waited for: 12 -> 11; matrix products, arithmetic and copies ran while one was open for 5% -> 4% of each run, Pallas kernels for 22% -> 23%
where the time goes in v16:
time: 307 us; the launch traced here: 303 us
  waiting for transfers between devices  157 us (51%)
  Pallas kernels  89.9 us (29%)
  starting transfers between devices  26.5 us (9%)
  between operations  14.2 us (5%)
  other arithmetic  8.5 us (3%)
  local copies, waits for them, and re-layouts  7.27 us (2%)
    ppermute x6, waiting for transfers between devices, ring_shards(): lax.ppermute(up, 'batch', ahead)  105 us
    pallas_call x5, Pallas kernels, attend(): pl.pallas_call(functools.partial(attend_kernel, count, begins, ends), gri...  76.8 us
    psum x1, waiting for transfers between devices, ring_shards(): sums = lax.psum(tuple((sums[row] for row in range(4))), 'batch')  28.1 us
    ppermute x1, waiting for transfers between devices, ring_shards(): last_one = lax.ppermute(ends[0][0], 'batch', ahead)  15.2 us
    ppermute x10, starting transfers between devices, swapped(): return lax.ppermute(value, 'batch', [(i, i ^ bit) for i in range(batches)])  12.7 us
    ppermute x10, waiting for transfers between devices, swapped(): return lax.ppermute(value, 'batch', [(i, i ^ bit) for i in range(batches)])  6.77 us
    ppermute x6, starting transfers between devices, ring_shards(): lax.ppermute(up, 'batch', ahead)  6.75 us
    pallas_call x1, Pallas kernels, finish_grads(): pl.pallas_call(functools.partial(finish_kernel, samples, width), grid=(ti...  6.67 us
  transfers between devices with their start and end apart: 25, of which 11 were waited for; matrix products, arithmetic and copies ran while one was open for 4% of the time, Pallas kernels for 23%

profile of v16, /device:TPU:1, one launch (start us, length us, event | category | flops | bytes accessed | tf_op | source)
XLA Modules:
  0.0 303.0 jit_solution(12396558913035180087)
XLA Ops:
  7.2 2.2 collective-permute-start
  10.9 32.9 %collective-permute-done.refs_3_ = bf16[192,4096]{1,0:T(8,128)(2,1)} collective-permute-done((bf16[192,4096]{1,0:T(8,128)(2,1)}, bf16[192,4096]{1,0:T(8,128)(2,1)}, u32[]{:S(2)}, u32[]{:S(2)}) %collective-permute-start) | collective-permute-done | bytes 1572896 | tf_op jit(solution)/shard_map/ppermute | solution.py:417
  45.0 3.0 collective-permute-start.9
  48.0 3.2 %first_sums.1 = f32[4,4096]{1,0:T(4,128)} custom-call(bf16[192,4096]{1,0:T(8,128)(2,1)} %refs_3_.1, bf16[192,4096]{1,0:T(8,128)(2,1)} %refs_4_.1), custom_call_target="tpu_custom_call" | custom-call | flops 4096 | bytes 4096 | tf_op jit(solution)/shard_map/first_sums/pallas_call | solution.py:112
  51.1 1.7 fusion.1
  52.9 25.0 %collective-permute-done.4.refs_5_ = bf16[192,4096]{1,0:T(8,128)(2,1)} collective-permute-done((bf16[192,4096]{1,0:T(8,128)(2,1)}, bf16[192,4096]{1,0:T(8,128)(2,1)}, u32[]{:S(2)}, u32[]{:S(2)}) %collective-permute-start.4) | collective-permute-done | bytes 1572896 | tf_op jit(solution)/shard_map/ppermute | solution.py:417
  80.4 31.5 %collective-permute-done.1.refs_3_ = bf16[192,4096]{1,0:T(8,128)(2,1)} collective-permute-done((bf16[192,4096]{1,0:T(8,128)(2,1)}, bf16[192,4096]{1,0:T(8,128)(2,1)}, u32[]{:S(2)}, u32[]{:S(2)}) %collective-permute-start.1) | collective-permute-done | bytes 1572896 | tf_op jit(solution)/shard_map/ppermute | solution.py:417
  111.8 1.9 collective-permute-start.7
  113.8 28.1 %all-reduce.3.cloned.1.call-done = (f32[4096]{0:T(1024)}, f32[4096]{0:T(1024)}, f32[4096]{0:T(1024)}, f32[4096]{0:T(1024)}) async-done(((f32[4096]{0:T(1024)}, f32[4096]{0:T(1024)}, f32[4096]{0:T(1024)}, f32[4096]{0:T(1024)}), (f32[4096]{0:T(1024)}, f32[4096]{0:T(1024)}, f32[4096]{0:T(1024)}, f32[4096]{0:T(1024)})) %all-reduce.3.cloned.1.call-update) | async-done | bytes 65552 | tf_op jit(solution)/shard_map/psum | solution.py:391
  144.2 3.9 %multiply_convert_fusion.1.refs_0_.norm_one = bf16[384,4096]{1,0:T(8,128)(2,1)S(1)} fusion(bf16[192,4096]{1,0:T(8,128)(2,1)} %collective-permute-done.8, bf16[192,4096]{1,0:T(8,128)(2,1)} %refs_3_.1, f32[4096]{0:T(1024)S(1)} %get-tuple-element.95, f32[4096]{0:T(1024)S(1)} %get-tuple-element.94), kind=kLoop, calls=%fused_computation.1 | loop fusion | flops 11010048 | bytes 6324224 | tf_op jit(solution)/shard_map/convert_element_type | solution.py:388
  154.1 11.6 %attend.5 = (f32[8,128]{1,0:T(8,128)}, f32[384,4096]{1,0:T(8,128)}, f32[384,4096]{1,0:T(8,128)}) custom-call(bf16[384,4096]{1,0:T(8,128)(2,1)} %copy-done.1, bf16[384,4096]{1,0:T(8,128)(2,1)} %copy-done, f32[4,4096]{1,0:T(4,128)} %pad_maximum_fusion.refs_2_.stat_ref, bf16[192,4096]{1,0:T(8,128)(2,1)} %refs_3_.1, ...), custom_call_target="tpu_custom_call", output_to_operand_aliasing={{0}: (5, {})} | custom-call | flops 4096 | bytes 4096 | tf_op jit(solution)/shard_map/attend/pallas_call | solution.py:276
  165.7 17.8 %attend.6 = (f32[8,128]{1,0:T(8,128)}, f32[384,4096]{1,0:T(8,128)}, f32[384,4096]{1,0:T(8,128)}) custom-call(bf16[384,4096]{1,0:T(8,128)(2,1)} %copy-done.1, bf16[384,4096]{1,0:T(8,128)(2,1)} %copy-done, f32[4,4096]{1,0:T(4,128)} %pad_maximum_fusion.refs_2_.stat_ref, ...), custom_call_target="tpu_custom_call", output_to_operand_aliasing={{0}: (7, {}), {1}: (8, {}), {2}: (9, {})} | custom-call | flops 4096 | bytes 4096 | tf_op jit(solution)/shard_map/attend/pallas_call | solution.py:276
  183.6 17.8 %attend.7 = (f32[8,128]{1,0:T(8,128)}, f32[384,4096]{1,0:T(8,128)}, f32[384,4096]{1,0:T(8,128)}) custom-call(bf16[384,4096]{1,0:T(8,128)(2,1)} %copy-done.1, bf16[384,4096]{1,0:T(8,128)(2,1)} %copy-done, f32[4,4096]{1,0:T(4,128)} %pad_maximum_fusion.refs_2_.stat_ref, ...), custom_call_target="tpu_custom_call", output_to_operand_aliasing={{0}: (7, {}), {1}: (8, {}), {2}: (9, {})} | custom-call | flops 4096 | bytes 4096 | tf_op jit(solution)/shard_map/attend/pallas_call | solution.py:276
  202.8 15.9 %collective-permute-done.12.refs_5_ = bf16[192,4096]{1,0:T(8,128)(2,1)} collective-permute-done((bf16[192,4096]{1,0:T(8,128)(2,1)}, bf16[192,4096]{1,0:T(8,128)(2,1)}, u32[]{:S(2)}, u32[]{:S(2)}) %collective-permute-start.12) | collective-permute-done | bytes 1572896 | tf_op jit(solution)/shard_map/ppermute | solution.py:417
  220.2 16.4 %attend.8 = (f32[8,128]{1,0:T(8,128)}, bf16[384,4096]{1,0:T(8,128)(2,1)}, bf16[384,4096]{1,0:T(8,128)(2,1)}) custom-call(bf16[384,4096]{1,0:T(8,128)(2,1)} %copy-done.1, bf16[384,4096]{1,0:T(8,128)(2,1)} %copy-done, f32[4,4096]{1,0:T(4,128)} %pad_maximum_fusion.refs_2_.stat_ref, bf16[192,4096]{1,0:T(8,128)(2,1)} %copy-done.7, ...), custom_call_target="tpu_custom_call", output_to_operand_aliasing={{0}: (7, {})} | custom-call | flops 4096 | bytes 4096 | tf_op jit(solution)/shard_map/attend/pallas_call | solution.py:276
  236.6 15.2 %collective-permute-done.14.refs_3_ = bf16[192,4096]{1,0:T(8,128)(2,1)S(1)} collective-permute-done((bf16[192,4096]{1,0:T(8,128)(2,1)S(1)}, bf16[192,4096]{1,0:T(8,128)(2,1)S(1)}, u32[]{:S(2)}, u32[]{:S(2)}) %collective-permute-start.14) | collective-permute-done | bytes 1572896 | tf_op jit(solution)/shard_map/ppermute | solution.py:422
  254.2 13.2 %attend.9 = (f32[8,128]{1,0:T(8,128)}, bf16[192,4096]{1,0:T(8,128)(2,1)}, bf16[192,4096]{1,0:T(8,128)(2,1)}, bf16[192,4096]{1,0:T(8,128)(2,1)}, bf16[192,4096]{1...) custom-call(bf16[384,4096]{1,0:T(8,128)(2,1)} %copy-done.1, ...), custom_call_target="tpu_custom_call", output_to_operand_aliasing={{0}: (5, {})} | custom-call | flops 4096 | bytes 4096 | tf_op jit(solution)/shard_map/attend/pallas_call | solution.py:276
  267.4 4.0 %collective-permute-start.16 = (bf16[192,4096]{1,0:T(8,128)(2,1)}, bf16[192,4096]{1,0:T(8,128)(2,1)S(1)}, u32[]{:S(2)}, u32[]{:S(2)}) collective-permute-start(bf16[192,4096]{1,0:T(8,128)(2,1)} %get-tuple-element.76), channel_id=1, source_target_pairs={{0,1},{1,0},{2,3},{3,2},{4,5},{5,4},{6,7},{7,6},{8,9},{9,8},{10,11... | collective-permute-start | bytes 4718600 | tf_op jit(solution)/shard_map/ppermute | solution.py:373
  273.4 1.7 collective-permute-start.20
  275.1 2.0 collective-permute-done.19.refs_2_
  279.4 1.7 add_totals.1.rest_0_.rest_4_
  281.6 3.0 collective-permute-start.23
  285.9 1.9 collective-permute-done.23.rest_3_.rest_7_
  289.5 6.7 %finish.1 = (bf16[192,4096]{1,0:T(8,128)(2,1)}, bf16[192,4096]{1,0:T(8,128)(2,1)}, f32[1]{0:T(128)}) custom-call(bf16[192,4096]{1,0:T(8,128)(2,1)} %get-tuple-element.75.own_one, bf16[192,4096]{1,0:T(8,128)(2,1)} %copy-done.3, bf16[192,4096]{1,0:T(8,128)(2,1)} %get-tuple-element.77.own_two, bf16[192,4096]{1,0:T(8,128)(2,1)} %copy-done.4, ...), custom_call_target="tpu_custom_call" | custom-call | flops 4096 | bytes 4096 | tf_op jit(solution)/shard_map/finish/pallas_call | solution.py:344
  (80 shorter events, 26.6 us)
Async XLA Ops:
  7.2 134.7 %all-reduce.3.cloned.1.call-start = ((), (), s32[]{:S(2)}) async-start(), calls=%async_computation | async-start | bytes 131072 | tf_op jit(solution)/shard_map/psum | solution.py:391
  7.2 36.6 %collective-permute-start = (bf16[192,4096]{1,0:T(8,128)(2,1)}, bf16[192,4096]{1,0:T(8,128)(2,1)}, u32[]{:S(2)}, u32[]{:S(2)}) collective-permute-start(bf16[192,4096]{1,0:T(8,128)(2,1)} %refs_3_.1), channel_id=1, source_target_pairs={{0,4},{1,5},{4,8},{5,9},{8,12},{9,13},{12,14},{13,15},{14,10},{15,... | collective-permute-start | bytes 4718600 | tf_op jit(solution)/shard_map/ppermute | solution.py:417
  9.4 41.7 %collective-permute-start.2 = (bf16[192,4096]{1,0:T(8,128)(2,1)}, bf16[192,4096]{1,0:T(8,128)(2,1)}, u32[]{:S(2)}, u32[]{:S(2)}) collective-permute-start(bf16[192,4096]{1,0:T(8,128)(2,1)} %refs_3_.1), channel_id=1, source_target_pairs={{4,0},{5,1},{8,4},{9,5},{12,8},{13,9},{14,12},{15,13},{10,14},{11,... | collective-permute-start | bytes 4718600 | tf_op jit(solution)/shard_map/ppermute | solution.py:417
  9.4 68.5 %collective-permute-start.4 = (bf16[192,4096]{1,0:T(8,128)(2,1)}, bf16[192,4096]{1,0:T(8,128)(2,1)}, u32[]{:S(2)}, u32[]{:S(2)}) collective-permute-start(bf16[192,4096]{1,0:T(8,128)(2,1)} %refs_4_.1), channel_id=1, source_target_pairs={{0,4},{1,5},{4,8},{5,9},{8,12},{9,13},{12,14},{13,15},{14,10},{15,... | collective-permute-start | bytes 4718600 | tf_op jit(solution)/shard_map/ppermute | solution.py:417
  10.9 68.5 %collective-permute-start.6 = (bf16[192,4096]{1,0:T(8,128)(2,1)}, bf16[192,4096]{1,0:T(8,128)(2,1)}, u32[]{:S(2)}, u32[]{:S(2)}) collective-permute-start(bf16[192,4096]{1,0:T(8,128)(2,1)} %refs_4_.1), channel_id=1, source_target_pairs={{4,0},{5,1},{8,4},{9,5},{12,8},{13,9},{14,12},{15,13},{10,14},{11,... | collective-permute-start | bytes 4718600 | tf_op jit(solution)/shard_map/ppermute | solution.py:417
  43.8 68.1 %collective-permute-start.1 = (bf16[192,4096]{1,0:T(8,128)(2,1)}, bf16[192,4096]{1,0:T(8,128)(2,1)}, u32[]{:S(2)}, u32[]{:S(2)}) collective-permute-start(bf16[192,4096]{1,0:T(8,128)(2,1)} %collective-permute-done.refs_3_), channel_id=1, source_target_pairs={{0,4},{1,5},{4,8},{5,9},{8,12},{9,13},{12,14},{13,15},{14,10},{15,... | collective-permute-start | bytes 4718600 | tf_op jit(solution)/shard_map/ppermute | solution.py:417
  45.0 98.4 %collective-permute-start.9 = (bf16[192,4096]{1,0:T(8,128)(2,1)}, bf16[192,4096]{1,0:T(8,128)(2,1)S(1)}, u32[]{:S(2)}, u32[]{:S(2)}) collective-permute-start(bf16[192,4096]{1,0:T(8,128)(2,1)} %refs_4_.1), channel_id=1, source_target_pairs={{0,1},{1,0},{2,3},{3,2},{4,5},{5,4},{6,7},{7,6},{8,9},{9,8},{10,11... | collective-permute-start | bytes 4718600 | tf_op jit(solution)/shard_map/ppermute | solution.py:373
  51.1 93.1 %collective-permute-start.8 = (bf16[192,4096]{1,0:T(8,128)(2,1)}, bf16[192,4096]{1,0:T(8,128)(2,1)}, u32[]{:S(2)}, u32[]{:S(2)}) collective-permute-start(bf16[192,4096]{1,0:T(8,128)(2,1)} %refs_3_.1), channel_id=1, source_target_pairs={{0,1},{1,0},{2,3},{3,2},{4,5},{5,4},{6,7},{7,6},{8,9},{9,8},{10,11... | collective-permute-start | bytes 4718600 | tf_op jit(solution)/shard_map/ppermute | solution.py:373
  77.9 71.9 %collective-permute-start.3 = (bf16[192,4096]{1,0:T(8,128)(2,1)}, bf16[192,4096]{1,0:T(8,128)(2,1)}, u32[]{:S(2)}, u32[]{:S(2)}) collective-permute-start(bf16[192,4096]{1,0:T(8,128)(2,1)} %collective-permute-done.2.refs_4_), channel_id=1, source_target_pairs={{4,0},{5,1},{8,4},{9,5},{12,8},{13,9},{14,12},{15,13},{10,14},{11,... | collective-permute-start | bytes 4718600 | tf_op jit(solution)/shard_map/ppermute | solution.py:417
  79.3 70.5 %collective-permute-start.5 = (bf16[192,4096]{1,0:T(8,128)(2,1)}, bf16[192,4096]{1,0:T(8,128)(2,1)}, u32[]{:S(2)}, u32[]{:S(2)}) collective-permute-start(bf16[192,4096]{1,0:T(8,128)(2,1)} %collective-permute-done.4.refs_5_), channel_id=1, source_target_pairs={{0,4},{1,5},{4,8},{5,9},{8,12},{9,13},{12,14},{13,15},{14,10},{15,... | collective-permute-start | bytes 4718600 | tf_op jit(solution)/shard_map/ppermute | solution.py:417
  111.8 38.0 %collective-permute-start.7 = (bf16[192,4096]{1,0:T(8,128)(2,1)}, bf16[192,4096]{1,0:T(8,128)(2,1)}, u32[]{:S(2)}, u32[]{:S(2)}) collective-permute-start(bf16[192,4096]{1,0:T(8,128)(2,1)} %collective-permute-done.6.refs_6_), channel_id=1, source_target_pairs={{4,0},{5,1},{8,4},{9,5},{12,8},{13,9},{14,12},{15,13},{10,14},{11,... | collective-permute-start | bytes 4718600 | tf_op jit(solution)/shard_map/ppermute | solution.py:417
  149.8 53.0 %collective-permute-start.10 = (bf16[192,4096]{1,0:T(8,128)(2,1)}, bf16[192,4096]{1,0:T(8,128)(2,1)S(1)}, u32[]{:S(2)}, u32[]{:S(2)}) collective-permute-start(bf16[192,4096]{1,0:T(8,128)(2,1)} %collective-permute-done.1.refs_3_), channel_id=1, source_target_pairs={{0,4},{1,5},{4,8},{5,9},{8,12},{9,13},{12,14},{13,15},{14,10},{15,... | collective-permute-start | bytes 4718600 | tf_op jit(solution)/shard_map/ppermute | solution.py:417
  149.9 52.9 %collective-permute-start.11 = (bf16[192,4096]{1,0:T(8,128)(2,1)}, bf16[192,4096]{1,0:T(8,128)(2,1)}, u32[]{:S(2)}, u32[]{:S(2)}) collective-permute-start(bf16[192,4096]{1,0:T(8,128)(2,1)} %collective-permute-done.3.refs_4_), channel_id=1, source_target_pairs={{4,0},{5,1},{8,4},{9,5},{12,8},{13,9},{14,12},{15,13},{10,14},{11,... | collective-permute-start | bytes 4718600 | tf_op jit(solution)/shard_map/ppermute | solution.py:417
  151.3 67.3 %collective-permute-start.12 = (bf16[192,4096]{1,0:T(8,128)(2,1)}, bf16[192,4096]{1,0:T(8,128)(2,1)}, u32[]{:S(2)}, u32[]{:S(2)}) collective-permute-start(bf16[192,4096]{1,0:T(8,128)(2,1)} %collective-permute-done.5.refs_5_), channel_id=1, source_target_pairs={{0,4},{1,5},{4,8},{5,9},{8,12},{9,13},{12,14},{13,15},{14,10},{15,... | collective-permute-start | bytes 4718600 | tf_op jit(solution)/shard_map/ppermute | solution.py:417
  152.2 66.5 %collective-permute-start.13 = (bf16[192,4096]{1,0:T(8,128)(2,1)}, bf16[192,4096]{1,0:T(8,128)(2,1)S(1)}, u32[]{:S(2)}, u32[]{:S(2)}) collective-permute-start(bf16[192,4096]{1,0:T(8,128)(2,1)} %collective-permute-done.7.refs_6_), channel_id=1, source_target_pairs={{4,0},{5,1},{8,4},{9,5},{12,8},{13,9},{14,12},{15,13},{10,14},{11,... | collective-permute-start | bytes 4718600 | tf_op jit(solution)/shard_map/ppermute | solution.py:417
  218.7 33.1 %collective-permute-start.14 = (bf16[192,4096]{1,0:T(8,128)(2,1)S(1)}, bf16[192,4096]{1,0:T(8,128)(2,1)S(1)}, u32[]{:S(2)}, u32[]{:S(2)}) collective-permute-start(bf16[192,4096]{1,0:T(8,128)(2,1)S(1)} %collective-permute-done.10.refs_3_), channel_id=1, source_target_pairs={{0,4},{1,5},{4,8},{5,9},{8,12},{9,13},{12,14},{13,15},{14,10},{15,... | collective-permute-start | bytes 4718600 | tf_op jit(solution)/shard_map/ppermute | solution.py:422
  220.2 32.9 %collective-permute-start.15 = (bf16[192,4096]{1,0:T(8,128)(2,1)S(1)}, bf16[192,4096]{1,0:T(8,128)(2,1)S(1)}, u32[]{:S(2)}, u32[]{:S(2)}) collective-permute-start(bf16[192,4096]{1,0:T(8,128)(2,1)S(1)} %collective-permute-done.13.refs_6_), channel_id=1, source_target_pairs={{4,0},{5,1},{8,4},{9,5},{12,8},{13,9},{14,12},{15,13},{10,14},{11,... | collective-permute-start | bytes 4718600 | tf_op jit(solution)/shard_map/ppermute | solution.py:423
  267.4 20.4 %collective-permute-start.16 = (bf16[192,4096]{1,0:T(8,128)(2,1)}, bf16[192,4096]{1,0:T(8,128)(2,1)S(1)}, u32[]{:S(2)}, u32[]{:S(2)}) collective-permute-start(bf16[192,4096]{1,0:T(8,128)(2,1)} %get-tuple-element.76), channel_id=1, source_target_pairs={{0,1},{1,0},{2,3},{3,2},{4,5},{5,4},{6,7},{7,6},{8,9},{9,8},{10,11... | collective-permute-start | bytes 4718600 | tf_op jit(solution)/shard_map/ppermute | solution.py:373
  271.4 16.4 %collective-permute-start.17 = (bf16[192,4096]{1,0:T(8,128)(2,1)}, bf16[192,4096]{1,0:T(8,128)(2,1)S(1)}, u32[]{:S(2)}, u32[]{:S(2)}) collective-permute-start(bf16[192,4096]{1,0:T(8,128)(2,1)} %get-tuple-element.78), channel_id=1, source_target_pairs={{0,1},{1,0},{2,3},{3,2},{4,5},{5,4},{6,7},{7,6},{8,9},{9,8},{10,11... | collective-permute-start | bytes 4718600 | tf_op jit(solution)/shard_map/ppermute | solution.py:373
  273.4 3.7 %collective-permute-start.19 = (bf16[8,4224]{1,0:T(8,128)(2,1)S(1)}, bf16[8,4224]{1,0:T(8,128)(2,1)S(1)}, u32[]{:S(2)}, u32[]{:S(2)}) collective-permute-start(bf16[8,4224]{1,0:T(8,128)(2,1)S(1)} %constant_dynamic-update-slice_fusion.refs_0_), channel_id=1, source_target_pairs={{0,2},{1,3},{2,0},{3,1},{4,6},{5,7},{6,4},{7,5},{8,10},{9,11},{10,... | collective-permute-start | bytes 202760 | tf_op jit(solution)/shard_map/ppermute | solution.py:373
  273.4 5.3 %collective-permute-start.20 = (bf16[8,4224]{1,0:T(8,128)(2,1)S(1)}, bf16[8,4224]{1,0:T(8,128)(2,1)S(1)}, u32[]{:S(2)}, u32[]{:S(2)}) collective-permute-start(bf16[8,4224]{1,0:T(8,128)(2,1)S(1)} %constant_dynamic-update-slice_fusion.refs_0_), channel_id=1, source_target_pairs={{0,3},{1,2},{2,1},{3,0},{4,7},{5,6},{6,5},{7,4},{8,11},{9,10},{10,... | collective-permute-start | bytes 202760 | tf_op jit(solution)/shard_map/ppermute | solution.py:373
  281.1 3.6 %collective-permute-start.21 = (bf16[8,4224]{1,0:T(8,128)(2,1)}, bf16[8,4224]{1,0:T(8,128)(2,1)S(1)}, u32[]{:S(2)}, u32[]{:S(2)}) collective-permute-start(bf16[8,4224]{1,0:T(8,128)(2,1)} %add_totals.1.rest_0_.rest_4_), channel_id=1, source_target_pairs={{0,4},{1,5},{2,6},{3,7},{4,0},{5,1},{6,2},{7,3},{8,12},{9,13},{10,... | collective-permute-start | bytes 202760 | tf_op jit(solution)/shard_map/ppermute | solution.py:373
  281.6 4.3 %collective-permute-start.22 = (bf16[8,4224]{1,0:T(8,128)(2,1)}, bf16[8,4224]{1,0:T(8,128)(2,1)S(1)}, u32[]{:S(2)}, u32[]{:S(2)}) collective-permute-start(bf16[8,4224]{1,0:T(8,128)(2,1)} %add_totals.1.rest_0_.rest_4_), channel_id=1, source_target_pairs={{0,8},{1,9},{2,10},{3,11},{4,12},{5,13},{6,14},{7,15},{8,0},{9,1},... | collective-permute-start | bytes 202760 | tf_op jit(solution)/shard_map/ppermute | solution.py:373
  281.6 6.2 %collective-permute-start.23 = (bf16[8,4224]{1,0:T(8,128)(2,1)}, bf16[8,4224]{1,0:T(8,128)(2,1)S(1)}, u32[]{:S(2)}, u32[]{:S(2)}) collective-permute-start(bf16[8,4224]{1,0:T(8,128)(2,1)} %add_totals.1.rest_0_.rest_4_), channel_id=1, source_target_pairs={{0,12},{1,13},{2,14},{3,15},{4,8},{5,9},{6,10},{7,11},{8,4},{9,5},... | collective-permute-start | bytes 202760 | tf_op jit(solution)/shard_map/ppermute | solution.py:373
  (17 other events, 189.7 us)
Sparse Core Ops, SparseCore 0:
  52.9 88.9 all-reduce.2

commit v17 on v16

--- a/solution.py
+++ b/solution.py
@@ -8,7 +8,7 @@
 from jax.sharding import PartitionSpec as P
 
 off_weight = 0.0051
-tiles = 4
+tiles = 2
 vmem = 56 * 1024 * 1024
 strip = 16
 

time: 307 us -> 305 us (level)
  Pallas kernels: 89.9 us -> 86.6 us
where the time goes in v17:
time: 305 us; the launch traced here: 302 us
  waiting for transfers between devices  159 us (52%)
  Pallas kernels  86.6 us (28%)
  starting transfers between devices  26.5 us (9%)
  between operations  14.2 us (5%)
  other arithmetic  8.5 us (3%)
  local copies, waits for them, and re-layouts  7.27 us (2%)
    ppermute x6, waiting for transfers between devices, ring_shards(): lax.ppermute(up, 'batch', ahead)  107 us
    pallas_call x5, Pallas kernels, attend(): pl.pallas_call(functools.partial(attend_kernel, count, begins, ends), gri...  74.1 us
    psum x1, waiting for transfers between devices, ring_shards(): sums = lax.psum(tuple((sums[row] for row in range(4))), 'batch')  28.1 us
    ppermute x1, waiting for transfers between devices, ring_shards(): last_one = lax.ppermute(ends[0][0], 'batch', ahead)  15.3 us
    ppermute x10, starting transfers between devices, swapped(): return lax.ppermute(value, 'batch', [(i, i ^ bit) for i in range(batches)])  12.7 us
    ppermute x10, waiting for transfers between devices, swapped(): return lax.ppermute(value, 'batch', [(i, i ^ bit) for i in range(batches)])  6.77 us
    ppermute x6, starting transfers between devices, ring_shards(): lax.ppermute(up, 'batch', ahead)  6.75 us
    pallas_call x1, Pallas kernels, finish_grads(): pl.pallas_call(functools.partial(finish_kernel, samples, width), grid=(ti...  6.15 us
  transfers between devices with their start and end apart: 25, of which 11 were waited for; matrix products, arithmetic and copies ran while one was open for 4% of the time, Pallas kernels for 23%

profile of v17, /device:TPU:1, one launch (start us, length us, event | category | flops | bytes accessed | tf_op | source)
XLA Modules:
  0.0 301.7 jit_solution(3300888086352875995)
XLA Ops:
  7.2 2.2 collective-permute-start
  10.9 32.9 %collective-permute-done.refs_3_ = bf16[192,4096]{1,0:T(8,128)(2,1)} collective-permute-done((bf16[192,4096]{1,0:T(8,128)(2,1)}, bf16[192,4096]{1,0:T(8,128)(2,1)}, u32[]{:S(2)}, u32[]{:S(2)}) %collective-permute-start) | collective-permute-done | bytes 1572896 | tf_op jit(solution)/shard_map/ppermute | solution.py:417
  45.0 3.0 collective-permute-start.9
  48.0 3.2 %first_sums.1 = f32[4,4096]{1,0:T(4,128)} custom-call(bf16[192,4096]{1,0:T(8,128)(2,1)} %refs_3_.1, bf16[192,4096]{1,0:T(8,128)(2,1)} %refs_4_.1), custom_call_target="tpu_custom_call" | custom-call | flops 4096 | bytes 4096 | tf_op jit(solution)/shard_map/first_sums/pallas_call | solution.py:112
  51.1 1.7 fusion.1
  52.9 25.0 %collective-permute-done.4.refs_5_ = bf16[192,4096]{1,0:T(8,128)(2,1)} collective-permute-done((bf16[192,4096]{1,0:T(8,128)(2,1)}, bf16[192,4096]{1,0:T(8,128)(2,1)}, u32[]{:S(2)}, u32[]{:S(2)}) %collective-permute-start.4) | collective-permute-done | bytes 1572896 | tf_op jit(solution)/shard_map/ppermute | solution.py:417
  80.4 31.5 %collective-permute-done.1.refs_3_ = bf16[192,4096]{1,0:T(8,128)(2,1)} collective-permute-done((bf16[192,4096]{1,0:T(8,128)(2,1)}, bf16[192,4096]{1,0:T(8,128)(2,1)}, u32[]{:S(2)}, u32[]{:S(2)}) %collective-permute-start.1) | collective-permute-done | bytes 1572896 | tf_op jit(solution)/shard_map/ppermute | solution.py:417
  111.8 1.9 collective-permute-start.7
  113.8 28.1 %all-reduce.3.cloned.1.call-done = (f32[4096]{0:T(1024)}, f32[4096]{0:T(1024)}, f32[4096]{0:T(1024)}, f32[4096]{0:T(1024)}) async-done(((f32[4096]{0:T(1024)}, f32[4096]{0:T(1024)}, f32[4096]{0:T(1024)}, f32[4096]{0:T(1024)}), (f32[4096]{0:T(1024)}, f32[4096]{0:T(1024)}, f32[4096]{0:T(1024)}, f32[4096]{0:T(1024)})) %all-reduce.3.cloned.1.call-update) | async-done | bytes 65552 | tf_op jit(solution)/shard_map/psum | solution.py:391
  144.2 3.9 %multiply_convert_fusion.1.refs_0_.norm_one = bf16[384,4096]{1,0:T(8,128)(2,1)S(1)} fusion(bf16[192,4096]{1,0:T(8,128)(2,1)} %collective-permute-done.8, bf16[192,4096]{1,0:T(8,128)(2,1)} %refs_3_.1, f32[4096]{0:T(1024)S(1)} %get-tuple-element.95, f32[4096]{0:T(1024)S(1)} %get-tuple-element.94), kind=kLoop, calls=%fused_computation.1 | loop fusion | flops 11010048 | bytes 6324224 | tf_op jit(solution)/shard_map/convert_element_type | solution.py:388
  154.1 11.2 %attend.5 = (f32[8,128]{1,0:T(8,128)}, f32[384,4096]{1,0:T(8,128)}, f32[384,4096]{1,0:T(8,128)}) custom-call(bf16[384,4096]{1,0:T(8,128)(2,1)} %copy-done.1, bf16[384,4096]{1,0:T(8,128)(2,1)} %copy-done, f32[4,4096]{1,0:T(4,128)} %pad_maximum_fusion.refs_2_.stat_ref, bf16[192,4096]{1,0:T(8,128)(2,1)} %refs_3_.1, ...), custom_call_target="tpu_custom_call", output_to_operand_aliasing={{0}: (5, {})} | custom-call | flops 4096 | bytes 4096 | tf_op jit(solution)/shard_map/attend/pallas_call | solution.py:276
  165.3 17.2 %attend.6 = (f32[8,128]{1,0:T(8,128)}, f32[384,4096]{1,0:T(8,128)}, f32[384,4096]{1,0:T(8,128)}) custom-call(bf16[384,4096]{1,0:T(8,128)(2,1)} %copy-done.1, bf16[384,4096]{1,0:T(8,128)(2,1)} %copy-done, f32[4,4096]{1,0:T(4,128)} %pad_maximum_fusion.refs_2_.stat_ref, ...), custom_call_target="tpu_custom_call", output_to_operand_aliasing={{0}: (7, {}), {1}: (8, {}), {2}: (9, {})} | custom-call | flops 4096 | bytes 4096 | tf_op jit(solution)/shard_map/attend/pallas_call | solution.py:276
  182.5 16.9 %attend.7 = (f32[8,128]{1,0:T(8,128)}, f32[384,4096]{1,0:T(8,128)}, f32[384,4096]{1,0:T(8,128)}) custom-call(bf16[384,4096]{1,0:T(8,128)(2,1)} %copy-done.1, bf16[384,4096]{1,0:T(8,128)(2,1)} %copy-done, f32[4,4096]{1,0:T(4,128)} %pad_maximum_fusion.refs_2_.stat_ref, ...), custom_call_target="tpu_custom_call", output_to_operand_aliasing={{0}: (7, {}), {1}: (8, {}), {2}: (9, {})} | custom-call | flops 4096 | bytes 4096 | tf_op jit(solution)/shard_map/attend/pallas_call | solution.py:276
  201.0 17.7 %collective-permute-done.12.refs_5_ = bf16[192,4096]{1,0:T(8,128)(2,1)} collective-permute-done((bf16[192,4096]{1,0:T(8,128)(2,1)}, bf16[192,4096]{1,0:T(8,128)(2,1)}, u32[]{:S(2)}, u32[]{:S(2)}) %collective-permute-start.12) | collective-permute-done | bytes 1572896 | tf_op jit(solution)/shard_map/ppermute | solution.py:417
  220.2 16.3 %attend.8 = (f32[8,128]{1,0:T(8,128)}, bf16[384,4096]{1,0:T(8,128)(2,1)}, bf16[384,4096]{1,0:T(8,128)(2,1)}) custom-call(bf16[384,4096]{1,0:T(8,128)(2,1)} %copy-done.1, bf16[384,4096]{1,0:T(8,128)(2,1)} %copy-done, f32[4,4096]{1,0:T(4,128)} %pad_maximum_fusion.refs_2_.stat_ref, bf16[192,4096]{1,0:T(8,128)(2,1)} %copy-done.7, ...), custom_call_target="tpu_custom_call", output_to_operand_aliasing={{0}: (7, {})} | custom-call | flops 4096 | bytes 4096 | tf_op jit(solution)/shard_map/attend/pallas_call | solution.py:276
  236.5 15.3 %collective-permute-done.14.refs_3_ = bf16[192,4096]{1,0:T(8,128)(2,1)S(1)} collective-permute-done((bf16[192,4096]{1,0:T(8,128)(2,1)S(1)}, bf16[192,4096]{1,0:T(8,128)(2,1)S(1)}, u32[]{:S(2)}, u32[]{:S(2)}) %collective-permute-start.14) | collective-permute-done | bytes 1572896 | tf_op jit(solution)/shard_map/ppermute | solution.py:422
  254.2 12.4 %attend.9 = (f32[8,128]{1,0:T(8,128)}, bf16[192,4096]{1,0:T(8,128)(2,1)}, bf16[192,4096]{1,0:T(8,128)(2,1)}, bf16[192,4096]{1,0:T(8,128)(2,1)}, bf16[192,4096]{1...) custom-call(bf16[384,4096]{1,0:T(8,128)(2,1)} %copy-done.1, ...), custom_call_target="tpu_custom_call", output_to_operand_aliasing={{0}: (5, {})} | custom-call | flops 4096 | bytes 4096 | tf_op jit(solution)/shard_map/attend/pallas_call | solution.py:276
  266.6 4.0 %collective-permute-start.16 = (bf16[192,4096]{1,0:T(8,128)(2,1)}, bf16[192,4096]{1,0:T(8,128)(2,1)S(1)}, u32[]{:S(2)}, u32[]{:S(2)}) collective-permute-start(bf16[192,4096]{1,0:T(8,128)(2,1)} %get-tuple-element.76), channel_id=1, source_target_pairs={{0,1},{1,0},{2,3},{3,2},{4,5},{5,4},{6,7},{7,6},{8,9},{9,8},{10,11... | collective-permute-start | bytes 4718600 | tf_op jit(solution)/shard_map/ppermute | solution.py:373
  272.7 1.7 collective-permute-start.20
  274.4 2.0 collective-permute-done.19.refs_2_
  278.6 1.7 add_totals.1.rest_0_.rest_4_
  280.8 3.0 %collective-permute-start.23 = (bf16[8,4224]{1,0:T(8,128)(2,1)}, bf16[8,4224]{1,0:T(8,128)(2,1)S(1)}, u32[]{:S(2)}, u32[]{:S(2)}) collective-permute-start(bf16[8,4224]{1,0:T(8,128)(2,1)} %add_totals.1.rest_0_.rest_4_), channel_id=1, source_target_pairs={{0,12},{1,13},{2,14},{3,15},{4,8},{5,9},{6,10},{7,11},{8,4},{9,5},... | collective-permute-start | bytes 202760 | tf_op jit(solution)/shard_map/ppermute | solution.py:373
  285.2 1.9 collective-permute-done.23.rest_3_.rest_7_
  288.7 6.2 %finish.1 = (bf16[192,4096]{1,0:T(8,128)(2,1)}, bf16[192,4096]{1,0:T(8,128)(2,1)}, f32[1]{0:T(128)}) custom-call(bf16[192,4096]{1,0:T(8,128)(2,1)} %get-tuple-element.75.own_one, bf16[192,4096]{1,0:T(8,128)(2,1)} %copy-done.3, bf16[192,4096]{1,0:T(8,128)(2,1)} %get-tuple-element.77.own_two, bf16[192,4096]{1,0:T(8,128)(2,1)} %copy-done.4, ...), custom_call_target="tpu_custom_call" | custom-call | flops 4096 | bytes 4096 | tf_op jit(solution)/shard_map/finish/pallas_call | solution.py:344
  (80 shorter events, 26.6 us)
Async XLA Ops:
  7.2 134.7 %all-reduce.3.cloned.1.call-start = ((), (), s32[]{:S(2)}) async-start(), calls=%async_computation | async-start | bytes 131072 | tf_op jit(solution)/shard_map/psum | solution.py:391
  7.2 36.6 %collective-permute-start = (bf16[192,4096]{1,0:T(8,128)(2,1)}, bf16[192,4096]{1,0:T(8,128)(2,1)}, u32[]{:S(2)}, u32[]{:S(2)}) collective-permute-start(bf16[192,4096]{1,0:T(8,128)(2,1)} %refs_3_.1), channel_id=1, source_target_pairs={{0,4},{1,5},{4,8},{5,9},{8,12},{9,13},{12,14},{13,15},{14,10},{15,... | collective-permute-start | bytes 4718600 | tf_op jit(solution)/shard_map/ppermute | solution.py:417
  9.4 41.7 %collective-permute-start.2 = (bf16[192,4096]{1,0:T(8,128)(2,1)}, bf16[192,4096]{1,0:T(8,128)(2,1)}, u32[]{:S(2)}, u32[]{:S(2)}) collective-permute-start(bf16[192,4096]{1,0:T(8,128)(2,1)} %refs_3_.1), channel_id=1, source_target_pairs={{4,0},{5,1},{8,4},{9,5},{12,8},{13,9},{14,12},{15,13},{10,14},{11,... | collective-permute-start | bytes 4718600 | tf_op jit(solution)/shard_map/ppermute | solution.py:417
  9.4 68.5 %collective-permute-start.4 = (bf16[192,4096]{1,0:T(8,128)(2,1)}, bf16[192,4096]{1,0:T(8,128)(2,1)}, u32[]{:S(2)}, u32[]{:S(2)}) collective-permute-start(bf16[192,4096]{1,0:T(8,128)(2,1)} %refs_4_.1), channel_id=1, source_target_pairs={{0,4},{1,5},{4,8},{5,9},{8,12},{9,13},{12,14},{13,15},{14,10},{15,... | collective-permute-start | bytes 4718600 | tf_op jit(solution)/shard_map/ppermute | solution.py:417
  10.9 68.5 %collective-permute-start.6 = (bf16[192,4096]{1,0:T(8,128)(2,1)}, bf16[192,4096]{1,0:T(8,128)(2,1)}, u32[]{:S(2)}, u32[]{:S(2)}) collective-permute-start(bf16[192,4096]{1,0:T(8,128)(2,1)} %refs_4_.1), channel_id=1, source_target_pairs={{4,0},{5,1},{8,4},{9,5},{12,8},{13,9},{14,12},{15,13},{10,14},{11,... | collective-permute-start | bytes 4718600 | tf_op jit(solution)/shard_map/ppermute | solution.py:417
  43.8 68.1 %collective-permute-start.1 = (bf16[192,4096]{1,0:T(8,128)(2,1)}, bf16[192,4096]{1,0:T(8,128)(2,1)}, u32[]{:S(2)}, u32[]{:S(2)}) collective-permute-start(bf16[192,4096]{1,0:T(8,128)(2,1)} %collective-permute-done.refs_3_), channel_id=1, source_target_pairs={{0,4},{1,5},{4,8},{5,9},{8,12},{9,13},{12,14},{13,15},{14,10},{15,... | collective-permute-start | bytes 4718600 | tf_op jit(solution)/shard_map/ppermute | solution.py:417
  45.0 98.4 %collective-permute-start.9 = (bf16[192,4096]{1,0:T(8,128)(2,1)}, bf16[192,4096]{1,0:T(8,128)(2,1)S(1)}, u32[]{:S(2)}, u32[]{:S(2)}) collective-permute-start(bf16[192,4096]{1,0:T(8,128)(2,1)} %refs_4_.1), channel_id=1, source_target_pairs={{0,1},{1,0},{2,3},{3,2},{4,5},{5,4},{6,7},{7,6},{8,9},{9,8},{10,11... | collective-permute-start | bytes 4718600 | tf_op jit(solution)/shard_map/ppermute | solution.py:373
  51.1 93.1 %collective-permute-start.8 = (bf16[192,4096]{1,0:T(8,128)(2,1)}, bf16[192,4096]{1,0:T(8,128)(2,1)}, u32[]{:S(2)}, u32[]{:S(2)}) collective-permute-start(bf16[192,4096]{1,0:T(8,128)(2,1)} %refs_3_.1), channel_id=1, source_target_pairs={{0,1},{1,0},{2,3},{3,2},{4,5},{5,4},{6,7},{7,6},{8,9},{9,8},{10,11... | collective-permute-start | bytes 4718600 | tf_op jit(solution)/shard_map/ppermute | solution.py:373
  77.9 71.9 %collective-permute-start.3 = (bf16[192,4096]{1,0:T(8,128)(2,1)}, bf16[192,4096]{1,0:T(8,128)(2,1)}, u32[]{:S(2)}, u32[]{:S(2)}) collective-permute-start(bf16[192,4096]{1,0:T(8,128)(2,1)} %collective-permute-done.2.refs_4_), channel_id=1, source_target_pairs={{4,0},{5,1},{8,4},{9,5},{12,8},{13,9},{14,12},{15,13},{10,14},{11,... | collective-permute-start | bytes 4718600 | tf_op jit(solution)/shard_map/ppermute | solution.py:417
  79.3 70.5 %collective-permute-start.5 = (bf16[192,4096]{1,0:T(8,128)(2,1)}, bf16[192,4096]{1,0:T(8,128)(2,1)}, u32[]{:S(2)}, u32[]{:S(2)}) collective-permute-start(bf16[192,4096]{1,0:T(8,128)(2,1)} %collective-permute-done.4.refs_5_), channel_id=1, source_target_pairs={{0,4},{1,5},{4,8},{5,9},{8,12},{9,13},{12,14},{13,15},{14,10},{15,... | collective-permute-start | bytes 4718600 | tf_op jit(solution)/shard_map/ppermute | solution.py:417
  111.8 38.0 %collective-permute-start.7 = (bf16[192,4096]{1,0:T(8,128)(2,1)}, bf16[192,4096]{1,0:T(8,128)(2,1)}, u32[]{:S(2)}, u32[]{:S(2)}) collective-permute-start(bf16[192,4096]{1,0:T(8,128)(2,1)} %collective-permute-done.6.refs_6_), channel_id=1, source_target_pairs={{4,0},{5,1},{8,4},{9,5},{12,8},{13,9},{14,12},{15,13},{10,14},{11,... | collective-permute-start | bytes 4718600 | tf_op jit(solution)/shard_map/ppermute | solution.py:417
  149.8 51.1 %collective-permute-start.10 = (bf16[192,4096]{1,0:T(8,128)(2,1)}, bf16[192,4096]{1,0:T(8,128)(2,1)S(1)}, u32[]{:S(2)}, u32[]{:S(2)}) collective-permute-start(bf16[192,4096]{1,0:T(8,128)(2,1)} %collective-permute-done.1.refs_3_), channel_id=1, source_target_pairs={{0,4},{1,5},{4,8},{5,9},{8,12},{9,13},{12,14},{13,15},{14,10},{15,... | collective-permute-start | bytes 4718600 | tf_op jit(solution)/shard_map/ppermute | solution.py:417
  149.9 51.1 %collective-permute-start.11 = (bf16[192,4096]{1,0:T(8,128)(2,1)}, bf16[192,4096]{1,0:T(8,128)(2,1)}, u32[]{:S(2)}, u32[]{:S(2)}) collective-permute-start(bf16[192,4096]{1,0:T(8,128)(2,1)} %collective-permute-done.3.refs_4_), channel_id=1, source_target_pairs={{4,0},{5,1},{8,4},{9,5},{12,8},{13,9},{14,12},{15,13},{10,14},{11,... | collective-permute-start | bytes 4718600 | tf_op jit(solution)/shard_map/ppermute | solution.py:417
  151.3 67.3 %collective-permute-start.12 = (bf16[192,4096]{1,0:T(8,128)(2,1)}, bf16[192,4096]{1,0:T(8,128)(2,1)}, u32[]{:S(2)}, u32[]{:S(2)}) collective-permute-start(bf16[192,4096]{1,0:T(8,128)(2,1)} %collective-permute-done.5.refs_5_), channel_id=1, source_target_pairs={{0,4},{1,5},{4,8},{5,9},{8,12},{9,13},{12,14},{13,15},{14,10},{15,... | collective-permute-start | bytes 4718600 | tf_op jit(solution)/shard_map/ppermute | solution.py:417
  152.2 66.5 %collective-permute-start.13 = (bf16[192,4096]{1,0:T(8,128)(2,1)}, bf16[192,4096]{1,0:T(8,128)(2,1)S(1)}, u32[]{:S(2)}, u32[]{:S(2)}) collective-permute-start(bf16[192,4096]{1,0:T(8,128)(2,1)} %collective-permute-done.7.refs_6_), channel_id=1, source_target_pairs={{4,0},{5,1},{8,4},{9,5},{12,8},{13,9},{14,12},{15,13},{10,14},{11,... | collective-permute-start | bytes 4718600 | tf_op jit(solution)/shard_map/ppermute | solution.py:417
  218.7 33.1 %collective-permute-start.14 = (bf16[192,4096]{1,0:T(8,128)(2,1)S(1)}, bf16[192,4096]{1,0:T(8,128)(2,1)S(1)}, u32[]{:S(2)}, u32[]{:S(2)}) collective-permute-start(bf16[192,4096]{1,0:T(8,128)(2,1)S(1)} %collective-permute-done.10.refs_3_), channel_id=1, source_target_pairs={{0,4},{1,5},{4,8},{5,9},{8,12},{9,13},{12,14},{13,15},{14,10},{15,... | collective-permute-start | bytes 4718600 | tf_op jit(solution)/shard_map/ppermute | solution.py:422
  220.2 32.9 %collective-permute-start.15 = (bf16[192,4096]{1,0:T(8,128)(2,1)S(1)}, bf16[192,4096]{1,0:T(8,128)(2,1)S(1)}, u32[]{:S(2)}, u32[]{:S(2)}) collective-permute-start(bf16[192,4096]{1,0:T(8,128)(2,1)S(1)} %collective-permute-done.13.refs_6_), channel_id=1, source_target_pairs={{4,0},{5,1},{8,4},{9,5},{12,8},{13,9},{14,12},{15,13},{10,14},{11,... | collective-permute-start | bytes 4718600 | tf_op jit(solution)/shard_map/ppermute | solution.py:423
  266.6 20.4 %collective-permute-start.16 = (bf16[192,4096]{1,0:T(8,128)(2,1)}, bf16[192,4096]{1,0:T(8,128)(2,1)S(1)}, u32[]{:S(2)}, u32[]{:S(2)}) collective-permute-start(bf16[192,4096]{1,0:T(8,128)(2,1)} %get-tuple-element.76), channel_id=1, source_target_pairs={{0,1},{1,0},{2,3},{3,2},{4,5},{5,4},{6,7},{7,6},{8,9},{9,8},{10,11... | collective-permute-start | bytes 4718600 | tf_op jit(solution)/shard_map/ppermute | solution.py:373
  270.6 16.4 %collective-permute-start.17 = (bf16[192,4096]{1,0:T(8,128)(2,1)}, bf16[192,4096]{1,0:T(8,128)(2,1)S(1)}, u32[]{:S(2)}, u32[]{:S(2)}) collective-permute-start(bf16[192,4096]{1,0:T(8,128)(2,1)} %get-tuple-element.78), channel_id=1, source_target_pairs={{0,1},{1,0},{2,3},{3,2},{4,5},{5,4},{6,7},{7,6},{8,9},{9,8},{10,11... | collective-permute-start | bytes 4718600 | tf_op jit(solution)/shard_map/ppermute | solution.py:373
  272.6 3.7 %collective-permute-start.19 = (bf16[8,4224]{1,0:T(8,128)(2,1)S(1)}, bf16[8,4224]{1,0:T(8,128)(2,1)S(1)}, u32[]{:S(2)}, u32[]{:S(2)}) collective-permute-start(bf16[8,4224]{1,0:T(8,128)(2,1)S(1)} %constant_dynamic-update-slice_fusion.refs_0_), channel_id=1, source_target_pairs={{0,2},{1,3},{2,0},{3,1},{4,6},{5,7},{6,4},{7,5},{8,10},{9,11},{10,... | collective-permute-start | bytes 202760 | tf_op jit(solution)/shard_map/ppermute | solution.py:373
  272.7 5.3 %collective-permute-start.20 = (bf16[8,4224]{1,0:T(8,128)(2,1)S(1)}, bf16[8,4224]{1,0:T(8,128)(2,1)S(1)}, u32[]{:S(2)}, u32[]{:S(2)}) collective-permute-start(bf16[8,4224]{1,0:T(8,128)(2,1)S(1)} %constant_dynamic-update-slice_fusion.refs_0_), channel_id=1, source_target_pairs={{0,3},{1,2},{2,1},{3,0},{4,7},{5,6},{6,5},{7,4},{8,11},{9,10},{10,... | collective-permute-start | bytes 202760 | tf_op jit(solution)/shard_map/ppermute | solution.py:373
  280.3 3.6 %collective-permute-start.21 = (bf16[8,4224]{1,0:T(8,128)(2,1)}, bf16[8,4224]{1,0:T(8,128)(2,1)S(1)}, u32[]{:S(2)}, u32[]{:S(2)}) collective-permute-start(bf16[8,4224]{1,0:T(8,128)(2,1)} %add_totals.1.rest_0_.rest_4_), channel_id=1, source_target_pairs={{0,4},{1,5},{2,6},{3,7},{4,0},{5,1},{6,2},{7,3},{8,12},{9,13},{10,... | collective-permute-start | bytes 202760 | tf_op jit(solution)/shard_map/ppermute | solution.py:373
  280.8 4.3 %collective-permute-start.22 = (bf16[8,4224]{1,0:T(8,128)(2,1)}, bf16[8,4224]{1,0:T(8,128)(2,1)S(1)}, u32[]{:S(2)}, u32[]{:S(2)}) collective-permute-start(bf16[8,4224]{1,0:T(8,128)(2,1)} %add_totals.1.rest_0_.rest_4_), channel_id=1, source_target_pairs={{0,8},{1,9},{2,10},{3,11},{4,12},{5,13},{6,14},{7,15},{8,0},{9,1},... | collective-permute-start | bytes 202760 | tf_op jit(solution)/shard_map/ppermute | solution.py:373
  280.8 6.2 %collective-permute-start.23 = (bf16[8,4224]{1,0:T(8,128)(2,1)}, bf16[8,4224]{1,0:T(8,128)(2,1)S(1)}, u32[]{:S(2)}, u32[]{:S(2)}) collective-permute-start(bf16[8,4224]{1,0:T(8,128)(2,1)} %add_totals.1.rest_0_.rest_4_), channel_id=1, source_target_pairs={{0,12},{1,13},{2,14},{3,15},{4,8},{5,9},{6,10},{7,11},{8,4},{9,5},... | collective-permute-start | bytes 202760 | tf_op jit(solution)/shard_map/ppermute | solution.py:373
  (17 other events, 191.5 us)
Sparse Core Ops, SparseCore 0:
  52.9 88.9 all-reduce.2
